TPU v7x, 32 devices: a whole 2x2x4 slice. The times are simulated.
32 devices in a mesh: chan: 8 (over y, x, core), hour: 4 (over z).
Axes of the slice: x: 2, y: 2, z: 4, core: 2. Of those that a mesh axis runs over, the one named last changes fastest.
Arguments:
- spectra: bfloat16 [2, 64, 800, 1024], P(None, 'hour', None, 'chan'), may hold values from -6 to 6
- quality: int32 [64, 1024], P('hour', 'chan'), may hold values 0 or 1
- sources: int32 [32], replicated, may hold values from 0 to 1023
Outputs:
- correlation: bfloat16 [32, 512, 1024], P('hour', None, 'chan')
Inputs may be any that keep to these rules, and one draw needn't show every extreme that they name: `sources`: indices may repeat.
All inputs are finite; a program needn't handle non-finite values. No bound on the sum of `quality` on one device may be relied on, other than what follows from the above.
Results may differ from a plain program's by a relative error of at most 0.01.
Values may be sent and summed in bfloat16 or wider, within the bound.
No kernel may reach another device: no remote copies, remote signals or barrier semaphores. Data moves between devices by JAX's collectives and lax.ppermute only.
A program may use at most 128 MiB of HBM per device.

v0:
```python
import math

import jax
import jax.numpy as jnp
from jax import lax
from jax.sharding import PartitionSpec as P

LAGS = 512


def whiten(record, usable):
    as_float = record.astype(jnp.float32)
    power = jnp.mean(as_float[0] * as_float[0] + as_float[1] * as_float[1], axis=1)
    scale = lax.rsqrt(power + 1e-06) * usable.astype(jnp.float32)
    return (as_float * scale[None, :, None, :]).astype(jnp.bfloat16)


def lag_table(freq_count, lag_count):
    bin_number = jnp.arange(freq_count, dtype=jnp.float32) + 1.0
    lag_offset = jnp.arange(lag_count, dtype=jnp.float32) - float(lag_count // 2)
    phase = math.pi * bin_number[:, None] * lag_offset[None, :] / freq_count
    return (jnp.stack([jnp.cos(phase), -jnp.sin(phase)]) / freq_count).astype(jnp.bfloat16)


def cross_spectrum(source_spec, receivers):
    real_part = jnp.einsum(
        "kwfs,kwfc->fsc", source_spec, receivers, preferred_element_type=jnp.float32
    )
    left_pair = jnp.stack([source_spec[0], -source_spec[1]])
    right_pair = jnp.stack([receivers[1], receivers[0]])
    imag_part = jnp.einsum(
        "kwfs,kwfc->fsc", left_pair, right_pair, preferred_element_type=jnp.float32
    )
    return jnp.stack([real_part, imag_part]).astype(jnp.bfloat16)


def body(spectra, quality, sources):
    channels_here = spectra.shape[3]
    freq_count = spectra.shape[2]
    whitened = whiten(spectra, quality)
    local_index = sources - lax.axis_index("chan") * channels_here
    onehot = (jnp.arange(channels_here, dtype=jnp.int32)[:, None] == local_index[None, :]).astype(
        jnp.bfloat16
    )
    picked = jnp.einsum("kwfc,cs->kwfs", whitened, onehot, preferred_element_type=jnp.float32)
    source_spec = lax.psum(picked, "chan").astype(jnp.bfloat16)
    partial_value = cross_spectrum(source_spec, whitened)
    table = lag_table(freq_count, LAGS)
    correlation = lax.psum_scatter(
        jnp.einsum("kfsc,kfl->slc", partial_value, table, preferred_element_type=jnp.float32),
        "hour",
        scatter_dimension=0,
        tiled=True,
    )
    return correlation.astype(jnp.bfloat16)


def solution(mesh):
    placed = (P(None, "hour", None, "chan"), P("hour", "chan"), P())
    return jax.shard_map(
        body, mesh=mesh, in_specs=placed, out_specs=P("hour", None, "chan"), check_vma=False
    )
```

profile of v0, /device:TPU:16, one launch (start us, length us, event | category | flops | bytes accessed | tf_op | source)
XLA Modules:
  0.0 349.0 jit_solution(7770510937242613012)
XLA Ops:
  6.5 0.0 reduce-scatter.2.cloned.1.call-start
  6.6 5.0 %copy_convert_fusion = f32[2,16,800,128]{3,1,0,2:T(8,128)S(1)} fusion(bf16[2,16,800,128]{3,2,1,0:T(8,128)(2,1)} %param.3), kind=kLoop, calls=%fused_computation.15 | loop fusion | flops 3276800 | bytes 19660800 | tf_op jit(solution)/shard_map/convert_element_type | solution.py:12
  11.5 0.0 copy-start.4
  11.5 0.9 fusion.3
  12.4 0.0 copy-done.4
  12.5 0.0 copy-start.5
  12.5 8.2 %multiply_convert_fusion = bf16[2,16,800,128]{3,1,0,2:T(8,128)(2,1)} fusion(f32[16,128]{1,0:T(8,128)S(1)} %convert_multiply_fusion, bf16[2,16,800,128]{3,2,1,0:T(8,128)(2,1)} %param.3), kind=kLoop, calls=%fused_computation.5 | loop fusion | flops 9830400 | bytes 13115392 | tf_op jit(solution)/shard_map/convert_element_type | solution.py:15
  20.6 0.0 copy-done.5
  20.6 11.3 %fusion.7 = f32[2,16,800,32]{2,3,1,0:T(8,128)} fusion(bf16[2,16,800,128]{3,1,0,2:T(8,128)(2,1)} %multiply_convert_fusion, s32[32]{0:T(128)S(1)} %broadcast_subtract_fusion), kind=kOutput, calls=%fused_computation.13 | convolution fusion | flops 209719296 | bytes 9830528 | tf_op jit(solution)/shard_map/kwfc,cs->kwfs/dot_general | solution.py:45
  31.9 77.8 %all-reduce.1 = bf16[2,16,800,32]{2,3,1,0:T(8,128)(2,1)S(1)} all-reduce(f32[2,16,800,32]{2,3,1,0:T(8,128)} %fusion.7), channel_id=1, replica_groups=mesh['chan'=8,'hour'=4] {'chan'}, use_global_device_ids=true, to_apply=%region_1.0 | all-reduce | flops 819200 | bytes 4915200 | tf_op jit(solution)/shard_map/psum | solution.py:46
  109.7 1.4 fusion.28
  111.0 10.3 %copy.6 = bf16[2,16,800,32]{3,1,0,2:T(8,128)(2,1)} copy(bf16[2,16,800,32]{2,3,1,0:T(8,128)(2,1)S(1)} %all-reduce.1) | data formatting | bytes 3276800 | tf_op jit(solution)/shard_map/convert_element_type | solution.py:46
  121.3 0.0 copy-start
  121.3 0.0 copy-start.1
  121.3 5.9 %fusion.27 = (bf16[1,16,800,128]{3,1,0,2:T(8,128)(2,1)S(1)}, bf16[1,16,800,128]{3,1,0,2:T(8,128)(2,1)}) fusion(bf16[2,16,800,128]{3,1,0,2:T(8,128)(2,1)} %multiply_convert_fusion), kind=kLoop, calls=%fused_computation.38 | loop fusion | bytes 13107200 | tf_op jit(solution)/shard_map/slice | solution.py:30
  127.2 0.0 copy-done
  127.2 0.0 copy-done.1
  127.2 1.5 pad_maximum_fusion.1
  128.7 10.9 %copy.7 = bf16[2,16,800,32]{3,1,0,2:T(8,128)(2,1)} copy(bf16[2,16,800,32]{2,3,1,0:T(8,128)(2,1)} %pad_maximum_fusion.1) | data formatting | bytes 3276800 | tf_op jit(solution)/shard_map/stack | solution.py:29
  139.6 9.8 %fusion.9 = bf16[1,800,32,128]{3,2,1,0:T(8,128)(2,1)} fusion(bf16[2,16,800,32]{3,1,0,2:T(8,128)(2,1)} %copy.6, bf16[2,16,800,128]{3,1,0,2:T(8,128)(2,1)} %multiply_convert_fusion), kind=kOutput, calls=%fused_computation.16 | convolution fusion | flops 212992000 | bytes 14745600 | tf_op jit(solution)/shard_map/kwfs,kwfc->fsc/dot_general | solution.py:26
  149.4 7.7 %fusion.20 = (f32[1,800,512]{2,1,0:T(8,128)}, f32[1,800,512]{2,1,0:T(8,128)}) fusion(f32[512]{0:T(512)S(1)} %iota_add_fusion, f32[800]{0:T(1024)S(1)} %add_multiply_fusion), kind=kLoop, calls=%fused_computation.26 | loop fusion | flops 1228800 | bytes 3282048 | tf_op jit(solution)/shard_map/cos | solution.py:22
  157.1 8.9 %fusion.10 = bf16[1,800,32,128]{3,2,1,0:T(8,128)(2,1)} fusion(bf16[2,16,800,32]{3,1,0,2:T(8,128)(2,1)} %copy.7, bf16[1,16,800,128]{3,1,0,2:T(8,128)(2,1)} %get-tuple-element.6, bf16[1,16,800,128]{3,1,0,2:T(8,128)(2,1)S(1)} %get-tuple-element.5), kind=kOutput, calls=%fused_computation.17 | convolution fusion | flops 216268800 | bytes 14745600 | tf_op jit(solution)/shard_map/kwfs,kwfc->fsc/dot_general | solution.py:31
  165.9 0.0 copy-start.2
  165.9 0.0 copy-start.3
  165.9 6.8 %pad_maximum_fusion = bf16[2,800,32,128]{3,2,1,0:T(8,128)(2,1)S(1)} fusion(bf16[1,800,32,128]{3,2,1,0:T(8,128)(2,1)} %fusion.10, bf16[1,800,32,128]{3,2,1,0:T(8,128)(2,1)} %fusion.9), kind=kLoop, calls=%fused_computation | loop fusion | flops 6553600 | bytes 26214400 | tf_op jit(solution)/shard_map/stack | solution.py:34
  172.7 0.0 copy-done.2
  172.7 0.0 copy-done.3
  172.7 21.3 %fusion.14 = f32[32,512,128]{2,1,0:T(8,128)} fusion(bf16[2,800,32,128]{3,2,1,0:T(8,128)(2,1)S(1)} %pad_maximum_fusion, f32[1,800,512]{2,1,0:T(8,128)S(1)} %copy-done.3, f32[1,800,512]{2,1,0:T(8,128)S(1)} %copy-done.2), kind=kOutput, calls=%fused_computation.20 | convolution fusion | flops 6713344000 | bytes 24772608 | tf_op jit(solution)/shard_map/kfsc,kfl->slc/dot_general | solution.py:50
  194.0 0.0 reduce-scatter.2.cloned.1.call-update
  194.1 145.4 %reduce-scatter.2.cloned.1.call-done = f32[8,512,128]{2,1,0:T(8,128)} async-done(((f32[32,512,128]{2,1,0:T(8,128)}), f32[8,512,128]{2,1,0:T(8,128)}) %reduce-scatter.2.cloned.1.call-update) | async-done | bytes 2097168 | tf_op jit(solution)/shard_map/reduce_scatter | solution.py:49
  339.4 2.7 convert_element_type.25
  (4 shorter events, 0.0 us)
Async XLA Ops:
  6.5 332.9 %reduce-scatter.2.cloned.1.call-start = ((), (), s32[]{:S(2)}) async-start(), calls=%async_computation.1 | async-start | bytes 10485760 | tf_op jit(solution)/shard_map/reduce_scatter | solution.py:49
  11.5 0.9 copy-start.4
  12.5 8.2 %copy-start.5 = (s32[32]{0:T(128)S(1)}, s32[32]{0:T(128)}, u32[]{:S(2)}) copy-start(s32[32]{0:T(128)} %param.5) | copy-start | bytes 388
  121.3 5.9 %copy-start = (bf16[1,16,800,32]{2,3,1,0:T(8,128)(2,1)S(1)}, bf16[1,16,800,32]{2,3,1,0:T(8,128)(2,1)}, u32[]{:S(2)}) copy-start(bf16[1,16,800,32]{2,3,1,0:T(8,128)(2,1)} %get-tuple-element.7) | copy-start | bytes 2457604
  121.3 5.9 %copy-start.1 = (bf16[1,16,800,32]{2,3,1,0:T(8,128)(2,1)S(1)}, bf16[1,16,800,32]{2,3,1,0:T(8,128)(2,1)}, u32[]{:S(2)}) copy-start(bf16[1,16,800,32]{2,3,1,0:T(8,128)(2,1)} %get-tuple-element.8) | copy-start | bytes 2457604
  165.9 6.8 %copy-start.2 = (f32[1,800,512]{2,1,0:T(8,128)S(1)}, f32[1,800,512]{2,1,0:T(8,128)}, u32[]{:S(2)}) copy-start(f32[1,800,512]{2,1,0:T(8,128)} %get-tuple-element.9) | copy-start | bytes 4915204
  165.9 6.8 %copy-start.3 = (f32[1,800,512]{2,1,0:T(8,128)S(1)}, f32[1,800,512]{2,1,0:T(8,128)}, u32[]{:S(2)}) copy-start(f32[1,800,512]{2,1,0:T(8,128)} %get-tuple-element.10) | copy-start | bytes 4915204
Sparse Core Ops, SparseCore 0:
  194.2 145.1 reduce-scatter.1
where the time goes:
time: 350 us; the launch traced here: 349 us
  waiting for transfers between devices  145 us (41%)
  blocking collectives  77.8 us (22%)
  matrix products  51.3 us (15%)
  other arithmetic  34.1 us (10%)
  local copies, waits for them, and re-layouts  27.1 us (8%)
  between operations  13.5 us (4%)
    reduce_scatter x1, waiting for transfers between devices, body(): lax.psum_scatter(jnp.einsum('kfsc,kfl->slc', partial_value, table, prefer...  145 us
    psum x1, blocking collectives, body(): source_spec = lax.psum(picked, 'chan').astype(jnp.bfloat16)  77.8 us
    dot_general x1, matrix products, body(): jnp.einsum('kfsc,kfl->slc', partial_value, table, preferred_element_type=...  21.3 us
    dot_general x1, matrix products, body(): jnp.einsum('kwfc,cs->kwfs', whitened, onehot, preferred_element_type=jnp....  11.3 us
    another operation x1, local copies, waits for them, and re-layouts, cross_spectrum(): left_pair = jnp.stack([source_spec[0], -source_spec[1]])  10.9 us
    convert_element_type x1, local copies, waits for them, and re-layouts, body(): source_spec = lax.psum(picked, 'chan').astype(jnp.bfloat16)  10.3 us
    dot_general x1, matrix products, cross_spectrum(): jnp.einsum('kwfs,kwfc->fsc', source_spec, receivers, preferred_element_ty...  9.8 us
    dot_general x1, matrix products, cross_spectrum(): jnp.einsum('kwfs,kwfc->fsc', left_pair, right_pair, preferred_element_typ...  8.86 us
  transfers between devices with their start and end apart: 1, of which 1 were waited for; matrix products, arithmetic and copies ran while one was open for 0% of the time, Pallas kernels for 0%

commit v1 on v0

v1 whole, which is shorter than its diff:
```python
import functools
import math

import jax
import jax.numpy as jnp
from jax import lax
from jax.experimental import pallas as pl
from jax.experimental.pallas import tpu as pltpu
from jax.sharding import PartitionSpec as P

LAGS = 512
GROUP = 16
STEP_BINS = 160
ORDER = ((3, 2, 1, 0), (3, 2, 0, 1), (0, 1, 3, 2), (0, 1, 2, 3))
INWARD = ((0, 1), (3, 2))
MIDDLE = ((1, 2), (2, 1))
OUTWARD = ((1, 0), (2, 3))
VMEM_LIMIT = 40 * 1024 * 1024


def quarter_of(hour, slot):
    quarter = jnp.int32(ORDER[0][slot])
    for row in range(1, 4):
        quarter = jnp.where(hour == row, jnp.int32(ORDER[row][slot]), quarter)
    return quarter


def pick_kernel(sources_ref, spectra_ref, quality_ref, *refs):
    out_refs, (onehot_ref, usable_ref) = refs[:-2], refs[-2:]
    source_count = onehot_ref.shape[0]
    per_slot = source_count // 4
    window_count, channels_here = quality_ref.shape
    wide = window_count * GROUP
    chan = lax.axis_index("chan")

    @pl.when(pl.program_id(0) == 0)
    def _():
        hour = lax.axis_index("hour")
        row = lax.broadcasted_iota(jnp.int32, (source_count, channels_here), 0)
        lane = lax.broadcasted_iota(jnp.int32, (source_count, channels_here), 1)
        wanted = jnp.full((source_count, channels_here), -1, jnp.int32)
        for slot in range(4):
            first = quarter_of(hour, slot) * per_slot
            for at in range(per_slot):
                wanted = jnp.where(row == slot * per_slot + at, sources_ref[first + at], wanted)
        onehot = (wanted - chan * channels_here == lane).astype(jnp.float32).astype(jnp.bfloat16)
        onehot_ref[...] = onehot
        usable = lax.dot_general(
            onehot,
            quality_ref[...].astype(jnp.float32).astype(jnp.bfloat16),
            (((1,), (1,)), ((), ())),
            preferred_element_type=jnp.float32,
        )
        spread = (
            lax.broadcasted_iota(jnp.int32, (window_count, wide), 1) // GROUP
            == lax.broadcasted_iota(jnp.int32, (window_count, wide), 0)
        )
        usable_ref[...] = jnp.dot(
            usable.astype(jnp.bfloat16),
            spread.astype(jnp.float32).astype(jnp.bfloat16),
            preferred_element_type=jnp.float32,
        )

    even = (chan % 2) == 0
    onehot = onehot_ref[...]
    usable = usable_ref[...]
    own, other = [], []
    for group in range(spectra_ref.shape[2] // GROUP):
        picked = []
        for part in range(2):
            columns = spectra_ref[part, :, group * GROUP : (group + 1) * GROUP, :]
            columns = columns.reshape(wide, channels_here)
            picked.append(
                lax.dot_general(
                    onehot, columns, (((1,), (1,)), ((), ())), preferred_element_type=jnp.float32
                )
                * usable
            )
        own.append(jnp.where(even, picked[0], picked[1]))
        other.append(jnp.where(even, picked[1], picked[0]))
    for slot in range(4):
        rows = slice(slot * per_slot, (slot + 1) * per_slot)
        out_refs[slot][...] = jnp.concatenate([v[rows] for v in own], 0).astype(jnp.bfloat16)
        out_refs[4 + slot][...] = jnp.concatenate([v[rows] for v in other], 0).astype(jnp.bfloat16)


def pick(spectra, quality, sources):
    _, window_count, freq_count, channels_here = spectra.shape
    source_count = sources.shape[0]
    per_slot = source_count // 4
    rows = freq_count // GROUP * per_slot
    step_rows = STEP_BINS // GROUP * per_slot
    wide = window_count * GROUP
    return pl.pallas_call(
        pick_kernel,
        grid=(freq_count // STEP_BINS,),
        in_specs=[
            pl.BlockSpec(memory_space=pltpu.SMEM),
            pl.BlockSpec((2, window_count, STEP_BINS, channels_here), lambda i: (0, 0, i, 0)),
            pl.BlockSpec((window_count, channels_here), lambda i: (0, 0)),
        ],
        out_specs=[pl.BlockSpec((step_rows, wide), lambda i: (i, 0))] * 8,
        out_shape=[jax.ShapeDtypeStruct((rows, wide), jnp.bfloat16)] * 8,
        scratch_shapes=[
            pltpu.VMEM((source_count, channels_here), jnp.bfloat16),
            pltpu.VMEM((source_count, wide), jnp.float32),
        ],
        compiler_params=pltpu.CompilerParams(vmem_limit_bytes=VMEM_LIMIT),
        cost_estimate=pl.CostEstimate(
            flops=2 * spectra.size * 256, bytes_accessed=spectra.size * 2, transcendentals=0
        ),
        name="pick_sources",
    )(sources, spectra, quality)


def whiten_kernel(spectra_ref, quality_ref, out_ref):
    _, windows, freq_count, channels_here = spectra_ref.shape
    chunk = 80

    for window in range(windows):

        def add(i, total):
            rows = pl.ds(pl.multiple_of(i * chunk, chunk), chunk)
            real = spectra_ref[0, window, rows, :].astype(jnp.float32)
            imag = spectra_ref[1, window, rows, :].astype(jnp.float32)
            square = real * real + imag * imag
            return total + jnp.sum(square.reshape(chunk // 8, 8, channels_here), axis=0)

        total = lax.fori_loop(0, freq_count // chunk, add, jnp.zeros((8, channels_here), jnp.float32))
        power = jnp.sum(total, axis=0, keepdims=True) / freq_count
        usable = quality_ref[pl.ds(pl.program_id(0) * windows + window, 1), :].astype(jnp.float32)
        scale = lax.rsqrt(power + 1e-06) * usable

        def apply(i, carry):
            rows = pl.ds(pl.multiple_of(i * chunk, chunk), chunk)
            for part in range(2):
                value = spectra_ref[part, window, rows, :].astype(jnp.float32) * scale
                out_ref[part, window, rows, :] = value.astype(jnp.bfloat16)
            return carry

        lax.fori_loop(0, freq_count // chunk, apply, 0)


def whiten(spectra, quality):
    _, window_count, freq_count, channels_here = spectra.shape
    windows = 2
    block = pl.BlockSpec((2, windows, freq_count, channels_here), lambda i: (0, i, 0, 0))
    return pl.pallas_call(
        whiten_kernel,
        grid=(window_count // windows,),
        in_specs=[block, pl.BlockSpec((window_count, channels_here), lambda i: (0, 0))],
        out_specs=block,
        out_shape=jax.ShapeDtypeStruct(spectra.shape, jnp.bfloat16),
        compiler_params=pltpu.CompilerParams(vmem_limit_bytes=VMEM_LIMIT),
        cost_estimate=pl.CostEstimate(
            flops=6 * spectra.size, bytes_accessed=spectra.size * 4, transcendentals=0
        ),
        name="whiten_receivers",
    )(spectra, quality)


def lags_kernel(first, count, own_ref, other_ref, receivers_ref, table_ref, out_ref, spec_ref, cross_ref):
    step = pl.program_id(0)
    freq_count = table_ref.shape[1] // 2
    _, window_count, step_bins, channels_here = receivers_ref.shape
    wide = own_ref.shape[1]
    groups = own_ref.shape[0] // 8
    chan = lax.axis_index("chan")

    @pl.when(step == 0)
    def _():
        even = (chan % 2) == 0

        def load(i):
            rows = pl.ds(pl.multiple_of(i * 16, 16), 16)
            own = own_ref[rows, :].astype(jnp.float32)
            other = other_ref[rows, :].astype(jnp.float32)
            return jnp.where(even, own, other), jnp.where(even, other, own)

        def add(i, total):
            real, imag = load(i)
            square = real * real + imag * imag
            return total + square[:8] + square[8:]

        total = lax.fori_loop(0, groups // 2, add, jnp.zeros((8, wide), jnp.float32))
        same = (
            lax.broadcasted_iota(jnp.int32, (wide, wide), 0) // GROUP
            == lax.broadcasted_iota(jnp.int32, (wide, wide), 1) // GROUP
        ).astype(jnp.float32)
        power = jnp.dot(
            total, same, preferred_element_type=jnp.float32, precision=lax.Precision.HIGHEST
        )
        scale = lax.rsqrt(power / freq_count + 1e-06)
        scale = jnp.concatenate([scale, scale], 0)

        def apply(i, carry):
            rows = pl.ds(pl.multiple_of(i * 16, 16), 16)
            for part, value in enumerate(load(i)):
                spec_ref[part, rows, :] = (value * scale).astype(jnp.bfloat16).astype(jnp.float32)
            return carry

        lax.fori_loop(0, groups // 2, apply, 0)

    diagonal = [
        lax.broadcasted_iota(jnp.int32, (8, wide), 1) % GROUP
        == lax.broadcasted_iota(jnp.int32, (8, wide), 0) + low
        for low in (0, 8)
    ]
    zero = jnp.zeros((8, wide), jnp.float32)
    step_groups = step_bins // GROUP
    for group in range(step_groups):
        left = []
        for part in range(2):
            rows = spec_ref[part, pl.ds(pl.multiple_of((step * step_groups + group) * 8, 8), 8), :]
            tiles = []
            for at in range(count):
                row = jnp.broadcast_to(rows[first + at : first + at + 1, :], (8, wide))
                tiles += [jnp.where(mask, row, zero) for mask in diagonal]
            left.append(jnp.concatenate(tiles, 0).astype(jnp.bfloat16))
        bins = slice(group * GROUP, (group + 1) * GROUP)
        real = receivers_ref[0, :, bins, :].reshape(wide, channels_here)
        imag = receivers_ref[1, :, bins, :].reshape(wide, channels_here)
        cross = jnp.dot(
            left[0], jnp.concatenate([real, imag], 1), preferred_element_type=jnp.float32
        ) + jnp.dot(left[1], jnp.concatenate([imag, -real], 1), preferred_element_type=jnp.float32)
        cross = cross.astype(jnp.bfloat16)
        for at in range(count):
            for part in range(2):
                rows = pl.ds(
                    pl.multiple_of(part * freq_count + step * step_bins + group * GROUP, GROUP), GROUP
                )
                cross_ref[at // 2, rows, (at % 2) * channels_here : (at % 2 + 1) * channels_here] = cross[
                    at * GROUP : (at + 1) * GROUP, part * channels_here : (part + 1) * channels_here
                ]

    @pl.when(step == pl.num_programs(0) - 1)
    def _():
        rows = 128
        for pair in range(count // 2):
            for block in range(table_ref.shape[0] // rows):
                lags = slice(block * rows, (block + 1) * rows)
                value = jnp.dot(
                    table_ref[lags, :], cross_ref[pair], preferred_element_type=jnp.float32
                ).astype(jnp.bfloat16)
                out_ref[2 * pair, lags, :] = value[:, :channels_here]
                out_ref[2 * pair + 1, lags, :] = value[:, channels_here:]


def lags_of(own, other, receivers, table, first, count):
    _, window_count, freq_count, channels_here = receivers.shape
    lag_count = table.shape[0]
    rows, wide = own.shape
    whole = lambda shape: pl.BlockSpec(shape, lambda i: (0,) * len(shape))
    return pl.pallas_call(
        functools.partial(lags_kernel, first, count),
        grid=(freq_count // STEP_BINS,),
        in_specs=[
            whole((rows, wide)),
            whole((rows, wide)),
            pl.BlockSpec((2, window_count, STEP_BINS, channels_here), lambda i: (0, 0, i, 0)),
            whole(table.shape),
        ],
        out_specs=whole((count, lag_count, channels_here)),
        out_shape=jax.ShapeDtypeStruct((count, lag_count, channels_here), jnp.bfloat16),
        scratch_shapes=[
            pltpu.VMEM((2, rows, wide), jnp.float32),
            pltpu.VMEM((count // 2, 2 * freq_count, 2 * channels_here), jnp.bfloat16),
        ],
        compiler_params=pltpu.CompilerParams(vmem_limit_bytes=VMEM_LIMIT),
        cost_estimate=pl.CostEstimate(
            flops=count * 16 * 2 * receivers.size * 4, bytes_accessed=receivers.size * 2, transcendentals=0
        ),
        name="lags",
    )(own, other, receivers, table)


def lag_table(freq_count, lag_count):
    lag = lax.broadcasted_iota(jnp.int32, (lag_count, 2 * freq_count), 0) - lag_count // 2
    column = lax.broadcasted_iota(jnp.int32, (lag_count, 2 * freq_count), 1)
    part = (column >= freq_count).astype(jnp.int32)
    turns = (column - part * freq_count + 1) * lag + part * (freq_count // 2)
    turns = lax.rem(lax.rem(turns, 2 * freq_count) + 2 * freq_count, 2 * freq_count)
    return (jnp.cos(turns.astype(jnp.float32) * (math.pi / freq_count)) / freq_count).astype(jnp.bfloat16)


def sum_over_chan(own, other, chan_count):
    bits = [1 << b for b in range(1, chan_count.bit_length() - 1)]
    turned = bits[1:] + bits[:1]
    swap = [(i, i ^ 1) for i in range(chan_count)]
    own = own + lax.ppermute(other, "chan", swap)
    for even_bit, odd_bit in zip(bits, turned):
        pairs = [(i, i ^ (odd_bit if i % 2 else even_bit)) for i in range(chan_count)]
        own = own + lax.ppermute(own, "chan", pairs)
    return own, lax.ppermute(own, "chan", swap)


def add(*values):
    return sum(v.astype(jnp.float32) for v in values).astype(jnp.bfloat16)


def body(chan_count, spectra, quality, sources):
    picked = pick(spectra, quality, sources)
    per_slot = sources.shape[0] // 4
    half = per_slot // 2
    receivers = whiten(spectra, quality)
    table = lag_table(spectra.shape[2], LAGS)
    gathered = [sum_over_chan(picked[t], picked[4 + t], chan_count) for t in range(4)]
    send = lambda value, pairs: lax.ppermute(value, "hour", pairs)
    mine = [
        [lags_of(*gathered[t], receivers, table, h * half, half) for h in range(2)] for t in range(4)
    ]
    inward = [[send(mine[t][h], INWARD) for h in range(2)] for t in range(3)]
    middle = [[send(add(mine[t][h], inward[t][h]), MIDDLE) for h in range(2)] for t in range(2)]
    outward = [send(add(mine[2][h], middle[0][h]), OUTWARD) for h in range(2)]
    return jnp.concatenate(
        [add(mine[3][h], inward[2][h], middle[1][h], outward[h]) for h in range(2)], 0
    )


def solution(mesh):
    placed = (P(None, "hour", None, "chan"), P("hour", "chan"), P())
    return jax.shard_map(
        functools.partial(body, mesh.shape["chan"]),
        mesh=mesh,
        in_specs=placed,
        out_specs=P("hour", None, "chan"),
        check_vma=False,
    )
```

time: 350 us -> 158 us (0.45)
  waiting for transfers between devices: 145 us -> 46.3 us
  blocking collectives: 77.8 us -> 0 us
  Pallas kernels: 0 us -> 52.7 us
  matrix products: 51.3 us -> 0 us
  starting transfers between devices: 0.01 us -> 33.9 us
  local copies, waits for them, and re-layouts: 27.1 us -> 4.22 us
  other arithmetic: 34.1 us -> 17.6 us
  between operations: 13.5 us -> 0.44 us
    reduce_scatter x1 -> x0, waiting for transfers between devices: 145 us -> none  [body(): lax.psum_scatter(jnp.einsum('kfsc,kfl->slc', partial_value, table, prefer...]
    psum x1 -> x0, blocking collectives: 77.8 us -> none  [body(): source_spec = lax.psum(picked, 'chan').astype(jnp.bfloat16)]
    pallas_call x0 -> x10, Pallas kernels: none -> 52.7 us  [the longest x8 42.8 us: lags_of(): pl.pallas_call(functools.partial(lags_kernel, first, count), grid=(freq_c...]
    dot_general x4 -> x0, matrix products: 51.3 us -> none  [the longest x1 21.3 us: body(): jnp.einsum('kfsc,kfl->slc', partial_value, table, preferred_element_type=...]
    ppermute x0 -> x28, waiting for transfers between devices: none -> 46.3 us  [the longest x12 38.3 us: body(): send = lambda value, pairs: lax.ppermute(value, 'hour', pairs)]
    ppermute x0 -> x28, starting transfers between devices: none -> 33.9 us  [the longest x12 20.9 us: body(): send = lambda value, pairs: lax.ppermute(value, 'hour', pairs)]
    another operation x1 -> x0, local copies, waits for them, and re-layouts: 10.9 us -> none  [cross_spectrum(): left_pair = jnp.stack([source_spec[0], -source_spec[1]])]
    convert_element_type x1 -> x0, local copies, waits for them, and re-layouts: 10.3 us -> none  [body(): source_spec = lax.psum(picked, 'chan').astype(jnp.bfloat16)]
  transfers between devices with their start and end apart: 1 -> 28, of which waited for: 1 -> 10; matrix products, arithmetic and copies ran while one was open for 0% -> 10% of each run, Pallas kernels for 0% -> 31%
where the time goes in v1:
time: 158 us; the launch traced here: 155 us
  Pallas kernels  52.7 us (33%)
  waiting for transfers between devices  46.3 us (29%)
  starting transfers between devices  33.9 us (21%)
  other arithmetic  17.6 us (11%)
  local copies, waits for them, and re-layouts  4.22 us (3%)
    pallas_call x8, Pallas kernels, lags_of(): pl.pallas_call(functools.partial(lags_kernel, first, count), grid=(freq_c...  42.8 us
    ppermute x12, waiting for transfers between devices, body(): send = lambda value, pairs: lax.ppermute(value, 'hour', pairs)  38.3 us
    ppermute x12, starting transfers between devices, body(): send = lambda value, pairs: lax.ppermute(value, 'hour', pairs)  20.9 us
    convert_element_type x1, other arithmetic, lag_table(): (jnp.cos(turns.astype(jnp.float32) * (math.pi / freq_count)) / freq_count...  14.4 us
    ppermute x8, starting transfers between devices, sum_over_chan(): own = own + lax.ppermute(own, 'chan', pairs)  10.6 us
    ppermute x8, waiting for transfers between devices, sum_over_chan(): own = own + lax.ppermute(own, 'chan', pairs)  7.48 us
    pallas_call x1, Pallas kernels, whiten(): pl.pallas_call(whiten_kernel, grid=(window_count // windows,), in_specs=[...  5.89 us
    unnamed x10, local copies, waits for them, and re-layouts  4.22 us
  transfers between devices with their start and end apart: 28, of which 10 were waited for; matrix products, arithmetic and copies ran while one was open for 10% of the time, Pallas kernels for 31%

profile of v1, /device:TPU:16, one launch (start us, length us, event | category | flops | bytes accessed | tf_op | source)
XLA Modules:
  0.0 155.0 jit_solution(9536143553040876489)
XLA Ops:
  0.0 2.9 %copy-done = bf16[2,16,800,128]{3,2,1,0:T(8,128)(2,1)S(1)} copy-done((bf16[2,16,800,128]{3,2,1,0:T(8,128)(2,1)S(1)}, bf16[2,16,800,128]{3,2,1,0:T(8,128)(2,1)}, u32[]{:S(2)}) %copy-start) | copy-done | bytes 6553624
  2.9 0.7 copy-done.2
  3.6 0.7 copy-done.4
  4.2 4.0 %pick_sources.1 = (bf16[400,256]{1,0:T(8,128)(2,1)S(1)}, bf16[400,256]{1,0:T(8,128)(2,1)S(1)}, bf16[400,256]{1,0:T(8,128)(2,1)S(1)}, bf16[400,256]{1,0:T(8,128)(...) custom-call(s32[32]{0:T(128)S(1)} %copy-done.4, ...), custom_call_target="tpu_custom_call" | custom-call | flops 1677721600 | bytes 6553600 | tf_op jit(solution)/shard_map/pick_sources/pallas_call | solution.py:94
  8.3 0.5 collective-permute-start.9
  8.9 0.4 collective-permute-start
  9.3 0.4 collective-permute-done.15
  9.8 1.6 %collective-permute-start.16 = (bf16[400,256]{1,0:T(8,128)(2,1)S(1)}, bf16[400,256]{1,0:T(8,128)(2,1)S(1)}, u32[]{:S(2)}, u32[]{:S(2)}) collective-permute-start(bf16[400,256]{1,0:T(8,128)(2,1)S(1)} %add.145), channel_id=1, source_target_pairs={{0,8},{4,20},{8,0},{12,28},{16,24},{20,4},{24,16},{28,12},{1,9},{5... | collective-permute-start | bytes 614408 | tf_op jit(solution)/shard_map/ppermute | solution.py:293
  11.4 0.6 collective-permute-start.10
  12.1 1.6 %collective-permute-start.5 = (bf16[400,256]{1,0:T(8,128)(2,1)S(1)}, bf16[400,256]{1,0:T(8,128)(2,1)S(1)}, u32[]{:S(2)}, u32[]{:S(2)}) collective-permute-start(bf16[400,256]{1,0:T(8,128)(2,1)S(1)} %add.136), channel_id=1, source_target_pairs={{0,8},{4,20},{8,0},{12,28},{16,24},{20,4},{24,16},{28,12},{1,9},{5... | collective-permute-start | bytes 614408 | tf_op jit(solution)/shard_map/ppermute | solution.py:293
  13.7 0.6 collective-permute-start.1
  14.3 1.3 collective-permute-done.16
  15.7 1.6 %collective-permute-start.17 = (bf16[400,256]{1,0:T(8,128)(2,1)S(1)}, bf16[400,256]{1,0:T(8,128)(2,1)S(1)}, u32[]{:S(2)}, u32[]{:S(2)}) collective-permute-start(bf16[400,256]{1,0:T(8,128)(2,1)S(1)} %add.146), channel_id=1, source_target_pairs={{0,16},{4,12},{8,24},{12,4},{16,0},{20,28},{24,8},{28,20},{1,17},{... | collective-permute-start | bytes 614408 | tf_op jit(solution)/shard_map/ppermute | solution.py:293
  17.3 0.7 collective-permute-done.10
  18.0 1.6 %collective-permute-start.11 = (bf16[400,256]{1,0:T(8,128)(2,1)S(1)}, bf16[400,256]{1,0:T(8,128)(2,1)S(1)}, u32[]{:S(2)}, u32[]{:S(2)}) collective-permute-start(bf16[400,256]{1,0:T(8,128)(2,1)S(1)} %add.141), channel_id=1, source_target_pairs={{0,16},{4,12},{8,24},{12,4},{16,0},{20,28},{24,8},{28,20},{1,17},{... | collective-permute-start | bytes 614408 | tf_op jit(solution)/shard_map/ppermute | solution.py:293
  19.6 2.7 %collective-permute-done.5 = bf16[400,256]{1,0:T(8,128)(2,1)S(1)} collective-permute-done((bf16[400,256]{1,0:T(8,128)(2,1)S(1)}, bf16[400,256]{1,0:T(8,128)(2,1)S(1)}, u32[]{:S(2)}, u32[]{:S(2)}) %collective-permute-start.5) | collective-permute-done | bytes 204832 | tf_op jit(solution)/shard_map/ppermute | solution.py:293
  22.4 1.6 %collective-permute-start.6 = (bf16[400,256]{1,0:T(8,128)(2,1)S(1)}, bf16[400,256]{1,0:T(8,128)(2,1)S(1)}, u32[]{:S(2)}, u32[]{:S(2)}) collective-permute-start(bf16[400,256]{1,0:T(8,128)(2,1)S(1)} %add.137), channel_id=1, source_target_pairs={{0,16},{4,12},{8,24},{12,4},{16,0},{20,28},{24,8},{28,20},{1,17},{... | collective-permute-start | bytes 614408 | tf_op jit(solution)/shard_map/ppermute | solution.py:293
  24.0 2.7 %collective-permute-done.1 = bf16[400,256]{1,0:T(8,128)(2,1)S(1)} collective-permute-done((bf16[400,256]{1,0:T(8,128)(2,1)S(1)}, bf16[400,256]{1,0:T(8,128)(2,1)S(1)}, u32[]{:S(2)}, u32[]{:S(2)}) %collective-permute-start.1) | collective-permute-done | bytes 204832 | tf_op jit(solution)/shard_map/ppermute | solution.py:293
  26.8 1.6 %collective-permute-start.2 = (bf16[400,256]{1,0:T(8,128)(2,1)S(1)}, bf16[400,256]{1,0:T(8,128)(2,1)S(1)}, u32[]{:S(2)}, u32[]{:S(2)}) collective-permute-start(bf16[400,256]{1,0:T(8,128)(2,1)S(1)} %add.130), channel_id=1, source_target_pairs={{0,16},{4,12},{8,24},{12,4},{16,0},{20,28},{24,8},{28,20},{1,17},{... | collective-permute-start | bytes 614408 | tf_op jit(solution)/shard_map/ppermute | solution.py:293
  28.6 0.5 collective-permute-start.12
  29.1 14.4 %multiply_convert_fusion.table_ref = bf16[512,1600]{1,0:T(8,128)(2,1)S(1)} fusion(s32[1600]{0:T(1024)S(1)} %get-tuple-element.21, s32[512]{0:T(512)S(1)} %iota_add_fusion, s32[1600]{0:T(1024)S(1)} %get-tuple-element.22), kind=kLoop, calls=%fused_computation | loop fusion | flops 7372800 | bytes 1653248 | tf_op jit(solution)/shard_map/convert_element_type | solution.py:283
  43.6 5.9 %whiten_receivers.1.receivers_ref = bf16[2,16,800,128]{3,2,1,0:T(8,128)(2,1)S(1)} custom-call(bf16[2,16,800,128]{3,2,1,0:T(8,128)(2,1)S(1)} %copy-done.1, s32[16,128]{1,0:T(8,128)S(1)} %copy-done.3), custom_call_target="tpu_custom_call" | custom-call | flops 19660800 | bytes 13107200 | tf_op jit(solution)/shard_map/whiten_receivers/pallas_call | solution.py:148
  49.7 0.5 collective-permute-start.3
  50.3 5.3 %lags.15 = bf16[4,512,128]{2,1,0:T(8,128)(2,1)S(1)} custom-call(bf16[400,256]{1,0:T(8,128)(2,1)S(1)} %add.147.own_ref, bf16[400,256]{1,0:T(8,128)(2,1)S(1)} %collective-permute-done.18.other_ref, bf16[2,16,800,128]{3,2,1,0:T(8,128)(2,1)S(1)} %whiten_receivers.1.receivers_ref, bf16[512,1600]{1,0:T(8,128)(2,1)S(1)} %multiply_convert_fusion.table_ref), custom_call_target="tpu_custom_call" | custom-call | flops 1677721600 | bytes 6553600 | tf_op jit(solution)/shard_map/lags/pallas_call | solution.py:254
  55.6 1.3 collective-permute-start.25
  56.9 5.3 %lags.14 = bf16[4,512,128]{2,1,0:T(8,128)(2,1)S(1)} custom-call(bf16[400,256]{1,0:T(8,128)(2,1)S(1)} %add.142.own_ref, bf16[400,256]{1,0:T(8,128)(2,1)S(1)} %collective-permute-done.12.other_ref, bf16[2,16,800,128]{3,2,1,0:T(8,128)(2,1)S(1)} %whiten_receivers.1.receivers_ref, bf16[512,1600]{1,0:T(8,128)(2,1)S(1)} %multiply_convert_fusion.table_ref), custom_call_target="tpu_custom_call" | custom-call | flops 1677721600 | bytes 6553600 | tf_op jit(solution)/shard_map/lags/pallas_call | solution.py:254
  62.3 1.3 collective-permute-start.23
  63.6 5.3 %lags.13 = bf16[4,512,128]{2,1,0:T(8,128)(2,1)S(1)} custom-call(bf16[400,256]{1,0:T(8,128)(2,1)S(1)} %add.138.own_ref, bf16[400,256]{1,0:T(8,128)(2,1)S(1)} %collective-permute-done.7.other_ref, bf16[2,16,800,128]{3,2,1,0:T(8,128)(2,1)S(1)} %whiten_receivers.1.receivers_ref, bf16[512,1600]{1,0:T(8,128)(2,1)S(1)} %multiply_convert_fusion.table_ref), custom_call_target="tpu_custom_call" | custom-call | flops 1677721600 | bytes 6553600 | tf_op jit(solution)/shard_map/lags/pallas_call | solution.py:254
  68.9 1.3 collective-permute-start.22
  70.2 5.4 %lags.11 = bf16[4,512,128]{2,1,0:T(8,128)(2,1)S(1)} custom-call(bf16[400,256]{1,0:T(8,128)(2,1)S(1)} %add.147.own_ref, bf16[400,256]{1,0:T(8,128)(2,1)S(1)} %collective-permute-done.18.other_ref, bf16[2,16,800,128]{3,2,1,0:T(8,128)(2,1)S(1)} %whiten_receivers.1.receivers_ref, bf16[512,1600]{1,0:T(8,128)(2,1)S(1)} %multiply_convert_fusion.table_ref), custom_call_target="tpu_custom_call" | custom-call | flops 1677721600 | bytes 6553600 | tf_op jit(solution)/shard_map/lags/pallas_call | solution.py:254
  75.6 1.5 collective-permute-start.19
  77.1 5.4 %lags.9 = bf16[4,512,128]{2,1,0:T(8,128)(2,1)S(1)} custom-call(bf16[400,256]{1,0:T(8,128)(2,1)S(1)} %add.138.own_ref, bf16[400,256]{1,0:T(8,128)(2,1)S(1)} %collective-permute-done.7.other_ref, bf16[2,16,800,128]{3,2,1,0:T(8,128)(2,1)S(1)} %whiten_receivers.1.receivers_ref, bf16[512,1600]{1,0:T(8,128)(2,1)S(1)} %multiply_convert_fusion.table_ref), custom_call_target="tpu_custom_call" | custom-call | flops 1677721600 | bytes 6553600 | tf_op jit(solution)/shard_map/lags/pallas_call | solution.py:254
  82.4 5.4 %lags.10 = bf16[4,512,128]{2,1,0:T(8,128)(2,1)S(1)} custom-call(bf16[400,256]{1,0:T(8,128)(2,1)S(1)} %add.142.own_ref, bf16[400,256]{1,0:T(8,128)(2,1)S(1)} %collective-permute-done.12.other_ref, bf16[2,16,800,128]{3,2,1,0:T(8,128)(2,1)S(1)} %whiten_receivers.1.receivers_ref, bf16[512,1600]{1,0:T(8,128)(2,1)S(1)} %multiply_convert_fusion.table_ref), custom_call_target="tpu_custom_call" | custom-call | flops 1677721600 | bytes 6553600 | tf_op jit(solution)/shard_map/lags/pallas_call | solution.py:254
  87.8 1.3 collective-permute-start.13
  89.3 1.3 collective-permute-start.8
  90.7 15.3 %collective-permute-done.19 = bf16[4,512,128]{2,1,0:T(8,128)(2,1)S(1)} collective-permute-done((bf16[4,512,128]{2,1,0:T(8,128)(2,1)S(1)}, bf16[4,512,128]{2,1,0:T(8,128)(2,1)S(1)}, u32[]{:S(2)}, u32[]{:S(2)}) %collective-permute-start.19) | collective-permute-done | bytes 524320 | tf_op jit(solution)/shard_map/ppermute | solution.py:308
  106.0 2.3 %collective-permute-start.26 = (bf16[4,512,128]{2,1,0:T(8,128)(2,1)S(1)}, bf16[4,512,128]{2,1,0:T(8,128)(2,1)S(1)}, u32[]{:S(2)}, u32[]{:S(2)}) collective-permute-start(bf16[4,512,128]{2,1,0:T(8,128)(2,1)S(1)} %add_convert_fusion.2), channel_id=1, source_target_pairs={{1,2},{2,1},{5,6},{6,5},{9,10},{10,9},{13,14},{14,13},{17,18},{18,... | collective-permute-start | bytes 1572872 | tf_op jit(solution)/shard_map/ppermute | solution.py:308
  108.5 8.7 %collective-permute-done.13 = bf16[4,512,128]{2,1,0:T(8,128)(2,1)S(1)} collective-permute-done((bf16[4,512,128]{2,1,0:T(8,128)(2,1)S(1)}, bf16[4,512,128]{2,1,0:T(8,128)(2,1)S(1)}, u32[]{:S(2)}, u32[]{:S(2)}) %collective-permute-start.13) | collective-permute-done | bytes 524320 | tf_op jit(solution)/shard_map/ppermute | solution.py:308
  117.2 2.3 %collective-permute-start.20 = (bf16[4,512,128]{2,1,0:T(8,128)(2,1)S(1)}, bf16[4,512,128]{2,1,0:T(8,128)(2,1)S(1)}, u32[]{:S(2)}, u32[]{:S(2)}) collective-permute-start(bf16[4,512,128]{2,1,0:T(8,128)(2,1)S(1)} %add_convert_fusion.6), channel_id=1, source_target_pairs={{1,2},{2,1},{5,6},{6,5},{9,10},{10,9},{13,14},{14,13},{17,18},{18,... | collective-permute-start | bytes 1572872 | tf_op jit(solution)/shard_map/ppermute | solution.py:308
  120.0 3.3 %collective-permute-start.24 = (bf16[4,512,128]{2,1,0:T(8,128)(2,1)S(1)}, bf16[4,512,128]{2,1,0:T(8,128)(2,1)S(1)}, u32[]{:S(2)}, u32[]{:S(2)}) collective-permute-start(bf16[4,512,128]{2,1,0:T(8,128)(2,1)S(1)} %add_convert_fusion.3), channel_id=1, source_target_pairs={{1,2},{2,1},{5,6},{6,5},{9,10},{10,9},{13,14},{14,13},{17,18},{18,... | collective-permute-start | bytes 1572872 | tf_op jit(solution)/shard_map/ppermute | solution.py:308
  123.4 10.6 %collective-permute-done.20 = bf16[4,512,128]{2,1,0:T(8,128)(2,1)S(1)} collective-permute-done((bf16[4,512,128]{2,1,0:T(8,128)(2,1)S(1)}, bf16[4,512,128]{2,1,0:T(8,128)(2,1)S(1)}, u32[]{:S(2)}, u32[]{:S(2)}) %collective-permute-start.20) | collective-permute-done | bytes 524320 | tf_op jit(solution)/shard_map/ppermute | solution.py:308
  134.0 1.3 collective-permute-start.27
  135.5 2.4 %collective-permute-start.14 = (bf16[4,512,128]{2,1,0:T(8,128)(2,1)S(1)}, bf16[4,512,128]{2,1,0:T(8,128)(2,1)S(1)}, u32[]{:S(2)}, u32[]{:S(2)}) collective-permute-start(bf16[4,512,128]{2,1,0:T(8,128)(2,1)S(1)} %add_convert_fusion.7), channel_id=1, source_target_pairs={{1,2},{2,1},{5,6},{6,5},{9,10},{10,9},{13,14},{14,13},{17,18},{18,... | collective-permute-start | bytes 1572872 | tf_op jit(solution)/shard_map/ppermute | solution.py:308
  137.8 1.3 collective-permute-start.21
  139.2 5.3 %lags.12 = bf16[4,512,128]{2,1,0:T(8,128)(2,1)S(1)} custom-call(bf16[400,256]{1,0:T(8,128)(2,1)S(1)} %add.131.own_ref, bf16[400,256]{1,0:T(8,128)(2,1)S(1)} %collective-permute-done.3.other_ref, bf16[2,16,800,128]{3,2,1,0:T(8,128)(2,1)S(1)} %whiten_receivers.1.receivers_ref, bf16[512,1600]{1,0:T(8,128)(2,1)S(1)} %multiply_convert_fusion.table_ref), custom_call_target="tpu_custom_call" | custom-call | flops 1677721600 | bytes 6553600 | tf_op jit(solution)/shard_map/lags/pallas_call | solution.py:254
  144.5 5.4 %lags.8 = bf16[4,512,128]{2,1,0:T(8,128)(2,1)S(1)} custom-call(bf16[400,256]{1,0:T(8,128)(2,1)S(1)} %add.131.own_ref, bf16[400,256]{1,0:T(8,128)(2,1)S(1)} %collective-permute-done.3.other_ref, bf16[2,16,800,128]{3,2,1,0:T(8,128)(2,1)S(1)} %whiten_receivers.1.receivers_ref, bf16[512,1600]{1,0:T(8,128)(2,1)S(1)} %multiply_convert_fusion.table_ref), custom_call_target="tpu_custom_call" | custom-call | flops 1677721600 | bytes 6553600 | tf_op jit(solution)/shard_map/lags/pallas_call | solution.py:254
  150.2 3.5 %collective-permute-done.14 = bf16[4,512,128]{2,1,0:T(8,128)(2,1)S(1)} collective-permute-done((bf16[4,512,128]{2,1,0:T(8,128)(2,1)S(1)}, bf16[4,512,128]{2,1,0:T(8,128)(2,1)S(1)}, u32[]{:S(2)}, u32[]{:S(2)}) %collective-permute-start.14) | collective-permute-done | bytes 524320 | tf_op jit(solution)/shard_map/ppermute | solution.py:308
  154.0 1.1 pad_maximum_fusion
  (52 shorter events, 2.7 us)
Async XLA Ops:
  0.0 2.9 %copy-start = (bf16[2,16,800,128]{3,2,1,0:T(8,128)(2,1)S(1)}, bf16[2,16,800,128]{3,2,1,0:T(8,128)(2,1)}, u32[]{:S(2)}) copy-start(bf16[2,16,800,128]{3,2,1,0:T(8,128)(2,1)} %spectra_ref.3) | copy-start | bytes 19660804
  2.9 0.7 copy-start.2
  3.6 0.7 copy-start.4
  8.2 1.5 collective-permute-start.15
  8.3 3.1 %collective-permute-start.9 = (bf16[400,256]{1,0:T(8,128)(2,1)S(1)}, bf16[400,256]{1,0:T(8,128)(2,1)S(1)}, u32[]{:S(2)}, u32[]{:S(2)}) collective-permute-start(bf16[400,256]{1,0:T(8,128)(2,1)S(1)} %get-tuple-element.18), channel_id=1, source_target_pairs={{0,4},{4,0},{8,12},{12,8},{16,20},{20,16},{24,28},{28,24},{1,5},{5... | collective-permute-start | bytes 614408 | tf_op jit(solution)/shard_map/ppermute | solution.py:290
  8.8 3.2 %collective-permute-start.4 = (bf16[400,256]{1,0:T(8,128)(2,1)S(1)}, bf16[400,256]{1,0:T(8,128)(2,1)S(1)}, u32[]{:S(2)}, u32[]{:S(2)}) collective-permute-start(bf16[400,256]{1,0:T(8,128)(2,1)S(1)} %get-tuple-element.16), channel_id=1, source_target_pairs={{0,4},{4,0},{8,12},{12,8},{16,20},{20,16},{24,28},{28,24},{1,5},{5... | collective-permute-start | bytes 614408 | tf_op jit(solution)/shard_map/ppermute | solution.py:290
  8.9 4.8 %collective-permute-start = (bf16[400,256]{1,0:T(8,128)(2,1)S(1)}, bf16[400,256]{1,0:T(8,128)(2,1)S(1)}, u32[]{:S(2)}, u32[]{:S(2)}) collective-permute-start(bf16[400,256]{1,0:T(8,128)(2,1)S(1)} %get-tuple-element.14), channel_id=1, source_target_pairs={{0,4},{4,0},{8,12},{12,8},{16,20},{20,16},{24,28},{28,24},{1,5},{5... | collective-permute-start | bytes 614408 | tf_op jit(solution)/shard_map/ppermute | solution.py:290
  9.8 5.8 %collective-permute-start.16 = (bf16[400,256]{1,0:T(8,128)(2,1)S(1)}, bf16[400,256]{1,0:T(8,128)(2,1)S(1)}, u32[]{:S(2)}, u32[]{:S(2)}) collective-permute-start(bf16[400,256]{1,0:T(8,128)(2,1)S(1)} %add.145), channel_id=1, source_target_pairs={{0,8},{4,20},{8,0},{12,28},{16,24},{20,4},{24,16},{28,12},{1,9},{5... | collective-permute-start | bytes 614408 | tf_op jit(solution)/shard_map/ppermute | solution.py:293
  11.4 32.2 %copy-start.1 = (bf16[2,16,800,128]{3,2,1,0:T(8,128)(2,1)S(1)}, bf16[2,16,800,128]{3,2,1,0:T(8,128)(2,1)}, u32[]{:S(2)}) copy-start(bf16[2,16,800,128]{3,2,1,0:T(8,128)(2,1)} %spectra_ref.3) | copy-start | bytes 19660804
  11.4 32.2 %copy-start.3 = (s32[16,128]{1,0:T(8,128)S(1)}, s32[16,128]{1,0:T(8,128)}, u32[]{:S(2)}) copy-start(s32[16,128]{1,0:T(8,128)} %quality_ref.3) | copy-start | bytes 24580
  11.4 6.5 %collective-permute-start.10 = (bf16[400,256]{1,0:T(8,128)(2,1)S(1)}, bf16[400,256]{1,0:T(8,128)(2,1)S(1)}, u32[]{:S(2)}, u32[]{:S(2)}) collective-permute-start(bf16[400,256]{1,0:T(8,128)(2,1)S(1)} %add.140), channel_id=1, source_target_pairs={{0,8},{4,20},{8,0},{12,28},{16,24},{20,4},{24,16},{28,12},{1,9},{5... | collective-permute-start | bytes 614408 | tf_op jit(solution)/shard_map/ppermute | solution.py:293
  12.1 10.2 %collective-permute-start.5 = (bf16[400,256]{1,0:T(8,128)(2,1)S(1)}, bf16[400,256]{1,0:T(8,128)(2,1)S(1)}, u32[]{:S(2)}, u32[]{:S(2)}) collective-permute-start(bf16[400,256]{1,0:T(8,128)(2,1)S(1)} %add.136), channel_id=1, source_target_pairs={{0,8},{4,20},{8,0},{12,28},{16,24},{20,4},{24,16},{28,12},{1,9},{5... | collective-permute-start | bytes 614408 | tf_op jit(solution)/shard_map/ppermute | solution.py:293
  13.7 13.0 %collective-permute-start.1 = (bf16[400,256]{1,0:T(8,128)(2,1)S(1)}, bf16[400,256]{1,0:T(8,128)(2,1)S(1)}, u32[]{:S(2)}, u32[]{:S(2)}) collective-permute-start(bf16[400,256]{1,0:T(8,128)(2,1)S(1)} %add.129), channel_id=1, source_target_pairs={{0,8},{4,20},{8,0},{12,28},{16,24},{20,4},{24,16},{28,12},{1,9},{5... | collective-permute-start | bytes 614408 | tf_op jit(solution)/shard_map/ppermute | solution.py:293
  15.7 12.7 %collective-permute-start.17 = (bf16[400,256]{1,0:T(8,128)(2,1)S(1)}, bf16[400,256]{1,0:T(8,128)(2,1)S(1)}, u32[]{:S(2)}, u32[]{:S(2)}) collective-permute-start(bf16[400,256]{1,0:T(8,128)(2,1)S(1)} %add.146), channel_id=1, source_target_pairs={{0,16},{4,12},{8,24},{12,4},{16,0},{20,28},{24,8},{28,20},{1,17},{... | collective-permute-start | bytes 614408 | tf_op jit(solution)/shard_map/ppermute | solution.py:293
  18.0 10.5 %collective-permute-start.11 = (bf16[400,256]{1,0:T(8,128)(2,1)S(1)}, bf16[400,256]{1,0:T(8,128)(2,1)S(1)}, u32[]{:S(2)}, u32[]{:S(2)}) collective-permute-start(bf16[400,256]{1,0:T(8,128)(2,1)S(1)} %add.141), channel_id=1, source_target_pairs={{0,16},{4,12},{8,24},{12,4},{16,0},{20,28},{24,8},{28,20},{1,17},{... | collective-permute-start | bytes 614408 | tf_op jit(solution)/shard_map/ppermute | solution.py:293
  22.4 27.1 %collective-permute-start.6 = (bf16[400,256]{1,0:T(8,128)(2,1)S(1)}, bf16[400,256]{1,0:T(8,128)(2,1)S(1)}, u32[]{:S(2)}, u32[]{:S(2)}) collective-permute-start(bf16[400,256]{1,0:T(8,128)(2,1)S(1)} %add.137), channel_id=1, source_target_pairs={{0,16},{4,12},{8,24},{12,4},{16,0},{20,28},{24,8},{28,20},{1,17},{... | collective-permute-start | bytes 614408 | tf_op jit(solution)/shard_map/ppermute | solution.py:293
  26.8 22.9 %collective-permute-start.2 = (bf16[400,256]{1,0:T(8,128)(2,1)S(1)}, bf16[400,256]{1,0:T(8,128)(2,1)S(1)}, u32[]{:S(2)}, u32[]{:S(2)}) collective-permute-start(bf16[400,256]{1,0:T(8,128)(2,1)S(1)} %add.130), channel_id=1, source_target_pairs={{0,16},{4,12},{8,24},{12,4},{16,0},{20,28},{24,8},{28,20},{1,17},{... | collective-permute-start | bytes 614408 | tf_op jit(solution)/shard_map/ppermute | solution.py:293
  28.4 21.8 %collective-permute-start.18 = (bf16[400,256]{1,0:T(8,128)(2,1)S(1)}, bf16[400,256]{1,0:T(8,128)(2,1)S(1)}, u32[]{:S(2)}, u32[]{:S(2)}) collective-permute-start(bf16[400,256]{1,0:T(8,128)(2,1)S(1)} %add.147.own_ref), channel_id=1, source_target_pairs={{0,4},{4,0},{8,12},{12,8},{16,20},{20,16},{24,28},{28,24},{1,5},{5... | collective-permute-start | bytes 614408 | tf_op jit(solution)/shard_map/ppermute | solution.py:294
  28.6 28.3 %collective-permute-start.12 = (bf16[400,256]{1,0:T(8,128)(2,1)S(1)}, bf16[400,256]{1,0:T(8,128)(2,1)S(1)}, u32[]{:S(2)}, u32[]{:S(2)}) collective-permute-start(bf16[400,256]{1,0:T(8,128)(2,1)S(1)} %add.142.own_ref), channel_id=1, source_target_pairs={{0,4},{4,0},{8,12},{12,8},{16,20},{20,16},{24,28},{28,24},{1,5},{5... | collective-permute-start | bytes 614408 | tf_op jit(solution)/shard_map/ppermute | solution.py:294
  49.6 14.0 %collective-permute-start.7 = (bf16[400,256]{1,0:T(8,128)(2,1)S(1)}, bf16[400,256]{1,0:T(8,128)(2,1)S(1)}, u32[]{:S(2)}, u32[]{:S(2)}) collective-permute-start(bf16[400,256]{1,0:T(8,128)(2,1)S(1)} %add.138.own_ref), channel_id=1, source_target_pairs={{0,4},{4,0},{8,12},{12,8},{16,20},{20,16},{24,28},{28,24},{1,5},{5... | collective-permute-start | bytes 614408 | tf_op jit(solution)/shard_map/ppermute | solution.py:294
  49.7 85.7 %collective-permute-start.3 = (bf16[400,256]{1,0:T(8,128)(2,1)S(1)}, bf16[400,256]{1,0:T(8,128)(2,1)S(1)}, u32[]{:S(2)}, u32[]{:S(2)}) collective-permute-start(bf16[400,256]{1,0:T(8,128)(2,1)S(1)} %add.131.own_ref), channel_id=1, source_target_pairs={{0,4},{4,0},{8,12},{12,8},{16,20},{20,16},{24,28},{28,24},{1,5},{5... | collective-permute-start | bytes 614408 | tf_op jit(solution)/shard_map/ppermute | solution.py:294
  55.6 32.2 %collective-permute-start.25 = (bf16[4,512,128]{2,1,0:T(8,128)(2,1)S(1)}, bf16[4,512,128]{2,1,0:T(8,128)(2,1)S(1)}, u32[]{:S(2)}, u32[]{:S(2)}) collective-permute-start(bf16[4,512,128]{2,1,0:T(8,128)(2,1)S(1)} %lags.15), channel_id=1, source_target_pairs={{0,1},{3,2},{4,5},{7,6},{8,9},{11,10},{12,13},{15,14},{16,17},{19,... | collective-permute-start | bytes 1572872 | tf_op jit(solution)/shard_map/ppermute | solution.py:308
  62.3 27.0 %collective-permute-start.23 = (bf16[4,512,128]{2,1,0:T(8,128)(2,1)S(1)}, bf16[4,512,128]{2,1,0:T(8,128)(2,1)S(1)}, u32[]{:S(2)}, u32[]{:S(2)}) collective-permute-start(bf16[4,512,128]{2,1,0:T(8,128)(2,1)S(1)} %lags.14), channel_id=1, source_target_pairs={{0,1},{3,2},{4,5},{7,6},{8,9},{11,10},{12,13},{15,14},{16,17},{19,... | collective-permute-start | bytes 1572872 | tf_op jit(solution)/shard_map/ppermute | solution.py:308
  68.9 68.9 %collective-permute-start.22 = (bf16[4,512,128]{2,1,0:T(8,128)(2,1)S(1)}, bf16[4,512,128]{2,1,0:T(8,128)(2,1)S(1)}, u32[]{:S(2)}, u32[]{:S(2)}) collective-permute-start(bf16[4,512,128]{2,1,0:T(8,128)(2,1)S(1)} %lags.13), channel_id=1, source_target_pairs={{0,1},{3,2},{4,5},{7,6},{8,9},{11,10},{12,13},{15,14},{16,17},{19,... | collective-permute-start | bytes 1572872 | tf_op jit(solution)/shard_map/ppermute | solution.py:308
  75.6 30.4 %collective-permute-start.19 = (bf16[4,512,128]{2,1,0:T(8,128)(2,1)S(1)}, bf16[4,512,128]{2,1,0:T(8,128)(2,1)S(1)}, u32[]{:S(2)}, u32[]{:S(2)}) collective-permute-start(bf16[4,512,128]{2,1,0:T(8,128)(2,1)S(1)} %lags.11), channel_id=1, source_target_pairs={{0,1},{3,2},{4,5},{7,6},{8,9},{11,10},{12,13},{15,14},{16,17},{19,... | collective-permute-start | bytes 1572872 | tf_op jit(solution)/shard_map/ppermute | solution.py:308
  87.8 29.4 %collective-permute-start.13 = (bf16[4,512,128]{2,1,0:T(8,128)(2,1)S(1)}, bf16[4,512,128]{2,1,0:T(8,128)(2,1)S(1)}, u32[]{:S(2)}, u32[]{:S(2)}) collective-permute-start(bf16[4,512,128]{2,1,0:T(8,128)(2,1)S(1)} %lags.10), channel_id=1, source_target_pairs={{0,1},{3,2},{4,5},{7,6},{8,9},{11,10},{12,13},{15,14},{16,17},{19,... | collective-permute-start | bytes 1572872 | tf_op jit(solution)/shard_map/ppermute | solution.py:308
  89.3 60.9 %collective-permute-start.8 = (bf16[4,512,128]{2,1,0:T(8,128)(2,1)S(1)}, bf16[4,512,128]{2,1,0:T(8,128)(2,1)S(1)}, u32[]{:S(2)}, u32[]{:S(2)}) collective-permute-start(bf16[4,512,128]{2,1,0:T(8,128)(2,1)S(1)} %lags.9), channel_id=1, source_target_pairs={{0,1},{3,2},{4,5},{7,6},{8,9},{11,10},{12,13},{15,14},{16,17},{19,... | collective-permute-start | bytes 1572872 | tf_op jit(solution)/shard_map/ppermute | solution.py:308
  106.0 14.0 %collective-permute-start.26 = (bf16[4,512,128]{2,1,0:T(8,128)(2,1)S(1)}, bf16[4,512,128]{2,1,0:T(8,128)(2,1)S(1)}, u32[]{:S(2)}, u32[]{:S(2)}) collective-permute-start(bf16[4,512,128]{2,1,0:T(8,128)(2,1)S(1)} %add_convert_fusion.2), channel_id=1, source_target_pairs={{1,2},{2,1},{5,6},{6,5},{9,10},{10,9},{13,14},{14,13},{17,18},{18,... | collective-permute-start | bytes 1572872 | tf_op jit(solution)/shard_map/ppermute | solution.py:308
  117.2 16.7 %collective-permute-start.20 = (bf16[4,512,128]{2,1,0:T(8,128)(2,1)S(1)}, bf16[4,512,128]{2,1,0:T(8,128)(2,1)S(1)}, u32[]{:S(2)}, u32[]{:S(2)}) collective-permute-start(bf16[4,512,128]{2,1,0:T(8,128)(2,1)S(1)} %add_convert_fusion.6), channel_id=1, source_target_pairs={{1,2},{2,1},{5,6},{6,5},{9,10},{10,9},{13,14},{14,13},{17,18},{18,... | collective-permute-start | bytes 1572872 | tf_op jit(solution)/shard_map/ppermute | solution.py:308
  120.0 29.9 %collective-permute-start.24 = (bf16[4,512,128]{2,1,0:T(8,128)(2,1)S(1)}, bf16[4,512,128]{2,1,0:T(8,128)(2,1)S(1)}, u32[]{:S(2)}, u32[]{:S(2)}) collective-permute-start(bf16[4,512,128]{2,1,0:T(8,128)(2,1)S(1)} %add_convert_fusion.3), channel_id=1, source_target_pairs={{1,2},{2,1},{5,6},{6,5},{9,10},{10,9},{13,14},{14,13},{17,18},{18,... | collective-permute-start | bytes 1572872 | tf_op jit(solution)/shard_map/ppermute | solution.py:308
  134.0 15.9 %collective-permute-start.27 = (bf16[4,512,128]{2,1,0:T(8,128)(2,1)S(1)}, bf16[4,512,128]{2,1,0:T(8,128)(2,1)S(1)}, u32[]{:S(2)}, u32[]{:S(2)}) collective-permute-start(bf16[4,512,128]{2,1,0:T(8,128)(2,1)S(1)} %add_convert_fusion.1), channel_id=1, source_target_pairs={{1,0},{2,3},{5,4},{6,7},{9,8},{10,11},{13,12},{14,15},{17,16},{18,... | collective-permute-start | bytes 1572872 | tf_op jit(solution)/shard_map/ppermute | solution.py:308
  135.5 18.2 %collective-permute-start.14 = (bf16[4,512,128]{2,1,0:T(8,128)(2,1)S(1)}, bf16[4,512,128]{2,1,0:T(8,128)(2,1)S(1)}, u32[]{:S(2)}, u32[]{:S(2)}) collective-permute-start(bf16[4,512,128]{2,1,0:T(8,128)(2,1)S(1)} %add_convert_fusion.7), channel_id=1, source_target_pairs={{1,2},{2,1},{5,6},{6,5},{9,10},{10,9},{13,14},{14,13},{17,18},{18,... | collective-permute-start | bytes 1572872 | tf_op jit(solution)/shard_map/ppermute | solution.py:308
  137.8 15.8 %collective-permute-start.21 = (bf16[4,512,128]{2,1,0:T(8,128)(2,1)S(1)}, bf16[4,512,128]{2,1,0:T(8,128)(2,1)S(1)}, u32[]{:S(2)}, u32[]{:S(2)}) collective-permute-start(bf16[4,512,128]{2,1,0:T(8,128)(2,1)S(1)} %add_convert_fusion.5), channel_id=1, source_target_pairs={{1,0},{2,3},{5,4},{6,7},{9,8},{10,11},{13,12},{14,15},{17,16},{18,... | collective-permute-start | bytes 1572872 | tf_op jit(solution)/shard_map/ppermute | solution.py:308

commit v2 on v0

v2 whole, which is shorter than its diff:
```python
import functools
import math

import jax
import jax.numpy as jnp
from jax import lax
from jax.experimental import pallas as pl
from jax.experimental.pallas import tpu as pltpu
from jax.sharding import PartitionSpec as P

LAGS = 512
GROUP = 16
ORDER = ((3, 2, 1, 0), (3, 2, 0, 1), (0, 1, 3, 2), (0, 1, 2, 3))
SPLITS = (4, 4)
INWARD = ((0, 1), (3, 2))
MIDDLE = ((1, 2), (2, 1))
OUTWARD = ((1, 0), (2, 3))
MIB = 1024 * 1024
COST = pl.CostEstimate(flops=1, bytes_accessed=1, transcendentals=0)

HBM = pl.BlockSpec(memory_space=pltpu.HBM)
ANY = pl.BlockSpec(memory_space=pl.ANY)
VMEM = pl.BlockSpec(memory_space=pltpu.VMEM)


def quarter_of(hour, slot):
    quarter = jnp.int32(ORDER[0][slot])
    for row in range(1, 4):
        quarter = jnp.where(hour == row, jnp.int32(ORDER[row][slot]), quarter)
    return quarter


def shares(window_count, freq_count):
    middle = (freq_count // (2 * GROUP) + 1) // 2 * 2 * GROUP
    half = window_count // 2
    return [
        ((low, low + half), bins) for low in (0, half) for bins in ((0, middle), (middle, freq_count))
    ]


def front_kernel(
    sources_hbm, spectra_hbm, quality_hbm,
    own_first_ref, own_second_ref, own_rest_ref, other_first_ref, other_second_ref, other_rest_ref,
    scale_ref, data_ref,
    sources_ref, quality_ref, sems, small_sems,
):
    small = [
        pltpu.make_async_copy(sources_hbm, sources_ref, small_sems.at[0]),
        pltpu.make_async_copy(quality_hbm, quality_ref, small_sems.at[1]),
    ]
    _, window_count, freq_count, channels_here = data_ref.shape
    large = []
    for at, (windows, bins) in enumerate(shares(window_count, freq_count)):
        part = (slice(None), pl.ds(windows[0], windows[1] - windows[0]), pl.ds(bins[0], bins[1] - bins[0]))
        large.append(pltpu.make_async_copy(spectra_hbm.at[part], data_ref.at[part], sems.at[at]))
    for copy in small + large:
        copy.start()
    source_count = sources_ref.shape[0]
    per_slot = source_count // 4
    wide = window_count * GROUP
    chan = lax.axis_index("chan")
    hour = lax.axis_index("hour")
    even = (chan % 2) == 0
    for copy in small:
        copy.wait()
    row = lax.broadcasted_iota(jnp.int32, (source_count, channels_here), 0)
    lane = lax.broadcasted_iota(jnp.int32, (source_count, channels_here), 1)
    wanted = jnp.full((source_count, channels_here), -1, jnp.int32)
    for slot in range(4):
        first = quarter_of(hour, slot) * per_slot
        for at in range(per_slot):
            wanted = jnp.where(row == slot * per_slot + at, sources_ref[first + at], wanted)
    onehot = (wanted - chan * channels_here == lane).astype(jnp.float32).astype(jnp.bfloat16)
    quality = quality_ref[...].astype(jnp.float32)
    usable = lax.dot_general(
        onehot, quality.astype(jnp.bfloat16), (((1,), (1,)), ((), ())), preferred_element_type=jnp.float32
    )
    spread = (
        lax.broadcasted_iota(jnp.int32, (window_count, wide), 1) // GROUP
        == lax.broadcasted_iota(jnp.int32, (window_count, wide), 0)
    )
    usable = jnp.dot(
        usable.astype(jnp.bfloat16),
        spread.astype(jnp.float32).astype(jnp.bfloat16),
        preferred_element_type=jnp.float32,
    )
    narrow = wide // 2
    totals = {}
    for copy, (windows, bins) in zip(large, shares(window_count, freq_count)):
        copy.wait()
        lanes = slice(windows[0] * GROUP, windows[1] * GROUP)
        usable_here = jnp.concatenate([usable[:, lanes]] * 2, 1)
        total = totals.get(windows, jnp.zeros((windows[1] - windows[0], 8, channels_here), jnp.float32))
        for pair in range(bins[0] // (2 * GROUP), bins[1] // (2 * GROUP)):
            picked = []
            for part in range(2):
                both = []
                for group in (2 * pair, 2 * pair + 1):
                    columns = data_ref[
                        part, windows[0] : windows[1], group * GROUP : (group + 1) * GROUP, :
                    ]
                    value = columns.astype(jnp.float32)
                    square = value * value
                    total = total + (square[:, :8] + square[:, 8:])
                    both.append(columns.reshape(narrow, channels_here))
                picked.append(
                    lax.dot_general(
                        onehot,
                        jnp.concatenate(both, 0),
                        (((1,), (1,)), ((), ())),
                        preferred_element_type=jnp.float32,
                    )
                    * usable_here
                )
            own = jnp.where(even, picked[0], picked[1])
            other = jnp.where(even, picked[1], picked[0])
            for value, first_ref, second_ref, rest_ref in (
                (own, own_first_ref, own_second_ref, own_rest_ref),
                (other, other_first_ref, other_second_ref, other_rest_ref),
            ):
                for slot, ref in enumerate((first_ref, second_ref, rest_ref, rest_ref)):
                    rows = slice(slot * per_slot, (slot + 1) * per_slot)
                    at = pair * 16 + max(slot - 2, 0) * freq_count // GROUP * per_slot
                    both = jnp.concatenate([value[rows, :narrow], value[rows, narrow:]], 0)
                    ref[at : at + 16, lanes] = both.astype(jnp.bfloat16)
        totals[windows] = total
    power = jnp.concatenate([jnp.sum(total, axis=1) for total in totals.values()], 0) / freq_count
    scale_ref[...] = lax.rsqrt(power + 1e-06) * quality


def front(spectra, quality, sources):
    _, window_count, freq_count, channels_here = spectra.shape
    rows = freq_count // GROUP * sources.shape[0] // 4
    wide = window_count * GROUP
    steps = len(shares(window_count, freq_count))
    shape = lambda count: jax.ShapeDtypeStruct((count * rows, wide), jnp.bfloat16)
    return pl.pallas_call(
        front_kernel,
        in_specs=[HBM, HBM, HBM],
        out_specs=[VMEM] * 8,
        out_shape=[
            *(shape(slots) for slots in (1, 1, 2) * 2),
            jax.ShapeDtypeStruct(quality.shape, jnp.float32),
            jax.ShapeDtypeStruct(spectra.shape, jnp.bfloat16),
        ],
        scratch_shapes=[
            pltpu.SMEM(sources.shape, jnp.int32),
            pltpu.VMEM(quality.shape, jnp.int32),
            pltpu.SemaphoreType.DMA((steps,)),
            pltpu.SemaphoreType.DMA((2,)),
        ],
        compiler_params=pltpu.CompilerParams(vmem_limit_bytes=16 * MIB),
        cost_estimate=COST,
        name="pick_sources",
    )(*(pltpu.with_memory_space_constraint(value, pltpu.HBM) for value in (sources, spectra, quality)))


def whiten_kernel(data_ref, scale_ref, after_ref, out_ref):
    _, window_count, freq_count, _ = data_ref.shape
    step = freq_count // 5
    for window in range(window_count):
        scale = scale_ref[window : window + 1, :]

        def apply(i, carry):
            bins = pl.ds(pl.multiple_of(i * step, step), step)
            for part in range(2):
                value = data_ref[part, window, bins, :].astype(jnp.float32) * scale
                out_ref[part, window, bins, :] = value.astype(jnp.bfloat16)
            return carry

        lax.fori_loop(0, freq_count // step, apply, 0)


def whiten(data, scale, after):
    return pl.pallas_call(
        whiten_kernel,
        in_specs=[VMEM, VMEM, ANY],
        out_specs=VMEM,
        out_shape=jax.ShapeDtypeStruct(data.shape, jnp.bfloat16),
        compiler_params=pltpu.CompilerParams(vmem_limit_bytes=16 * MIB),
        cost_estimate=COST,
        name="whiten_receivers",
    )(data, scale, after)


def add_kernel(count, *refs):
    total = refs[0][...].astype(jnp.float32)
    for ref in refs[1:count]:
        total = total + ref[...].astype(jnp.float32)
    refs[-1][...] = total.astype(refs[-1].dtype)


def add_after(after, *values):
    return pl.pallas_call(
        functools.partial(add_kernel, len(values)),
        in_specs=[VMEM] * len(values) + [ANY],
        out_specs=VMEM,
        out_shape=jax.ShapeDtypeStruct(values[0].shape, values[0].dtype),
        compiler_params=pltpu.CompilerParams(vmem_limit_bytes=16 * MIB),
        cost_estimate=COST,
        name="add",
    )(*values, after)


def table_kernel(after_ref, out_ref):
    lag_count, columns = out_ref.shape
    freq_count = columns // 2
    highs = lag_count // GROUP

    def angle(count, lag_of, offset):
        lag = lag_of(lax.broadcasted_iota(jnp.int32, (count, columns), 0)).astype(jnp.float32)
        column = lax.broadcasted_iota(jnp.int32, (count, columns), 1).astype(jnp.float32)
        part = (column >= freq_count).astype(jnp.float32)
        turns = (column - part * freq_count + 1.0) * lag + part * offset
        turns = turns - columns * jnp.round(turns * (1.0 / columns))
        return turns * (math.pi / freq_count)

    high = angle(highs, lambda row: row * GROUP - lag_count // 2, freq_count // 2)
    low = angle(GROUP, lambda row: row, 0)
    cos_high, sin_high = jnp.cos(high), jnp.sin(high)
    cos_low, sin_low = jnp.cos(low) / freq_count, jnp.sin(low) / freq_count
    for row in range(highs):
        value = cos_high[row : row + 1] * cos_low - sin_high[row : row + 1] * sin_low
        out_ref[row * GROUP : (row + 1) * GROUP, :] = value.astype(jnp.bfloat16)


def lag_table(freq_count, lag_count, after):
    return pl.pallas_call(
        table_kernel,
        in_specs=[ANY],
        out_specs=VMEM,
        out_shape=jax.ShapeDtypeStruct((lag_count, 2 * freq_count), jnp.bfloat16),
        compiler_params=pltpu.CompilerParams(vmem_limit_bytes=16 * MIB),
        cost_estimate=COST,
        name="lag_table",
    )(after)


def lags_kernel(
    base, done,
    own_ref, other_ref, receivers_ref, table_ref, after_ref, out_ref, *refs,
):
    spec_ref, cross_ref = refs[-2:]
    count = 8
    _, window_count, freq_count, channels_here = receivers_ref.shape
    wide = own_ref.shape[1]
    groups = freq_count // GROUP
    even = (lax.axis_index("chan") % 2) == 0

    def load(i):
        rows = pl.ds(pl.multiple_of(base + i * 16, 16), 16)
        own = own_ref[rows, :].astype(jnp.float32)
        other = other_ref[rows, :].astype(jnp.float32)
        return jnp.where(even, own, other), jnp.where(even, other, own)

    def add(i, total):
        real, imag = load(i)
        square = real * real + imag * imag
        return total + square[:8] + square[8:]

    total = lax.fori_loop(0, groups // 2, add, jnp.zeros((8, wide), jnp.float32), unroll=5)
    same = (
        lax.broadcasted_iota(jnp.int32, (wide, wide), 0) // GROUP
        == lax.broadcasted_iota(jnp.int32, (wide, wide), 1) // GROUP
    ).astype(jnp.float32)
    power = jnp.dot(total, same, preferred_element_type=jnp.float32, precision=lax.Precision.HIGHEST)
    scale = lax.rsqrt(power / freq_count + 1e-06)
    scale = jnp.concatenate([scale, scale], 0)

    def apply(i, carry):
        rows = pl.ds(pl.multiple_of(i * 16, 16), 16)
        for part, value in enumerate(load(i)):
            spec_ref[part, rows, :] = (value * scale).astype(jnp.bfloat16).astype(jnp.float32)
        return carry

    lax.fori_loop(0, groups // 2, apply, 0, unroll=5)

    diagonal = [
        lax.broadcasted_iota(jnp.int32, (8, wide), 1) % GROUP
        == lax.broadcasted_iota(jnp.int32, (8, wide), 0) + low
        for low in (0, 8)
    ]
    zero = jnp.zeros((8, wide), jnp.float32)

    def cross_of(group, carry):
        tiles = []
        for part in range(2):
            rows = spec_ref[part, pl.ds(pl.multiple_of(group * 8, 8), 8), :]
            for at in range(count):
                row = jnp.broadcast_to(rows[at : at + 1, :], (8, wide))
                tiles += [jnp.where(mask, row, zero) for mask in diagonal]
        bins = pl.ds(pl.multiple_of(group * GROUP, GROUP), GROUP)
        real = receivers_ref[0, :, bins, :].reshape(wide, channels_here)
        imag = receivers_ref[1, :, bins, :].reshape(wide, channels_here)
        cross = jnp.dot(
            jnp.concatenate(tiles, 0).astype(jnp.bfloat16),
            jnp.concatenate([real, imag], 1),
            preferred_element_type=jnp.float32,
        )
        half = count * GROUP
        parts = (
            cross[:half, :channels_here] + cross[half:, channels_here:],
            cross[:half, channels_here:] - cross[half:, :channels_here],
        )
        for part, value in enumerate(parts):
            value = value.astype(jnp.bfloat16)
            rows = pl.ds(pl.multiple_of(part * freq_count + group * GROUP, GROUP), GROUP)
            for at in range(count):
                ref, pair = (cross_ref, at // 2) if at < done else (refs[0], (at - done) // 2)
                lanes = slice((at % 2) * channels_here, (at % 2 + 1) * channels_here)
                ref[pair, rows, lanes] = value[at * GROUP : (at + 1) * GROUP]
        return carry

    lax.fori_loop(0, groups, cross_of, 0, unroll=25)
    transform(cross_ref, table_ref, out_ref)


def transform(cross_ref, table_ref, out_ref):
    channels_here = out_ref.shape[2]
    rows = 128
    for pair in range(cross_ref.shape[0]):
        for block in range(table_ref.shape[0] // rows):
            lags = slice(block * rows, (block + 1) * rows)
            value = jnp.dot(
                table_ref[lags, :], cross_ref[pair], preferred_element_type=jnp.float32
            ).astype(jnp.bfloat16)
            out_ref[2 * pair, lags, :] = value[:, :channels_here]
            out_ref[2 * pair + 1, lags, :] = value[:, channels_here:]


def lags_of(own, other, receivers, table, base, done, after):
    _, window_count, freq_count, channels_here = receivers.shape
    wide = own.shape[1]
    count = 8
    cross = lambda sources: (sources // 2, 2 * freq_count, 2 * channels_here)
    out_shape = [jax.ShapeDtypeStruct((done, table.shape[0], channels_here), jnp.bfloat16)]
    if done < count:
        out_shape.append(jax.ShapeDtypeStruct(cross(count - done), jnp.bfloat16))
    return pl.pallas_call(
        functools.partial(lags_kernel, base, done),
        in_specs=[VMEM] * 4 + [ANY],
        out_specs=[VMEM] * len(out_shape),
        out_shape=out_shape,
        scratch_shapes=[
            pltpu.VMEM((2, freq_count // GROUP * 8, wide), jnp.float32),
            pltpu.VMEM(cross(done), jnp.bfloat16),
        ],
        compiler_params=pltpu.CompilerParams(vmem_limit_bytes=16 * MIB),
        cost_estimate=COST,
        name="lags",
    )(own, other, receivers, table, after)


def lags_of_rest(cross, table, after):
    pairs, _, lanes = cross.shape
    return pl.pallas_call(
        lambda cross_ref, table_ref, after_ref, out_ref: transform(cross_ref, table_ref, out_ref),
        in_specs=[VMEM, VMEM, ANY],
        out_specs=VMEM,
        out_shape=jax.ShapeDtypeStruct((2 * pairs, table.shape[0], lanes // 2), jnp.bfloat16),
        compiler_params=pltpu.CompilerParams(vmem_limit_bytes=16 * MIB),
        cost_estimate=COST,
        name="lags_rest",
    )(cross, table, after)


def chip_stages(chan_count):
    bits = [1 << b for b in range(1, chan_count.bit_length() - 1)]
    turned = bits[1:] + bits[:1]
    return [
        [(i, i ^ (odd_bit if i % 2 else even_bit)) for i in range(chan_count)]
        for even_bit, odd_bit in zip(bits, turned)
    ]


def body(chan_count, spectra, quality, sources):
    own, other, (scale, data) = (lambda v: (v[:3], v[3:6], v[6:]))(front(spectra, quality, sources))
    freq_count = spectra.shape[2]
    slot_rows = own[0].shape[0]
    stages = chip_stages(chan_count)
    cores = [(i, i ^ 1) for i in range(chan_count)]
    over_chan = lambda value, pairs: lax.ppermute(value, "chan", pairs)
    over_hour = lambda value, pairs: lax.ppermute(value, "hour", pairs)

    moved = [over_chan(value, cores) for value in other]
    state = list(own)

    def receive(at, pairs):
        state[at] = add_after(last, state[at], moved[at])
        moved[at] = over_chan(state[at], pairs)
        return state[at]

    last = scale
    last = receive(0, stages[0])
    table = last = lag_table(freq_count, LAGS, last)
    for pairs in stages[1:]:
        last = receive(0, pairs)
    last = receive(1, stages[0])
    receivers = last = whiten(data, scale, last)
    last = receive(0, cores)
    for pairs in stages[1:]:
        last = receive(1, pairs)
    last = receive(2, stages[0])

    def lags(chunk, base=0, done=8):
        return lags_of(*chunk, receivers, table, base, done, last)

    mine = [[], [], [], []]
    inward = [[], [], []]
    middle = [[], []]

    def send_inward(slot, value):
        mine[slot].append(value)
        inward[slot].append(over_hour(value, INWARD))
        return value

    def send_middle(slot, at):
        value = add_after(last, mine[slot][at], inward[slot][at])
        middle[slot].append(over_hour(value, MIDDLE))
        return value

    value, cross = lags((state[0], moved[0]), 0, SPLITS[0])
    last = send_inward(0, value)
    last = receive(1, cores)
    for pairs in stages[1:]:
        last = receive(2, pairs)
    last = send_inward(0, lags_of_rest(cross, table, last))
    last = receive(2, cores)
    value, cross = lags((state[1], moved[1]), 0, SPLITS[1])
    last = send_inward(1, value)
    last = send_inward(1, lags_of_rest(cross, table, last))
    last = send_middle(0, 0)
    last = send_middle(0, 1)
    rest = (state[2], moved[2])
    last = send_inward(2, lags(rest)[0])
    last = own_lags = lags(rest, slot_rows)[0]
    outward = []
    cuts = (0, SPLITS[0], 8)
    sums = [mine[2][0][low:high] for low, high in zip(cuts, cuts[1:])]
    last = send_middle(1, 0)
    for at in range(2):
        last = add_after(last, sums[at], middle[0][at])
        outward.append(over_hour(last, OUTWARD))
    last = send_middle(1, 1)
    whole = lambda values: values[0] if len(values) == 1 else jnp.concatenate(values, 0)
    values = [own_lags] + [whole(values) for values in (middle[1], outward, inward[2])]
    return sum(value.astype(jnp.float32) for value in values).astype(jnp.bfloat16)


def solution(mesh):
    placed = (P(None, "hour", None, "chan"), P("hour", "chan"), P())
    return jax.shard_map(
        functools.partial(body, mesh.shape["chan"]),
        mesh=mesh,
        in_specs=placed,
        out_specs=P("hour", None, "chan"),
        check_vma=False,
    )
```

time: 350 us -> 103 us (0.29)
  waiting for transfers between devices: 145 us -> 42.5 us
  blocking collectives: 77.8 us -> 0 us
  matrix products: 51.3 us -> 0 us
  other arithmetic: 34.1 us -> 1.52 us
  starting transfers between devices: 0.01 us -> 29.9 us
  Pallas kernels: 0 us -> 28.4 us
  local copies, waits for them, and re-layouts: 27.1 us -> 0.07 us
  between operations: 13.5 us -> 0.3 us
    reduce_scatter x1 -> x0, waiting for transfers between devices: 145 us -> none  [body(): lax.psum_scatter(jnp.einsum('kfsc,kfl->slc', partial_value, table, prefer...]
    psum x1 -> x0, blocking collectives: 77.8 us -> none  [body(): source_spec = lax.psum(picked, 'chan').astype(jnp.bfloat16)]
    dot_general x4 -> x0, matrix products: 51.3 us -> none  [the longest x1 21.3 us: body(): jnp.einsum('kfsc,kfl->slc', partial_value, table, preferred_element_type=...]
    ppermute x0 -> x23, waiting for transfers between devices: none -> 42.5 us  [the longest x11 27.7 us: body(): over_hour = lambda value, pairs: lax.ppermute(value, 'hour', pairs)]
    ppermute x0 -> x23, starting transfers between devices: none -> 29.9 us  [the longest x11 20.4 us: body(): over_hour = lambda value, pairs: lax.ppermute(value, 'hour', pairs)]
    pallas_call x0 -> x24, Pallas kernels: none -> 28.4 us  [the longest x4 17.2 us: lags_of(): pl.pallas_call(functools.partial(lags_kernel, base, done), in_specs=[VMEM...]
    convert_element_type x3 -> x1, other arithmetic: 15.9 us -> 1.52 us  [body(): sum((value.astype(jnp.float32) for value in values)).astype(jnp.bfloat16)]
    another operation x1 -> x0, local copies, waits for them, and re-layouts: 10.9 us -> none  [cross_spectrum(): left_pair = jnp.stack([source_spec[0], -source_spec[1]])]
  transfers between devices with their start and end apart: 1 -> 23, of which waited for: 1 -> 14; matrix products, arithmetic and copies ran while one was open for 0% -> 0% of each run, Pallas kernels for 0% -> 23%
where the time goes in v2:
time: 103 us
  waiting for transfers between devices  42.5 us (41%)
  starting transfers between devices  29.9 us (29%)
  Pallas kernels  28.4 us (28%)
  other arithmetic  1.52 us (1%)
    ppermute x11, waiting for transfers between devices, body(): over_hour = lambda value, pairs: lax.ppermute(value, 'hour', pairs)  27.7 us
    ppermute x11, starting transfers between devices, body(): over_hour = lambda value, pairs: lax.ppermute(value, 'hour', pairs)  20.4 us
    pallas_call x4, Pallas kernels, lags_of(): pl.pallas_call(functools.partial(lags_kernel, base, done), in_specs=[VMEM...  17.2 us
    ppermute x12, waiting for transfers between devices, body(): over_chan = lambda value, pairs: lax.ppermute(value, 'chan', pairs)  14.8 us
    ppermute x12, starting transfers between devices, body(): over_chan = lambda value, pairs: lax.ppermute(value, 'chan', pairs)  9.55 us
    pallas_call x1, Pallas kernels, front(): pl.pallas_call(front_kernel, in_specs=[HBM, HBM, HBM], out_specs=[VMEM] *...  4.23 us
    pallas_call x2, Pallas kernels, lags_of_rest(): pl.pallas_call(lambda cross_ref, table_ref, after_ref, out_ref: transform...  2.26 us
  transfers between devices with their start and end apart: 23, of which 14 were waited for; matrix products, arithmetic and copies ran while one was open for 0% of the time, Pallas kernels for 23%

profile of v2, /device:TPU:16, one launch (start us, length us, event | category | flops | bytes accessed | tf_op | source)
XLA Modules:
  0.0 102.6 jit_solution(2553475688114871832)
XLA Ops:
  0.0 4.2 %pick_sources.1 = (bf16[400,256]{1,0:T(8,128)(2,1)S(1)}, bf16[400,256]{1,0:T(8,128)(2,1)S(1)}, bf16[800,256]{1,0:T(8,128)(2,1)S(1)}, bf16[400,256]{1,0:T(8,128)(...) custom-call(s32[32]{0:T(128)} %sources_hbm.1, ...), custom_call_target="tpu_custom_call" | custom-call | flops 1 | bytes 1 | tf_op jit(solution)/shard_map/pick_sources/pallas_call | solution.py:137
  4.3 1.4 %collective-permute-done.2.refs_1_ = bf16[400,256]{1,0:T(8,128)(2,1)S(1)} collective-permute-done((bf16[400,256]{1,0:T(8,128)(2,1)S(1)}, bf16[400,256]{1,0:T(8,128)(2,1)S(1)}, u32[]{:S(2)}, u32[]{:S(2)}) %collective-permute-start.2) | collective-permute-done | bytes 204832 | tf_op jit(solution)/shard_map/ppermute | solution.py:382
  5.8 1.6 %collective-permute-start.3 = (bf16[400,256]{1,0:T(8,128)(2,1)S(1)}, bf16[400,256]{1,0:T(8,128)(2,1)S(1)}, u32[]{:S(2)}, u32[]{:S(2)}) collective-permute-start(bf16[400,256]{1,0:T(8,128)(2,1)S(1)} %add.30.after_ref.refs_0_), channel_id=1, source_target_pairs={{0,8},{4,20},{8,0},{12,28},{16,24},{20,4},{24,16},{28,12},{1,9},{5... | collective-permute-start | bytes 614408 | tf_op jit(solution)/shard_map/ppermute | solution.py:382
  7.4 0.5 collective-permute-start
  7.9 1.9 %lag_table.1.refs_2_.table_ref = bf16[512,1600]{1,0:T(8,128)(2,1)S(1)} custom-call(bf16[400,256]{1,0:T(8,128)(2,1)S(1)} %add.30.after_ref.refs_0_), custom_call_target="tpu_custom_call" | custom-call | flops 1 | bytes 1 | tf_op jit(solution)/shard_map/lag_table/pallas_call | solution.py:228
  9.7 1.9 %collective-permute-done.3.refs_1_ = bf16[400,256]{1,0:T(8,128)(2,1)S(1)} collective-permute-done((bf16[400,256]{1,0:T(8,128)(2,1)S(1)}, bf16[400,256]{1,0:T(8,128)(2,1)S(1)}, u32[]{:S(2)}, u32[]{:S(2)}) %collective-permute-start.3) | collective-permute-done | bytes 204832 | tf_op jit(solution)/shard_map/ppermute | solution.py:382
  11.7 1.6 %collective-permute-start.5 = (bf16[400,256]{1,0:T(8,128)(2,1)S(1)}, bf16[400,256]{1,0:T(8,128)(2,1)S(1)}, u32[]{:S(2)}, u32[]{:S(2)}) collective-permute-start(bf16[400,256]{1,0:T(8,128)(2,1)S(1)} %add.31.refs_2_.refs_0_), channel_id=1, source_target_pairs={{0,16},{4,12},{8,24},{12,4},{16,0},{20,28},{24,8},{28,20},{1,17},{... | collective-permute-start | bytes 614408 | tf_op jit(solution)/shard_map/ppermute | solution.py:382
  13.3 1.6 %collective-permute-start.4 = (bf16[400,256]{1,0:T(8,128)(2,1)S(1)}, bf16[400,256]{1,0:T(8,128)(2,1)S(1)}, u32[]{:S(2)}, u32[]{:S(2)}) collective-permute-start(bf16[400,256]{1,0:T(8,128)(2,1)S(1)} %add.32.after_ref.refs_0_), channel_id=1, source_target_pairs={{0,8},{4,20},{8,0},{12,28},{16,24},{20,4},{24,16},{28,12},{1,9},{5... | collective-permute-start | bytes 614408 | tf_op jit(solution)/shard_map/ppermute | solution.py:382
  14.9 1.5 %whiten_receivers.1.refs_2_.receivers_ref = bf16[2,16,800,128]{3,2,1,0:T(8,128)(2,1)S(1)} custom-call(bf16[2,16,800,128]{3,2,1,0:T(8,128)(2,1)S(1)} %get-tuple-element.24.data_ref, f32[16,128]{1,0:T(8,128)S(1)} %get-tuple-element.23.refs_2_.scale_ref, bf16[400,256]{1,0:T(8,128)(2,1)S(1)} %add.32.after_ref.refs_0_), custom_call_target="tpu_custom_call" | custom-call | flops 1 | bytes 1 | tf_op jit(solution)/shard_map/whiten_receivers/pallas_call | solution.py:175
  16.4 3.0 %collective-permute-done.5.refs_1_ = bf16[400,256]{1,0:T(8,128)(2,1)S(1)} collective-permute-done((bf16[400,256]{1,0:T(8,128)(2,1)S(1)}, bf16[400,256]{1,0:T(8,128)(2,1)S(1)}, u32[]{:S(2)}, u32[]{:S(2)}) %collective-permute-start.5) | collective-permute-done | bytes 204832 | tf_op jit(solution)/shard_map/ppermute | solution.py:382
  19.6 1.3 %collective-permute-start.6 = (bf16[800,256]{1,0:T(8,128)(2,1)S(1)}, bf16[800,256]{1,0:T(8,128)(2,1)S(1)}, u32[]{:S(2)}, u32[]{:S(2)}) collective-permute-start(bf16[800,256]{1,0:T(8,128)(2,1)S(1)} %add.35.after_ref.refs_0_), channel_id=1, source_target_pairs={{0,8},{4,20},{8,0},{12,28},{16,24},{20,4},{24,16},{28,12},{1,9},{5... | collective-permute-start | bytes 1228808 | tf_op jit(solution)/shard_map/ppermute | solution.py:382
  20.9 0.8 collective-permute-start.7
  21.7 0.6 collective-permute-done.8.other_ref
  22.3 3.8 %lags.4 = (bf16[4,512,128]{2,1,0:T(8,128)(2,1)S(1)}, bf16[2,1600,256]{2,1,0:T(8,128)(2,1)S(1)}) custom-call(bf16[400,256]{1,0:T(8,128)(2,1)S(1)} %add.33.refs_2_.own_ref, bf16[400,256]{1,0:T(8,128)(2,1)S(1)} %collective-permute-done.8.other_ref, bf16[2,16,800,128]{3,2,1,0:T(8,128)(2,1)S(1)} %whiten_receivers.1.refs_2_.receivers_ref, ...), custom_call_target="tpu_custom_call" | custom-call | flops 1 | bytes 1 | tf_op jit(solution)/shard_map/lags/pallas_call | solution.py:339
  26.1 2.5 %collective-permute-done.7.refs_1_ = bf16[400,256]{1,0:T(8,128)(2,1)S(1)} collective-permute-done((bf16[400,256]{1,0:T(8,128)(2,1)S(1)}, bf16[400,256]{1,0:T(8,128)(2,1)S(1)}, u32[]{:S(2)}, u32[]{:S(2)}) %collective-permute-start.7) | collective-permute-done | bytes 204832 | tf_op jit(solution)/shard_map/ppermute | solution.py:382
  28.7 1.1 %collective-permute-done.6.refs_1_ = bf16[800,256]{1,0:T(8,128)(2,1)S(1)} collective-permute-done((bf16[800,256]{1,0:T(8,128)(2,1)S(1)}, bf16[800,256]{1,0:T(8,128)(2,1)S(1)}, u32[]{:S(2)}, u32[]{:S(2)}) %collective-permute-start.6) | collective-permute-done | bytes 409632 | tf_op jit(solution)/shard_map/ppermute | solution.py:382
  29.9 1.6 %collective-permute-start.9 = (bf16[800,256]{1,0:T(8,128)(2,1)S(1)}, bf16[800,256]{1,0:T(8,128)(2,1)S(1)}, u32[]{:S(2)}, u32[]{:S(2)}) collective-permute-start(bf16[800,256]{1,0:T(8,128)(2,1)S(1)} %add.37.after_ref.refs_0_), channel_id=1, source_target_pairs={{0,16},{4,12},{8,24},{12,4},{16,0},{20,28},{24,8},{28,20},{1,17},{... | collective-permute-start | bytes 1228808 | tf_op jit(solution)/shard_map/ppermute | solution.py:382
  31.5 1.3 %collective-permute-start.12 = (bf16[4,512,128]{2,1,0:T(8,128)(2,1)S(1)}, bf16[4,512,128]{2,1,0:T(8,128)(2,1)S(1)}, u32[]{:S(2)}, u32[]{:S(2)}) collective-permute-start(bf16[4,512,128]{2,1,0:T(8,128)(2,1)S(1)} %get-tuple-element.25.refs_2_.refs_0_), channel_id=1, source_target_pairs={{0,1},{3,2},{4,5},{7,6},{8,9},{11,10},{12,13},{15,14},{16,17},{19,... | collective-permute-start | bytes 1572872 | tf_op jit(solution)/shard_map/ppermute | solution.py:383
  32.8 1.1 %lags_rest.2.refs_2_.refs_0_ = bf16[4,512,128]{2,1,0:T(8,128)(2,1)S(1)} custom-call(bf16[2,1600,256]{2,1,0:T(8,128)(2,1)S(1)} %get-tuple-element.26.cross_ref, bf16[512,1600]{1,0:T(8,128)(2,1)S(1)} %lag_table.1.refs_2_.table_ref, bf16[800,256]{1,0:T(8,128)(2,1)S(1)} %add.37.after_ref.refs_0_), custom_call_target="tpu_custom_call" | custom-call | flops 1 | bytes 1 | tf_op jit(solution)/shard_map/lags_rest/pallas_call | solution.py:356
  33.9 1.3 %collective-permute-start.11 = (bf16[4,512,128]{2,1,0:T(8,128)(2,1)S(1)}, bf16[4,512,128]{2,1,0:T(8,128)(2,1)S(1)}, u32[]{:S(2)}, u32[]{:S(2)}) collective-permute-start(bf16[4,512,128]{2,1,0:T(8,128)(2,1)S(1)} %lags_rest.2.refs_2_.refs_0_), channel_id=1, source_target_pairs={{0,1},{3,2},{4,5},{7,6},{8,9},{11,10},{12,13},{15,14},{16,17},{19,... | collective-permute-start | bytes 1572872 | tf_op jit(solution)/shard_map/ppermute | solution.py:383
  35.2 2.7 %collective-permute-done.9.refs_1_ = bf16[800,256]{1,0:T(8,128)(2,1)S(1)} collective-permute-done((bf16[800,256]{1,0:T(8,128)(2,1)S(1)}, bf16[800,256]{1,0:T(8,128)(2,1)S(1)}, u32[]{:S(2)}, u32[]{:S(2)}) %collective-permute-start.9) | collective-permute-done | bytes 409632 | tf_op jit(solution)/shard_map/ppermute | solution.py:382
  38.1 0.5 collective-permute-start.13
  38.6 1.5 %collective-permute-done.13.other_ref = bf16[400,256]{1,0:T(8,128)(2,1)S(1)} collective-permute-done((bf16[400,256]{1,0:T(8,128)(2,1)S(1)}, bf16[400,256]{1,0:T(8,128)(2,1)S(1)}, u32[]{:S(2)}, u32[]{:S(2)}) %collective-permute-start.13) | collective-permute-done | bytes 204832 | tf_op jit(solution)/shard_map/ppermute | solution.py:382
  40.1 3.8 %lags.5 = (bf16[4,512,128]{2,1,0:T(8,128)(2,1)S(1)}, bf16[2,1600,256]{2,1,0:T(8,128)(2,1)S(1)}) custom-call(bf16[400,256]{1,0:T(8,128)(2,1)S(1)} %add.36.refs_2_.own_ref, bf16[400,256]{1,0:T(8,128)(2,1)S(1)} %collective-permute-done.13.other_ref, bf16[2,16,800,128]{3,2,1,0:T(8,128)(2,1)S(1)} %whiten_receivers.1.refs_2_.receivers_ref, ...), custom_call_target="tpu_custom_call" | custom-call | flops 1 | bytes 1 | tf_op jit(solution)/shard_map/lags/pallas_call | solution.py:339
  43.9 1.5 %collective-permute-start.14 = (bf16[4,512,128]{2,1,0:T(8,128)(2,1)S(1)}, bf16[4,512,128]{2,1,0:T(8,128)(2,1)S(1)}, u32[]{:S(2)}, u32[]{:S(2)}) collective-permute-start(bf16[4,512,128]{2,1,0:T(8,128)(2,1)S(1)} %get-tuple-element.28.after_ref.refs_0_), channel_id=1, source_target_pairs={{0,1},{3,2},{4,5},{7,6},{8,9},{11,10},{12,13},{15,14},{16,17},{19,... | collective-permute-start | bytes 1572872 | tf_op jit(solution)/shard_map/ppermute | solution.py:383
  45.4 1.1 %lags_rest.3.refs_2_.refs_0_ = bf16[4,512,128]{2,1,0:T(8,128)(2,1)S(1)} custom-call(bf16[2,1600,256]{2,1,0:T(8,128)(2,1)S(1)} %get-tuple-element.27.cross_ref, bf16[512,1600]{1,0:T(8,128)(2,1)S(1)} %lag_table.1.refs_2_.table_ref, bf16[4,512,128]{2,1,0:T(8,128)(2,1)S(1)} %get-tuple-element.28.after_ref.refs_0_), custom_call_target="tpu_custom_call" | custom-call | flops 1 | bytes 1 | tf_op jit(solution)/shard_map/lags_rest/pallas_call | solution.py:356
  46.5 1.7 %collective-permute-done.12.refs_1_ = bf16[4,512,128]{2,1,0:T(8,128)(2,1)S(1)} collective-permute-done((bf16[4,512,128]{2,1,0:T(8,128)(2,1)S(1)}, bf16[4,512,128]{2,1,0:T(8,128)(2,1)S(1)}, u32[]{:S(2)}, u32[]{:S(2)}) %collective-permute-start.12) | collective-permute-done | bytes 524320 | tf_op jit(solution)/shard_map/ppermute | solution.py:383
  48.2 0.1 add.39.refs_2_
  48.4 2.4 %collective-permute-start.18 = (bf16[4,512,128]{2,1,0:T(8,128)(2,1)S(1)}, bf16[4,512,128]{2,1,0:T(8,128)(2,1)S(1)}, u32[]{:S(2)}, u32[]{:S(2)}) collective-permute-start(bf16[4,512,128]{2,1,0:T(8,128)(2,1)S(1)} %add.39.refs_2_), channel_id=1, source_target_pairs={{1,2},{2,1},{5,6},{6,5},{9,10},{10,9},{13,14},{14,13},{17,18},{18,... | collective-permute-start | bytes 1572872 | tf_op jit(solution)/shard_map/ppermute | solution.py:383
  50.7 8.7 %collective-permute-done.11.refs_1_ = bf16[4,512,128]{2,1,0:T(8,128)(2,1)S(1)} collective-permute-done((bf16[4,512,128]{2,1,0:T(8,128)(2,1)S(1)}, bf16[4,512,128]{2,1,0:T(8,128)(2,1)S(1)}, u32[]{:S(2)}, u32[]{:S(2)}) %collective-permute-start.11) | collective-permute-done | bytes 524320 | tf_op jit(solution)/shard_map/ppermute | solution.py:383
  59.5 0.1 add.40.after_ref
  59.6 2.4 %collective-permute-start.17 = (bf16[4,512,128]{2,1,0:T(8,128)(2,1)S(1)}, bf16[4,512,128]{2,1,0:T(8,128)(2,1)S(1)}, u32[]{:S(2)}, u32[]{:S(2)}) collective-permute-start(bf16[4,512,128]{2,1,0:T(8,128)(2,1)S(1)} %add.40.after_ref), channel_id=1, source_target_pairs={{1,2},{2,1},{5,6},{6,5},{9,10},{10,9},{13,14},{14,13},{17,18},{18,... | collective-permute-start | bytes 1572872 | tf_op jit(solution)/shard_map/ppermute | solution.py:383
  62.0 1.3 %collective-permute-start.16 = (bf16[4,512,128]{2,1,0:T(8,128)(2,1)S(1)}, bf16[4,512,128]{2,1,0:T(8,128)(2,1)S(1)}, u32[]{:S(2)}, u32[]{:S(2)}) collective-permute-start(bf16[4,512,128]{2,1,0:T(8,128)(2,1)S(1)} %lags_rest.3.refs_2_.refs_0_), channel_id=1, source_target_pairs={{0,1},{3,2},{4,5},{7,6},{8,9},{11,10},{12,13},{15,14},{16,17},{19,... | collective-permute-start | bytes 1572872 | tf_op jit(solution)/shard_map/ppermute | solution.py:383
  63.3 4.8 %lags.6.after_ref = bf16[8,512,128]{2,1,0:T(8,128)(2,1)S(1)} custom-call(bf16[800,256]{1,0:T(8,128)(2,1)S(1)} %add.38.after_ref.own_ref, bf16[800,256]{1,0:T(8,128)(2,1)S(1)} %collective-permute-done.10.other_ref, bf16[2,16,800,128]{3,2,1,0:T(8,128)(2,1)S(1)} %whiten_receivers.1.refs_2_.receivers_ref, bf16[512,1600]{1,0:T(8,128)(2,1)S(1)} %lag_table.1.refs_2_.table_ref, ...), custom_call_target="tpu_custom_call" | custom-call | flops 1 | bytes 1 | tf_op jit(solution)/shard_map/lags/pallas_call | solution.py:339
  68.1 1.3 %collective-permute-start.22 = (bf16[8,512,128]{2,1,0:T(8,128)(2,1)S(1)}, bf16[8,512,128]{2,1,0:T(8,128)(2,1)S(1)}, u32[]{:S(2)}, u32[]{:S(2)}) collective-permute-start(bf16[8,512,128]{2,1,0:T(8,128)(2,1)S(1)} %lags.6.after_ref), channel_id=1, source_target_pairs={{0,1},{3,2},{4,5},{7,6},{8,9},{11,10},{12,13},{15,14},{16,17},{19,... | collective-permute-start | bytes 3145736 | tf_op jit(solution)/shard_map/ppermute | solution.py:383
  69.4 4.8 %lags.7.refs_2_ = bf16[8,512,128]{2,1,0:T(8,128)(2,1)S(1)} custom-call(bf16[800,256]{1,0:T(8,128)(2,1)S(1)} %add.38.after_ref.own_ref, bf16[800,256]{1,0:T(8,128)(2,1)S(1)} %collective-permute-done.10.other_ref, bf16[2,16,800,128]{3,2,1,0:T(8,128)(2,1)S(1)} %whiten_receivers.1.refs_2_.receivers_ref, bf16[512,1600]{1,0:T(8,128)(2,1)S(1)} %lag_table.1.refs_2_.table_ref, ...), custom_call_target="tpu_custom_call" | custom-call | flops 1 | bytes 1 | tf_op jit(solution)/shard_map/lags/pallas_call | solution.py:339
  74.3 0.1 add.41.refs_2_
  74.4 3.5 %collective-permute-start.15 = (bf16[4,512,128]{2,1,0:T(8,128)(2,1)S(1)}, bf16[4,512,128]{2,1,0:T(8,128)(2,1)S(1)}, u32[]{:S(2)}, u32[]{:S(2)}) collective-permute-start(bf16[4,512,128]{2,1,0:T(8,128)(2,1)S(1)} %add.41.refs_2_), channel_id=1, source_target_pairs={{1,2},{2,1},{5,6},{6,5},{9,10},{10,9},{13,14},{14,13},{17,18},{18,... | collective-permute-start | bytes 1572872 | tf_op jit(solution)/shard_map/ppermute | solution.py:383
  77.9 0.1 add.42.refs_2_
  78.0 1.9 %collective-permute-start.20 = (bf16[4,512,128]{2,1,0:T(8,128)(2,1)S(1)}, bf16[4,512,128]{2,1,0:T(8,128)(2,1)S(1)}, u32[]{:S(2)}, u32[]{:S(2)}) collective-permute-start(bf16[4,512,128]{2,1,0:T(8,128)(2,1)S(1)} %add.42.refs_2_), channel_id=1, source_target_pairs={{1,0},{2,3},{5,4},{6,7},{9,8},{10,11},{13,12},{14,15},{17,16},{18,... | collective-permute-start | bytes 1572872 | tf_op jit(solution)/shard_map/ppermute | solution.py:383
  79.9 0.1 add.43.refs_2_
  80.1 1.9 %collective-permute-done.16.refs_1_ = bf16[4,512,128]{2,1,0:T(8,128)(2,1)S(1)} collective-permute-done((bf16[4,512,128]{2,1,0:T(8,128)(2,1)S(1)}, bf16[4,512,128]{2,1,0:T(8,128)(2,1)S(1)}, u32[]{:S(2)}, u32[]{:S(2)}) %collective-permute-start.16) | collective-permute-done | bytes 524320 | tf_op jit(solution)/shard_map/ppermute | solution.py:383
  82.1 2.4 %collective-permute-start.19 = (bf16[4,512,128]{2,1,0:T(8,128)(2,1)S(1)}, bf16[4,512,128]{2,1,0:T(8,128)(2,1)S(1)}, u32[]{:S(2)}, u32[]{:S(2)}) collective-permute-start(bf16[4,512,128]{2,1,0:T(8,128)(2,1)S(1)} %add.44), channel_id=1, source_target_pairs={{1,2},{2,1},{5,6},{6,5},{9,10},{10,9},{13,14},{14,13},{17,18},{18,... | collective-permute-start | bytes 1572872 | tf_op jit(solution)/shard_map/ppermute | solution.py:383
  84.4 1.3 %collective-permute-start.21 = (bf16[4,512,128]{2,1,0:T(8,128)(2,1)S(1)}, bf16[4,512,128]{2,1,0:T(8,128)(2,1)S(1)}, u32[]{:S(2)}, u32[]{:S(2)}) collective-permute-start(bf16[4,512,128]{2,1,0:T(8,128)(2,1)S(1)} %add.43.refs_2_), channel_id=1, source_target_pairs={{1,0},{2,3},{5,4},{6,7},{9,8},{10,11},{13,12},{14,15},{17,16},{18,... | collective-permute-start | bytes 1572872 | tf_op jit(solution)/shard_map/ppermute | solution.py:383
  85.8 5.1 %collective-permute-done.15 = bf16[4,512,128]{2,1,0:T(8,128)(2,1)S(1)} collective-permute-done((bf16[4,512,128]{2,1,0:T(8,128)(2,1)S(1)}, bf16[4,512,128]{2,1,0:T(8,128)(2,1)S(1)}, u32[]{:S(2)}, u32[]{:S(2)}) %collective-permute-start.15) | collective-permute-done | bytes 524320 | tf_op jit(solution)/shard_map/ppermute | solution.py:383
  90.8 5.9 %collective-permute-done.19 = bf16[4,512,128]{2,1,0:T(8,128)(2,1)S(1)} collective-permute-done((bf16[4,512,128]{2,1,0:T(8,128)(2,1)S(1)}, bf16[4,512,128]{2,1,0:T(8,128)(2,1)S(1)}, u32[]{:S(2)}, u32[]{:S(2)}) %collective-permute-start.19) | collective-permute-done | bytes 524320 | tf_op jit(solution)/shard_map/ppermute | solution.py:383
  96.7 4.4 %collective-permute-done.22 = bf16[8,512,128]{2,1,0:T(8,128)(2,1)S(1)} collective-permute-done((bf16[8,512,128]{2,1,0:T(8,128)(2,1)S(1)}, bf16[8,512,128]{2,1,0:T(8,128)(2,1)S(1)}, u32[]{:S(2)}, u32[]{:S(2)}) %collective-permute-start.22) | collective-permute-done | bytes 1048608 | tf_op jit(solution)/shard_map/ppermute | solution.py:383
  101.1 1.5 %add_convert_fusion = bf16[8,512,128]{2,1,0:T(8,128)(2,1)} fusion(bf16[8,512,128]{2,1,0:T(8,128)(2,1)S(1)} %collective-permute-done.22, bf16[8,512,128]{2,1,0:T(8,128)(2,1)S(1)} %lags.7.refs_2_, bf16[4,512,128]{2,1,0:T(8,128)(2,1)S(1)} %collective-permute-done.19, bf16[4,512,128]{2,1,0:T(8,128)(2,1)S(1)} %collective-permute-done.15, ...), kind=kLoop, calls=%fused_computation | loop fusion | flops 5242880 | bytes 5242880 | tf_op jit(solution)/shard_map/convert_element_type | solution.py:447
  (24 shorter events, 0.9 us)
Async XLA Ops:
  4.2 1.5 %collective-permute-start.2 = (bf16[400,256]{1,0:T(8,128)(2,1)S(1)}, bf16[400,256]{1,0:T(8,128)(2,1)S(1)}, u32[]{:S(2)}, u32[]{:S(2)}) collective-permute-start(bf16[400,256]{1,0:T(8,128)(2,1)S(1)} %get-tuple-element.22), channel_id=1, source_target_pairs={{0,4},{4,0},{8,12},{12,8},{16,20},{20,16},{24,28},{28,24},{1,5},{5... | collective-permute-start | bytes 614408 | tf_op jit(solution)/shard_map/ppermute | solution.py:382
  5.8 5.8 %collective-permute-start.3 = (bf16[400,256]{1,0:T(8,128)(2,1)S(1)}, bf16[400,256]{1,0:T(8,128)(2,1)S(1)}, u32[]{:S(2)}, u32[]{:S(2)}) collective-permute-start(bf16[400,256]{1,0:T(8,128)(2,1)S(1)} %add.30.after_ref.refs_0_), channel_id=1, source_target_pairs={{0,8},{4,20},{8,0},{12,28},{16,24},{20,4},{24,16},{28,12},{1,9},{5... | collective-permute-start | bytes 614408 | tf_op jit(solution)/shard_map/ppermute | solution.py:382
  7.4 5.9 %collective-permute-start.1 = (bf16[400,256]{1,0:T(8,128)(2,1)S(1)}, bf16[400,256]{1,0:T(8,128)(2,1)S(1)}, u32[]{:S(2)}, u32[]{:S(2)}) collective-permute-start(bf16[400,256]{1,0:T(8,128)(2,1)S(1)} %get-tuple-element.20), channel_id=1, source_target_pairs={{0,4},{4,0},{8,12},{12,8},{16,20},{20,16},{24,28},{28,24},{1,5},{5... | collective-permute-start | bytes 614408 | tf_op jit(solution)/shard_map/ppermute | solution.py:382
  7.4 12.1 %collective-permute-start = (bf16[800,256]{1,0:T(8,128)(2,1)S(1)}, bf16[800,256]{1,0:T(8,128)(2,1)S(1)}, u32[]{:S(2)}, u32[]{:S(2)}) collective-permute-start(bf16[800,256]{1,0:T(8,128)(2,1)S(1)} %get-tuple-element.18), channel_id=1, source_target_pairs={{0,4},{4,0},{8,12},{12,8},{16,20},{20,16},{24,28},{28,24},{1,5},{5... | collective-permute-start | bytes 1228808 | tf_op jit(solution)/shard_map/ppermute | solution.py:382
  11.7 7.7 %collective-permute-start.5 = (bf16[400,256]{1,0:T(8,128)(2,1)S(1)}, bf16[400,256]{1,0:T(8,128)(2,1)S(1)}, u32[]{:S(2)}, u32[]{:S(2)}) collective-permute-start(bf16[400,256]{1,0:T(8,128)(2,1)S(1)} %add.31.refs_2_.refs_0_), channel_id=1, source_target_pairs={{0,16},{4,12},{8,24},{12,4},{16,0},{20,28},{24,8},{28,20},{1,17},{... | collective-permute-start | bytes 614408 | tf_op jit(solution)/shard_map/ppermute | solution.py:382
  13.3 6.1 %collective-permute-start.4 = (bf16[400,256]{1,0:T(8,128)(2,1)S(1)}, bf16[400,256]{1,0:T(8,128)(2,1)S(1)}, u32[]{:S(2)}, u32[]{:S(2)}) collective-permute-start(bf16[400,256]{1,0:T(8,128)(2,1)S(1)} %add.32.after_ref.refs_0_), channel_id=1, source_target_pairs={{0,8},{4,20},{8,0},{12,28},{16,24},{20,4},{24,16},{28,12},{1,9},{5... | collective-permute-start | bytes 614408 | tf_op jit(solution)/shard_map/ppermute | solution.py:382
  19.6 10.2 %collective-permute-start.6 = (bf16[800,256]{1,0:T(8,128)(2,1)S(1)}, bf16[800,256]{1,0:T(8,128)(2,1)S(1)}, u32[]{:S(2)}, u32[]{:S(2)}) collective-permute-start(bf16[800,256]{1,0:T(8,128)(2,1)S(1)} %add.35.after_ref.refs_0_), channel_id=1, source_target_pairs={{0,8},{4,20},{8,0},{12,28},{16,24},{20,4},{24,16},{28,12},{1,9},{5... | collective-permute-start | bytes 1228808 | tf_op jit(solution)/shard_map/ppermute | solution.py:382
  20.9 1.5 %collective-permute-start.8 = (bf16[400,256]{1,0:T(8,128)(2,1)S(1)}, bf16[400,256]{1,0:T(8,128)(2,1)S(1)}, u32[]{:S(2)}, u32[]{:S(2)}) collective-permute-start(bf16[400,256]{1,0:T(8,128)(2,1)S(1)} %add.33.refs_2_.own_ref), channel_id=1, source_target_pairs={{0,4},{4,0},{8,12},{12,8},{16,20},{20,16},{24,28},{28,24},{1,5},{5... | collective-permute-start | bytes 614408 | tf_op jit(solution)/shard_map/ppermute | solution.py:382
  20.9 7.7 %collective-permute-start.7 = (bf16[400,256]{1,0:T(8,128)(2,1)S(1)}, bf16[400,256]{1,0:T(8,128)(2,1)S(1)}, u32[]{:S(2)}, u32[]{:S(2)}) collective-permute-start(bf16[400,256]{1,0:T(8,128)(2,1)S(1)} %add.34.refs_2_.refs_0_), channel_id=1, source_target_pairs={{0,16},{4,12},{8,24},{12,4},{16,0},{20,28},{24,8},{28,20},{1,17},{... | collective-permute-start | bytes 614408 | tf_op jit(solution)/shard_map/ppermute | solution.py:382
  29.9 8.0 %collective-permute-start.9 = (bf16[800,256]{1,0:T(8,128)(2,1)S(1)}, bf16[800,256]{1,0:T(8,128)(2,1)S(1)}, u32[]{:S(2)}, u32[]{:S(2)}) collective-permute-start(bf16[800,256]{1,0:T(8,128)(2,1)S(1)} %add.37.after_ref.refs_0_), channel_id=1, source_target_pairs={{0,16},{4,12},{8,24},{12,4},{16,0},{20,28},{24,8},{28,20},{1,17},{... | collective-permute-start | bytes 1228808 | tf_op jit(solution)/shard_map/ppermute | solution.py:382
  31.5 16.7 %collective-permute-start.12 = (bf16[4,512,128]{2,1,0:T(8,128)(2,1)S(1)}, bf16[4,512,128]{2,1,0:T(8,128)(2,1)S(1)}, u32[]{:S(2)}, u32[]{:S(2)}) collective-permute-start(bf16[4,512,128]{2,1,0:T(8,128)(2,1)S(1)} %get-tuple-element.25.refs_2_.refs_0_), channel_id=1, source_target_pairs={{0,1},{3,2},{4,5},{7,6},{8,9},{11,10},{12,13},{15,14},{16,17},{19,... | collective-permute-start | bytes 1572872 | tf_op jit(solution)/shard_map/ppermute | solution.py:383
  33.9 25.6 %collective-permute-start.11 = (bf16[4,512,128]{2,1,0:T(8,128)(2,1)S(1)}, bf16[4,512,128]{2,1,0:T(8,128)(2,1)S(1)}, u32[]{:S(2)}, u32[]{:S(2)}) collective-permute-start(bf16[4,512,128]{2,1,0:T(8,128)(2,1)S(1)} %lags_rest.2.refs_2_.refs_0_), channel_id=1, source_target_pairs={{0,1},{3,2},{4,5},{7,6},{8,9},{11,10},{12,13},{15,14},{16,17},{19,... | collective-permute-start | bytes 1572872 | tf_op jit(solution)/shard_map/ppermute | solution.py:383
  38.0 25.2 %collective-permute-start.10 = (bf16[800,256]{1,0:T(8,128)(2,1)S(1)}, bf16[800,256]{1,0:T(8,128)(2,1)S(1)}, u32[]{:S(2)}, u32[]{:S(2)}) collective-permute-start(bf16[800,256]{1,0:T(8,128)(2,1)S(1)} %add.38.after_ref.own_ref), channel_id=1, source_target_pairs={{0,4},{4,0},{8,12},{12,8},{16,20},{20,16},{24,28},{28,24},{1,5},{5... | collective-permute-start | bytes 1228808 | tf_op jit(solution)/shard_map/ppermute | solution.py:382
  38.1 2.0 %collective-permute-start.13 = (bf16[400,256]{1,0:T(8,128)(2,1)S(1)}, bf16[400,256]{1,0:T(8,128)(2,1)S(1)}, u32[]{:S(2)}, u32[]{:S(2)}) collective-permute-start(bf16[400,256]{1,0:T(8,128)(2,1)S(1)} %add.36.refs_2_.own_ref), channel_id=1, source_target_pairs={{0,4},{4,0},{8,12},{12,8},{16,20},{20,16},{24,28},{28,24},{1,5},{5... | collective-permute-start | bytes 614408 | tf_op jit(solution)/shard_map/ppermute | solution.py:382
  43.9 30.3 %collective-permute-start.14 = (bf16[4,512,128]{2,1,0:T(8,128)(2,1)S(1)}, bf16[4,512,128]{2,1,0:T(8,128)(2,1)S(1)}, u32[]{:S(2)}, u32[]{:S(2)}) collective-permute-start(bf16[4,512,128]{2,1,0:T(8,128)(2,1)S(1)} %get-tuple-element.28.after_ref.refs_0_), channel_id=1, source_target_pairs={{0,1},{3,2},{4,5},{7,6},{8,9},{11,10},{12,13},{15,14},{16,17},{19,... | collective-permute-start | bytes 1572872 | tf_op jit(solution)/shard_map/ppermute | solution.py:383
  48.4 29.5 %collective-permute-start.18 = (bf16[4,512,128]{2,1,0:T(8,128)(2,1)S(1)}, bf16[4,512,128]{2,1,0:T(8,128)(2,1)S(1)}, u32[]{:S(2)}, u32[]{:S(2)}) collective-permute-start(bf16[4,512,128]{2,1,0:T(8,128)(2,1)S(1)} %add.39.refs_2_), channel_id=1, source_target_pairs={{1,2},{2,1},{5,6},{6,5},{9,10},{10,9},{13,14},{14,13},{17,18},{18,... | collective-permute-start | bytes 1572872 | tf_op jit(solution)/shard_map/ppermute | solution.py:383
  59.6 20.3 %collective-permute-start.17 = (bf16[4,512,128]{2,1,0:T(8,128)(2,1)S(1)}, bf16[4,512,128]{2,1,0:T(8,128)(2,1)S(1)}, u32[]{:S(2)}, u32[]{:S(2)}) collective-permute-start(bf16[4,512,128]{2,1,0:T(8,128)(2,1)S(1)} %add.40.after_ref), channel_id=1, source_target_pairs={{1,2},{2,1},{5,6},{6,5},{9,10},{10,9},{13,14},{14,13},{17,18},{18,... | collective-permute-start | bytes 1572872 | tf_op jit(solution)/shard_map/ppermute | solution.py:383
  62.0 20.0 %collective-permute-start.16 = (bf16[4,512,128]{2,1,0:T(8,128)(2,1)S(1)}, bf16[4,512,128]{2,1,0:T(8,128)(2,1)S(1)}, u32[]{:S(2)}, u32[]{:S(2)}) collective-permute-start(bf16[4,512,128]{2,1,0:T(8,128)(2,1)S(1)} %lags_rest.3.refs_2_.refs_0_), channel_id=1, source_target_pairs={{0,1},{3,2},{4,5},{7,6},{8,9},{11,10},{12,13},{15,14},{16,17},{19,... | collective-permute-start | bytes 1572872 | tf_op jit(solution)/shard_map/ppermute | solution.py:383
  68.1 33.1 %collective-permute-start.22 = (bf16[8,512,128]{2,1,0:T(8,128)(2,1)S(1)}, bf16[8,512,128]{2,1,0:T(8,128)(2,1)S(1)}, u32[]{:S(2)}, u32[]{:S(2)}) collective-permute-start(bf16[8,512,128]{2,1,0:T(8,128)(2,1)S(1)} %lags.6.after_ref), channel_id=1, source_target_pairs={{0,1},{3,2},{4,5},{7,6},{8,9},{11,10},{12,13},{15,14},{16,17},{19,... | collective-permute-start | bytes 3145736 | tf_op jit(solution)/shard_map/ppermute | solution.py:383
  74.4 16.4 %collective-permute-start.15 = (bf16[4,512,128]{2,1,0:T(8,128)(2,1)S(1)}, bf16[4,512,128]{2,1,0:T(8,128)(2,1)S(1)}, u32[]{:S(2)}, u32[]{:S(2)}) collective-permute-start(bf16[4,512,128]{2,1,0:T(8,128)(2,1)S(1)} %add.41.refs_2_), channel_id=1, source_target_pairs={{1,2},{2,1},{5,6},{6,5},{9,10},{10,9},{13,14},{14,13},{17,18},{18,... | collective-permute-start | bytes 1572872 | tf_op jit(solution)/shard_map/ppermute | solution.py:383
  78.0 12.8 %collective-permute-start.20 = (bf16[4,512,128]{2,1,0:T(8,128)(2,1)S(1)}, bf16[4,512,128]{2,1,0:T(8,128)(2,1)S(1)}, u32[]{:S(2)}, u32[]{:S(2)}) collective-permute-start(bf16[4,512,128]{2,1,0:T(8,128)(2,1)S(1)} %add.42.refs_2_), channel_id=1, source_target_pairs={{1,0},{2,3},{5,4},{6,7},{9,8},{10,11},{13,12},{14,15},{17,16},{18,... | collective-permute-start | bytes 1572872 | tf_op jit(solution)/shard_map/ppermute | solution.py:383
  82.1 14.6 %collective-permute-start.19 = (bf16[4,512,128]{2,1,0:T(8,128)(2,1)S(1)}, bf16[4,512,128]{2,1,0:T(8,128)(2,1)S(1)}, u32[]{:S(2)}, u32[]{:S(2)}) collective-permute-start(bf16[4,512,128]{2,1,0:T(8,128)(2,1)S(1)} %add.44), channel_id=1, source_target_pairs={{1,2},{2,1},{5,6},{6,5},{9,10},{10,9},{13,14},{14,13},{17,18},{18,... | collective-permute-start | bytes 1572872 | tf_op jit(solution)/shard_map/ppermute | solution.py:383
  84.4 12.3 %collective-permute-start.21 = (bf16[4,512,128]{2,1,0:T(8,128)(2,1)S(1)}, bf16[4,512,128]{2,1,0:T(8,128)(2,1)S(1)}, u32[]{:S(2)}, u32[]{:S(2)}) collective-permute-start(bf16[4,512,128]{2,1,0:T(8,128)(2,1)S(1)} %add.43.refs_2_), channel_id=1, source_target_pairs={{1,0},{2,3},{5,4},{6,7},{9,8},{10,11},{13,12},{14,15},{17,16},{18,... | collective-permute-start | bytes 1572872 | tf_op jit(solution)/shard_map/ppermute | solution.py:383

commit v3 on v2

--- a/solution.py
+++ b/solution.py
@@ -11,7 +11,8 @@
 LAGS = 512
 GROUP = 16
 ORDER = ((3, 2, 1, 0), (3, 2, 0, 1), (0, 1, 3, 2), (0, 1, 2, 3))
-SPLITS = (4, 4)
+SPLITS = (4, 2, 8, 8)
+STEPS = "r0 r1 t r0 w r1 r2 r0 l0 r1 k0 r2 l1 m0 r2 k1 l3 n0 l2 m1 f g h n1 p".split()
 INWARD = ((0, 1), (3, 2))
 MIDDLE = ((1, 2), (2, 1))
 OUTWARD = ((1, 0), (2, 3))
@@ -364,6 +365,41 @@
     )(cross, table, after)
 
 
+def sum_kernel(firsts, low, *refs):
+    out_ref, rest = refs[len(firsts) + 1], refs[len(firsts) + 2 :]
+    total_ref = rest[0] if rest else out_ref
+    copies = []
+    for source in range(low, low + out_ref.shape[0]):
+        total = 0.0
+        for first, ref in zip(firsts, refs):
+            if first <= source < first + ref.shape[0]:
+                total = total + ref[source - first].astype(jnp.float32)
+        total_ref[source - low] = total.astype(total_ref.dtype)
+        if rest:
+            copies.append(
+                pltpu.make_async_copy(total_ref.at[source], out_ref.at[source], rest[1].at[source])
+            )
+            copies[-1].start()
+    for copy in copies:
+        copy.wait()
+
+
+def sum_of(parts, low, high, dtype, after, final=False):
+    firsts, values = zip(*parts)
+    shape = (high - low,) + values[0].shape[1:]
+    scratch = [pltpu.VMEM(shape, dtype), pltpu.SemaphoreType.DMA((high - low,))]
+    return pl.pallas_call(
+        functools.partial(sum_kernel, firsts, low),
+        in_specs=[VMEM] * len(values) + [ANY],
+        out_specs=HBM if final else VMEM,
+        out_shape=jax.ShapeDtypeStruct(shape, dtype),
+        scratch_shapes=scratch if final else [],
+        compiler_params=pltpu.CompilerParams(vmem_limit_bytes=16 * MIB),
+        cost_estimate=COST,
+        name="sum",
+    )(*values, after)
+
+
 def chip_stages(chan_count):
     bits = [1 << b for b in range(1, chan_count.bit_length() - 1)]
     turned = bits[1:] + bits[:1]
@@ -374,77 +410,62 @@
 
 
 def body(chan_count, spectra, quality, sources):
-    own, other, (scale, data) = (lambda v: (v[:3], v[3:6], v[6:]))(front(spectra, quality, sources))
     freq_count = spectra.shape[2]
-    slot_rows = own[0].shape[0]
     stages = chip_stages(chan_count)
     cores = [(i, i ^ 1) for i in range(chan_count)]
     over_chan = lambda value, pairs: lax.ppermute(value, "chan", pairs)
     over_hour = lambda value, pairs: lax.ppermute(value, "hour", pairs)
 
-    moved = [over_chan(value, cores) for value in other]
-    state = list(own)
-
-    def receive(at, pairs):
-        state[at] = add_after(last, state[at], moved[at])
-        moved[at] = over_chan(state[at], pairs)
-        return state[at]
-
+    front_out = front(spectra, quality, sources)
+    (*state, scale, data) = front_out[:3] + front_out[6:]
+    slot_rows = state[0].shape[0]
+    moved = [over_chan(value, cores) for value in front_out[3:6]]
+    passes = [0, 0, 0]
+    made, mine, cross, middle, outward = {}, {}, {}, {}, {}
+    inward = {}
+    cuts = (0, SPLITS[0], 8)
     last = scale
-    last = receive(0, stages[0])
-    table = last = lag_table(freq_count, LAGS, last)
-    for pairs in stages[1:]:
-        last = receive(0, pairs)
-    last = receive(1, stages[0])
-    receivers = last = whiten(data, scale, last)
-    last = receive(0, cores)
-    for pairs in stages[1:]:
-        last = receive(1, pairs)
-    last = receive(2, stages[0])
-
-    def lags(chunk, base=0, done=8):
-        return lags_of(*chunk, receivers, table, base, done, last)
-
-    mine = [[], [], [], []]
-    inward = [[], [], []]
-    middle = [[], []]
-
-    def send_inward(slot, value):
-        mine[slot].append(value)
-        inward[slot].append(over_hour(value, INWARD))
-        return value
-
-    def send_middle(slot, at):
-        value = add_after(last, mine[slot][at], inward[slot][at])
-        middle[slot].append(over_hour(value, MIDDLE))
-        return value
-
-    value, cross = lags((state[0], moved[0]), 0, SPLITS[0])
-    last = send_inward(0, value)
-    last = receive(1, cores)
-    for pairs in stages[1:]:
-        last = receive(2, pairs)
-    last = send_inward(0, lags_of_rest(cross, table, last))
-    last = receive(2, cores)
-    value, cross = lags((state[1], moved[1]), 0, SPLITS[1])
-    last = send_inward(1, value)
-    last = send_inward(1, lags_of_rest(cross, table, last))
-    last = send_middle(0, 0)
-    last = send_middle(0, 1)
-    rest = (state[2], moved[2])
-    last = send_inward(2, lags(rest)[0])
-    last = own_lags = lags(rest, slot_rows)[0]
-    outward = []
-    cuts = (0, SPLITS[0], 8)
-    sums = [mine[2][0][low:high] for low, high in zip(cuts, cuts[1:])]
-    last = send_middle(1, 0)
-    for at in range(2):
-        last = add_after(last, sums[at], middle[0][at])
-        outward.append(over_hour(last, OUTWARD))
-    last = send_middle(1, 1)
-    whole = lambda values: values[0] if len(values) == 1 else jnp.concatenate(values, 0)
-    values = [own_lags] + [whole(values) for values in (middle[1], outward, inward[2])]
-    return sum(value.astype(jnp.float32) for value in values).astype(jnp.bfloat16)
+    for step in STEPS:
+        kind, at = step[0], int(step[1:] or 0)
+        if kind == "r":
+            for pairs in (stages[:1], stages[1:], [cores])[passes[at]]:
+                last = state[at] = add_after(last, state[at], moved[at])
+                moved[at] = over_chan(last, pairs)
+            passes[at] += 1
+        elif kind == "t":
+            table = last = lag_table(freq_count, LAGS, last)
+        elif kind == "w":
+            receivers = last = whiten(data, scale, last)
+        elif kind in "lk":
+            if kind == "l":
+                chunk = min(at, 2)
+                values = lags_of(
+                    state[chunk], moved[chunk], receivers, table, slot_rows * (at - chunk), SPLITS[at], last
+                )
+                last = values[0]
+                cross[at] = values[-1]
+            else:
+                last = lags_of_rest(cross[at], table, last)
+            mine[at, kind] = last
+            if at < 3:
+                inward[at, kind] = over_hour(last, INWARD)
+        elif kind in "mn":
+            which = "l" if kind == "m" else "k"
+            last = add_after(last, mine[at, which], inward[at, which])
+            middle[at, which] = over_hour(last, MIDDLE)
+        elif kind in "fg":
+            which, part = ("l", 0) if kind == "f" else ("k", 1)
+            parts = [(0, mine[2, "l"]), (cuts[part], middle[0, which])]
+            last = sum_of(parts, cuts[part], cuts[part + 1], jnp.bfloat16, last)
+            outward[which] = over_hour(last, OUTWARD)
+        elif kind == "h":
+            parts = [(0, mine[3, "l"]), (0, outward["l"]), (0, middle[1, "l"])]
+            early = last = sum_of(parts, 0, cuts[1], jnp.float32, last)
+        elif kind == "p":
+            parts = [(0, early), (cuts[1], mine[3, "l"][cuts[1] :]), (cuts[1], outward["k"])]
+            parts += [(SPLITS[1], middle[1, "k"])]
+            last = sum_of(parts, 0, 8, jnp.float32, last)
+    return sum_of([(0, last), (0, inward[2, "l"])], 0, 8, jnp.bfloat16, last, final=True)
 
 
 def solution(mesh):

time: 103 us -> 97.8 us (0.950); the launches traced: 103 us -> 96.3 us
  waiting for transfers between devices: 42.5 us -> 33.8 us
  starting transfers between devices: 29.9 us -> 32.2 us
  other arithmetic: 1.52 us -> 0 us
  Pallas kernels: 28.4 us -> 29.8 us
    ppermute x12, waiting for transfers between devices: 14.8 us -> 9.57 us  [body(): over_chan = lambda value, pairs: lax.ppermute(value, 'chan', pairs)]
    ppermute x11, waiting for transfers between devices: 27.7 us -> 24.2 us  [body(): over_hour = lambda value, pairs: lax.ppermute(value, 'hour', pairs)]
    ppermute x11, starting transfers between devices: 20.4 us -> 22.9 us  [body(): over_hour = lambda value, pairs: lax.ppermute(value, 'hour', pairs)]
    pallas_call x0 -> x5, Pallas kernels: none -> 1.68 us  [sum_of(): pl.pallas_call(functools.partial(sum_kernel, firsts, low), in_specs=[VMEM...]
    convert_element_type x1 -> x0, other arithmetic: 1.52 us -> none  [body(): sum((value.astype(jnp.float32) for value in values)).astype(jnp.bfloat16)]
  transfers between devices with their start and end apart: 23 -> 23, of which waited for: 14 -> 11; matrix products, arithmetic and copies ran while one was open for 0% -> 0% of each run, Pallas kernels for 23% -> 25%
where the time goes in v3:
time: 97.8 us; the launch traced here: 96.3 us
  waiting for transfers between devices  33.8 us (35%)
  starting transfers between devices  32.2 us (33%)
  Pallas kernels  29.8 us (30%)
    ppermute x11, waiting for transfers between devices, body(): over_hour = lambda value, pairs: lax.ppermute(value, 'hour', pairs)  24.2 us
    ppermute x11, starting transfers between devices, body(): over_hour = lambda value, pairs: lax.ppermute(value, 'hour', pairs)  22.9 us
    pallas_call x4, Pallas kernels, lags_of(): pl.pallas_call(functools.partial(lags_kernel, base, done), in_specs=[VMEM...  16.7 us
    ppermute x12, waiting for transfers between devices, body(): over_chan = lambda value, pairs: lax.ppermute(value, 'chan', pairs)  9.57 us
    ppermute x12, starting transfers between devices, body(): over_chan = lambda value, pairs: lax.ppermute(value, 'chan', pairs)  9.26 us
    pallas_call x1, Pallas kernels, front(): pl.pallas_call(front_kernel, in_specs=[HBM, HBM, HBM], out_specs=[VMEM] *...  4.23 us
    pallas_call x2, Pallas kernels, lags_of_rest(): pl.pallas_call(lambda cross_ref, table_ref, after_ref, out_ref: transform...  2.71 us
  transfers between devices with their start and end apart: 23, of which 11 were waited for; matrix products, arithmetic and copies ran while one was open for 0% of the time, Pallas kernels for 25%

profile of v3, /device:TPU:16, one launch (start us, length us, event | category | flops | bytes accessed | tf_op | source)
XLA Modules:
  0.0 96.3 jit_solution(12421132699641881782)
XLA Ops:
  0.0 4.2 %pick_sources.1 = (bf16[400,256]{1,0:T(8,128)(2,1)S(1)}, bf16[400,256]{1,0:T(8,128)(2,1)S(1)}, bf16[800,256]{1,0:T(8,128)(2,1)S(1)}, bf16[400,256]{1,0:T(8,128)(...) custom-call(s32[32]{0:T(128)} %sources_hbm.1, ...), custom_call_target="tpu_custom_call" | custom-call | flops 1 | bytes 1 | tf_op jit(solution)/shard_map/pick_sources/pallas_call | solution.py:138
  4.3 0.5 collective-permute-start.1
  4.9 0.9 collective-permute-done.2.refs_1_
  5.8 1.6 %collective-permute-start.4 = (bf16[400,256]{1,0:T(8,128)(2,1)S(1)}, bf16[400,256]{1,0:T(8,128)(2,1)S(1)}, u32[]{:S(2)}, u32[]{:S(2)}) collective-permute-start(bf16[400,256]{1,0:T(8,128)(2,1)S(1)} %add.13.refs_2_.refs_0_), channel_id=1, source_target_pairs={{0,8},{4,20},{8,0},{12,28},{16,24},{20,4},{24,16},{28,12},{1,9},{5... | collective-permute-start | bytes 614408 | tf_op jit(solution)/shard_map/ppermute | solution.py:416
  7.4 0.6 collective-permute-start.3
  8.0 1.9 %lag_table.1.refs_2_.table_ref = bf16[512,1600]{1,0:T(8,128)(2,1)S(1)} custom-call(bf16[400,256]{1,0:T(8,128)(2,1)S(1)} %add.14.after_ref.refs_0_), custom_call_target="tpu_custom_call" | custom-call | flops 1 | bytes 1 | tf_op jit(solution)/shard_map/lag_table/pallas_call | solution.py:229
  9.9 1.7 %collective-permute-done.4.refs_1_ = bf16[400,256]{1,0:T(8,128)(2,1)S(1)} collective-permute-done((bf16[400,256]{1,0:T(8,128)(2,1)S(1)}, bf16[400,256]{1,0:T(8,128)(2,1)S(1)}, u32[]{:S(2)}, u32[]{:S(2)}) %collective-permute-start.4) | collective-permute-done | bytes 204832 | tf_op jit(solution)/shard_map/ppermute | solution.py:416
  11.7 1.6 %collective-permute-start.6 = (bf16[400,256]{1,0:T(8,128)(2,1)S(1)}, bf16[400,256]{1,0:T(8,128)(2,1)S(1)}, u32[]{:S(2)}, u32[]{:S(2)}) collective-permute-start(bf16[400,256]{1,0:T(8,128)(2,1)S(1)} %add.15.after_ref.refs_0_), channel_id=1, source_target_pairs={{0,16},{4,12},{8,24},{12,4},{16,0},{20,28},{24,8},{28,20},{1,17},{... | collective-permute-start | bytes 614408 | tf_op jit(solution)/shard_map/ppermute | solution.py:416
  13.3 1.5 %whiten_receivers.1.refs_2_.receivers_ref = bf16[2,16,800,128]{3,2,1,0:T(8,128)(2,1)S(1)} custom-call(bf16[2,16,800,128]{3,2,1,0:T(8,128)(2,1)S(1)} %get-tuple-element.24.data_ref, f32[16,128]{1,0:T(8,128)S(1)} %get-tuple-element.23.refs_2_.scale_ref, bf16[400,256]{1,0:T(8,128)(2,1)S(1)} %add.15.after_ref.refs_0_), custom_call_target="tpu_custom_call" | custom-call | flops 1 | bytes 1 | tf_op jit(solution)/shard_map/whiten_receivers/pallas_call | solution.py:176
  14.9 0.1 add.17.refs_2_.refs_0_
  15.0 2.5 %collective-permute-done.6.refs_1_ = bf16[400,256]{1,0:T(8,128)(2,1)S(1)} collective-permute-done((bf16[400,256]{1,0:T(8,128)(2,1)S(1)}, bf16[400,256]{1,0:T(8,128)(2,1)S(1)}, u32[]{:S(2)}, u32[]{:S(2)}) %collective-permute-start.6) | collective-permute-done | bytes 204832 | tf_op jit(solution)/shard_map/ppermute | solution.py:416
  17.6 1.6 %collective-permute-start.5 = (bf16[800,256]{1,0:T(8,128)(2,1)S(1)}, bf16[800,256]{1,0:T(8,128)(2,1)S(1)}, u32[]{:S(2)}, u32[]{:S(2)}) collective-permute-start(bf16[800,256]{1,0:T(8,128)(2,1)S(1)} %add.17.refs_2_.refs_0_), channel_id=1, source_target_pairs={{0,8},{4,20},{8,0},{12,28},{16,24},{20,4},{24,16},{28,12},{1,9},{5... | collective-permute-start | bytes 1228808 | tf_op jit(solution)/shard_map/ppermute | solution.py:416
  19.2 3.8 %lags.4 = (bf16[4,512,128]{2,1,0:T(8,128)(2,1)S(1)}, bf16[2,1600,256]{2,1,0:T(8,128)(2,1)S(1)}) custom-call(bf16[400,256]{1,0:T(8,128)(2,1)S(1)} %add.18.own_ref.after_ref, bf16[400,256]{1,0:T(8,128)(2,1)S(1)} %collective-permute-done.7.other_ref, bf16[2,16,800,128]{3,2,1,0:T(8,128)(2,1)S(1)} %whiten_receivers.1.refs_2_.receivers_ref, ...), custom_call_target="tpu_custom_call" | custom-call | flops 1 | bytes 1 | tf_op jit(solution)/shard_map/lags/pallas_call | solution.py:340
  23.0 1.3 %collective-permute-start.10 = (bf16[4,512,128]{2,1,0:T(8,128)(2,1)S(1)}, bf16[4,512,128]{2,1,0:T(8,128)(2,1)S(1)}, u32[]{:S(2)}, u32[]{:S(2)}) collective-permute-start(bf16[4,512,128]{2,1,0:T(8,128)(2,1)S(1)} %get-tuple-element.26.refs_2_.refs_0_), channel_id=1, source_target_pairs={{0,1},{3,2},{4,5},{7,6},{8,9},{11,10},{12,13},{15,14},{16,17},{19,... | collective-permute-start | bytes 1572872 | tf_op jit(solution)/shard_map/ppermute | solution.py:417
  24.3 1.6 %collective-permute-start.8 = (bf16[400,256]{1,0:T(8,128)(2,1)S(1)}, bf16[400,256]{1,0:T(8,128)(2,1)S(1)}, u32[]{:S(2)}, u32[]{:S(2)}) collective-permute-start(bf16[400,256]{1,0:T(8,128)(2,1)S(1)} %add.16.refs_2_.refs_0_), channel_id=1, source_target_pairs={{0,16},{4,12},{8,24},{12,4},{16,0},{20,28},{24,8},{28,20},{1,17},{... | collective-permute-start | bytes 614408 | tf_op jit(solution)/shard_map/ppermute | solution.py:416
  25.9 4.2 %collective-permute-done.8.refs_1_ = bf16[400,256]{1,0:T(8,128)(2,1)S(1)} collective-permute-done((bf16[400,256]{1,0:T(8,128)(2,1)S(1)}, bf16[400,256]{1,0:T(8,128)(2,1)S(1)}, u32[]{:S(2)}, u32[]{:S(2)}) %collective-permute-start.8) | collective-permute-done | bytes 204832 | tf_op jit(solution)/shard_map/ppermute | solution.py:416
  30.2 1.1 %lags_rest.2.refs_2_.refs_0_ = bf16[4,512,128]{2,1,0:T(8,128)(2,1)S(1)} custom-call(bf16[2,1600,256]{2,1,0:T(8,128)(2,1)S(1)} %get-tuple-element.25.cross_ref, bf16[512,1600]{1,0:T(8,128)(2,1)S(1)} %lag_table.1.refs_2_.table_ref, bf16[400,256]{1,0:T(8,128)(2,1)S(1)} %add.19.after_ref.own_ref), custom_call_target="tpu_custom_call" | custom-call | flops 1 | bytes 1 | tf_op jit(solution)/shard_map/lags_rest/pallas_call | solution.py:357
  31.4 1.6 %collective-permute-start.9 = (bf16[800,256]{1,0:T(8,128)(2,1)S(1)}, bf16[800,256]{1,0:T(8,128)(2,1)S(1)}, u32[]{:S(2)}, u32[]{:S(2)}) collective-permute-start(bf16[800,256]{1,0:T(8,128)(2,1)S(1)} %add.20.after_ref.refs_0_), channel_id=1, source_target_pairs={{0,16},{4,12},{8,24},{12,4},{16,0},{20,28},{24,8},{28,20},{1,17},{... | collective-permute-start | bytes 1228808 | tf_op jit(solution)/shard_map/ppermute | solution.py:416
  33.0 1.3 %collective-permute-start.13 = (bf16[4,512,128]{2,1,0:T(8,128)(2,1)S(1)}, bf16[4,512,128]{2,1,0:T(8,128)(2,1)S(1)}, u32[]{:S(2)}, u32[]{:S(2)}) collective-permute-start(bf16[4,512,128]{2,1,0:T(8,128)(2,1)S(1)} %lags_rest.2.refs_2_.refs_0_), channel_id=1, source_target_pairs={{0,1},{3,2},{4,5},{7,6},{8,9},{11,10},{12,13},{15,14},{16,17},{19,... | collective-permute-start | bytes 1572872 | tf_op jit(solution)/shard_map/ppermute | solution.py:417
  34.3 0.2 collective-permute-done.11.other_ref
  34.5 3.3 %lags.5 = (bf16[2,512,128]{2,1,0:T(8,128)(2,1)S(1)}, bf16[3,1600,256]{2,1,0:T(8,128)(2,1)S(1)}) custom-call(bf16[400,256]{1,0:T(8,128)(2,1)S(1)} %add.19.after_ref.own_ref, bf16[400,256]{1,0:T(8,128)(2,1)S(1)} %collective-permute-done.11.other_ref, bf16[2,16,800,128]{3,2,1,0:T(8,128)(2,1)S(1)} %whiten_receivers.1.refs_2_.receivers_ref, ...), custom_call_target="tpu_custom_call" | custom-call | flops 1 | bytes 1 | tf_op jit(solution)/shard_map/lags/pallas_call | solution.py:340
  37.8 1.7 %collective-permute-done.10.refs_1_ = bf16[4,512,128]{2,1,0:T(8,128)(2,1)S(1)} collective-permute-done((bf16[4,512,128]{2,1,0:T(8,128)(2,1)S(1)}, bf16[4,512,128]{2,1,0:T(8,128)(2,1)S(1)}, u32[]{:S(2)}, u32[]{:S(2)}) %collective-permute-start.10) | collective-permute-done | bytes 524320 | tf_op jit(solution)/shard_map/ppermute | solution.py:417
  39.5 0.1 add.21.refs_2_
  39.6 2.4 %collective-permute-start.14 = (bf16[4,512,128]{2,1,0:T(8,128)(2,1)S(1)}, bf16[4,512,128]{2,1,0:T(8,128)(2,1)S(1)}, u32[]{:S(2)}, u32[]{:S(2)}) collective-permute-start(bf16[4,512,128]{2,1,0:T(8,128)(2,1)S(1)} %add.21.refs_2_), channel_id=1, source_target_pairs={{1,2},{2,1},{5,6},{6,5},{9,10},{10,9},{13,14},{14,13},{17,18},{18,... | collective-permute-start | bytes 1572872 | tf_op jit(solution)/shard_map/ppermute | solution.py:417
  42.0 0.1 add.22.after_ref.own_ref
  42.1 1.5 %collective-permute-start.15 = (bf16[2,512,128]{2,1,0:T(8,128)(2,1)S(1)}, bf16[2,512,128]{2,1,0:T(8,128)(2,1)S(1)}, u32[]{:S(2)}, u32[]{:S(2)}) collective-permute-start(bf16[2,512,128]{2,1,0:T(8,128)(2,1)S(1)} %get-tuple-element.27.refs_2_.refs_0_), channel_id=1, source_target_pairs={{0,1},{3,2},{4,5},{7,6},{8,9},{11,10},{12,13},{15,14},{16,17},{19,... | collective-permute-start | bytes 786440 | tf_op jit(solution)/shard_map/ppermute | solution.py:417
  43.6 1.6 %lags_rest.3.after_ref.refs_0_ = bf16[6,512,128]{2,1,0:T(8,128)(2,1)S(1)} custom-call(bf16[3,1600,256]{2,1,0:T(8,128)(2,1)S(1)} %get-tuple-element.28.cross_ref, bf16[512,1600]{1,0:T(8,128)(2,1)S(1)} %lag_table.1.refs_2_.table_ref, bf16[800,256]{1,0:T(8,128)(2,1)S(1)} %add.22.after_ref.own_ref), custom_call_target="tpu_custom_call" | custom-call | flops 1 | bytes 1 | tf_op jit(solution)/shard_map/lags_rest/pallas_call | solution.py:357
  45.2 1.3 %collective-permute-start.20 = (bf16[6,512,128]{2,1,0:T(8,128)(2,1)S(1)}, bf16[6,512,128]{2,1,0:T(8,128)(2,1)S(1)}, u32[]{:S(2)}, u32[]{:S(2)}) collective-permute-start(bf16[6,512,128]{2,1,0:T(8,128)(2,1)S(1)} %lags_rest.3.after_ref.refs_0_), channel_id=1, source_target_pairs={{0,1},{3,2},{4,5},{7,6},{8,9},{11,10},{12,13},{15,14},{16,17},{19,... | collective-permute-start | bytes 2359304 | tf_op jit(solution)/shard_map/ppermute | solution.py:417
  46.5 4.8 %lags.6.refs_2_.refs_0_ = bf16[8,512,128]{2,1,0:T(8,128)(2,1)S(1)} custom-call(bf16[800,256]{1,0:T(8,128)(2,1)S(1)} %add.22.after_ref.own_ref, bf16[800,256]{1,0:T(8,128)(2,1)S(1)} %collective-permute-done.12.other_ref, bf16[2,16,800,128]{3,2,1,0:T(8,128)(2,1)S(1)} %whiten_receivers.1.refs_2_.receivers_ref, ...), custom_call_target="tpu_custom_call" | custom-call | flops 1 | bytes 1 | tf_op jit(solution)/shard_map/lags/pallas_call | solution.py:340
  51.3 0.1 add.23.after_ref
  51.5 3.5 %collective-permute-start.18 = (bf16[4,512,128]{2,1,0:T(8,128)(2,1)S(1)}, bf16[4,512,128]{2,1,0:T(8,128)(2,1)S(1)}, u32[]{:S(2)}, u32[]{:S(2)}) collective-permute-start(bf16[4,512,128]{2,1,0:T(8,128)(2,1)S(1)} %add.23.after_ref), channel_id=1, source_target_pairs={{1,2},{2,1},{5,6},{6,5},{9,10},{10,9},{13,14},{14,13},{17,18},{18,... | collective-permute-start | bytes 1572872 | tf_op jit(solution)/shard_map/ppermute | solution.py:417
  55.0 4.8 %lags.7.refs_2_.refs_0_ = bf16[8,512,128]{2,1,0:T(8,128)(2,1)S(1)} custom-call(bf16[800,256]{1,0:T(8,128)(2,1)S(1)} %add.22.after_ref.own_ref, bf16[800,256]{1,0:T(8,128)(2,1)S(1)} %collective-permute-done.12.other_ref, bf16[2,16,800,128]{3,2,1,0:T(8,128)(2,1)S(1)} %whiten_receivers.1.refs_2_.receivers_ref, ...), custom_call_target="tpu_custom_call" | custom-call | flops 1 | bytes 1 | tf_op jit(solution)/shard_map/lags/pallas_call | solution.py:340
  59.9 0.1 sum.5.refs_2_
  60.0 1.9 %collective-permute-start.16 = (bf16[4,512,128]{2,1,0:T(8,128)(2,1)S(1)}, bf16[4,512,128]{2,1,0:T(8,128)(2,1)S(1)}, u32[]{:S(2)}, u32[]{:S(2)}) collective-permute-start(bf16[4,512,128]{2,1,0:T(8,128)(2,1)S(1)} %sum.5.refs_2_), channel_id=1, source_target_pairs={{1,0},{2,3},{5,4},{6,7},{9,8},{10,11},{13,12},{14,15},{17,16},{18,... | collective-permute-start | bytes 1572872 | tf_op jit(solution)/shard_map/ppermute | solution.py:417
  61.9 3.5 %collective-permute-start.17 = (bf16[2,512,128]{2,1,0:T(8,128)(2,1)S(1)}, bf16[2,512,128]{2,1,0:T(8,128)(2,1)S(1)}, u32[]{:S(2)}, u32[]{:S(2)}) collective-permute-start(bf16[2,512,128]{2,1,0:T(8,128)(2,1)S(1)} %add.24.refs_2_), channel_id=1, source_target_pairs={{1,2},{2,1},{5,6},{6,5},{9,10},{10,9},{13,14},{14,13},{17,18},{18,... | collective-permute-start | bytes 786440 | tf_op jit(solution)/shard_map/ppermute | solution.py:417
  65.3 1.3 %collective-permute-start.22 = (bf16[8,512,128]{2,1,0:T(8,128)(2,1)S(1)}, bf16[8,512,128]{2,1,0:T(8,128)(2,1)S(1)}, u32[]{:S(2)}, u32[]{:S(2)}) collective-permute-start(bf16[8,512,128]{2,1,0:T(8,128)(2,1)S(1)} %lags.7.refs_2_.refs_0_), channel_id=1, source_target_pairs={{0,1},{3,2},{4,5},{7,6},{8,9},{11,10},{12,13},{15,14},{16,17},{19,... | collective-permute-start | bytes 3145736 | tf_op jit(solution)/shard_map/ppermute | solution.py:417
  66.6 1.5 %collective-permute-done.18.refs_1_ = bf16[4,512,128]{2,1,0:T(8,128)(2,1)S(1)} collective-permute-done((bf16[4,512,128]{2,1,0:T(8,128)(2,1)S(1)}, bf16[4,512,128]{2,1,0:T(8,128)(2,1)S(1)}, u32[]{:S(2)}, u32[]{:S(2)}) %collective-permute-start.18) | collective-permute-done | bytes 524320 | tf_op jit(solution)/shard_map/ppermute | solution.py:417
  68.1 0.1 sum.6.refs_3_
  68.2 5.1 %collective-permute-done.17.refs_2_ = bf16[2,512,128]{2,1,0:T(8,128)(2,1)S(1)} collective-permute-done((bf16[2,512,128]{2,1,0:T(8,128)(2,1)S(1)}, bf16[2,512,128]{2,1,0:T(8,128)(2,1)S(1)}, u32[]{:S(2)}, u32[]{:S(2)}) %collective-permute-start.17) | collective-permute-done | bytes 262176 | tf_op jit(solution)/shard_map/ppermute | solution.py:417
  73.3 0.1 sum.7.refs_2_.refs_0_
  73.5 0.2 add.25.refs_4_
  73.7 3.5 %collective-permute-start.21 = (bf16[6,512,128]{2,1,0:T(8,128)(2,1)S(1)}, bf16[6,512,128]{2,1,0:T(8,128)(2,1)S(1)}, u32[]{:S(2)}, u32[]{:S(2)}) collective-permute-start(bf16[6,512,128]{2,1,0:T(8,128)(2,1)S(1)} %add.25.refs_4_), channel_id=1, source_target_pairs={{1,2},{2,1},{5,6},{6,5},{9,10},{10,9},{13,14},{14,13},{17,18},{18,... | collective-permute-start | bytes 2359304 | tf_op jit(solution)/shard_map/ppermute | solution.py:417
  77.2 1.6 %collective-permute-start.19 = (bf16[4,512,128]{2,1,0:T(8,128)(2,1)S(1)}, bf16[4,512,128]{2,1,0:T(8,128)(2,1)S(1)}, u32[]{:S(2)}, u32[]{:S(2)}) collective-permute-start(bf16[4,512,128]{2,1,0:T(8,128)(2,1)S(1)} %sum.6.refs_3_), channel_id=1, source_target_pairs={{1,0},{2,3},{5,4},{6,7},{9,8},{10,11},{13,12},{14,15},{17,16},{18,... | collective-permute-start | bytes 1572872 | tf_op jit(solution)/shard_map/ppermute | solution.py:417
  78.9 10.6 %collective-permute-done.19.refs_2_ = bf16[4,512,128]{2,1,0:T(8,128)(2,1)S(1)} collective-permute-done((bf16[4,512,128]{2,1,0:T(8,128)(2,1)S(1)}, bf16[4,512,128]{2,1,0:T(8,128)(2,1)S(1)}, u32[]{:S(2)}, u32[]{:S(2)}) %collective-permute-start.19) | collective-permute-done | bytes 524320 | tf_op jit(solution)/shard_map/ppermute | solution.py:417
  89.5 5.2 %collective-permute-done.21.refs_3_ = bf16[6,512,128]{2,1,0:T(8,128)(2,1)S(1)} collective-permute-done((bf16[6,512,128]{2,1,0:T(8,128)(2,1)S(1)}, bf16[6,512,128]{2,1,0:T(8,128)(2,1)S(1)}, u32[]{:S(2)}, u32[]{:S(2)}) %collective-permute-start.21) | collective-permute-done | bytes 786464 | tf_op jit(solution)/shard_map/ppermute | solution.py:417
  94.7 0.2 sum.8.refs_0_.refs_2_
  94.9 0.1 collective-permute-done.22.refs_1_
  95.1 1.0 %sum.9 = bf16[8,512,128]{2,1,0:T(8,128)(2,1)} custom-call(f32[8,512,128]{2,1,0:T(8,128)S(1)} %sum.8.refs_0_.refs_2_, bf16[8,512,128]{2,1,0:T(8,128)(2,1)S(1)} %collective-permute-done.22.refs_1_, f32[8,512,128]{2,1,0:T(8,128)S(1)} %sum.8.refs_0_.refs_2_), custom_call_target="tpu_custom_call" | custom-call | flops 1 | bytes 1 | tf_op jit(solution)/shard_map/sum/pallas_call | solution.py:391
  (26 shorter events, 0.9 us)
Async XLA Ops:
  4.2 1.5 %collective-permute-start.2 = (bf16[400,256]{1,0:T(8,128)(2,1)S(1)}, bf16[400,256]{1,0:T(8,128)(2,1)S(1)}, u32[]{:S(2)}, u32[]{:S(2)}) collective-permute-start(bf16[400,256]{1,0:T(8,128)(2,1)S(1)} %get-tuple-element.22), channel_id=1, source_target_pairs={{0,4},{4,0},{8,12},{12,8},{16,20},{20,16},{24,28},{28,24},{1,5},{5... | collective-permute-start | bytes 614408 | tf_op jit(solution)/shard_map/ppermute | solution.py:416
  4.3 3.1 %collective-permute-start.1 = (bf16[400,256]{1,0:T(8,128)(2,1)S(1)}, bf16[400,256]{1,0:T(8,128)(2,1)S(1)}, u32[]{:S(2)}, u32[]{:S(2)}) collective-permute-start(bf16[400,256]{1,0:T(8,128)(2,1)S(1)} %get-tuple-element.20), channel_id=1, source_target_pairs={{0,4},{4,0},{8,12},{12,8},{16,20},{20,16},{24,28},{28,24},{1,5},{5... | collective-permute-start | bytes 614408 | tf_op jit(solution)/shard_map/ppermute | solution.py:416
  4.8 10.0 %collective-permute-start = (bf16[800,256]{1,0:T(8,128)(2,1)S(1)}, bf16[800,256]{1,0:T(8,128)(2,1)S(1)}, u32[]{:S(2)}, u32[]{:S(2)}) collective-permute-start(bf16[800,256]{1,0:T(8,128)(2,1)S(1)} %get-tuple-element.18), channel_id=1, source_target_pairs={{0,4},{4,0},{8,12},{12,8},{16,20},{20,16},{24,28},{28,24},{1,5},{5... | collective-permute-start | bytes 1228808 | tf_op jit(solution)/shard_map/ppermute | solution.py:416
  5.8 5.8 %collective-permute-start.4 = (bf16[400,256]{1,0:T(8,128)(2,1)S(1)}, bf16[400,256]{1,0:T(8,128)(2,1)S(1)}, u32[]{:S(2)}, u32[]{:S(2)}) collective-permute-start(bf16[400,256]{1,0:T(8,128)(2,1)S(1)} %add.13.refs_2_.refs_0_), channel_id=1, source_target_pairs={{0,8},{4,20},{8,0},{12,28},{16,24},{20,4},{24,16},{28,12},{1,9},{5... | collective-permute-start | bytes 614408 | tf_op jit(solution)/shard_map/ppermute | solution.py:416
  7.4 7.4 %collective-permute-start.3 = (bf16[400,256]{1,0:T(8,128)(2,1)S(1)}, bf16[400,256]{1,0:T(8,128)(2,1)S(1)}, u32[]{:S(2)}, u32[]{:S(2)}) collective-permute-start(bf16[400,256]{1,0:T(8,128)(2,1)S(1)} %add.14.after_ref.refs_0_), channel_id=1, source_target_pairs={{0,8},{4,20},{8,0},{12,28},{16,24},{20,4},{24,16},{28,12},{1,9},{5... | collective-permute-start | bytes 614408 | tf_op jit(solution)/shard_map/ppermute | solution.py:416
  11.7 5.8 %collective-permute-start.6 = (bf16[400,256]{1,0:T(8,128)(2,1)S(1)}, bf16[400,256]{1,0:T(8,128)(2,1)S(1)}, u32[]{:S(2)}, u32[]{:S(2)}) collective-permute-start(bf16[400,256]{1,0:T(8,128)(2,1)S(1)} %add.15.after_ref.refs_0_), channel_id=1, source_target_pairs={{0,16},{4,12},{8,24},{12,4},{16,0},{20,28},{24,8},{28,20},{1,17},{... | collective-permute-start | bytes 614408 | tf_op jit(solution)/shard_map/ppermute | solution.py:416
  17.6 1.6 %collective-permute-start.7 = (bf16[400,256]{1,0:T(8,128)(2,1)S(1)}, bf16[400,256]{1,0:T(8,128)(2,1)S(1)}, u32[]{:S(2)}, u32[]{:S(2)}) collective-permute-start(bf16[400,256]{1,0:T(8,128)(2,1)S(1)} %add.18.own_ref.after_ref), channel_id=1, source_target_pairs={{0,4},{4,0},{8,12},{12,8},{16,20},{20,16},{24,28},{28,24},{1,5},{5... | collective-permute-start | bytes 614408 | tf_op jit(solution)/shard_map/ppermute | solution.py:416
  17.6 13.7 %collective-permute-start.5 = (bf16[800,256]{1,0:T(8,128)(2,1)S(1)}, bf16[800,256]{1,0:T(8,128)(2,1)S(1)}, u32[]{:S(2)}, u32[]{:S(2)}) collective-permute-start(bf16[800,256]{1,0:T(8,128)(2,1)S(1)} %add.17.refs_2_.refs_0_), channel_id=1, source_target_pairs={{0,8},{4,20},{8,0},{12,28},{16,24},{20,4},{24,16},{28,12},{1,9},{5... | collective-permute-start | bytes 1228808 | tf_op jit(solution)/shard_map/ppermute | solution.py:416
  23.0 16.5 %collective-permute-start.10 = (bf16[4,512,128]{2,1,0:T(8,128)(2,1)S(1)}, bf16[4,512,128]{2,1,0:T(8,128)(2,1)S(1)}, u32[]{:S(2)}, u32[]{:S(2)}) collective-permute-start(bf16[4,512,128]{2,1,0:T(8,128)(2,1)S(1)} %get-tuple-element.26.refs_2_.refs_0_), channel_id=1, source_target_pairs={{0,1},{3,2},{4,5},{7,6},{8,9},{11,10},{12,13},{15,14},{16,17},{19,... | collective-permute-start | bytes 1572872 | tf_op jit(solution)/shard_map/ppermute | solution.py:417
  24.3 5.8 %collective-permute-start.8 = (bf16[400,256]{1,0:T(8,128)(2,1)S(1)}, bf16[400,256]{1,0:T(8,128)(2,1)S(1)}, u32[]{:S(2)}, u32[]{:S(2)}) collective-permute-start(bf16[400,256]{1,0:T(8,128)(2,1)S(1)} %add.16.refs_2_.refs_0_), channel_id=1, source_target_pairs={{0,16},{4,12},{8,24},{12,4},{16,0},{20,28},{24,8},{28,20},{1,17},{... | collective-permute-start | bytes 614408 | tf_op jit(solution)/shard_map/ppermute | solution.py:416
  31.4 10.5 %collective-permute-start.9 = (bf16[800,256]{1,0:T(8,128)(2,1)S(1)}, bf16[800,256]{1,0:T(8,128)(2,1)S(1)}, u32[]{:S(2)}, u32[]{:S(2)}) collective-permute-start(bf16[800,256]{1,0:T(8,128)(2,1)S(1)} %add.20.after_ref.refs_0_), channel_id=1, source_target_pairs={{0,16},{4,12},{8,24},{12,4},{16,0},{20,28},{24,8},{28,20},{1,17},{... | collective-permute-start | bytes 1228808 | tf_op jit(solution)/shard_map/ppermute | solution.py:416
  33.0 1.5 %collective-permute-start.11 = (bf16[400,256]{1,0:T(8,128)(2,1)S(1)}, bf16[400,256]{1,0:T(8,128)(2,1)S(1)}, u32[]{:S(2)}, u32[]{:S(2)}) collective-permute-start(bf16[400,256]{1,0:T(8,128)(2,1)S(1)} %add.19.after_ref.own_ref), channel_id=1, source_target_pairs={{0,4},{4,0},{8,12},{12,8},{16,20},{20,16},{24,28},{28,24},{1,5},{5... | collective-permute-start | bytes 614408 | tf_op jit(solution)/shard_map/ppermute | solution.py:416
  33.0 18.3 %collective-permute-start.13 = (bf16[4,512,128]{2,1,0:T(8,128)(2,1)S(1)}, bf16[4,512,128]{2,1,0:T(8,128)(2,1)S(1)}, u32[]{:S(2)}, u32[]{:S(2)}) collective-permute-start(bf16[4,512,128]{2,1,0:T(8,128)(2,1)S(1)} %lags_rest.2.refs_2_.refs_0_), channel_id=1, source_target_pairs={{0,1},{3,2},{4,5},{7,6},{8,9},{11,10},{12,13},{15,14},{16,17},{19,... | collective-permute-start | bytes 1572872 | tf_op jit(solution)/shard_map/ppermute | solution.py:417
  39.6 20.3 %collective-permute-start.14 = (bf16[4,512,128]{2,1,0:T(8,128)(2,1)S(1)}, bf16[4,512,128]{2,1,0:T(8,128)(2,1)S(1)}, u32[]{:S(2)}, u32[]{:S(2)}) collective-permute-start(bf16[4,512,128]{2,1,0:T(8,128)(2,1)S(1)} %add.21.refs_2_), channel_id=1, source_target_pairs={{1,2},{2,1},{5,6},{6,5},{9,10},{10,9},{13,14},{14,13},{17,18},{18,... | collective-permute-start | bytes 1572872 | tf_op jit(solution)/shard_map/ppermute | solution.py:417
  42.1 4.5 %collective-permute-start.12 = (bf16[800,256]{1,0:T(8,128)(2,1)S(1)}, bf16[800,256]{1,0:T(8,128)(2,1)S(1)}, u32[]{:S(2)}, u32[]{:S(2)}) collective-permute-start(bf16[800,256]{1,0:T(8,128)(2,1)S(1)} %add.22.after_ref.own_ref), channel_id=1, source_target_pairs={{0,4},{4,0},{8,12},{12,8},{16,20},{20,16},{24,28},{28,24},{1,5},{5... | collective-permute-start | bytes 1228808 | tf_op jit(solution)/shard_map/ppermute | solution.py:416
  42.1 17.6 %collective-permute-start.15 = (bf16[2,512,128]{2,1,0:T(8,128)(2,1)S(1)}, bf16[2,512,128]{2,1,0:T(8,128)(2,1)S(1)}, u32[]{:S(2)}, u32[]{:S(2)}) collective-permute-start(bf16[2,512,128]{2,1,0:T(8,128)(2,1)S(1)} %get-tuple-element.27.refs_2_.refs_0_), channel_id=1, source_target_pairs={{0,1},{3,2},{4,5},{7,6},{8,9},{11,10},{12,13},{15,14},{16,17},{19,... | collective-permute-start | bytes 786440 | tf_op jit(solution)/shard_map/ppermute | solution.py:417
  45.2 28.3 %collective-permute-start.20 = (bf16[6,512,128]{2,1,0:T(8,128)(2,1)S(1)}, bf16[6,512,128]{2,1,0:T(8,128)(2,1)S(1)}, u32[]{:S(2)}, u32[]{:S(2)}) collective-permute-start(bf16[6,512,128]{2,1,0:T(8,128)(2,1)S(1)} %lags_rest.3.after_ref.refs_0_), channel_id=1, source_target_pairs={{0,1},{3,2},{4,5},{7,6},{8,9},{11,10},{12,13},{15,14},{16,17},{19,... | collective-permute-start | bytes 2359304 | tf_op jit(solution)/shard_map/ppermute | solution.py:417
  51.5 16.6 %collective-permute-start.18 = (bf16[4,512,128]{2,1,0:T(8,128)(2,1)S(1)}, bf16[4,512,128]{2,1,0:T(8,128)(2,1)S(1)}, u32[]{:S(2)}, u32[]{:S(2)}) collective-permute-start(bf16[4,512,128]{2,1,0:T(8,128)(2,1)S(1)} %add.23.after_ref), channel_id=1, source_target_pairs={{1,2},{2,1},{5,6},{6,5},{9,10},{10,9},{13,14},{14,13},{17,18},{18,... | collective-permute-start | bytes 1572872 | tf_op jit(solution)/shard_map/ppermute | solution.py:417
  60.0 13.3 %collective-permute-start.16 = (bf16[4,512,128]{2,1,0:T(8,128)(2,1)S(1)}, bf16[4,512,128]{2,1,0:T(8,128)(2,1)S(1)}, u32[]{:S(2)}, u32[]{:S(2)}) collective-permute-start(bf16[4,512,128]{2,1,0:T(8,128)(2,1)S(1)} %sum.5.refs_2_), channel_id=1, source_target_pairs={{1,0},{2,3},{5,4},{6,7},{9,8},{10,11},{13,12},{14,15},{17,16},{18,... | collective-permute-start | bytes 1572872 | tf_op jit(solution)/shard_map/ppermute | solution.py:417
  61.9 11.4 %collective-permute-start.17 = (bf16[2,512,128]{2,1,0:T(8,128)(2,1)S(1)}, bf16[2,512,128]{2,1,0:T(8,128)(2,1)S(1)}, u32[]{:S(2)}, u32[]{:S(2)}) collective-permute-start(bf16[2,512,128]{2,1,0:T(8,128)(2,1)S(1)} %add.24.refs_2_), channel_id=1, source_target_pairs={{1,2},{2,1},{5,6},{6,5},{9,10},{10,9},{13,14},{14,13},{17,18},{18,... | collective-permute-start | bytes 786440 | tf_op jit(solution)/shard_map/ppermute | solution.py:417
  65.3 29.8 %collective-permute-start.22 = (bf16[8,512,128]{2,1,0:T(8,128)(2,1)S(1)}, bf16[8,512,128]{2,1,0:T(8,128)(2,1)S(1)}, u32[]{:S(2)}, u32[]{:S(2)}) collective-permute-start(bf16[8,512,128]{2,1,0:T(8,128)(2,1)S(1)} %lags.7.refs_2_.refs_0_), channel_id=1, source_target_pairs={{0,1},{3,2},{4,5},{7,6},{8,9},{11,10},{12,13},{15,14},{16,17},{19,... | collective-permute-start | bytes 3145736 | tf_op jit(solution)/shard_map/ppermute | solution.py:417
  73.7 21.0 %collective-permute-start.21 = (bf16[6,512,128]{2,1,0:T(8,128)(2,1)S(1)}, bf16[6,512,128]{2,1,0:T(8,128)(2,1)S(1)}, u32[]{:S(2)}, u32[]{:S(2)}) collective-permute-start(bf16[6,512,128]{2,1,0:T(8,128)(2,1)S(1)} %add.25.refs_4_), channel_id=1, source_target_pairs={{1,2},{2,1},{5,6},{6,5},{9,10},{10,9},{13,14},{14,13},{17,18},{18,... | collective-permute-start | bytes 2359304 | tf_op jit(solution)/shard_map/ppermute | solution.py:417
  77.2 12.3 %collective-permute-start.19 = (bf16[4,512,128]{2,1,0:T(8,128)(2,1)S(1)}, bf16[4,512,128]{2,1,0:T(8,128)(2,1)S(1)}, u32[]{:S(2)}, u32[]{:S(2)}) collective-permute-start(bf16[4,512,128]{2,1,0:T(8,128)(2,1)S(1)} %sum.6.refs_3_), channel_id=1, source_target_pairs={{1,0},{2,3},{5,4},{6,7},{9,8},{10,11},{13,12},{14,15},{17,16},{18,... | collective-permute-start | bytes 1572872 | tf_op jit(solution)/shard_map/ppermute | solution.py:417

commit v4 on v3

--- a/solution.py
+++ b/solution.py
@@ -12,10 +12,14 @@
 GROUP = 16
 ORDER = ((3, 2, 1, 0), (3, 2, 0, 1), (0, 1, 3, 2), (0, 1, 2, 3))
 SPLITS = (4, 2, 8, 8)
-STEPS = "r0 r1 t r0 w r1 r2 r0 l0 r1 k0 r2 l1 m0 r2 k1 l3 n0 l2 m1 f g h n1 p".split()
+STEPS = (
+    "r0", "r1", "t", "r0", "w", "r1", "r2", "r0", "l0", "i0", "r1", "k0",
+    "r2", "l1", "m0", "r2", "k1", "n0", "l2", "m1", "f", "l3", "g", "h", "n1", "p",
+)
 INWARD = ((0, 1), (3, 2))
 MIDDLE = ((1, 2), (2, 1))
 OUTWARD = ((1, 0), (2, 3))
+ENDS, INNER = (0, 3), (1, 2)
 MIB = 1024 * 1024
 COST = pl.CostEstimate(flops=1, bytes_accessed=1, transcendentals=0)
 
@@ -237,10 +241,16 @@
     )(after)
 
 
-def lags_kernel(
-    base, done,
-    own_ref, other_ref, receivers_ref, table_ref, after_ref, out_ref, *refs,
-):
+def lags_kernel(base, done, hours, *refs):
+    hour = lax.axis_index("hour")
+    here = functools.reduce(jnp.logical_or, [hour == value for value in hours])
+
+    @pl.when(here)
+    def _():
+        make_lags(base, done, *refs)
+
+
+def make_lags(base, done, own_ref, other_ref, receivers_ref, table_ref, after_ref, out_ref, *refs):
     spec_ref, cross_ref = refs[-2:]
     count = 8
     _, window_count, freq_count, channels_here = receivers_ref.shape
@@ -329,7 +339,7 @@
             out_ref[2 * pair + 1, lags, :] = value[:, channels_here:]
 
 
-def lags_of(own, other, receivers, table, base, done, after):
+def lags_of(own, other, receivers, table, base, done, hours, after):
     _, window_count, freq_count, channels_here = receivers.shape
     wide = own.shape[1]
     count = 8
@@ -338,7 +348,7 @@
     if done < count:
         out_shape.append(jax.ShapeDtypeStruct(cross(count - done), jnp.bfloat16))
     return pl.pallas_call(
-        functools.partial(lags_kernel, base, done),
+        functools.partial(lags_kernel, base, done, hours),
         in_specs=[VMEM] * 4 + [ANY],
         out_specs=[VMEM] * len(out_shape),
         out_shape=out_shape,
@@ -436,22 +446,26 @@
             table = last = lag_table(freq_count, LAGS, last)
         elif kind == "w":
             receivers = last = whiten(data, scale, last)
-        elif kind in "lk":
+        elif kind in "li":
+            chunk = min(at, 2)
+            first, hours = SPLITS[at], (0, 1, 2, 3)
+            if at == 0:
+                first, hours = (first, ENDS) if kind == "l" else (8, INNER)
+            base = slot_rows * (at - chunk)
+            values = lags_of(state[chunk], moved[chunk], receivers, table, base, first, hours, last)
+            last = mine[at, kind] = values[0]
             if kind == "l":
-                chunk = min(at, 2)
-                values = lags_of(
-                    state[chunk], moved[chunk], receivers, table, slot_rows * (at - chunk), SPLITS[at], last
-                )
-                last = values[0]
                 cross[at] = values[-1]
-            else:
-                last = lags_of_rest(cross[at], table, last)
-            mine[at, kind] = last
-            if at < 3:
-                inward[at, kind] = over_hour(last, INWARD)
+                if at < 3:
+                    inward[at, kind] = over_hour(last, INWARD)
+        elif kind == "k":
+            last = mine[at, kind] = lags_of_rest(cross[at], table, last)
+            inward[at, kind] = over_hour(last, INWARD)
         elif kind in "mn":
-            which = "l" if kind == "m" else "k"
-            last = add_after(last, mine[at, which], inward[at, which])
+            which, low = ("l", 0) if kind == "m" else ("k", SPLITS[at])
+            part = (0, mine[0, "i"]) if at == 0 else (low, mine[at, which])
+            high = low + inward[at, which].shape[0]
+            last = sum_of([part, (low, inward[at, which])], low, high, jnp.bfloat16, last)
             middle[at, which] = over_hour(last, MIDDLE)
         elif kind in "fg":
             which, part = ("l", 0) if kind == "f" else ("k", 1)

time: 97.8 us -> 95.8 us (0.980); the launches traced: 96.3 us -> 95.5 us
  starting transfers between devices: 32.2 us -> 28.3 us
  waiting for transfers between devices: 33.8 us -> 35.7 us
  Pallas kernels: 29.8 us -> 31 us
    ppermute x11, waiting for transfers between devices: 24.2 us -> 30.1 us  [body(): over_hour = lambda value, pairs: lax.ppermute(value, 'hour', pairs)]
    ppermute x11, starting transfers between devices: 22.9 us -> 18.8 us  [body(): over_hour = lambda value, pairs: lax.ppermute(value, 'hour', pairs)]
    ppermute x12, waiting for transfers between devices: 9.57 us -> 5.64 us  [body(): over_chan = lambda value, pairs: lax.ppermute(value, 'chan', pairs)]
    pallas_call x4 -> x5, Pallas kernels: 16.7 us -> 17.9 us  [lags_of(): pl.pallas_call(functools.partial(lags_kernel, base, done, hours), in_spec...]
    pallas_call x5 -> x9, Pallas kernels: 1.68 us -> 2.17 us  [sum_of(): pl.pallas_call(functools.partial(sum_kernel, firsts, low), in_specs=[VMEM...]
  transfers between devices with their start and end apart: 23 -> 23, of which waited for: 11 -> 11; matrix products, arithmetic and copies ran while one was open for 0% -> 0% of each run, Pallas kernels for 25% -> 27%
where the time goes in v4:
time: 95.8 us; the launch traced here: 95.5 us
  waiting for transfers between devices  35.7 us (37%)
  Pallas kernels  31 us (32%)
  starting transfers between devices  28.3 us (30%)
    ppermute x11, waiting for transfers between devices, body(): over_hour = lambda value, pairs: lax.ppermute(value, 'hour', pairs)  30.1 us
    ppermute x11, starting transfers between devices, body(): over_hour = lambda value, pairs: lax.ppermute(value, 'hour', pairs)  18.8 us
    pallas_call x5, Pallas kernels, lags_of(): pl.pallas_call(functools.partial(lags_kernel, base, done, hours), in_spec...  17.9 us
    ppermute x12, starting transfers between devices, body(): over_chan = lambda value, pairs: lax.ppermute(value, 'chan', pairs)  9.53 us
    ppermute x12, waiting for transfers between devices, body(): over_chan = lambda value, pairs: lax.ppermute(value, 'chan', pairs)  5.64 us
    pallas_call x1, Pallas kernels, front(): pl.pallas_call(front_kernel, in_specs=[HBM, HBM, HBM], out_specs=[VMEM] *...  4.23 us
    pallas_call x2, Pallas kernels, lags_of_rest(): pl.pallas_call(lambda cross_ref, table_ref, after_ref, out_ref: transform...  2.71 us
    pallas_call x9, Pallas kernels, sum_of(): pl.pallas_call(functools.partial(sum_kernel, firsts, low), in_specs=[VMEM...  2.17 us
  transfers between devices with their start and end apart: 23, of which 11 were waited for; matrix products, arithmetic and copies ran while one was open for 0% of the time, Pallas kernels for 27%

profile of v4, /device:TPU:16, one launch (start us, length us, event | category | flops | bytes accessed | tf_op | source)
XLA Modules:
  0.0 95.5 jit_solution(7684801871358411241)
XLA Ops:
  0.0 4.2 %pick_sources.1 = (bf16[400,256]{1,0:T(8,128)(2,1)S(1)}, bf16[400,256]{1,0:T(8,128)(2,1)S(1)}, bf16[800,256]{1,0:T(8,128)(2,1)S(1)}, bf16[400,256]{1,0:T(8,128)(...) custom-call(s32[32]{0:T(128)} %sources_hbm.1, ...), custom_call_target="tpu_custom_call" | custom-call | flops 1 | bytes 1 | tf_op jit(solution)/shard_map/pick_sources/pallas_call | solution.py:142
  4.3 0.5 collective-permute-start.1
  4.9 0.9 collective-permute-done.2.refs_1_
  5.8 1.6 %collective-permute-start.4 = (bf16[400,256]{1,0:T(8,128)(2,1)S(1)}, bf16[400,256]{1,0:T(8,128)(2,1)S(1)}, u32[]{:S(2)}, u32[]{:S(2)}) collective-permute-start(bf16[400,256]{1,0:T(8,128)(2,1)S(1)} %add.9.refs_2_.refs_0_), channel_id=1, source_target_pairs={{0,8},{4,20},{8,0},{12,28},{16,24},{20,4},{24,16},{28,12},{1,9},{5... | collective-permute-start | bytes 614408 | tf_op jit(solution)/shard_map/ppermute | solution.py:426
  7.4 0.6 collective-permute-start.3
  8.0 1.9 %lag_table.1.refs_2_.refs_3_.table_ref = bf16[512,1600]{1,0:T(8,128)(2,1)S(1)} custom-call(bf16[400,256]{1,0:T(8,128)(2,1)S(1)} %add.10.after_ref.refs_0_), custom_call_target="tpu_custom_call" | custom-call | flops 1 | bytes 1 | tf_op jit(solution)/shard_map/lag_table/pallas_call | solution.py:233
  9.9 1.7 %collective-permute-done.4.refs_1_ = bf16[400,256]{1,0:T(8,128)(2,1)S(1)} collective-permute-done((bf16[400,256]{1,0:T(8,128)(2,1)S(1)}, bf16[400,256]{1,0:T(8,128)(2,1)S(1)}, u32[]{:S(2)}, u32[]{:S(2)}) %collective-permute-start.4) | collective-permute-done | bytes 204832 | tf_op jit(solution)/shard_map/ppermute | solution.py:426
  11.7 1.6 %collective-permute-start.6 = (bf16[400,256]{1,0:T(8,128)(2,1)S(1)}, bf16[400,256]{1,0:T(8,128)(2,1)S(1)}, u32[]{:S(2)}, u32[]{:S(2)}) collective-permute-start(bf16[400,256]{1,0:T(8,128)(2,1)S(1)} %add.11.after_ref.refs_0_), channel_id=1, source_target_pairs={{0,16},{4,12},{8,24},{12,4},{16,0},{20,28},{24,8},{28,20},{1,17},{... | collective-permute-start | bytes 614408 | tf_op jit(solution)/shard_map/ppermute | solution.py:426
  13.3 1.5 %whiten_receivers.1.refs_2_ = bf16[2,16,800,128]{3,2,1,0:T(8,128)(2,1)S(1)} custom-call(bf16[2,16,800,128]{3,2,1,0:T(8,128)(2,1)S(1)} %get-tuple-element.24.data_ref, f32[16,128]{1,0:T(8,128)S(1)} %get-tuple-element.23.refs_2_.scale_ref, bf16[400,256]{1,0:T(8,128)(2,1)S(1)} %add.11.after_ref.refs_0_), custom_call_target="tpu_custom_call" | custom-call | flops 1 | bytes 1 | tf_op jit(solution)/shard_map/whiten_receivers/pallas_call | solution.py:180
  14.9 0.1 add.13.refs_2_.refs_0_
  15.0 2.5 %collective-permute-done.6.refs_1_ = bf16[400,256]{1,0:T(8,128)(2,1)S(1)} collective-permute-done((bf16[400,256]{1,0:T(8,128)(2,1)S(1)}, bf16[400,256]{1,0:T(8,128)(2,1)S(1)}, u32[]{:S(2)}, u32[]{:S(2)}) %collective-permute-start.6) | collective-permute-done | bytes 204832 | tf_op jit(solution)/shard_map/ppermute | solution.py:426
  17.6 1.6 %collective-permute-start.5 = (bf16[800,256]{1,0:T(8,128)(2,1)S(1)}, bf16[800,256]{1,0:T(8,128)(2,1)S(1)}, u32[]{:S(2)}, u32[]{:S(2)}) collective-permute-start(bf16[800,256]{1,0:T(8,128)(2,1)S(1)} %add.13.refs_2_.refs_0_), channel_id=1, source_target_pairs={{0,8},{4,20},{8,0},{12,28},{16,24},{20,4},{24,16},{28,12},{1,9},{5... | collective-permute-start | bytes 1228808 | tf_op jit(solution)/shard_map/ppermute | solution.py:426
  19.2 1.3 %collective-permute-start.10 = (bf16[4,512,128]{2,1,0:T(8,128)(2,1)S(1)}, bf16[4,512,128]{2,1,0:T(8,128)(2,1)S(1)}, u32[]{:S(2)}, u32[]{:S(2)}) collective-permute-start(bf16[4,512,128]{2,1,0:T(8,128)(2,1)S(1)} %get-tuple-element.26.refs_4_), channel_id=1, source_target_pairs={{0,1},{3,2},{4,5},{7,6},{8,9},{11,10},{12,13},{15,14},{16,17},{19,... | collective-permute-start | bytes 1572872 | tf_op jit(solution)/shard_map/ppermute | solution.py:427
  20.5 1.6 %collective-permute-start.8 = (bf16[400,256]{1,0:T(8,128)(2,1)S(1)}, bf16[400,256]{1,0:T(8,128)(2,1)S(1)}, u32[]{:S(2)}, u32[]{:S(2)}) collective-permute-start(bf16[400,256]{1,0:T(8,128)(2,1)S(1)} %add.12.refs_2_.refs_0_), channel_id=1, source_target_pairs={{0,16},{4,12},{8,24},{12,4},{16,0},{20,28},{24,8},{28,20},{1,17},{... | collective-permute-start | bytes 614408 | tf_op jit(solution)/shard_map/ppermute | solution.py:426
  22.1 4.8 %lags.6.refs_2_.refs_0_ = bf16[8,512,128]{2,1,0:T(8,128)(2,1)S(1)} custom-call(bf16[400,256]{1,0:T(8,128)(2,1)S(1)} %add.14.refs_0_.refs_4_, bf16[400,256]{1,0:T(8,128)(2,1)S(1)} %collective-permute-done.7.refs_1_, bf16[2,16,800,128]{3,2,1,0:T(8,128)(2,1)S(1)} %whiten_receivers.1.refs_2_, bf16[512,1600]{1,0:T(8,128)(2,1)S(1)} %lag_table.1.refs_2_.refs_3_.table_ref, ...), custom_call_target="tpu_custom_call" | custom-call | flops 1 | bytes 1 | tf_op jit(solution)/shard_map/lags/pallas_call | solution.py:350
  26.9 0.5 collective-permute-done.8.refs_1_
  27.4 1.1 %lags_rest.2.refs_2_ = bf16[4,512,128]{2,1,0:T(8,128)(2,1)S(1)} custom-call(bf16[2,1600,256]{2,1,0:T(8,128)(2,1)S(1)} %get-tuple-element.25.cross_ref, bf16[512,1600]{1,0:T(8,128)(2,1)S(1)} %lag_table.1.refs_2_.refs_3_.table_ref, bf16[400,256]{1,0:T(8,128)(2,1)S(1)} %add.15.after_ref.refs_0_), custom_call_target="tpu_custom_call" | custom-call | flops 1 | bytes 1 | tf_op jit(solution)/shard_map/lags_rest/pallas_call | solution.py:367
  28.6 1.6 %collective-permute-start.9 = (bf16[800,256]{1,0:T(8,128)(2,1)S(1)}, bf16[800,256]{1,0:T(8,128)(2,1)S(1)}, u32[]{:S(2)}, u32[]{:S(2)}) collective-permute-start(bf16[800,256]{1,0:T(8,128)(2,1)S(1)} %add.16.refs_4_.refs_0_), channel_id=1, source_target_pairs={{0,16},{4,12},{8,24},{12,4},{16,0},{20,28},{24,8},{28,20},{1,17},{... | collective-permute-start | bytes 1228808 | tf_op jit(solution)/shard_map/ppermute | solution.py:426
  30.2 0.3 collective-permute-start.11
  30.5 1.3 %collective-permute-start.13 = (bf16[4,512,128]{2,1,0:T(8,128)(2,1)S(1)}, bf16[4,512,128]{2,1,0:T(8,128)(2,1)S(1)}, u32[]{:S(2)}, u32[]{:S(2)}) collective-permute-start(bf16[4,512,128]{2,1,0:T(8,128)(2,1)S(1)} %lags_rest.2.refs_2_), channel_id=1, source_target_pairs={{0,1},{3,2},{4,5},{7,6},{8,9},{11,10},{12,13},{15,14},{16,17},{19,... | collective-permute-start | bytes 1572872 | tf_op jit(solution)/shard_map/ppermute | solution.py:427
  31.8 3.5 %lags.7 = (bf16[2,512,128]{2,1,0:T(8,128)(2,1)S(1)}, bf16[3,1600,256]{2,1,0:T(8,128)(2,1)S(1)}) custom-call(bf16[400,256]{1,0:T(8,128)(2,1)S(1)} %add.15.after_ref.refs_0_, bf16[400,256]{1,0:T(8,128)(2,1)S(1)} %collective-permute-done.11.refs_1_, bf16[2,16,800,128]{3,2,1,0:T(8,128)(2,1)S(1)} %whiten_receivers.1.refs_2_, ...), custom_call_target="tpu_custom_call" | custom-call | flops 1 | bytes 1 | tf_op jit(solution)/shard_map/lags/pallas_call | solution.py:350
  35.3 3.2 %collective-permute-done.10.refs_1_ = bf16[4,512,128]{2,1,0:T(8,128)(2,1)S(1)} collective-permute-done((bf16[4,512,128]{2,1,0:T(8,128)(2,1)S(1)}, bf16[4,512,128]{2,1,0:T(8,128)(2,1)S(1)}, u32[]{:S(2)}, u32[]{:S(2)}) %collective-permute-start.10) | collective-permute-done | bytes 524320 | tf_op jit(solution)/shard_map/ppermute | solution.py:427
  38.6 0.1 sum.9.refs_2_
  38.7 1.9 %collective-permute-start.14 = (bf16[4,512,128]{2,1,0:T(8,128)(2,1)S(1)}, bf16[4,512,128]{2,1,0:T(8,128)(2,1)S(1)}, u32[]{:S(2)}, u32[]{:S(2)}) collective-permute-start(bf16[4,512,128]{2,1,0:T(8,128)(2,1)S(1)} %sum.9.refs_2_), channel_id=1, source_target_pairs={{1,2},{2,1},{5,6},{6,5},{9,10},{10,9},{13,14},{14,13},{17,18},{18,... | collective-permute-start | bytes 1572872 | tf_op jit(solution)/shard_map/ppermute | solution.py:427
  40.8 1.3 %collective-permute-start.15 = (bf16[2,512,128]{2,1,0:T(8,128)(2,1)S(1)}, bf16[2,512,128]{2,1,0:T(8,128)(2,1)S(1)}, u32[]{:S(2)}, u32[]{:S(2)}) collective-permute-start(bf16[2,512,128]{2,1,0:T(8,128)(2,1)S(1)} %get-tuple-element.27.refs_2_.refs_0_), channel_id=1, source_target_pairs={{0,1},{3,2},{4,5},{7,6},{8,9},{11,10},{12,13},{15,14},{16,17},{19,... | collective-permute-start | bytes 786440 | tf_op jit(solution)/shard_map/ppermute | solution.py:427
  42.1 1.6 %lags_rest.3.refs_2_.refs_0_ = bf16[6,512,128]{2,1,0:T(8,128)(2,1)S(1)} custom-call(bf16[3,1600,256]{2,1,0:T(8,128)(2,1)S(1)} %get-tuple-element.28.cross_ref, bf16[512,1600]{1,0:T(8,128)(2,1)S(1)} %lag_table.1.refs_2_.refs_3_.table_ref, bf16[800,256]{1,0:T(8,128)(2,1)S(1)} %add.17.after_ref.refs_0_), custom_call_target="tpu_custom_call" | custom-call | flops 1 | bytes 1 | tf_op jit(solution)/shard_map/lags_rest/pallas_call | solution.py:367
  43.7 1.3 %collective-permute-start.20 = (bf16[6,512,128]{2,1,0:T(8,128)(2,1)S(1)}, bf16[6,512,128]{2,1,0:T(8,128)(2,1)S(1)}, u32[]{:S(2)}, u32[]{:S(2)}) collective-permute-start(bf16[6,512,128]{2,1,0:T(8,128)(2,1)S(1)} %lags_rest.3.refs_2_.refs_0_), channel_id=1, source_target_pairs={{0,1},{3,2},{4,5},{7,6},{8,9},{11,10},{12,13},{15,14},{16,17},{19,... | collective-permute-start | bytes 2359304 | tf_op jit(solution)/shard_map/ppermute | solution.py:427
  45.0 4.8 %collective-permute-done.13.refs_1_ = bf16[4,512,128]{2,1,0:T(8,128)(2,1)S(1)} collective-permute-done((bf16[4,512,128]{2,1,0:T(8,128)(2,1)S(1)}, bf16[4,512,128]{2,1,0:T(8,128)(2,1)S(1)}, u32[]{:S(2)}, u32[]{:S(2)}) %collective-permute-start.13) | collective-permute-done | bytes 524320 | tf_op jit(solution)/shard_map/ppermute | solution.py:427
  49.8 0.1 sum.10.refs_4_
  49.9 1.9 %collective-permute-start.18 = (bf16[4,512,128]{2,1,0:T(8,128)(2,1)S(1)}, bf16[4,512,128]{2,1,0:T(8,128)(2,1)S(1)}, u32[]{:S(2)}, u32[]{:S(2)}) collective-permute-start(bf16[4,512,128]{2,1,0:T(8,128)(2,1)S(1)} %sum.10.refs_4_), channel_id=1, source_target_pairs={{1,2},{2,1},{5,6},{6,5},{9,10},{10,9},{13,14},{14,13},{17,18},{18,... | collective-permute-start | bytes 1572872 | tf_op jit(solution)/shard_map/ppermute | solution.py:427
  51.9 4.8 %lags.8.refs_2_.refs_0_ = bf16[8,512,128]{2,1,0:T(8,128)(2,1)S(1)} custom-call(bf16[800,256]{1,0:T(8,128)(2,1)S(1)} %add.17.after_ref.refs_0_, bf16[800,256]{1,0:T(8,128)(2,1)S(1)} %collective-permute-done.12.refs_1_, bf16[2,16,800,128]{3,2,1,0:T(8,128)(2,1)S(1)} %whiten_receivers.1.refs_2_, bf16[512,1600]{1,0:T(8,128)(2,1)S(1)} %lag_table.1.refs_2_.refs_3_.table_ref, ...), custom_call_target="tpu_custom_call" | custom-call | flops 1 | bytes 1 | tf_op jit(solution)/shard_map/lags/pallas_call | solution.py:350
  56.8 0.1 sum.12.refs_4_
  56.9 1.3 %collective-permute-start.16 = (bf16[4,512,128]{2,1,0:T(8,128)(2,1)S(1)}, bf16[4,512,128]{2,1,0:T(8,128)(2,1)S(1)}, u32[]{:S(2)}, u32[]{:S(2)}) collective-permute-start(bf16[4,512,128]{2,1,0:T(8,128)(2,1)S(1)} %sum.12.refs_4_), channel_id=1, source_target_pairs={{1,0},{2,3},{5,4},{6,7},{9,8},{10,11},{13,12},{14,15},{17,16},{18,... | collective-permute-start | bytes 1572872 | tf_op jit(solution)/shard_map/ppermute | solution.py:427
  58.2 3.9 %collective-permute-start.17 = (bf16[2,512,128]{2,1,0:T(8,128)(2,1)S(1)}, bf16[2,512,128]{2,1,0:T(8,128)(2,1)S(1)}, u32[]{:S(2)}, u32[]{:S(2)}) collective-permute-start(bf16[2,512,128]{2,1,0:T(8,128)(2,1)S(1)} %sum.11.refs_2_), channel_id=1, source_target_pairs={{1,2},{2,1},{5,6},{6,5},{9,10},{10,9},{13,14},{14,13},{17,18},{18,... | collective-permute-start | bytes 786440 | tf_op jit(solution)/shard_map/ppermute | solution.py:427
  62.2 1.3 %collective-permute-start.22 = (bf16[8,512,128]{2,1,0:T(8,128)(2,1)S(1)}, bf16[8,512,128]{2,1,0:T(8,128)(2,1)S(1)}, u32[]{:S(2)}, u32[]{:S(2)}) collective-permute-start(bf16[8,512,128]{2,1,0:T(8,128)(2,1)S(1)} %lags.8.refs_2_.refs_0_), channel_id=1, source_target_pairs={{0,1},{3,2},{4,5},{7,6},{8,9},{11,10},{12,13},{15,14},{16,17},{19,... | collective-permute-start | bytes 3145736 | tf_op jit(solution)/shard_map/ppermute | solution.py:427
  63.5 4.8 %lags.9.refs_2_.refs_0_ = bf16[8,512,128]{2,1,0:T(8,128)(2,1)S(1)} custom-call(bf16[800,256]{1,0:T(8,128)(2,1)S(1)} %add.17.after_ref.refs_0_, bf16[800,256]{1,0:T(8,128)(2,1)S(1)} %collective-permute-done.12.refs_1_, bf16[2,16,800,128]{3,2,1,0:T(8,128)(2,1)S(1)} %whiten_receivers.1.refs_2_, bf16[512,1600]{1,0:T(8,128)(2,1)S(1)} %lag_table.1.refs_2_.refs_3_.table_ref, ...), custom_call_target="tpu_custom_call" | custom-call | flops 1 | bytes 1 | tf_op jit(solution)/shard_map/lags/pallas_call | solution.py:350
  68.3 0.1 sum.13.refs_3_
  68.4 2.1 %collective-permute-done.17.refs_2_ = bf16[2,512,128]{2,1,0:T(8,128)(2,1)S(1)} collective-permute-done((bf16[2,512,128]{2,1,0:T(8,128)(2,1)S(1)}, bf16[2,512,128]{2,1,0:T(8,128)(2,1)S(1)}, u32[]{:S(2)}, u32[]{:S(2)}) %collective-permute-start.17) | collective-permute-done | bytes 262176 | tf_op jit(solution)/shard_map/ppermute | solution.py:427
  70.5 0.1 sum.14.refs_2_.refs_0_
  70.7 1.6 %collective-permute-done.20.refs_1_ = bf16[6,512,128]{2,1,0:T(8,128)(2,1)S(1)} collective-permute-done((bf16[6,512,128]{2,1,0:T(8,128)(2,1)S(1)}, bf16[6,512,128]{2,1,0:T(8,128)(2,1)S(1)}, u32[]{:S(2)}, u32[]{:S(2)}) %collective-permute-start.20) | collective-permute-done | bytes 786464 | tf_op jit(solution)/shard_map/ppermute | solution.py:427
  72.3 0.2 sum.15.refs_4_
  72.4 1.9 %collective-permute-start.21 = (bf16[6,512,128]{2,1,0:T(8,128)(2,1)S(1)}, bf16[6,512,128]{2,1,0:T(8,128)(2,1)S(1)}, u32[]{:S(2)}, u32[]{:S(2)}) collective-permute-start(bf16[6,512,128]{2,1,0:T(8,128)(2,1)S(1)} %sum.15.refs_4_), channel_id=1, source_target_pairs={{1,2},{2,1},{5,6},{6,5},{9,10},{10,9},{13,14},{14,13},{17,18},{18,... | collective-permute-start | bytes 2359304 | tf_op jit(solution)/shard_map/ppermute | solution.py:427
  74.4 1.3 %collective-permute-start.19 = (bf16[4,512,128]{2,1,0:T(8,128)(2,1)S(1)}, bf16[4,512,128]{2,1,0:T(8,128)(2,1)S(1)}, u32[]{:S(2)}, u32[]{:S(2)}) collective-permute-start(bf16[4,512,128]{2,1,0:T(8,128)(2,1)S(1)} %sum.13.refs_3_), channel_id=1, source_target_pairs={{1,0},{2,3},{5,4},{6,7},{9,8},{10,11},{13,12},{14,15},{17,16},{18,... | collective-permute-start | bytes 1572872 | tf_op jit(solution)/shard_map/ppermute | solution.py:427
  75.7 10.8 %collective-permute-done.19.refs_2_ = bf16[4,512,128]{2,1,0:T(8,128)(2,1)S(1)} collective-permute-done((bf16[4,512,128]{2,1,0:T(8,128)(2,1)S(1)}, bf16[4,512,128]{2,1,0:T(8,128)(2,1)S(1)}, u32[]{:S(2)}, u32[]{:S(2)}) %collective-permute-start.19) | collective-permute-done | bytes 524320 | tf_op jit(solution)/shard_map/ppermute | solution.py:427
  86.5 6.5 %collective-permute-done.21.refs_3_ = bf16[6,512,128]{2,1,0:T(8,128)(2,1)S(1)} collective-permute-done((bf16[6,512,128]{2,1,0:T(8,128)(2,1)S(1)}, bf16[6,512,128]{2,1,0:T(8,128)(2,1)S(1)}, u32[]{:S(2)}, u32[]{:S(2)}) %collective-permute-start.21) | collective-permute-done | bytes 786464 | tf_op jit(solution)/shard_map/ppermute | solution.py:427
  93.1 0.2 sum.16.refs_0_.refs_2_
  93.3 1.0 %collective-permute-done.22.refs_1_ = bf16[8,512,128]{2,1,0:T(8,128)(2,1)S(1)} collective-permute-done((bf16[8,512,128]{2,1,0:T(8,128)(2,1)S(1)}, bf16[8,512,128]{2,1,0:T(8,128)(2,1)S(1)}, u32[]{:S(2)}, u32[]{:S(2)}) %collective-permute-start.22) | collective-permute-done | bytes 1048608 | tf_op jit(solution)/shard_map/ppermute | solution.py:427
  94.3 1.0 %sum.17 = bf16[8,512,128]{2,1,0:T(8,128)(2,1)} custom-call(f32[8,512,128]{2,1,0:T(8,128)S(1)} %sum.16.refs_0_.refs_2_, bf16[8,512,128]{2,1,0:T(8,128)(2,1)S(1)} %collective-permute-done.22.refs_1_, f32[8,512,128]{2,1,0:T(8,128)S(1)} %sum.16.refs_0_.refs_2_), custom_call_target="tpu_custom_call" | custom-call | flops 1 | bytes 1 | tf_op jit(solution)/shard_map/sum/pallas_call | solution.py:401
  (27 shorter events, 0.9 us)
Async XLA Ops:
  4.2 1.5 %collective-permute-start.2 = (bf16[400,256]{1,0:T(8,128)(2,1)S(1)}, bf16[400,256]{1,0:T(8,128)(2,1)S(1)}, u32[]{:S(2)}, u32[]{:S(2)}) collective-permute-start(bf16[400,256]{1,0:T(8,128)(2,1)S(1)} %get-tuple-element.22), channel_id=1, source_target_pairs={{0,4},{4,0},{8,12},{12,8},{16,20},{20,16},{24,28},{28,24},{1,5},{5... | collective-permute-start | bytes 614408 | tf_op jit(solution)/shard_map/ppermute | solution.py:426
  4.3 3.1 %collective-permute-start.1 = (bf16[400,256]{1,0:T(8,128)(2,1)S(1)}, bf16[400,256]{1,0:T(8,128)(2,1)S(1)}, u32[]{:S(2)}, u32[]{:S(2)}) collective-permute-start(bf16[400,256]{1,0:T(8,128)(2,1)S(1)} %get-tuple-element.20), channel_id=1, source_target_pairs={{0,4},{4,0},{8,12},{12,8},{16,20},{20,16},{24,28},{28,24},{1,5},{5... | collective-permute-start | bytes 614408 | tf_op jit(solution)/shard_map/ppermute | solution.py:426
  4.8 10.0 %collective-permute-start = (bf16[800,256]{1,0:T(8,128)(2,1)S(1)}, bf16[800,256]{1,0:T(8,128)(2,1)S(1)}, u32[]{:S(2)}, u32[]{:S(2)}) collective-permute-start(bf16[800,256]{1,0:T(8,128)(2,1)S(1)} %get-tuple-element.18), channel_id=1, source_target_pairs={{0,4},{4,0},{8,12},{12,8},{16,20},{20,16},{24,28},{28,24},{1,5},{5... | collective-permute-start | bytes 1228808 | tf_op jit(solution)/shard_map/ppermute | solution.py:426
  5.8 5.8 %collective-permute-start.4 = (bf16[400,256]{1,0:T(8,128)(2,1)S(1)}, bf16[400,256]{1,0:T(8,128)(2,1)S(1)}, u32[]{:S(2)}, u32[]{:S(2)}) collective-permute-start(bf16[400,256]{1,0:T(8,128)(2,1)S(1)} %add.9.refs_2_.refs_0_), channel_id=1, source_target_pairs={{0,8},{4,20},{8,0},{12,28},{16,24},{20,4},{24,16},{28,12},{1,9},{5... | collective-permute-start | bytes 614408 | tf_op jit(solution)/shard_map/ppermute | solution.py:426
  7.4 7.4 %collective-permute-start.3 = (bf16[400,256]{1,0:T(8,128)(2,1)S(1)}, bf16[400,256]{1,0:T(8,128)(2,1)S(1)}, u32[]{:S(2)}, u32[]{:S(2)}) collective-permute-start(bf16[400,256]{1,0:T(8,128)(2,1)S(1)} %add.10.after_ref.refs_0_), channel_id=1, source_target_pairs={{0,8},{4,20},{8,0},{12,28},{16,24},{20,4},{24,16},{28,12},{1,9},{5... | collective-permute-start | bytes 614408 | tf_op jit(solution)/shard_map/ppermute | solution.py:426
  11.7 5.8 %collective-permute-start.6 = (bf16[400,256]{1,0:T(8,128)(2,1)S(1)}, bf16[400,256]{1,0:T(8,128)(2,1)S(1)}, u32[]{:S(2)}, u32[]{:S(2)}) collective-permute-start(bf16[400,256]{1,0:T(8,128)(2,1)S(1)} %add.11.after_ref.refs_0_), channel_id=1, source_target_pairs={{0,16},{4,12},{8,24},{12,4},{16,0},{20,28},{24,8},{28,20},{1,17},{... | collective-permute-start | bytes 614408 | tf_op jit(solution)/shard_map/ppermute | solution.py:426
  17.6 1.6 %collective-permute-start.7 = (bf16[400,256]{1,0:T(8,128)(2,1)S(1)}, bf16[400,256]{1,0:T(8,128)(2,1)S(1)}, u32[]{:S(2)}, u32[]{:S(2)}) collective-permute-start(bf16[400,256]{1,0:T(8,128)(2,1)S(1)} %add.14.refs_0_.refs_4_), channel_id=1, source_target_pairs={{0,4},{4,0},{8,12},{12,8},{16,20},{20,16},{24,28},{28,24},{1,5},{5... | collective-permute-start | bytes 614408 | tf_op jit(solution)/shard_map/ppermute | solution.py:426
  17.6 10.9 %collective-permute-start.5 = (bf16[800,256]{1,0:T(8,128)(2,1)S(1)}, bf16[800,256]{1,0:T(8,128)(2,1)S(1)}, u32[]{:S(2)}, u32[]{:S(2)}) collective-permute-start(bf16[800,256]{1,0:T(8,128)(2,1)S(1)} %add.13.refs_2_.refs_0_), channel_id=1, source_target_pairs={{0,8},{4,20},{8,0},{12,28},{16,24},{20,4},{24,16},{28,12},{1,9},{5... | collective-permute-start | bytes 1228808 | tf_op jit(solution)/shard_map/ppermute | solution.py:426
  19.2 19.3 %collective-permute-start.10 = (bf16[4,512,128]{2,1,0:T(8,128)(2,1)S(1)}, bf16[4,512,128]{2,1,0:T(8,128)(2,1)S(1)}, u32[]{:S(2)}, u32[]{:S(2)}) collective-permute-start(bf16[4,512,128]{2,1,0:T(8,128)(2,1)S(1)} %get-tuple-element.26.refs_4_), channel_id=1, source_target_pairs={{0,1},{3,2},{4,5},{7,6},{8,9},{11,10},{12,13},{15,14},{16,17},{19,... | collective-permute-start | bytes 1572872 | tf_op jit(solution)/shard_map/ppermute | solution.py:427
  20.5 6.8 %collective-permute-start.8 = (bf16[400,256]{1,0:T(8,128)(2,1)S(1)}, bf16[400,256]{1,0:T(8,128)(2,1)S(1)}, u32[]{:S(2)}, u32[]{:S(2)}) collective-permute-start(bf16[400,256]{1,0:T(8,128)(2,1)S(1)} %add.12.refs_2_.refs_0_), channel_id=1, source_target_pairs={{0,16},{4,12},{8,24},{12,4},{16,0},{20,28},{24,8},{28,20},{1,17},{... | collective-permute-start | bytes 614408 | tf_op jit(solution)/shard_map/ppermute | solution.py:426
  28.6 12.0 %collective-permute-start.9 = (bf16[800,256]{1,0:T(8,128)(2,1)S(1)}, bf16[800,256]{1,0:T(8,128)(2,1)S(1)}, u32[]{:S(2)}, u32[]{:S(2)}) collective-permute-start(bf16[800,256]{1,0:T(8,128)(2,1)S(1)} %add.16.refs_4_.refs_0_), channel_id=1, source_target_pairs={{0,16},{4,12},{8,24},{12,4},{16,0},{20,28},{24,8},{28,20},{1,17},{... | collective-permute-start | bytes 1228808 | tf_op jit(solution)/shard_map/ppermute | solution.py:426
  30.2 1.6 %collective-permute-start.11 = (bf16[400,256]{1,0:T(8,128)(2,1)S(1)}, bf16[400,256]{1,0:T(8,128)(2,1)S(1)}, u32[]{:S(2)}, u32[]{:S(2)}) collective-permute-start(bf16[400,256]{1,0:T(8,128)(2,1)S(1)} %add.15.after_ref.refs_0_), channel_id=1, source_target_pairs={{0,4},{4,0},{8,12},{12,8},{16,20},{20,16},{24,28},{28,24},{1,5},{5... | collective-permute-start | bytes 614408 | tf_op jit(solution)/shard_map/ppermute | solution.py:426
  30.5 19.3 %collective-permute-start.13 = (bf16[4,512,128]{2,1,0:T(8,128)(2,1)S(1)}, bf16[4,512,128]{2,1,0:T(8,128)(2,1)S(1)}, u32[]{:S(2)}, u32[]{:S(2)}) collective-permute-start(bf16[4,512,128]{2,1,0:T(8,128)(2,1)S(1)} %lags_rest.2.refs_2_), channel_id=1, source_target_pairs={{0,1},{3,2},{4,5},{7,6},{8,9},{11,10},{12,13},{15,14},{16,17},{19,... | collective-permute-start | bytes 1572872 | tf_op jit(solution)/shard_map/ppermute | solution.py:427
  38.7 18.1 %collective-permute-start.14 = (bf16[4,512,128]{2,1,0:T(8,128)(2,1)S(1)}, bf16[4,512,128]{2,1,0:T(8,128)(2,1)S(1)}, u32[]{:S(2)}, u32[]{:S(2)}) collective-permute-start(bf16[4,512,128]{2,1,0:T(8,128)(2,1)S(1)} %sum.9.refs_2_), channel_id=1, source_target_pairs={{1,2},{2,1},{5,6},{6,5},{9,10},{10,9},{13,14},{14,13},{17,18},{18,... | collective-permute-start | bytes 1572872 | tf_op jit(solution)/shard_map/ppermute | solution.py:427
  40.7 11.1 %collective-permute-start.12 = (bf16[800,256]{1,0:T(8,128)(2,1)S(1)}, bf16[800,256]{1,0:T(8,128)(2,1)S(1)}, u32[]{:S(2)}, u32[]{:S(2)}) collective-permute-start(bf16[800,256]{1,0:T(8,128)(2,1)S(1)} %add.17.after_ref.refs_0_), channel_id=1, source_target_pairs={{0,4},{4,0},{8,12},{12,8},{16,20},{20,16},{24,28},{28,24},{1,5},{5... | collective-permute-start | bytes 1228808 | tf_op jit(solution)/shard_map/ppermute | solution.py:426
  40.8 15.9 %collective-permute-start.15 = (bf16[2,512,128]{2,1,0:T(8,128)(2,1)S(1)}, bf16[2,512,128]{2,1,0:T(8,128)(2,1)S(1)}, u32[]{:S(2)}, u32[]{:S(2)}) collective-permute-start(bf16[2,512,128]{2,1,0:T(8,128)(2,1)S(1)} %get-tuple-element.27.refs_2_.refs_0_), channel_id=1, source_target_pairs={{0,1},{3,2},{4,5},{7,6},{8,9},{11,10},{12,13},{15,14},{16,17},{19,... | collective-permute-start | bytes 786440 | tf_op jit(solution)/shard_map/ppermute | solution.py:427
  43.7 28.6 %collective-permute-start.20 = (bf16[6,512,128]{2,1,0:T(8,128)(2,1)S(1)}, bf16[6,512,128]{2,1,0:T(8,128)(2,1)S(1)}, u32[]{:S(2)}, u32[]{:S(2)}) collective-permute-start(bf16[6,512,128]{2,1,0:T(8,128)(2,1)S(1)} %lags_rest.3.refs_2_.refs_0_), channel_id=1, source_target_pairs={{0,1},{3,2},{4,5},{7,6},{8,9},{11,10},{12,13},{15,14},{16,17},{19,... | collective-permute-start | bytes 2359304 | tf_op jit(solution)/shard_map/ppermute | solution.py:427
  49.9 18.4 %collective-permute-start.18 = (bf16[4,512,128]{2,1,0:T(8,128)(2,1)S(1)}, bf16[4,512,128]{2,1,0:T(8,128)(2,1)S(1)}, u32[]{:S(2)}, u32[]{:S(2)}) collective-permute-start(bf16[4,512,128]{2,1,0:T(8,128)(2,1)S(1)} %sum.10.refs_4_), channel_id=1, source_target_pairs={{1,2},{2,1},{5,6},{6,5},{9,10},{10,9},{13,14},{14,13},{17,18},{18,... | collective-permute-start | bytes 1572872 | tf_op jit(solution)/shard_map/ppermute | solution.py:427
  56.9 13.6 %collective-permute-start.16 = (bf16[4,512,128]{2,1,0:T(8,128)(2,1)S(1)}, bf16[4,512,128]{2,1,0:T(8,128)(2,1)S(1)}, u32[]{:S(2)}, u32[]{:S(2)}) collective-permute-start(bf16[4,512,128]{2,1,0:T(8,128)(2,1)S(1)} %sum.12.refs_4_), channel_id=1, source_target_pairs={{1,0},{2,3},{5,4},{6,7},{9,8},{10,11},{13,12},{14,15},{17,16},{18,... | collective-permute-start | bytes 1572872 | tf_op jit(solution)/shard_map/ppermute | solution.py:427
  58.2 12.3 %collective-permute-start.17 = (bf16[2,512,128]{2,1,0:T(8,128)(2,1)S(1)}, bf16[2,512,128]{2,1,0:T(8,128)(2,1)S(1)}, u32[]{:S(2)}, u32[]{:S(2)}) collective-permute-start(bf16[2,512,128]{2,1,0:T(8,128)(2,1)S(1)} %sum.11.refs_2_), channel_id=1, source_target_pairs={{1,2},{2,1},{5,6},{6,5},{9,10},{10,9},{13,14},{14,13},{17,18},{18,... | collective-permute-start | bytes 786440 | tf_op jit(solution)/shard_map/ppermute | solution.py:427
  62.2 32.2 %collective-permute-start.22 = (bf16[8,512,128]{2,1,0:T(8,128)(2,1)S(1)}, bf16[8,512,128]{2,1,0:T(8,128)(2,1)S(1)}, u32[]{:S(2)}, u32[]{:S(2)}) collective-permute-start(bf16[8,512,128]{2,1,0:T(8,128)(2,1)S(1)} %lags.8.refs_2_.refs_0_), channel_id=1, source_target_pairs={{0,1},{3,2},{4,5},{7,6},{8,9},{11,10},{12,13},{15,14},{16,17},{19,... | collective-permute-start | bytes 3145736 | tf_op jit(solution)/shard_map/ppermute | solution.py:427
  72.4 20.6 %collective-permute-start.21 = (bf16[6,512,128]{2,1,0:T(8,128)(2,1)S(1)}, bf16[6,512,128]{2,1,0:T(8,128)(2,1)S(1)}, u32[]{:S(2)}, u32[]{:S(2)}) collective-permute-start(bf16[6,512,128]{2,1,0:T(8,128)(2,1)S(1)} %sum.15.refs_4_), channel_id=1, source_target_pairs={{1,2},{2,1},{5,6},{6,5},{9,10},{10,9},{13,14},{14,13},{17,18},{18,... | collective-permute-start | bytes 2359304 | tf_op jit(solution)/shard_map/ppermute | solution.py:427
  74.4 12.2 %collective-permute-start.19 = (bf16[4,512,128]{2,1,0:T(8,128)(2,1)S(1)}, bf16[4,512,128]{2,1,0:T(8,128)(2,1)S(1)}, u32[]{:S(2)}, u32[]{:S(2)}) collective-permute-start(bf16[4,512,128]{2,1,0:T(8,128)(2,1)S(1)} %sum.13.refs_3_), channel_id=1, source_target_pairs={{1,0},{2,3},{5,4},{6,7},{9,8},{10,11},{13,12},{14,15},{17,16},{18,... | collective-permute-start | bytes 1572872 | tf_op jit(solution)/shard_map/ppermute | solution.py:427

commit v5 on v4

--- a/solution.py
+++ b/solution.py
@@ -13,8 +13,8 @@
 ORDER = ((3, 2, 1, 0), (3, 2, 0, 1), (0, 1, 3, 2), (0, 1, 2, 3))
 SPLITS = (4, 2, 8, 8)
 STEPS = (
-    "r0", "r1", "t", "r0", "w", "r1", "r2", "r0", "l0", "i0", "r1", "k0",
-    "r2", "l1", "m0", "r2", "k1", "n0", "l2", "m1", "f", "l3", "g", "h", "n1", "p",
+    "r0", "r1", "t", "r0", "w", "r1", "r2", "r0", "l0", "k0",
+    "i0", "r1", "r2", "l1", "m0", "r2", "k1", "n0", "l2", "m1", "f", "l3", "g", "h", "n1", "p",
 )
 INWARD = ((0, 1), (3, 2))
 MIDDLE = ((1, 2), (2, 1))
@@ -241,18 +241,18 @@
     )(after)
 
 
-def lags_kernel(base, done, hours, *refs):
+def lags_kernel(base, sources, done, hours, *refs):
     hour = lax.axis_index("hour")
     here = functools.reduce(jnp.logical_or, [hour == value for value in hours])
 
     @pl.when(here)
     def _():
-        make_lags(base, done, *refs)
-
-
-def make_lags(base, done, own_ref, other_ref, receivers_ref, table_ref, after_ref, out_ref, *refs):
+        make_lags(base, sources, done, *refs)
+
+
+def make_lags(base, sources, done, own_ref, other_ref, receivers_ref, table_ref, after_ref, out_ref, *refs):
     spec_ref, cross_ref = refs[-2:]
-    count = 8
+    count = len(sources)
     _, window_count, freq_count, channels_here = receivers_ref.shape
     wide = own_ref.shape[1]
     groups = freq_count // GROUP
@@ -269,7 +269,7 @@
         square = real * real + imag * imag
         return total + square[:8] + square[8:]
 
-    total = lax.fori_loop(0, groups // 2, add, jnp.zeros((8, wide), jnp.float32), unroll=5)
+    total = lax.fori_loop(0, groups // 2, add, jnp.zeros((8, wide), jnp.float32), unroll=groups // 2)
     same = (
         lax.broadcasted_iota(jnp.int32, (wide, wide), 0) // GROUP
         == lax.broadcasted_iota(jnp.int32, (wide, wide), 1) // GROUP
@@ -284,7 +284,7 @@
             spec_ref[part, rows, :] = (value * scale).astype(jnp.bfloat16).astype(jnp.float32)
         return carry
 
-    lax.fori_loop(0, groups // 2, apply, 0, unroll=5)
+    lax.fori_loop(0, groups // 2, apply, 0, unroll=groups // 2)
 
     diagonal = [
         lax.broadcasted_iota(jnp.int32, (8, wide), 1) % GROUP
@@ -297,7 +297,7 @@
         tiles = []
         for part in range(2):
             rows = spec_ref[part, pl.ds(pl.multiple_of(group * 8, 8), 8), :]
-            for at in range(count):
+            for at in sources:
                 row = jnp.broadcast_to(rows[at : at + 1, :], (8, wide))
                 tiles += [jnp.where(mask, row, zero) for mask in diagonal]
         bins = pl.ds(pl.multiple_of(group * GROUP, GROUP), GROUP)
@@ -322,7 +322,7 @@
                 ref[pair, rows, lanes] = value[at * GROUP : (at + 1) * GROUP]
         return carry
 
-    lax.fori_loop(0, groups, cross_of, 0, unroll=25)
+    lax.fori_loop(0, groups, cross_of, 0, unroll=groups)
     transform(cross_ref, table_ref, out_ref)
 
 
@@ -339,16 +339,16 @@
             out_ref[2 * pair + 1, lags, :] = value[:, channels_here:]
 
 
-def lags_of(own, other, receivers, table, base, done, hours, after):
+def lags_of(own, other, receivers, table, base, sources, done, hours, after):
     _, window_count, freq_count, channels_here = receivers.shape
     wide = own.shape[1]
-    count = 8
-    cross = lambda sources: (sources // 2, 2 * freq_count, 2 * channels_here)
+    count = len(sources)
+    cross = lambda some: (some // 2, 2 * freq_count, 2 * channels_here)
     out_shape = [jax.ShapeDtypeStruct((done, table.shape[0], channels_here), jnp.bfloat16)]
     if done < count:
         out_shape.append(jax.ShapeDtypeStruct(cross(count - done), jnp.bfloat16))
     return pl.pallas_call(
-        functools.partial(lags_kernel, base, done, hours),
+        functools.partial(lags_kernel, base, sources, done, hours),
         in_specs=[VMEM] * 4 + [ANY],
         out_specs=[VMEM] * len(out_shape),
         out_shape=out_shape,
@@ -446,18 +446,18 @@
             table = last = lag_table(freq_count, LAGS, last)
         elif kind == "w":
             receivers = last = whiten(data, scale, last)
-        elif kind in "li":
+        elif kind in "li" or step == "k0":
             chunk = min(at, 2)
-            first, hours = SPLITS[at], (0, 1, 2, 3)
+            some, first, hours = range(8), SPLITS[at], (0, 1, 2, 3)
             if at == 0:
-                first, hours = (first, ENDS) if kind == "l" else (8, INNER)
+                some = {"l": range(first), "k": range(first, 8), "i": range(8)}[kind]
+                first, hours = len(some), INNER if kind == "i" else ENDS
             base = slot_rows * (at - chunk)
-            values = lags_of(state[chunk], moved[chunk], receivers, table, base, first, hours, last)
+            values = lags_of(state[chunk], moved[chunk], receivers, table, base, some, first, hours, last)
             last = mine[at, kind] = values[0]
-            if kind == "l":
-                cross[at] = values[-1]
-                if at < 3:
-                    inward[at, kind] = over_hour(last, INWARD)
+            cross[at] = values[-1]
+            if kind != "i" and at < 3:
+                inward[at, kind] = over_hour(last, INWARD)
         elif kind == "k":
             last = mine[at, kind] = lags_of_rest(cross[at], table, last)
             inward[at, kind] = over_hour(last, INWARD)

time: 95.8 us -> 94.7 us (0.989)
  Pallas kernels: 31 us -> 28 us
  waiting for transfers between devices: 35.7 us -> 37.8 us
    pallas_call x5 -> x6, Pallas kernels: 17.9 us -> 16 us  [lags_of(): pl.pallas_call(functools.partial(lags_kernel, base, sources, done, hours)...]
    pallas_call x2 -> x1, Pallas kernels: 2.71 us -> 1.6 us  [lags_of_rest(): pl.pallas_call(lambda cross_ref, table_ref, after_ref, out_ref: transform...]
    ppermute x12, waiting for transfers between devices: 5.64 us -> 6.73 us  [body(): over_chan = lambda value, pairs: lax.ppermute(value, 'chan', pairs)]
    ppermute x11, waiting for transfers between devices: 30.1 us -> 31.1 us  [body(): over_hour = lambda value, pairs: lax.ppermute(value, 'hour', pairs)]
  transfers between devices with their start and end apart: 23 -> 23, of which waited for: 11 -> 13; matrix products, arithmetic and copies ran while one was open for 0% -> 0% of each run, Pallas kernels for 27% -> 24%
where the time goes in v5:
time: 94.7 us; the launch traced here: 94.4 us
  waiting for transfers between devices  37.8 us (40%)
  Pallas kernels  28 us (30%)
  starting transfers between devices  28 us (30%)
    ppermute x11, waiting for transfers between devices, body(): over_hour = lambda value, pairs: lax.ppermute(value, 'hour', pairs)  31.1 us
    ppermute x11, starting transfers between devices, body(): over_hour = lambda value, pairs: lax.ppermute(value, 'hour', pairs)  18.8 us
    pallas_call x6, Pallas kernels, lags_of(): pl.pallas_call(functools.partial(lags_kernel, base, sources, done, hours)...  16 us
    ppermute x12, starting transfers between devices, body(): over_chan = lambda value, pairs: lax.ppermute(value, 'chan', pairs)  9.26 us
    ppermute x12, waiting for transfers between devices, body(): over_chan = lambda value, pairs: lax.ppermute(value, 'chan', pairs)  6.73 us
    pallas_call x1, Pallas kernels, front(): pl.pallas_call(front_kernel, in_specs=[HBM, HBM, HBM], out_specs=[VMEM] *...  4.23 us
    pallas_call x9, Pallas kernels, sum_of(): pl.pallas_call(functools.partial(sum_kernel, firsts, low), in_specs=[VMEM...  2.17 us
  transfers between devices with their start and end apart: 23, of which 13 were waited for; matrix products, arithmetic and copies ran while one was open for 0% of the time, Pallas kernels for 24%

profile of v5, /device:TPU:16, one launch (start us, length us, event | category | flops | bytes accessed | tf_op | source)
XLA Modules:
  0.0 94.4 jit_solution(9314112226210348048)
XLA Ops:
  0.0 4.2 %pick_sources.1 = (bf16[400,256]{1,0:T(8,128)(2,1)S(1)}, bf16[400,256]{1,0:T(8,128)(2,1)S(1)}, bf16[800,256]{1,0:T(8,128)(2,1)S(1)}, bf16[400,256]{1,0:T(8,128)(...) custom-call(s32[32]{0:T(128)} %sources_hbm.1, ...), custom_call_target="tpu_custom_call" | custom-call | flops 1 | bytes 1 | tf_op jit(solution)/shard_map/pick_sources/pallas_call | solution.py:142
  4.3 0.5 collective-permute-start.1
  4.9 0.9 collective-permute-done.2.refs_1_
  5.8 1.6 %collective-permute-start.4 = (bf16[400,256]{1,0:T(8,128)(2,1)S(1)}, bf16[400,256]{1,0:T(8,128)(2,1)S(1)}, u32[]{:S(2)}, u32[]{:S(2)}) collective-permute-start(bf16[400,256]{1,0:T(8,128)(2,1)S(1)} %add.9.refs_2_.refs_0_), channel_id=1, source_target_pairs={{0,8},{4,20},{8,0},{12,28},{16,24},{20,4},{24,16},{28,12},{1,9},{5... | collective-permute-start | bytes 614408 | tf_op jit(solution)/shard_map/ppermute | solution.py:426
  7.4 0.6 collective-permute-start.3
  8.0 1.9 %lag_table.1.refs_2_.refs_3_.table_ref = bf16[512,1600]{1,0:T(8,128)(2,1)S(1)} custom-call(bf16[400,256]{1,0:T(8,128)(2,1)S(1)} %add.10.after_ref.refs_0_), custom_call_target="tpu_custom_call" | custom-call | flops 1 | bytes 1 | tf_op jit(solution)/shard_map/lag_table/pallas_call | solution.py:233
  9.9 1.7 %collective-permute-done.4.refs_1_ = bf16[400,256]{1,0:T(8,128)(2,1)S(1)} collective-permute-done((bf16[400,256]{1,0:T(8,128)(2,1)S(1)}, bf16[400,256]{1,0:T(8,128)(2,1)S(1)}, u32[]{:S(2)}, u32[]{:S(2)}) %collective-permute-start.4) | collective-permute-done | bytes 204832 | tf_op jit(solution)/shard_map/ppermute | solution.py:426
  11.7 1.6 %collective-permute-start.7 = (bf16[400,256]{1,0:T(8,128)(2,1)S(1)}, bf16[400,256]{1,0:T(8,128)(2,1)S(1)}, u32[]{:S(2)}, u32[]{:S(2)}) collective-permute-start(bf16[400,256]{1,0:T(8,128)(2,1)S(1)} %add.11.after_ref.refs_0_), channel_id=1, source_target_pairs={{0,16},{4,12},{8,24},{12,4},{16,0},{20,28},{24,8},{28,20},{1,17},{... | collective-permute-start | bytes 614408 | tf_op jit(solution)/shard_map/ppermute | solution.py:426
  13.3 1.5 %whiten_receivers.1.refs_2_ = bf16[2,16,800,128]{3,2,1,0:T(8,128)(2,1)S(1)} custom-call(bf16[2,16,800,128]{3,2,1,0:T(8,128)(2,1)S(1)} %get-tuple-element.22.data_ref, f32[16,128]{1,0:T(8,128)S(1)} %get-tuple-element.21.refs_2_.scale_ref, bf16[400,256]{1,0:T(8,128)(2,1)S(1)} %add.11.after_ref.refs_0_), custom_call_target="tpu_custom_call" | custom-call | flops 1 | bytes 1 | tf_op jit(solution)/shard_map/whiten_receivers/pallas_call | solution.py:180
  14.9 0.1 add.13.refs_2_.refs_0_
  15.0 2.5 %collective-permute-done.7.refs_1_ = bf16[400,256]{1,0:T(8,128)(2,1)S(1)} collective-permute-done((bf16[400,256]{1,0:T(8,128)(2,1)S(1)}, bf16[400,256]{1,0:T(8,128)(2,1)S(1)}, u32[]{:S(2)}, u32[]{:S(2)}) %collective-permute-start.7) | collective-permute-done | bytes 204832 | tf_op jit(solution)/shard_map/ppermute | solution.py:426
  17.6 1.6 %collective-permute-start.5 = (bf16[800,256]{1,0:T(8,128)(2,1)S(1)}, bf16[800,256]{1,0:T(8,128)(2,1)S(1)}, u32[]{:S(2)}, u32[]{:S(2)}) collective-permute-start(bf16[800,256]{1,0:T(8,128)(2,1)S(1)} %add.13.refs_2_.refs_0_), channel_id=1, source_target_pairs={{0,8},{4,20},{8,0},{12,28},{16,24},{20,4},{24,16},{28,12},{1,9},{5... | collective-permute-start | bytes 1228808 | tf_op jit(solution)/shard_map/ppermute | solution.py:426
  19.2 1.3 %collective-permute-start.10 = (bf16[4,512,128]{2,1,0:T(8,128)(2,1)S(1)}, bf16[4,512,128]{2,1,0:T(8,128)(2,1)S(1)}, u32[]{:S(2)}, u32[]{:S(2)}) collective-permute-start(bf16[4,512,128]{2,1,0:T(8,128)(2,1)S(1)} %lags.6.refs_4_), channel_id=1, source_target_pairs={{0,1},{3,2},{4,5},{7,6},{8,9},{11,10},{12,13},{15,14},{16,17},{19,... | collective-permute-start | bytes 1572872 | tf_op jit(solution)/shard_map/ppermute | solution.py:427
  20.5 1.6 %collective-permute-start.6 = (bf16[400,256]{1,0:T(8,128)(2,1)S(1)}, bf16[400,256]{1,0:T(8,128)(2,1)S(1)}, u32[]{:S(2)}, u32[]{:S(2)}) collective-permute-start(bf16[400,256]{1,0:T(8,128)(2,1)S(1)} %add.12.refs_2_.refs_0_), channel_id=1, source_target_pairs={{0,16},{4,12},{8,24},{12,4},{16,0},{20,28},{24,8},{28,20},{1,17},{... | collective-permute-start | bytes 614408 | tf_op jit(solution)/shard_map/ppermute | solution.py:426
  22.1 4.3 %lags.8.refs_2_.refs_0_ = bf16[8,512,128]{2,1,0:T(8,128)(2,1)S(1)} custom-call(bf16[400,256]{1,0:T(8,128)(2,1)S(1)} %add.14.refs_0_.refs_4_, bf16[400,256]{1,0:T(8,128)(2,1)S(1)} %collective-permute-done.8.refs_1_, bf16[2,16,800,128]{3,2,1,0:T(8,128)(2,1)S(1)} %whiten_receivers.1.refs_2_, bf16[512,1600]{1,0:T(8,128)(2,1)S(1)} %lag_table.1.refs_2_.refs_3_.table_ref, ...), custom_call_target="tpu_custom_call" | custom-call | flops 1 | bytes 1 | tf_op jit(solution)/shard_map/lags/pallas_call | solution.py:350
  26.4 0.9 collective-permute-done.6.refs_1_
  27.4 0.5 collective-permute-done.5.refs_1_
  28.0 1.6 %collective-permute-start.9 = (bf16[800,256]{1,0:T(8,128)(2,1)S(1)}, bf16[800,256]{1,0:T(8,128)(2,1)S(1)}, u32[]{:S(2)}, u32[]{:S(2)}) collective-permute-start(bf16[800,256]{1,0:T(8,128)(2,1)S(1)} %add.16.refs_4_.refs_0_), channel_id=1, source_target_pairs={{0,16},{4,12},{8,24},{12,4},{16,0},{20,28},{24,8},{28,20},{1,17},{... | collective-permute-start | bytes 1228808 | tf_op jit(solution)/shard_map/ppermute | solution.py:426
  29.5 1.3 %collective-permute-start.13 = (bf16[4,512,128]{2,1,0:T(8,128)(2,1)S(1)}, bf16[4,512,128]{2,1,0:T(8,128)(2,1)S(1)}, u32[]{:S(2)}, u32[]{:S(2)}) collective-permute-start(bf16[4,512,128]{2,1,0:T(8,128)(2,1)S(1)} %lags.7.refs_4_), channel_id=1, source_target_pairs={{0,1},{3,2},{4,5},{7,6},{8,9},{11,10},{12,13},{15,14},{16,17},{19,... | collective-permute-start | bytes 1572872 | tf_op jit(solution)/shard_map/ppermute | solution.py:427
  30.8 0.2 collective-permute-done.11.refs_1_
  31.0 2.9 %lags.9 = (bf16[2,512,128]{2,1,0:T(8,128)(2,1)S(1)}, bf16[3,1600,256]{2,1,0:T(8,128)(2,1)S(1)}) custom-call(bf16[400,256]{1,0:T(8,128)(2,1)S(1)} %add.15.refs_2_.refs_0_, bf16[400,256]{1,0:T(8,128)(2,1)S(1)} %collective-permute-done.11.refs_1_, bf16[2,16,800,128]{3,2,1,0:T(8,128)(2,1)S(1)} %whiten_receivers.1.refs_2_, ...), custom_call_target="tpu_custom_call" | custom-call | flops 1 | bytes 1 | tf_op jit(solution)/shard_map/lags/pallas_call | solution.py:350
  33.9 3.5 %collective-permute-done.10.refs_1_ = bf16[4,512,128]{2,1,0:T(8,128)(2,1)S(1)} collective-permute-done((bf16[4,512,128]{2,1,0:T(8,128)(2,1)S(1)}, bf16[4,512,128]{2,1,0:T(8,128)(2,1)S(1)}, u32[]{:S(2)}, u32[]{:S(2)}) %collective-permute-start.10) | collective-permute-done | bytes 524320 | tf_op jit(solution)/shard_map/ppermute | solution.py:427
  37.4 0.1 sum.9.refs_2_
  37.5 1.9 %collective-permute-start.14 = (bf16[4,512,128]{2,1,0:T(8,128)(2,1)S(1)}, bf16[4,512,128]{2,1,0:T(8,128)(2,1)S(1)}, u32[]{:S(2)}, u32[]{:S(2)}) collective-permute-start(bf16[4,512,128]{2,1,0:T(8,128)(2,1)S(1)} %sum.9.refs_2_), channel_id=1, source_target_pairs={{1,2},{2,1},{5,6},{6,5},{9,10},{10,9},{13,14},{14,13},{17,18},{18,... | collective-permute-start | bytes 1572872 | tf_op jit(solution)/shard_map/ppermute | solution.py:427
  39.6 1.3 %collective-permute-start.15 = (bf16[2,512,128]{2,1,0:T(8,128)(2,1)S(1)}, bf16[2,512,128]{2,1,0:T(8,128)(2,1)S(1)}, u32[]{:S(2)}, u32[]{:S(2)}) collective-permute-start(bf16[2,512,128]{2,1,0:T(8,128)(2,1)S(1)} %get-tuple-element.23.refs_2_.refs_0_), channel_id=1, source_target_pairs={{0,1},{3,2},{4,5},{7,6},{8,9},{11,10},{12,13},{15,14},{16,17},{19,... | collective-permute-start | bytes 786440 | tf_op jit(solution)/shard_map/ppermute | solution.py:427
  40.9 1.6 %lags_rest.1.refs_2_.refs_0_ = bf16[6,512,128]{2,1,0:T(8,128)(2,1)S(1)} custom-call(bf16[3,1600,256]{2,1,0:T(8,128)(2,1)S(1)} %get-tuple-element.24.cross_ref, bf16[512,1600]{1,0:T(8,128)(2,1)S(1)} %lag_table.1.refs_2_.refs_3_.table_ref, bf16[800,256]{1,0:T(8,128)(2,1)S(1)} %add.17.after_ref.refs_0_), custom_call_target="tpu_custom_call" | custom-call | flops 1 | bytes 1 | tf_op jit(solution)/shard_map/lags_rest/pallas_call | solution.py:367
  42.5 1.3 %collective-permute-start.20 = (bf16[6,512,128]{2,1,0:T(8,128)(2,1)S(1)}, bf16[6,512,128]{2,1,0:T(8,128)(2,1)S(1)}, u32[]{:S(2)}, u32[]{:S(2)}) collective-permute-start(bf16[6,512,128]{2,1,0:T(8,128)(2,1)S(1)} %lags_rest.1.refs_2_.refs_0_), channel_id=1, source_target_pairs={{0,1},{3,2},{4,5},{7,6},{8,9},{11,10},{12,13},{15,14},{16,17},{19,... | collective-permute-start | bytes 2359304 | tf_op jit(solution)/shard_map/ppermute | solution.py:427
  43.8 4.8 %collective-permute-done.13.refs_1_ = bf16[4,512,128]{2,1,0:T(8,128)(2,1)S(1)} collective-permute-done((bf16[4,512,128]{2,1,0:T(8,128)(2,1)S(1)}, bf16[4,512,128]{2,1,0:T(8,128)(2,1)S(1)}, u32[]{:S(2)}, u32[]{:S(2)}) %collective-permute-start.13) | collective-permute-done | bytes 524320 | tf_op jit(solution)/shard_map/ppermute | solution.py:427
  48.6 0.1 sum.10.refs_4_
  48.7 1.9 %collective-permute-start.18 = (bf16[4,512,128]{2,1,0:T(8,128)(2,1)S(1)}, bf16[4,512,128]{2,1,0:T(8,128)(2,1)S(1)}, u32[]{:S(2)}, u32[]{:S(2)}) collective-permute-start(bf16[4,512,128]{2,1,0:T(8,128)(2,1)S(1)} %sum.10.refs_4_), channel_id=1, source_target_pairs={{1,2},{2,1},{5,6},{6,5},{9,10},{10,9},{13,14},{14,13},{17,18},{18,... | collective-permute-start | bytes 1572872 | tf_op jit(solution)/shard_map/ppermute | solution.py:427
  50.7 4.5 %lags.10.refs_2_.refs_0_ = bf16[8,512,128]{2,1,0:T(8,128)(2,1)S(1)} custom-call(bf16[800,256]{1,0:T(8,128)(2,1)S(1)} %add.17.after_ref.refs_0_, bf16[800,256]{1,0:T(8,128)(2,1)S(1)} %collective-permute-done.12.refs_1_, bf16[2,16,800,128]{3,2,1,0:T(8,128)(2,1)S(1)} %whiten_receivers.1.refs_2_, bf16[512,1600]{1,0:T(8,128)(2,1)S(1)} %lag_table.1.refs_2_.refs_3_.table_ref, ...), custom_call_target="tpu_custom_call" | custom-call | flops 1 | bytes 1 | tf_op jit(solution)/shard_map/lags/pallas_call | solution.py:350
  55.3 0.1 sum.12.refs_4_
  55.4 1.3 %collective-permute-start.16 = (bf16[4,512,128]{2,1,0:T(8,128)(2,1)S(1)}, bf16[4,512,128]{2,1,0:T(8,128)(2,1)S(1)}, u32[]{:S(2)}, u32[]{:S(2)}) collective-permute-start(bf16[4,512,128]{2,1,0:T(8,128)(2,1)S(1)} %sum.12.refs_4_), channel_id=1, source_target_pairs={{1,0},{2,3},{5,4},{6,7},{9,8},{10,11},{13,12},{14,15},{17,16},{18,... | collective-permute-start | bytes 1572872 | tf_op jit(solution)/shard_map/ppermute | solution.py:427
  56.8 3.9 %collective-permute-start.17 = (bf16[2,512,128]{2,1,0:T(8,128)(2,1)S(1)}, bf16[2,512,128]{2,1,0:T(8,128)(2,1)S(1)}, u32[]{:S(2)}, u32[]{:S(2)}) collective-permute-start(bf16[2,512,128]{2,1,0:T(8,128)(2,1)S(1)} %sum.11.refs_2_), channel_id=1, source_target_pairs={{1,2},{2,1},{5,6},{6,5},{9,10},{10,9},{13,14},{14,13},{17,18},{18,... | collective-permute-start | bytes 786440 | tf_op jit(solution)/shard_map/ppermute | solution.py:427
  60.7 1.3 %collective-permute-start.22 = (bf16[8,512,128]{2,1,0:T(8,128)(2,1)S(1)}, bf16[8,512,128]{2,1,0:T(8,128)(2,1)S(1)}, u32[]{:S(2)}, u32[]{:S(2)}) collective-permute-start(bf16[8,512,128]{2,1,0:T(8,128)(2,1)S(1)} %lags.10.refs_2_.refs_0_), channel_id=1, source_target_pairs={{0,1},{3,2},{4,5},{7,6},{8,9},{11,10},{12,13},{15,14},{16,17},{19,... | collective-permute-start | bytes 3145736 | tf_op jit(solution)/shard_map/ppermute | solution.py:427
  62.0 4.3 %lags.11.refs_2_.refs_0_ = bf16[8,512,128]{2,1,0:T(8,128)(2,1)S(1)} custom-call(bf16[800,256]{1,0:T(8,128)(2,1)S(1)} %add.17.after_ref.refs_0_, bf16[800,256]{1,0:T(8,128)(2,1)S(1)} %collective-permute-done.12.refs_1_, bf16[2,16,800,128]{3,2,1,0:T(8,128)(2,1)S(1)} %whiten_receivers.1.refs_2_, bf16[512,1600]{1,0:T(8,128)(2,1)S(1)} %lag_table.1.refs_2_.refs_3_.table_ref, ...), custom_call_target="tpu_custom_call" | custom-call | flops 1 | bytes 1 | tf_op jit(solution)/shard_map/lags/pallas_call | solution.py:350
  66.3 0.1 sum.13.refs_3_
  66.4 2.9 %collective-permute-done.17.refs_2_ = bf16[2,512,128]{2,1,0:T(8,128)(2,1)S(1)} collective-permute-done((bf16[2,512,128]{2,1,0:T(8,128)(2,1)S(1)}, bf16[2,512,128]{2,1,0:T(8,128)(2,1)S(1)}, u32[]{:S(2)}, u32[]{:S(2)}) %collective-permute-start.17) | collective-permute-done | bytes 262176 | tf_op jit(solution)/shard_map/ppermute | solution.py:427
  69.3 0.1 sum.14.refs_2_.refs_0_
  69.5 1.6 %collective-permute-done.20.refs_1_ = bf16[6,512,128]{2,1,0:T(8,128)(2,1)S(1)} collective-permute-done((bf16[6,512,128]{2,1,0:T(8,128)(2,1)S(1)}, bf16[6,512,128]{2,1,0:T(8,128)(2,1)S(1)}, u32[]{:S(2)}, u32[]{:S(2)}) %collective-permute-start.20) | collective-permute-done | bytes 786464 | tf_op jit(solution)/shard_map/ppermute | solution.py:427
  71.1 0.2 sum.15.refs_4_
  71.3 1.9 %collective-permute-start.21 = (bf16[6,512,128]{2,1,0:T(8,128)(2,1)S(1)}, bf16[6,512,128]{2,1,0:T(8,128)(2,1)S(1)}, u32[]{:S(2)}, u32[]{:S(2)}) collective-permute-start(bf16[6,512,128]{2,1,0:T(8,128)(2,1)S(1)} %sum.15.refs_4_), channel_id=1, source_target_pairs={{1,2},{2,1},{5,6},{6,5},{9,10},{10,9},{13,14},{14,13},{17,18},{18,... | collective-permute-start | bytes 2359304 | tf_op jit(solution)/shard_map/ppermute | solution.py:427
  73.2 1.3 %collective-permute-start.19 = (bf16[4,512,128]{2,1,0:T(8,128)(2,1)S(1)}, bf16[4,512,128]{2,1,0:T(8,128)(2,1)S(1)}, u32[]{:S(2)}, u32[]{:S(2)}) collective-permute-start(bf16[4,512,128]{2,1,0:T(8,128)(2,1)S(1)} %sum.13.refs_3_), channel_id=1, source_target_pairs={{1,0},{2,3},{5,4},{6,7},{9,8},{10,11},{13,12},{14,15},{17,16},{18,... | collective-permute-start | bytes 1572872 | tf_op jit(solution)/shard_map/ppermute | solution.py:427
  74.6 10.8 %collective-permute-done.19.refs_2_ = bf16[4,512,128]{2,1,0:T(8,128)(2,1)S(1)} collective-permute-done((bf16[4,512,128]{2,1,0:T(8,128)(2,1)S(1)}, bf16[4,512,128]{2,1,0:T(8,128)(2,1)S(1)}, u32[]{:S(2)}, u32[]{:S(2)}) %collective-permute-start.19) | collective-permute-done | bytes 524320 | tf_op jit(solution)/shard_map/ppermute | solution.py:427
  85.4 6.5 %collective-permute-done.21.refs_3_ = bf16[6,512,128]{2,1,0:T(8,128)(2,1)S(1)} collective-permute-done((bf16[6,512,128]{2,1,0:T(8,128)(2,1)S(1)}, bf16[6,512,128]{2,1,0:T(8,128)(2,1)S(1)}, u32[]{:S(2)}, u32[]{:S(2)}) %collective-permute-start.21) | collective-permute-done | bytes 786464 | tf_op jit(solution)/shard_map/ppermute | solution.py:427
  91.9 0.2 sum.16.refs_0_.refs_2_
  92.1 1.0 %collective-permute-done.22.refs_1_ = bf16[8,512,128]{2,1,0:T(8,128)(2,1)S(1)} collective-permute-done((bf16[8,512,128]{2,1,0:T(8,128)(2,1)S(1)}, bf16[8,512,128]{2,1,0:T(8,128)(2,1)S(1)}, u32[]{:S(2)}, u32[]{:S(2)}) %collective-permute-start.22) | collective-permute-done | bytes 1048608 | tf_op jit(solution)/shard_map/ppermute | solution.py:427
  93.1 1.0 %sum.17 = bf16[8,512,128]{2,1,0:T(8,128)(2,1)} custom-call(f32[8,512,128]{2,1,0:T(8,128)S(1)} %sum.16.refs_0_.refs_2_, bf16[8,512,128]{2,1,0:T(8,128)(2,1)S(1)} %collective-permute-done.22.refs_1_, f32[8,512,128]{2,1,0:T(8,128)S(1)} %sum.16.refs_0_.refs_2_), custom_call_target="tpu_custom_call" | custom-call | flops 1 | bytes 1 | tf_op jit(solution)/shard_map/sum/pallas_call | solution.py:401
  (27 shorter events, 0.9 us)
Async XLA Ops:
  4.2 1.5 %collective-permute-start.2 = (bf16[400,256]{1,0:T(8,128)(2,1)S(1)}, bf16[400,256]{1,0:T(8,128)(2,1)S(1)}, u32[]{:S(2)}, u32[]{:S(2)}) collective-permute-start(bf16[400,256]{1,0:T(8,128)(2,1)S(1)} %get-tuple-element.20), channel_id=1, source_target_pairs={{0,4},{4,0},{8,12},{12,8},{16,20},{20,16},{24,28},{28,24},{1,5},{5... | collective-permute-start | bytes 614408 | tf_op jit(solution)/shard_map/ppermute | solution.py:426
  4.3 3.1 %collective-permute-start.1 = (bf16[400,256]{1,0:T(8,128)(2,1)S(1)}, bf16[400,256]{1,0:T(8,128)(2,1)S(1)}, u32[]{:S(2)}, u32[]{:S(2)}) collective-permute-start(bf16[400,256]{1,0:T(8,128)(2,1)S(1)} %get-tuple-element.18), channel_id=1, source_target_pairs={{0,4},{4,0},{8,12},{12,8},{16,20},{20,16},{24,28},{28,24},{1,5},{5... | collective-permute-start | bytes 614408 | tf_op jit(solution)/shard_map/ppermute | solution.py:426
  4.8 10.0 %collective-permute-start = (bf16[800,256]{1,0:T(8,128)(2,1)S(1)}, bf16[800,256]{1,0:T(8,128)(2,1)S(1)}, u32[]{:S(2)}, u32[]{:S(2)}) collective-permute-start(bf16[800,256]{1,0:T(8,128)(2,1)S(1)} %get-tuple-element.16), channel_id=1, source_target_pairs={{0,4},{4,0},{8,12},{12,8},{16,20},{20,16},{24,28},{28,24},{1,5},{5... | collective-permute-start | bytes 1228808 | tf_op jit(solution)/shard_map/ppermute | solution.py:426
  5.8 5.8 %collective-permute-start.4 = (bf16[400,256]{1,0:T(8,128)(2,1)S(1)}, bf16[400,256]{1,0:T(8,128)(2,1)S(1)}, u32[]{:S(2)}, u32[]{:S(2)}) collective-permute-start(bf16[400,256]{1,0:T(8,128)(2,1)S(1)} %add.9.refs_2_.refs_0_), channel_id=1, source_target_pairs={{0,8},{4,20},{8,0},{12,28},{16,24},{20,4},{24,16},{28,12},{1,9},{5... | collective-permute-start | bytes 614408 | tf_op jit(solution)/shard_map/ppermute | solution.py:426
  7.4 7.4 %collective-permute-start.3 = (bf16[400,256]{1,0:T(8,128)(2,1)S(1)}, bf16[400,256]{1,0:T(8,128)(2,1)S(1)}, u32[]{:S(2)}, u32[]{:S(2)}) collective-permute-start(bf16[400,256]{1,0:T(8,128)(2,1)S(1)} %add.10.after_ref.refs_0_), channel_id=1, source_target_pairs={{0,8},{4,20},{8,0},{12,28},{16,24},{20,4},{24,16},{28,12},{1,9},{5... | collective-permute-start | bytes 614408 | tf_op jit(solution)/shard_map/ppermute | solution.py:426
  11.7 5.8 %collective-permute-start.7 = (bf16[400,256]{1,0:T(8,128)(2,1)S(1)}, bf16[400,256]{1,0:T(8,128)(2,1)S(1)}, u32[]{:S(2)}, u32[]{:S(2)}) collective-permute-start(bf16[400,256]{1,0:T(8,128)(2,1)S(1)} %add.11.after_ref.refs_0_), channel_id=1, source_target_pairs={{0,16},{4,12},{8,24},{12,4},{16,0},{20,28},{24,8},{28,20},{1,17},{... | collective-permute-start | bytes 614408 | tf_op jit(solution)/shard_map/ppermute | solution.py:426
  17.6 1.6 %collective-permute-start.8 = (bf16[400,256]{1,0:T(8,128)(2,1)S(1)}, bf16[400,256]{1,0:T(8,128)(2,1)S(1)}, u32[]{:S(2)}, u32[]{:S(2)}) collective-permute-start(bf16[400,256]{1,0:T(8,128)(2,1)S(1)} %add.14.refs_0_.refs_4_), channel_id=1, source_target_pairs={{0,4},{4,0},{8,12},{12,8},{16,20},{20,16},{24,28},{28,24},{1,5},{5... | collective-permute-start | bytes 614408 | tf_op jit(solution)/shard_map/ppermute | solution.py:426
  17.6 10.2 %collective-permute-start.5 = (bf16[800,256]{1,0:T(8,128)(2,1)S(1)}, bf16[800,256]{1,0:T(8,128)(2,1)S(1)}, u32[]{:S(2)}, u32[]{:S(2)}) collective-permute-start(bf16[800,256]{1,0:T(8,128)(2,1)S(1)} %add.13.refs_2_.refs_0_), channel_id=1, source_target_pairs={{0,8},{4,20},{8,0},{12,28},{16,24},{20,4},{24,16},{28,12},{1,9},{5... | collective-permute-start | bytes 1228808 | tf_op jit(solution)/shard_map/ppermute | solution.py:426
  19.2 18.2 %collective-permute-start.10 = (bf16[4,512,128]{2,1,0:T(8,128)(2,1)S(1)}, bf16[4,512,128]{2,1,0:T(8,128)(2,1)S(1)}, u32[]{:S(2)}, u32[]{:S(2)}) collective-permute-start(bf16[4,512,128]{2,1,0:T(8,128)(2,1)S(1)} %lags.6.refs_4_), channel_id=1, source_target_pairs={{0,1},{3,2},{4,5},{7,6},{8,9},{11,10},{12,13},{15,14},{16,17},{19,... | collective-permute-start | bytes 1572872 | tf_op jit(solution)/shard_map/ppermute | solution.py:427
  20.5 6.8 %collective-permute-start.6 = (bf16[400,256]{1,0:T(8,128)(2,1)S(1)}, bf16[400,256]{1,0:T(8,128)(2,1)S(1)}, u32[]{:S(2)}, u32[]{:S(2)}) collective-permute-start(bf16[400,256]{1,0:T(8,128)(2,1)S(1)} %add.12.refs_2_.refs_0_), channel_id=1, source_target_pairs={{0,16},{4,12},{8,24},{12,4},{16,0},{20,28},{24,8},{28,20},{1,17},{... | collective-permute-start | bytes 614408 | tf_op jit(solution)/shard_map/ppermute | solution.py:426
  28.0 11.5 %collective-permute-start.9 = (bf16[800,256]{1,0:T(8,128)(2,1)S(1)}, bf16[800,256]{1,0:T(8,128)(2,1)S(1)}, u32[]{:S(2)}, u32[]{:S(2)}) collective-permute-start(bf16[800,256]{1,0:T(8,128)(2,1)S(1)} %add.16.refs_4_.refs_0_), channel_id=1, source_target_pairs={{0,16},{4,12},{8,24},{12,4},{16,0},{20,28},{24,8},{28,20},{1,17},{... | collective-permute-start | bytes 1228808 | tf_op jit(solution)/shard_map/ppermute | solution.py:426
  29.5 1.5 %collective-permute-start.11 = (bf16[400,256]{1,0:T(8,128)(2,1)S(1)}, bf16[400,256]{1,0:T(8,128)(2,1)S(1)}, u32[]{:S(2)}, u32[]{:S(2)}) collective-permute-start(bf16[400,256]{1,0:T(8,128)(2,1)S(1)} %add.15.refs_2_.refs_0_), channel_id=1, source_target_pairs={{0,4},{4,0},{8,12},{12,8},{16,20},{20,16},{24,28},{28,24},{1,5},{5... | collective-permute-start | bytes 614408 | tf_op jit(solution)/shard_map/ppermute | solution.py:426
  29.5 19.1 %collective-permute-start.13 = (bf16[4,512,128]{2,1,0:T(8,128)(2,1)S(1)}, bf16[4,512,128]{2,1,0:T(8,128)(2,1)S(1)}, u32[]{:S(2)}, u32[]{:S(2)}) collective-permute-start(bf16[4,512,128]{2,1,0:T(8,128)(2,1)S(1)} %lags.7.refs_4_), channel_id=1, source_target_pairs={{0,1},{3,2},{4,5},{7,6},{8,9},{11,10},{12,13},{15,14},{16,17},{19,... | collective-permute-start | bytes 1572872 | tf_op jit(solution)/shard_map/ppermute | solution.py:427
  37.5 17.8 %collective-permute-start.14 = (bf16[4,512,128]{2,1,0:T(8,128)(2,1)S(1)}, bf16[4,512,128]{2,1,0:T(8,128)(2,1)S(1)}, u32[]{:S(2)}, u32[]{:S(2)}) collective-permute-start(bf16[4,512,128]{2,1,0:T(8,128)(2,1)S(1)} %sum.9.refs_2_), channel_id=1, source_target_pairs={{1,2},{2,1},{5,6},{6,5},{9,10},{10,9},{13,14},{14,13},{17,18},{18,... | collective-permute-start | bytes 1572872 | tf_op jit(solution)/shard_map/ppermute | solution.py:427
  39.5 11.1 %collective-permute-start.12 = (bf16[800,256]{1,0:T(8,128)(2,1)S(1)}, bf16[800,256]{1,0:T(8,128)(2,1)S(1)}, u32[]{:S(2)}, u32[]{:S(2)}) collective-permute-start(bf16[800,256]{1,0:T(8,128)(2,1)S(1)} %add.17.after_ref.refs_0_), channel_id=1, source_target_pairs={{0,4},{4,0},{8,12},{12,8},{16,20},{20,16},{24,28},{28,24},{1,5},{5... | collective-permute-start | bytes 1228808 | tf_op jit(solution)/shard_map/ppermute | solution.py:426
  39.6 15.6 %collective-permute-start.15 = (bf16[2,512,128]{2,1,0:T(8,128)(2,1)S(1)}, bf16[2,512,128]{2,1,0:T(8,128)(2,1)S(1)}, u32[]{:S(2)}, u32[]{:S(2)}) collective-permute-start(bf16[2,512,128]{2,1,0:T(8,128)(2,1)S(1)} %get-tuple-element.23.refs_2_.refs_0_), channel_id=1, source_target_pairs={{0,1},{3,2},{4,5},{7,6},{8,9},{11,10},{12,13},{15,14},{16,17},{19,... | collective-permute-start | bytes 786440 | tf_op jit(solution)/shard_map/ppermute | solution.py:427
  42.5 28.5 %collective-permute-start.20 = (bf16[6,512,128]{2,1,0:T(8,128)(2,1)S(1)}, bf16[6,512,128]{2,1,0:T(8,128)(2,1)S(1)}, u32[]{:S(2)}, u32[]{:S(2)}) collective-permute-start(bf16[6,512,128]{2,1,0:T(8,128)(2,1)S(1)} %lags_rest.1.refs_2_.refs_0_), channel_id=1, source_target_pairs={{0,1},{3,2},{4,5},{7,6},{8,9},{11,10},{12,13},{15,14},{16,17},{19,... | collective-permute-start | bytes 2359304 | tf_op jit(solution)/shard_map/ppermute | solution.py:427
  48.7 17.6 %collective-permute-start.18 = (bf16[4,512,128]{2,1,0:T(8,128)(2,1)S(1)}, bf16[4,512,128]{2,1,0:T(8,128)(2,1)S(1)}, u32[]{:S(2)}, u32[]{:S(2)}) collective-permute-start(bf16[4,512,128]{2,1,0:T(8,128)(2,1)S(1)} %sum.10.refs_4_), channel_id=1, source_target_pairs={{1,2},{2,1},{5,6},{6,5},{9,10},{10,9},{13,14},{14,13},{17,18},{18,... | collective-permute-start | bytes 1572872 | tf_op jit(solution)/shard_map/ppermute | solution.py:427
  55.4 13.9 %collective-permute-start.16 = (bf16[4,512,128]{2,1,0:T(8,128)(2,1)S(1)}, bf16[4,512,128]{2,1,0:T(8,128)(2,1)S(1)}, u32[]{:S(2)}, u32[]{:S(2)}) collective-permute-start(bf16[4,512,128]{2,1,0:T(8,128)(2,1)S(1)} %sum.12.refs_4_), channel_id=1, source_target_pairs={{1,0},{2,3},{5,4},{6,7},{9,8},{10,11},{13,12},{14,15},{17,16},{18,... | collective-permute-start | bytes 1572872 | tf_op jit(solution)/shard_map/ppermute | solution.py:427
  56.8 12.6 %collective-permute-start.17 = (bf16[2,512,128]{2,1,0:T(8,128)(2,1)S(1)}, bf16[2,512,128]{2,1,0:T(8,128)(2,1)S(1)}, u32[]{:S(2)}, u32[]{:S(2)}) collective-permute-start(bf16[2,512,128]{2,1,0:T(8,128)(2,1)S(1)} %sum.11.refs_2_), channel_id=1, source_target_pairs={{1,2},{2,1},{5,6},{6,5},{9,10},{10,9},{13,14},{14,13},{17,18},{18,... | collective-permute-start | bytes 786440 | tf_op jit(solution)/shard_map/ppermute | solution.py:427
  60.7 32.4 %collective-permute-start.22 = (bf16[8,512,128]{2,1,0:T(8,128)(2,1)S(1)}, bf16[8,512,128]{2,1,0:T(8,128)(2,1)S(1)}, u32[]{:S(2)}, u32[]{:S(2)}) collective-permute-start(bf16[8,512,128]{2,1,0:T(8,128)(2,1)S(1)} %lags.10.refs_2_.refs_0_), channel_id=1, source_target_pairs={{0,1},{3,2},{4,5},{7,6},{8,9},{11,10},{12,13},{15,14},{16,17},{19,... | collective-permute-start | bytes 3145736 | tf_op jit(solution)/shard_map/ppermute | solution.py:427
  71.3 20.6 %collective-permute-start.21 = (bf16[6,512,128]{2,1,0:T(8,128)(2,1)S(1)}, bf16[6,512,128]{2,1,0:T(8,128)(2,1)S(1)}, u32[]{:S(2)}, u32[]{:S(2)}) collective-permute-start(bf16[6,512,128]{2,1,0:T(8,128)(2,1)S(1)} %sum.15.refs_4_), channel_id=1, source_target_pairs={{1,2},{2,1},{5,6},{6,5},{9,10},{10,9},{13,14},{14,13},{17,18},{18,... | collective-permute-start | bytes 2359304 | tf_op jit(solution)/shard_map/ppermute | solution.py:427
  73.2 12.2 %collective-permute-start.19 = (bf16[4,512,128]{2,1,0:T(8,128)(2,1)S(1)}, bf16[4,512,128]{2,1,0:T(8,128)(2,1)S(1)}, u32[]{:S(2)}, u32[]{:S(2)}) collective-permute-start(bf16[4,512,128]{2,1,0:T(8,128)(2,1)S(1)} %sum.13.refs_3_), channel_id=1, source_target_pairs={{1,0},{2,3},{5,4},{6,7},{9,8},{10,11},{13,12},{14,15},{17,16},{18,... | collective-permute-start | bytes 1572872 | tf_op jit(solution)/shard_map/ppermute | solution.py:427

commit v6 on v5

--- a/solution.py
+++ b/solution.py
@@ -13,7 +13,7 @@
 ORDER = ((3, 2, 1, 0), (3, 2, 0, 1), (0, 1, 3, 2), (0, 1, 2, 3))
 SPLITS = (4, 2, 8, 8)
 STEPS = (
-    "r0", "r1", "t", "r0", "w", "r1", "r2", "r0", "l0", "k0",
+    "r0", "q", "r0", "w", "t", "r0", "r1", "r2", "l0", "r1", "k0",
     "i0", "r1", "r2", "l1", "m0", "r2", "k1", "n0", "l2", "m1", "f", "l3", "g", "h", "n1", "p",
 )
 INWARD = ((0, 1), (3, 2))
@@ -43,15 +43,52 @@
     ]
 
 
+def pick_share(data_ref, onehot, usable, windows, bins, own_refs, other_refs, total=None):
+    channels_here = data_ref.shape[3]
+    narrow = usable.shape[1] // 2
+    per_slot = onehot.shape[0] // len(own_refs)
+    lanes = slice(windows[0] * GROUP, windows[1] * GROUP)
+    usable_here = jnp.concatenate([usable[:, lanes]] * 2, 1)
+    even = (lax.axis_index("chan") % 2) == 0
+    for pair in range(bins[0] // (2 * GROUP), bins[1] // (2 * GROUP)):
+        picked = []
+        for part in range(2):
+            both = []
+            for group in (2 * pair, 2 * pair + 1):
+                columns = data_ref[part, windows[0] : windows[1], group * GROUP : (group + 1) * GROUP, :]
+                if total is not None:
+                    value = columns.astype(jnp.float32)
+                    square = value * value
+                    total = total + (square[:, :8] + square[:, 8:])
+                both.append(columns.reshape(narrow, channels_here))
+            picked.append(
+                lax.dot_general(
+                    onehot,
+                    jnp.concatenate(both, 0),
+                    (((1,), (1,)), ((), ())),
+                    preferred_element_type=jnp.float32,
+                )
+                * usable_here
+            )
+        for refs, value in (
+            (own_refs, jnp.where(even, picked[0], picked[1])),
+            (other_refs, jnp.where(even, picked[1], picked[0])),
+        ):
+            for at, (ref, base) in enumerate(refs):
+                rows = slice(at * per_slot, (at + 1) * per_slot)
+                both = jnp.concatenate([value[rows, :narrow], value[rows, narrow:]], 0)
+                ref[base + pair * 16 : base + pair * 16 + 16, lanes] = both.astype(jnp.bfloat16)
+    return total
+
+
 def front_kernel(
     sources_hbm, spectra_hbm, quality_hbm,
-    own_first_ref, own_second_ref, own_rest_ref, other_first_ref, other_second_ref, other_rest_ref,
-    scale_ref, data_ref,
-    sources_ref, quality_ref, sems, small_sems,
+    own_ref, other_ref, data_ref, onehot_ref, usable_ref, quality_ref,
+    sources_ref, flags_ref, sems, small_sems,
 ):
     small = [
         pltpu.make_async_copy(sources_hbm, sources_ref, small_sems.at[0]),
-        pltpu.make_async_copy(quality_hbm, quality_ref, small_sems.at[1]),
+        pltpu.make_async_copy(quality_hbm, flags_ref, small_sems.at[1]),
     ]
     _, window_count, freq_count, channels_here = data_ref.shape
     large = []
@@ -65,7 +102,6 @@
     wide = window_count * GROUP
     chan = lax.axis_index("chan")
     hour = lax.axis_index("hour")
-    even = (chan % 2) == 0
     for copy in small:
         copy.wait()
     row = lax.broadcasted_iota(jnp.int32, (source_count, channels_here), 0)
@@ -75,10 +111,13 @@
         first = quarter_of(hour, slot) * per_slot
         for at in range(per_slot):
             wanted = jnp.where(row == slot * per_slot + at, sources_ref[first + at], wanted)
-    onehot = (wanted - chan * channels_here == lane).astype(jnp.float32).astype(jnp.bfloat16)
-    quality = quality_ref[...].astype(jnp.float32)
+    onehot = (wanted - chan * channels_here == lane).astype(jnp.float32)
+    quality = flags_ref[...].astype(jnp.float32)
     usable = lax.dot_general(
-        onehot, quality.astype(jnp.bfloat16), (((1,), (1,)), ((), ())), preferred_element_type=jnp.float32
+        onehot.astype(jnp.bfloat16),
+        quality.astype(jnp.bfloat16),
+        (((1,), (1,)), ((), ())),
+        preferred_element_type=jnp.float32,
     )
     spread = (
         lax.broadcasted_iota(jnp.int32, (window_count, wide), 1) // GROUP
@@ -89,48 +128,13 @@
         spread.astype(jnp.float32).astype(jnp.bfloat16),
         preferred_element_type=jnp.float32,
     )
-    narrow = wide // 2
-    totals = {}
+    onehot_ref[...] = onehot
+    usable_ref[...] = usable
+    quality_ref[...] = quality
+    onehot = onehot[:per_slot].astype(jnp.bfloat16)
     for copy, (windows, bins) in zip(large, shares(window_count, freq_count)):
         copy.wait()
-        lanes = slice(windows[0] * GROUP, windows[1] * GROUP)
-        usable_here = jnp.concatenate([usable[:, lanes]] * 2, 1)
-        total = totals.get(windows, jnp.zeros((windows[1] - windows[0], 8, channels_here), jnp.float32))
-        for pair in range(bins[0] // (2 * GROUP), bins[1] // (2 * GROUP)):
-            picked = []
-            for part in range(2):
-                both = []
-                for group in (2 * pair, 2 * pair + 1):
-                    columns = data_ref[
-                        part, windows[0] : windows[1], group * GROUP : (group + 1) * GROUP, :
-                    ]
-                    value = columns.astype(jnp.float32)
-                    square = value * value
-                    total = total + (square[:, :8] + square[:, 8:])
-                    both.append(columns.reshape(narrow, channels_here))
-                picked.append(
-                    lax.dot_general(
-                        onehot,
-                        jnp.concatenate(both, 0),
-                        (((1,), (1,)), ((), ())),
-                        preferred_element_type=jnp.float32,
-                    )
-                    * usable_here
-                )
-            own = jnp.where(even, picked[0], picked[1])
-            other = jnp.where(even, picked[1], picked[0])
-            for value, first_ref, second_ref, rest_ref in (
-                (own, own_first_ref, own_second_ref, own_rest_ref),
-                (other, other_first_ref, other_second_ref, other_rest_ref),
-            ):
-                for slot, ref in enumerate((first_ref, second_ref, rest_ref, rest_ref)):
-                    rows = slice(slot * per_slot, (slot + 1) * per_slot)
-                    at = pair * 16 + max(slot - 2, 0) * freq_count // GROUP * per_slot
-                    both = jnp.concatenate([value[rows, :narrow], value[rows, narrow:]], 0)
-                    ref[at : at + 16, lanes] = both.astype(jnp.bfloat16)
-        totals[windows] = total
-    power = jnp.concatenate([jnp.sum(total, axis=1) for total in totals.values()], 0) / freq_count
-    scale_ref[...] = lax.rsqrt(power + 1e-06) * quality
+        pick_share(data_ref, onehot, usable[:per_slot], windows, bins, [(own_ref, 0)], [(other_ref, 0)])
 
 
 def front(spectra, quality, sources):
@@ -138,15 +142,17 @@
     rows = freq_count // GROUP * sources.shape[0] // 4
     wide = window_count * GROUP
     steps = len(shares(window_count, freq_count))
-    shape = lambda count: jax.ShapeDtypeStruct((count * rows, wide), jnp.bfloat16)
     return pl.pallas_call(
         front_kernel,
         in_specs=[HBM, HBM, HBM],
-        out_specs=[VMEM] * 8,
+        out_specs=[VMEM] * 6,
         out_shape=[
-            *(shape(slots) for slots in (1, 1, 2) * 2),
+            jax.ShapeDtypeStruct((rows, wide), jnp.bfloat16),
+            jax.ShapeDtypeStruct((rows, wide), jnp.bfloat16),
+            jax.ShapeDtypeStruct(spectra.shape, jnp.bfloat16),
+            jax.ShapeDtypeStruct((sources.shape[0], channels_here), jnp.float32),
+            jax.ShapeDtypeStruct((sources.shape[0], wide), jnp.float32),
             jax.ShapeDtypeStruct(quality.shape, jnp.float32),
-            jax.ShapeDtypeStruct(spectra.shape, jnp.bfloat16),
         ],
         scratch_shapes=[
             pltpu.SMEM(sources.shape, jnp.int32),
@@ -156,8 +162,40 @@
         ],
         compiler_params=pltpu.CompilerParams(vmem_limit_bytes=16 * MIB),
         cost_estimate=COST,
-        name="pick_sources",
+        name="pick_first",
     )(*(pltpu.with_memory_space_constraint(value, pltpu.HBM) for value in (sources, spectra, quality)))
+
+
+def rest_kernel(
+    data_ref, onehot_ref, usable_ref, quality_ref, after_ref,
+    own_second_ref, own_rest_ref, other_second_ref, other_rest_ref, scale_ref,
+):
+    _, window_count, freq_count, channels_here = data_ref.shape
+    rows = own_second_ref.shape[0]
+    per_slot = onehot_ref.shape[0] // 4
+    onehot = onehot_ref[per_slot:, :].astype(jnp.bfloat16)
+    usable = usable_ref[per_slot:, :]
+    own_refs = [(own_second_ref, 0), (own_rest_ref, 0), (own_rest_ref, rows)]
+    other_refs = [(other_second_ref, 0), (other_rest_ref, 0), (other_rest_ref, rows)]
+    totals = {}
+    for windows, bins in shares(window_count, freq_count):
+        total = totals.get(windows, jnp.zeros((windows[1] - windows[0], 8, channels_here), jnp.float32))
+        totals[windows] = pick_share(data_ref, onehot, usable, windows, bins, own_refs, other_refs, total)
+    power = jnp.concatenate([jnp.sum(total, axis=1) for total in totals.values()], 0) / freq_count
+    scale_ref[...] = lax.rsqrt(power + 1e-06) * quality_ref[...]
+
+
+def pick_rest(data, onehot, usable, quality, rows, after):
+    shape = lambda slots: jax.ShapeDtypeStruct((slots * rows, usable.shape[1]), jnp.bfloat16)
+    return pl.pallas_call(
+        rest_kernel,
+        in_specs=[VMEM] * 4 + [ANY],
+        out_specs=[VMEM] * 5,
+        out_shape=[shape(1), shape(2), shape(1), shape(2), jax.ShapeDtypeStruct(quality.shape, jnp.float32)],
+        compiler_params=pltpu.CompilerParams(vmem_limit_bytes=16 * MIB),
+        cost_estimate=COST,
+        name="pick_rest",
+    )(data, onehot, usable, quality, after)
 
 
 def whiten_kernel(data_ref, scale_ref, after_ref, out_ref):
@@ -426,15 +464,15 @@
     over_chan = lambda value, pairs: lax.ppermute(value, "chan", pairs)
     over_hour = lambda value, pairs: lax.ppermute(value, "hour", pairs)
 
-    front_out = front(spectra, quality, sources)
-    (*state, scale, data) = front_out[:3] + front_out[6:]
-    slot_rows = state[0].shape[0]
-    moved = [over_chan(value, cores) for value in front_out[3:6]]
+    own, other, data, onehot, usable, flags = front(spectra, quality, sources)
+    slot_rows = own.shape[0]
+    state = {0: own}
+    moved = {0: over_chan(other, cores)}
     passes = [0, 0, 0]
     made, mine, cross, middle, outward = {}, {}, {}, {}, {}
     inward = {}
     cuts = (0, SPLITS[0], 8)
-    last = scale
+    last = onehot
     for step in STEPS:
         kind, at = step[0], int(step[1:] or 0)
         if kind == "r":
@@ -442,6 +480,10 @@
                 last = state[at] = add_after(last, state[at], moved[at])
                 moved[at] = over_chan(last, pairs)
             passes[at] += 1
+        elif kind == "q":
+            state[1], state[2], *others, scale = pick_rest(data, onehot, usable, flags, slot_rows, last)
+            moved.update({1 + chunk: over_chan(value, cores) for chunk, value in enumerate(others)})
+            last = scale
         elif kind == "t":
             table = last = lag_table(freq_count, LAGS, last)
         elif kind == "w":

time: 94.7 us -> 94.6 us (level)
  Pallas kernels: 28 us -> 29.8 us
  waiting for transfers between devices: 37.8 us -> 36.4 us
    pallas_call x0 -> x1, Pallas kernels: none -> 2.34 us  [pick_rest(): pl.pallas_call(rest_kernel, in_specs=[VMEM] * 4 + [ANY], out_specs=[VMEM]...]
    ppermute x11, waiting for transfers between devices: 31.1 us -> 29.6 us  [body(): over_hour = lambda value, pairs: lax.ppermute(value, 'hour', pairs)]
  transfers between devices with their start and end apart: 23 -> 23, of which waited for: 13 -> 14; matrix products, arithmetic and copies ran while one was open for 0% -> 0% of each run, Pallas kernels for 24% -> 26%
where the time goes in v6:
time: 94.6 us; the launch traced here: 94.3 us
  waiting for transfers between devices  36.4 us (38%)
  Pallas kernels  29.8 us (32%)
  starting transfers between devices  27.6 us (29%)
    ppermute x11, waiting for transfers between devices, body(): over_hour = lambda value, pairs: lax.ppermute(value, 'hour', pairs)  29.6 us
    ppermute x11, starting transfers between devices, body(): over_hour = lambda value, pairs: lax.ppermute(value, 'hour', pairs)  18.8 us
    pallas_call x6, Pallas kernels, lags_of(): pl.pallas_call(functools.partial(lags_kernel, base, sources, done, hours)...  16 us
    ppermute x12, starting transfers between devices, body(): over_chan = lambda value, pairs: lax.ppermute(value, 'chan', pairs)  8.84 us
    ppermute x12, waiting for transfers between devices, body(): over_chan = lambda value, pairs: lax.ppermute(value, 'chan', pairs)  6.87 us
    pallas_call x1, Pallas kernels, front(): pl.pallas_call(front_kernel, in_specs=[HBM, HBM, HBM], out_specs=[VMEM] *...  3.7 us
    pallas_call x1, Pallas kernels, pick_rest(): pl.pallas_call(rest_kernel, in_specs=[VMEM] * 4 + [ANY], out_specs=[VMEM]...  2.34 us
    pallas_call x9, Pallas kernels, sum_of(): pl.pallas_call(functools.partial(sum_kernel, firsts, low), in_specs=[VMEM...  2.17 us
  transfers between devices with their start and end apart: 23, of which 14 were waited for; matrix products, arithmetic and copies ran while one was open for 0% of the time, Pallas kernels for 26%

profile of v6, /device:TPU:16, one launch (start us, length us, event | category | flops | bytes accessed | tf_op | source)
XLA Modules:
  0.0 94.3 jit_solution(18181418402029686600)
XLA Ops:
  0.0 3.7 %pick_first.1 = (bf16[400,256]{1,0:T(8,128)(2,1)S(1)}, bf16[400,256]{1,0:T(8,128)(2,1)S(1)}, bf16[2,16,800,128]{3,2,1,0:T(8,128)(2,1)S(1)}, f32[32,128]{1,0:T(8,...) custom-call(s32[32]{0:T(128)} %sources_hbm.1, bf16[2,16,800,128]{3,2,1,0:T(8,128)(2,1)} %spectra_hbm.1, ...), custom_call_target="tpu_custom_call" | custom-call | flops 1 | bytes 1 | tf_op jit(solution)/shard_map/pick_first/pallas_call | solution.py:145
  3.8 1.4 %collective-permute-done.refs_1_ = bf16[400,256]{1,0:T(8,128)(2,1)S(1)} collective-permute-done((bf16[400,256]{1,0:T(8,128)(2,1)S(1)}, bf16[400,256]{1,0:T(8,128)(2,1)S(1)}, u32[]{:S(2)}, u32[]{:S(2)}) %collective-permute-start) | collective-permute-done | bytes 204832 | tf_op jit(solution)/shard_map/ppermute | solution.py:464
  5.3 1.6 %collective-permute-start.3 = (bf16[400,256]{1,0:T(8,128)(2,1)S(1)}, bf16[400,256]{1,0:T(8,128)(2,1)S(1)}, u32[]{:S(2)}, u32[]{:S(2)}) collective-permute-start(bf16[400,256]{1,0:T(8,128)(2,1)S(1)} %add.9.after_ref.refs_0_), channel_id=1, source_target_pairs={{0,8},{4,20},{8,0},{12,28},{16,24},{20,4},{24,16},{28,12},{1,9},{5... | collective-permute-start | bytes 614408 | tf_op jit(solution)/shard_map/ppermute | solution.py:464
  6.8 2.3 %pick_rest.1 = (bf16[400,256]{1,0:T(8,128)(2,1)S(1)}, bf16[800,256]{1,0:T(8,128)(2,1)S(1)}, bf16[400,256]{1,0:T(8,128)(2,1)S(1)}, bf16[800,256]{1,0:T(8,128)(2,1)S(1)}, f32[16,128]{1,0:T(8,128)S(1)}) custom-call(bf16[2,16,800,128]{3,2,1,0:T(8,128)(2,1)S(1)} %get-tuple-element.18.data_ref, f32[32,128]{1,0:T(8,128)S(1)} %get-tuple-element.19.refs_2_.onehot_ref, ...), custom_call_target="tpu_custom_call" | custom-call | flops 1 | bytes 1 | tf_op jit(solution)/shard_map/pick_rest/pallas_call | solution.py:190
  9.3 1.8 %collective-permute-done.3.refs_1_ = bf16[400,256]{1,0:T(8,128)(2,1)S(1)} collective-permute-done((bf16[400,256]{1,0:T(8,128)(2,1)S(1)}, bf16[400,256]{1,0:T(8,128)(2,1)S(1)}, u32[]{:S(2)}, u32[]{:S(2)}) %collective-permute-start.3) | collective-permute-done | bytes 204832 | tf_op jit(solution)/shard_map/ppermute | solution.py:464
  11.2 1.6 %collective-permute-start.4 = (bf16[400,256]{1,0:T(8,128)(2,1)S(1)}, bf16[400,256]{1,0:T(8,128)(2,1)S(1)}, u32[]{:S(2)}, u32[]{:S(2)}) collective-permute-start(bf16[400,256]{1,0:T(8,128)(2,1)S(1)} %add.10.after_ref.refs_0_), channel_id=1, source_target_pairs={{0,16},{4,12},{8,24},{12,4},{16,0},{20,28},{24,8},{28,20},{1,17},{... | collective-permute-start | bytes 614408 | tf_op jit(solution)/shard_map/ppermute | solution.py:464
  12.7 1.5 %whiten_receivers.1.after_ref.refs_2_ = bf16[2,16,800,128]{3,2,1,0:T(8,128)(2,1)S(1)} custom-call(bf16[2,16,800,128]{3,2,1,0:T(8,128)(2,1)S(1)} %get-tuple-element.18.data_ref, f32[16,128]{1,0:T(8,128)S(1)} %get-tuple-element.28.refs_2_.scale_ref, bf16[400,256]{1,0:T(8,128)(2,1)S(1)} %add.10.after_ref.refs_0_), custom_call_target="tpu_custom_call" | custom-call | flops 1 | bytes 1 | tf_op jit(solution)/shard_map/whiten_receivers/pallas_call | solution.py:218
  14.3 1.9 %lag_table.1.refs_2_.refs_3_.table_ref = bf16[512,1600]{1,0:T(8,128)(2,1)S(1)} custom-call(bf16[2,16,800,128]{3,2,1,0:T(8,128)(2,1)S(1)} %whiten_receivers.1.after_ref.refs_2_), custom_call_target="tpu_custom_call" | custom-call | flops 1 | bytes 1 | tf_op jit(solution)/shard_map/lag_table/pallas_call | solution.py:271
  16.1 0.9 collective-permute-done.4.refs_1_
  17.2 1.6 %collective-permute-start.6 = (bf16[400,256]{1,0:T(8,128)(2,1)S(1)}, bf16[400,256]{1,0:T(8,128)(2,1)S(1)}, u32[]{:S(2)}, u32[]{:S(2)}) collective-permute-start(bf16[400,256]{1,0:T(8,128)(2,1)S(1)} %add.12.refs_2_.refs_0_), channel_id=1, source_target_pairs={{0,8},{4,20},{8,0},{12,28},{16,24},{20,4},{24,16},{28,12},{1,9},{5... | collective-permute-start | bytes 614408 | tf_op jit(solution)/shard_map/ppermute | solution.py:464
  18.8 0.6 collective-permute-start.5
  19.4 1.3 %collective-permute-start.10 = (bf16[4,512,128]{2,1,0:T(8,128)(2,1)S(1)}, bf16[4,512,128]{2,1,0:T(8,128)(2,1)S(1)}, u32[]{:S(2)}, u32[]{:S(2)}) collective-permute-start(bf16[4,512,128]{2,1,0:T(8,128)(2,1)S(1)} %lags.6.refs_2_), channel_id=1, source_target_pairs={{0,1},{3,2},{4,5},{7,6},{8,9},{11,10},{12,13},{15,14},{16,17},{19,... | collective-permute-start | bytes 1572872 | tf_op jit(solution)/shard_map/ppermute | solution.py:465
  20.7 2.3 %collective-permute-done.6.refs_1_ = bf16[400,256]{1,0:T(8,128)(2,1)S(1)} collective-permute-done((bf16[400,256]{1,0:T(8,128)(2,1)S(1)}, bf16[400,256]{1,0:T(8,128)(2,1)S(1)}, u32[]{:S(2)}, u32[]{:S(2)}) %collective-permute-start.6) | collective-permute-done | bytes 204832 | tf_op jit(solution)/shard_map/ppermute | solution.py:464
  23.1 1.6 %collective-permute-start.8 = (bf16[400,256]{1,0:T(8,128)(2,1)S(1)}, bf16[400,256]{1,0:T(8,128)(2,1)S(1)}, u32[]{:S(2)}, u32[]{:S(2)}) collective-permute-start(bf16[400,256]{1,0:T(8,128)(2,1)S(1)} %add.14.refs_4_.refs_0_), channel_id=1, source_target_pairs={{0,16},{4,12},{8,24},{12,4},{16,0},{20,28},{24,8},{28,20},{1,17},{... | collective-permute-start | bytes 614408 | tf_op jit(solution)/shard_map/ppermute | solution.py:464
  24.6 4.3 %lags.8.refs_2_.refs_0_ = bf16[8,512,128]{2,1,0:T(8,128)(2,1)S(1)} custom-call(bf16[400,256]{1,0:T(8,128)(2,1)S(1)} %add.11.refs_2_.refs_0_, bf16[400,256]{1,0:T(8,128)(2,1)S(1)} %collective-permute-done.7.refs_1_, bf16[2,16,800,128]{3,2,1,0:T(8,128)(2,1)S(1)} %whiten_receivers.1.after_ref.refs_2_, bf16[512,1600]{1,0:T(8,128)(2,1)S(1)} %lag_table.1.refs_2_.refs_3_.table_ref, ...), custom_call_target="tpu_custom_call" | custom-call | flops 1 | bytes 1 | tf_op jit(solution)/shard_map/lags/pallas_call | solution.py:388
  29.0 0.2 collective-permute-done.8.refs_1_
  29.2 0.2 collective-permute-done.5.refs_1_
  29.5 1.6 %collective-permute-start.9 = (bf16[800,256]{1,0:T(8,128)(2,1)S(1)}, bf16[800,256]{1,0:T(8,128)(2,1)S(1)}, u32[]{:S(2)}, u32[]{:S(2)}) collective-permute-start(bf16[800,256]{1,0:T(8,128)(2,1)S(1)} %add.16.refs_4_.refs_0_), channel_id=1, source_target_pairs={{0,16},{4,12},{8,24},{12,4},{16,0},{20,28},{24,8},{28,20},{1,17},{... | collective-permute-start | bytes 1228808 | tf_op jit(solution)/shard_map/ppermute | solution.py:464
  31.1 1.3 %collective-permute-start.13 = (bf16[4,512,128]{2,1,0:T(8,128)(2,1)S(1)}, bf16[4,512,128]{2,1,0:T(8,128)(2,1)S(1)}, u32[]{:S(2)}, u32[]{:S(2)}) collective-permute-start(bf16[4,512,128]{2,1,0:T(8,128)(2,1)S(1)} %lags.7.refs_4_), channel_id=1, source_target_pairs={{0,1},{3,2},{4,5},{7,6},{8,9},{11,10},{12,13},{15,14},{16,17},{19,... | collective-permute-start | bytes 1572872 | tf_op jit(solution)/shard_map/ppermute | solution.py:465
  32.5 2.9 %lags.9 = (bf16[2,512,128]{2,1,0:T(8,128)(2,1)S(1)}, bf16[3,1600,256]{2,1,0:T(8,128)(2,1)S(1)}) custom-call(bf16[400,256]{1,0:T(8,128)(2,1)S(1)} %add.15.refs_2_.refs_0_, bf16[400,256]{1,0:T(8,128)(2,1)S(1)} %collective-permute-done.11.refs_1_, bf16[2,16,800,128]{3,2,1,0:T(8,128)(2,1)S(1)} %whiten_receivers.1.after_ref.refs_2_, ...), custom_call_target="tpu_custom_call" | custom-call | flops 1 | bytes 1 | tf_op jit(solution)/shard_map/lags/pallas_call | solution.py:388
  35.4 2.2 %collective-permute-done.10.refs_1_ = bf16[4,512,128]{2,1,0:T(8,128)(2,1)S(1)} collective-permute-done((bf16[4,512,128]{2,1,0:T(8,128)(2,1)S(1)}, bf16[4,512,128]{2,1,0:T(8,128)(2,1)S(1)}, u32[]{:S(2)}, u32[]{:S(2)}) %collective-permute-start.10) | collective-permute-done | bytes 524320 | tf_op jit(solution)/shard_map/ppermute | solution.py:465
  37.7 0.1 sum.9.refs_2_
  37.8 1.9 %collective-permute-start.14 = (bf16[4,512,128]{2,1,0:T(8,128)(2,1)S(1)}, bf16[4,512,128]{2,1,0:T(8,128)(2,1)S(1)}, u32[]{:S(2)}, u32[]{:S(2)}) collective-permute-start(bf16[4,512,128]{2,1,0:T(8,128)(2,1)S(1)} %sum.9.refs_2_), channel_id=1, source_target_pairs={{1,2},{2,1},{5,6},{6,5},{9,10},{10,9},{13,14},{14,13},{17,18},{18,... | collective-permute-start | bytes 1572872 | tf_op jit(solution)/shard_map/ppermute | solution.py:465
  39.7 0.1 add.17.after_ref.refs_0_
  39.9 1.3 %collective-permute-start.15 = (bf16[2,512,128]{2,1,0:T(8,128)(2,1)S(1)}, bf16[2,512,128]{2,1,0:T(8,128)(2,1)S(1)}, u32[]{:S(2)}, u32[]{:S(2)}) collective-permute-start(bf16[2,512,128]{2,1,0:T(8,128)(2,1)S(1)} %get-tuple-element.29.refs_2_.refs_0_), channel_id=1, source_target_pairs={{0,1},{3,2},{4,5},{7,6},{8,9},{11,10},{12,13},{15,14},{16,17},{19,... | collective-permute-start | bytes 786440 | tf_op jit(solution)/shard_map/ppermute | solution.py:465
  41.2 1.6 %lags_rest.1.refs_2_.refs_0_ = bf16[6,512,128]{2,1,0:T(8,128)(2,1)S(1)} custom-call(bf16[3,1600,256]{2,1,0:T(8,128)(2,1)S(1)} %get-tuple-element.30.cross_ref, bf16[512,1600]{1,0:T(8,128)(2,1)S(1)} %lag_table.1.refs_2_.refs_3_.table_ref, bf16[800,256]{1,0:T(8,128)(2,1)S(1)} %add.17.after_ref.refs_0_), custom_call_target="tpu_custom_call" | custom-call | flops 1 | bytes 1 | tf_op jit(solution)/shard_map/lags_rest/pallas_call | solution.py:405
  42.8 1.3 %collective-permute-start.20 = (bf16[6,512,128]{2,1,0:T(8,128)(2,1)S(1)}, bf16[6,512,128]{2,1,0:T(8,128)(2,1)S(1)}, u32[]{:S(2)}, u32[]{:S(2)}) collective-permute-start(bf16[6,512,128]{2,1,0:T(8,128)(2,1)S(1)} %lags_rest.1.refs_2_.refs_0_), channel_id=1, source_target_pairs={{0,1},{3,2},{4,5},{7,6},{8,9},{11,10},{12,13},{15,14},{16,17},{19,... | collective-permute-start | bytes 2359304 | tf_op jit(solution)/shard_map/ppermute | solution.py:465
  44.1 4.8 %collective-permute-done.13.refs_1_ = bf16[4,512,128]{2,1,0:T(8,128)(2,1)S(1)} collective-permute-done((bf16[4,512,128]{2,1,0:T(8,128)(2,1)S(1)}, bf16[4,512,128]{2,1,0:T(8,128)(2,1)S(1)}, u32[]{:S(2)}, u32[]{:S(2)}) %collective-permute-start.13) | collective-permute-done | bytes 524320 | tf_op jit(solution)/shard_map/ppermute | solution.py:465
  48.9 0.1 sum.10.refs_4_
  49.0 1.9 %collective-permute-start.18 = (bf16[4,512,128]{2,1,0:T(8,128)(2,1)S(1)}, bf16[4,512,128]{2,1,0:T(8,128)(2,1)S(1)}, u32[]{:S(2)}, u32[]{:S(2)}) collective-permute-start(bf16[4,512,128]{2,1,0:T(8,128)(2,1)S(1)} %sum.10.refs_4_), channel_id=1, source_target_pairs={{1,2},{2,1},{5,6},{6,5},{9,10},{10,9},{13,14},{14,13},{17,18},{18,... | collective-permute-start | bytes 1572872 | tf_op jit(solution)/shard_map/ppermute | solution.py:465
  51.0 4.5 %lags.10.refs_2_.refs_0_ = bf16[8,512,128]{2,1,0:T(8,128)(2,1)S(1)} custom-call(bf16[800,256]{1,0:T(8,128)(2,1)S(1)} %add.17.after_ref.refs_0_, bf16[800,256]{1,0:T(8,128)(2,1)S(1)} %collective-permute-done.12.refs_1_, bf16[2,16,800,128]{3,2,1,0:T(8,128)(2,1)S(1)} %whiten_receivers.1.after_ref.refs_2_, ...), custom_call_target="tpu_custom_call" | custom-call | flops 1 | bytes 1 | tf_op jit(solution)/shard_map/lags/pallas_call | solution.py:388
  55.6 0.1 sum.12.refs_4_
  55.7 1.3 %collective-permute-start.16 = (bf16[4,512,128]{2,1,0:T(8,128)(2,1)S(1)}, bf16[4,512,128]{2,1,0:T(8,128)(2,1)S(1)}, u32[]{:S(2)}, u32[]{:S(2)}) collective-permute-start(bf16[4,512,128]{2,1,0:T(8,128)(2,1)S(1)} %sum.12.refs_4_), channel_id=1, source_target_pairs={{1,0},{2,3},{5,4},{6,7},{9,8},{10,11},{13,12},{14,15},{17,16},{18,... | collective-permute-start | bytes 1572872 | tf_op jit(solution)/shard_map/ppermute | solution.py:465
  57.0 3.9 %collective-permute-start.17 = (bf16[2,512,128]{2,1,0:T(8,128)(2,1)S(1)}, bf16[2,512,128]{2,1,0:T(8,128)(2,1)S(1)}, u32[]{:S(2)}, u32[]{:S(2)}) collective-permute-start(bf16[2,512,128]{2,1,0:T(8,128)(2,1)S(1)} %sum.11.refs_2_), channel_id=1, source_target_pairs={{1,2},{2,1},{5,6},{6,5},{9,10},{10,9},{13,14},{14,13},{17,18},{18,... | collective-permute-start | bytes 786440 | tf_op jit(solution)/shard_map/ppermute | solution.py:465
  61.0 1.3 %collective-permute-start.22 = (bf16[8,512,128]{2,1,0:T(8,128)(2,1)S(1)}, bf16[8,512,128]{2,1,0:T(8,128)(2,1)S(1)}, u32[]{:S(2)}, u32[]{:S(2)}) collective-permute-start(bf16[8,512,128]{2,1,0:T(8,128)(2,1)S(1)} %lags.10.refs_2_.refs_0_), channel_id=1, source_target_pairs={{0,1},{3,2},{4,5},{7,6},{8,9},{11,10},{12,13},{15,14},{16,17},{19,... | collective-permute-start | bytes 3145736 | tf_op jit(solution)/shard_map/ppermute | solution.py:465
  62.3 4.3 %lags.11.refs_2_.refs_0_ = bf16[8,512,128]{2,1,0:T(8,128)(2,1)S(1)} custom-call(bf16[800,256]{1,0:T(8,128)(2,1)S(1)} %add.17.after_ref.refs_0_, bf16[800,256]{1,0:T(8,128)(2,1)S(1)} %collective-permute-done.12.refs_1_, bf16[2,16,800,128]{3,2,1,0:T(8,128)(2,1)S(1)} %whiten_receivers.1.after_ref.refs_2_, ...), custom_call_target="tpu_custom_call" | custom-call | flops 1 | bytes 1 | tf_op jit(solution)/shard_map/lags/pallas_call | solution.py:388
  66.6 0.1 sum.13.refs_3_
  66.7 2.3 %collective-permute-done.17.refs_2_ = bf16[2,512,128]{2,1,0:T(8,128)(2,1)S(1)} collective-permute-done((bf16[2,512,128]{2,1,0:T(8,128)(2,1)S(1)}, bf16[2,512,128]{2,1,0:T(8,128)(2,1)S(1)}, u32[]{:S(2)}, u32[]{:S(2)}) %collective-permute-start.17) | collective-permute-done | bytes 262176 | tf_op jit(solution)/shard_map/ppermute | solution.py:465
  69.0 0.1 sum.14.refs_2_.refs_0_
  69.2 2.2 %collective-permute-done.20.refs_1_ = bf16[6,512,128]{2,1,0:T(8,128)(2,1)S(1)} collective-permute-done((bf16[6,512,128]{2,1,0:T(8,128)(2,1)S(1)}, bf16[6,512,128]{2,1,0:T(8,128)(2,1)S(1)}, u32[]{:S(2)}, u32[]{:S(2)}) %collective-permute-start.20) | collective-permute-done | bytes 786464 | tf_op jit(solution)/shard_map/ppermute | solution.py:465
  71.4 0.2 sum.15.refs_4_
  71.5 1.9 %collective-permute-start.21 = (bf16[6,512,128]{2,1,0:T(8,128)(2,1)S(1)}, bf16[6,512,128]{2,1,0:T(8,128)(2,1)S(1)}, u32[]{:S(2)}, u32[]{:S(2)}) collective-permute-start(bf16[6,512,128]{2,1,0:T(8,128)(2,1)S(1)} %sum.15.refs_4_), channel_id=1, source_target_pairs={{1,2},{2,1},{5,6},{6,5},{9,10},{10,9},{13,14},{14,13},{17,18},{18,... | collective-permute-start | bytes 2359304 | tf_op jit(solution)/shard_map/ppermute | solution.py:465
  73.5 1.3 %collective-permute-start.19 = (bf16[4,512,128]{2,1,0:T(8,128)(2,1)S(1)}, bf16[4,512,128]{2,1,0:T(8,128)(2,1)S(1)}, u32[]{:S(2)}, u32[]{:S(2)}) collective-permute-start(bf16[4,512,128]{2,1,0:T(8,128)(2,1)S(1)} %sum.13.refs_3_), channel_id=1, source_target_pairs={{1,0},{2,3},{5,4},{6,7},{9,8},{10,11},{13,12},{14,15},{17,16},{18,... | collective-permute-start | bytes 1572872 | tf_op jit(solution)/shard_map/ppermute | solution.py:465
  74.8 10.2 %collective-permute-done.19.refs_2_ = bf16[4,512,128]{2,1,0:T(8,128)(2,1)S(1)} collective-permute-done((bf16[4,512,128]{2,1,0:T(8,128)(2,1)S(1)}, bf16[4,512,128]{2,1,0:T(8,128)(2,1)S(1)}, u32[]{:S(2)}, u32[]{:S(2)}) %collective-permute-start.19) | collective-permute-done | bytes 524320 | tf_op jit(solution)/shard_map/ppermute | solution.py:465
  85.1 6.5 %collective-permute-done.21.refs_3_ = bf16[6,512,128]{2,1,0:T(8,128)(2,1)S(1)} collective-permute-done((bf16[6,512,128]{2,1,0:T(8,128)(2,1)S(1)}, bf16[6,512,128]{2,1,0:T(8,128)(2,1)S(1)}, u32[]{:S(2)}, u32[]{:S(2)}) %collective-permute-start.21) | collective-permute-done | bytes 786464 | tf_op jit(solution)/shard_map/ppermute | solution.py:465
  91.6 0.2 sum.16.refs_0_.refs_2_
  91.8 1.3 %collective-permute-done.22.refs_1_ = bf16[8,512,128]{2,1,0:T(8,128)(2,1)S(1)} collective-permute-done((bf16[8,512,128]{2,1,0:T(8,128)(2,1)S(1)}, bf16[8,512,128]{2,1,0:T(8,128)(2,1)S(1)}, u32[]{:S(2)}, u32[]{:S(2)}) %collective-permute-start.22) | collective-permute-done | bytes 1048608 | tf_op jit(solution)/shard_map/ppermute | solution.py:465
  93.1 1.0 %sum.17 = bf16[8,512,128]{2,1,0:T(8,128)(2,1)} custom-call(f32[8,512,128]{2,1,0:T(8,128)S(1)} %sum.16.refs_0_.refs_2_, bf16[8,512,128]{2,1,0:T(8,128)(2,1)S(1)} %collective-permute-done.22.refs_1_, f32[8,512,128]{2,1,0:T(8,128)S(1)} %sum.16.refs_0_.refs_2_), custom_call_target="tpu_custom_call" | custom-call | flops 1 | bytes 1 | tf_op jit(solution)/shard_map/sum/pallas_call | solution.py:439
  (28 shorter events, 1.1 us)
Async XLA Ops:
  3.7 1.5 %collective-permute-start = (bf16[400,256]{1,0:T(8,128)(2,1)S(1)}, bf16[400,256]{1,0:T(8,128)(2,1)S(1)}, u32[]{:S(2)}, u32[]{:S(2)}) collective-permute-start(bf16[400,256]{1,0:T(8,128)(2,1)S(1)} %get-tuple-element.23), channel_id=1, source_target_pairs={{0,4},{4,0},{8,12},{12,8},{16,20},{20,16},{24,28},{28,24},{1,5},{5... | collective-permute-start | bytes 614408 | tf_op jit(solution)/shard_map/ppermute | solution.py:464
  5.3 5.8 %collective-permute-start.3 = (bf16[400,256]{1,0:T(8,128)(2,1)S(1)}, bf16[400,256]{1,0:T(8,128)(2,1)S(1)}, u32[]{:S(2)}, u32[]{:S(2)}) collective-permute-start(bf16[400,256]{1,0:T(8,128)(2,1)S(1)} %add.9.after_ref.refs_0_), channel_id=1, source_target_pairs={{0,8},{4,20},{8,0},{12,28},{16,24},{20,4},{24,16},{28,12},{1,9},{5... | collective-permute-start | bytes 614408 | tf_op jit(solution)/shard_map/ppermute | solution.py:464
  9.2 9.6 %collective-permute-start.1 = (bf16[800,256]{1,0:T(8,128)(2,1)S(1)}, bf16[800,256]{1,0:T(8,128)(2,1)S(1)}, u32[]{:S(2)}, u32[]{:S(2)}) collective-permute-start(bf16[800,256]{1,0:T(8,128)(2,1)S(1)} %get-tuple-element.25), channel_id=1, source_target_pairs={{0,4},{4,0},{8,12},{12,8},{16,20},{20,16},{24,28},{28,24},{1,5},{5... | collective-permute-start | bytes 1228808 | tf_op jit(solution)/shard_map/ppermute | solution.py:464
  11.2 5.8 %collective-permute-start.4 = (bf16[400,256]{1,0:T(8,128)(2,1)S(1)}, bf16[400,256]{1,0:T(8,128)(2,1)S(1)}, u32[]{:S(2)}, u32[]{:S(2)}) collective-permute-start(bf16[400,256]{1,0:T(8,128)(2,1)S(1)} %add.10.after_ref.refs_0_), channel_id=1, source_target_pairs={{0,16},{4,12},{8,24},{12,4},{16,0},{20,28},{24,8},{28,20},{1,17},{... | collective-permute-start | bytes 614408 | tf_op jit(solution)/shard_map/ppermute | solution.py:464
  12.7 4.4 %collective-permute-start.2 = (bf16[400,256]{1,0:T(8,128)(2,1)S(1)}, bf16[400,256]{1,0:T(8,128)(2,1)S(1)}, u32[]{:S(2)}, u32[]{:S(2)}) collective-permute-start(bf16[400,256]{1,0:T(8,128)(2,1)S(1)} %get-tuple-element.27), channel_id=1, source_target_pairs={{0,4},{4,0},{8,12},{12,8},{16,20},{20,16},{24,28},{28,24},{1,5},{5... | collective-permute-start | bytes 614408 | tf_op jit(solution)/shard_map/ppermute | solution.py:464
  17.0 2.4 %collective-permute-start.7 = (bf16[400,256]{1,0:T(8,128)(2,1)S(1)}, bf16[400,256]{1,0:T(8,128)(2,1)S(1)}, u32[]{:S(2)}, u32[]{:S(2)}) collective-permute-start(bf16[400,256]{1,0:T(8,128)(2,1)S(1)} %add.11.refs_2_.refs_0_), channel_id=1, source_target_pairs={{0,4},{4,0},{8,12},{12,8},{16,20},{20,16},{24,28},{28,24},{1,5},{5... | collective-permute-start | bytes 614408 | tf_op jit(solution)/shard_map/ppermute | solution.py:464
  17.2 5.8 %collective-permute-start.6 = (bf16[400,256]{1,0:T(8,128)(2,1)S(1)}, bf16[400,256]{1,0:T(8,128)(2,1)S(1)}, u32[]{:S(2)}, u32[]{:S(2)}) collective-permute-start(bf16[400,256]{1,0:T(8,128)(2,1)S(1)} %add.12.refs_2_.refs_0_), channel_id=1, source_target_pairs={{0,8},{4,20},{8,0},{12,28},{16,24},{20,4},{24,16},{28,12},{1,9},{5... | collective-permute-start | bytes 614408 | tf_op jit(solution)/shard_map/ppermute | solution.py:464
  18.8 10.5 %collective-permute-start.5 = (bf16[800,256]{1,0:T(8,128)(2,1)S(1)}, bf16[800,256]{1,0:T(8,128)(2,1)S(1)}, u32[]{:S(2)}, u32[]{:S(2)}) collective-permute-start(bf16[800,256]{1,0:T(8,128)(2,1)S(1)} %add.13.refs_4_.refs_0_), channel_id=1, source_target_pairs={{0,8},{4,20},{8,0},{12,28},{16,24},{20,4},{24,16},{28,12},{1,9},{5... | collective-permute-start | bytes 1228808 | tf_op jit(solution)/shard_map/ppermute | solution.py:464
  19.4 18.2 %collective-permute-start.10 = (bf16[4,512,128]{2,1,0:T(8,128)(2,1)S(1)}, bf16[4,512,128]{2,1,0:T(8,128)(2,1)S(1)}, u32[]{:S(2)}, u32[]{:S(2)}) collective-permute-start(bf16[4,512,128]{2,1,0:T(8,128)(2,1)S(1)} %lags.6.refs_2_), channel_id=1, source_target_pairs={{0,1},{3,2},{4,5},{7,6},{8,9},{11,10},{12,13},{15,14},{16,17},{19,... | collective-permute-start | bytes 1572872 | tf_op jit(solution)/shard_map/ppermute | solution.py:465
  23.1 6.0 %collective-permute-start.8 = (bf16[400,256]{1,0:T(8,128)(2,1)S(1)}, bf16[400,256]{1,0:T(8,128)(2,1)S(1)}, u32[]{:S(2)}, u32[]{:S(2)}) collective-permute-start(bf16[400,256]{1,0:T(8,128)(2,1)S(1)} %add.14.refs_4_.refs_0_), channel_id=1, source_target_pairs={{0,16},{4,12},{8,24},{12,4},{16,0},{20,28},{24,8},{28,20},{1,17},{... | collective-permute-start | bytes 614408 | tf_op jit(solution)/shard_map/ppermute | solution.py:464
  29.5 10.2 %collective-permute-start.9 = (bf16[800,256]{1,0:T(8,128)(2,1)S(1)}, bf16[800,256]{1,0:T(8,128)(2,1)S(1)}, u32[]{:S(2)}, u32[]{:S(2)}) collective-permute-start(bf16[800,256]{1,0:T(8,128)(2,1)S(1)} %add.16.refs_4_.refs_0_), channel_id=1, source_target_pairs={{0,16},{4,12},{8,24},{12,4},{16,0},{20,28},{24,8},{28,20},{1,17},{... | collective-permute-start | bytes 1228808 | tf_op jit(solution)/shard_map/ppermute | solution.py:464
  31.1 1.5 %collective-permute-start.11 = (bf16[400,256]{1,0:T(8,128)(2,1)S(1)}, bf16[400,256]{1,0:T(8,128)(2,1)S(1)}, u32[]{:S(2)}, u32[]{:S(2)}) collective-permute-start(bf16[400,256]{1,0:T(8,128)(2,1)S(1)} %add.15.refs_2_.refs_0_), channel_id=1, source_target_pairs={{0,4},{4,0},{8,12},{12,8},{16,20},{20,16},{24,28},{28,24},{1,5},{5... | collective-permute-start | bytes 614408 | tf_op jit(solution)/shard_map/ppermute | solution.py:464
  31.1 17.7 %collective-permute-start.13 = (bf16[4,512,128]{2,1,0:T(8,128)(2,1)S(1)}, bf16[4,512,128]{2,1,0:T(8,128)(2,1)S(1)}, u32[]{:S(2)}, u32[]{:S(2)}) collective-permute-start(bf16[4,512,128]{2,1,0:T(8,128)(2,1)S(1)} %lags.7.refs_4_), channel_id=1, source_target_pairs={{0,1},{3,2},{4,5},{7,6},{8,9},{11,10},{12,13},{15,14},{16,17},{19,... | collective-permute-start | bytes 1572872 | tf_op jit(solution)/shard_map/ppermute | solution.py:465
  37.8 17.8 %collective-permute-start.14 = (bf16[4,512,128]{2,1,0:T(8,128)(2,1)S(1)}, bf16[4,512,128]{2,1,0:T(8,128)(2,1)S(1)}, u32[]{:S(2)}, u32[]{:S(2)}) collective-permute-start(bf16[4,512,128]{2,1,0:T(8,128)(2,1)S(1)} %sum.9.refs_2_), channel_id=1, source_target_pairs={{1,2},{2,1},{5,6},{6,5},{9,10},{10,9},{13,14},{14,13},{17,18},{18,... | collective-permute-start | bytes 1572872 | tf_op jit(solution)/shard_map/ppermute | solution.py:465
  39.8 11.1 %collective-permute-start.12 = (bf16[800,256]{1,0:T(8,128)(2,1)S(1)}, bf16[800,256]{1,0:T(8,128)(2,1)S(1)}, u32[]{:S(2)}, u32[]{:S(2)}) collective-permute-start(bf16[800,256]{1,0:T(8,128)(2,1)S(1)} %add.17.after_ref.refs_0_), channel_id=1, source_target_pairs={{0,4},{4,0},{8,12},{12,8},{16,20},{20,16},{24,28},{28,24},{1,5},{5... | collective-permute-start | bytes 1228808 | tf_op jit(solution)/shard_map/ppermute | solution.py:464
  39.9 15.6 %collective-permute-start.15 = (bf16[2,512,128]{2,1,0:T(8,128)(2,1)S(1)}, bf16[2,512,128]{2,1,0:T(8,128)(2,1)S(1)}, u32[]{:S(2)}, u32[]{:S(2)}) collective-permute-start(bf16[2,512,128]{2,1,0:T(8,128)(2,1)S(1)} %get-tuple-element.29.refs_2_.refs_0_), channel_id=1, source_target_pairs={{0,1},{3,2},{4,5},{7,6},{8,9},{11,10},{12,13},{15,14},{16,17},{19,... | collective-permute-start | bytes 786440 | tf_op jit(solution)/shard_map/ppermute | solution.py:465
  42.8 28.6 %collective-permute-start.20 = (bf16[6,512,128]{2,1,0:T(8,128)(2,1)S(1)}, bf16[6,512,128]{2,1,0:T(8,128)(2,1)S(1)}, u32[]{:S(2)}, u32[]{:S(2)}) collective-permute-start(bf16[6,512,128]{2,1,0:T(8,128)(2,1)S(1)} %lags_rest.1.refs_2_.refs_0_), channel_id=1, source_target_pairs={{0,1},{3,2},{4,5},{7,6},{8,9},{11,10},{12,13},{15,14},{16,17},{19,... | collective-permute-start | bytes 2359304 | tf_op jit(solution)/shard_map/ppermute | solution.py:465
  49.0 17.6 %collective-permute-start.18 = (bf16[4,512,128]{2,1,0:T(8,128)(2,1)S(1)}, bf16[4,512,128]{2,1,0:T(8,128)(2,1)S(1)}, u32[]{:S(2)}, u32[]{:S(2)}) collective-permute-start(bf16[4,512,128]{2,1,0:T(8,128)(2,1)S(1)} %sum.10.refs_4_), channel_id=1, source_target_pairs={{1,2},{2,1},{5,6},{6,5},{9,10},{10,9},{13,14},{14,13},{17,18},{18,... | collective-permute-start | bytes 1572872 | tf_op jit(solution)/shard_map/ppermute | solution.py:465
  55.7 13.3 %collective-permute-start.16 = (bf16[4,512,128]{2,1,0:T(8,128)(2,1)S(1)}, bf16[4,512,128]{2,1,0:T(8,128)(2,1)S(1)}, u32[]{:S(2)}, u32[]{:S(2)}) collective-permute-start(bf16[4,512,128]{2,1,0:T(8,128)(2,1)S(1)} %sum.12.refs_4_), channel_id=1, source_target_pairs={{1,0},{2,3},{5,4},{6,7},{9,8},{10,11},{13,12},{14,15},{17,16},{18,... | collective-permute-start | bytes 1572872 | tf_op jit(solution)/shard_map/ppermute | solution.py:465
  57.0 12.0 %collective-permute-start.17 = (bf16[2,512,128]{2,1,0:T(8,128)(2,1)S(1)}, bf16[2,512,128]{2,1,0:T(8,128)(2,1)S(1)}, u32[]{:S(2)}, u32[]{:S(2)}) collective-permute-start(bf16[2,512,128]{2,1,0:T(8,128)(2,1)S(1)} %sum.11.refs_2_), channel_id=1, source_target_pairs={{1,2},{2,1},{5,6},{6,5},{9,10},{10,9},{13,14},{14,13},{17,18},{18,... | collective-permute-start | bytes 786440 | tf_op jit(solution)/shard_map/ppermute | solution.py:465
  61.0 32.1 %collective-permute-start.22 = (bf16[8,512,128]{2,1,0:T(8,128)(2,1)S(1)}, bf16[8,512,128]{2,1,0:T(8,128)(2,1)S(1)}, u32[]{:S(2)}, u32[]{:S(2)}) collective-permute-start(bf16[8,512,128]{2,1,0:T(8,128)(2,1)S(1)} %lags.10.refs_2_.refs_0_), channel_id=1, source_target_pairs={{0,1},{3,2},{4,5},{7,6},{8,9},{11,10},{12,13},{15,14},{16,17},{19,... | collective-permute-start | bytes 3145736 | tf_op jit(solution)/shard_map/ppermute | solution.py:465
  71.5 20.0 %collective-permute-start.21 = (bf16[6,512,128]{2,1,0:T(8,128)(2,1)S(1)}, bf16[6,512,128]{2,1,0:T(8,128)(2,1)S(1)}, u32[]{:S(2)}, u32[]{:S(2)}) collective-permute-start(bf16[6,512,128]{2,1,0:T(8,128)(2,1)S(1)} %sum.15.refs_4_), channel_id=1, source_target_pairs={{1,2},{2,1},{5,6},{6,5},{9,10},{10,9},{13,14},{14,13},{17,18},{18,... | collective-permute-start | bytes 2359304 | tf_op jit(solution)/shard_map/ppermute | solution.py:465
  73.5 11.6 %collective-permute-start.19 = (bf16[4,512,128]{2,1,0:T(8,128)(2,1)S(1)}, bf16[4,512,128]{2,1,0:T(8,128)(2,1)S(1)}, u32[]{:S(2)}, u32[]{:S(2)}) collective-permute-start(bf16[4,512,128]{2,1,0:T(8,128)(2,1)S(1)} %sum.13.refs_3_), channel_id=1, source_target_pairs={{1,0},{2,3},{5,4},{6,7},{9,8},{10,11},{13,12},{14,15},{17,16},{18,... | collective-permute-start | bytes 1572872 | tf_op jit(solution)/shard_map/ppermute | solution.py:465

commit v7 on v6

--- a/solution.py
+++ b/solution.py
@@ -36,7 +36,7 @@
 
 
 def shares(window_count, freq_count):
-    middle = (freq_count // (2 * GROUP) + 1) // 2 * 2 * GROUP
+    middle = freq_count // (2 * GROUP) * 2 // 3 * 2 * GROUP
     half = window_count // 2
     return [
         ((low, low + half), bins) for low in (0, half) for bins in ((0, middle), (middle, freq_count))
@@ -423,9 +423,10 @@
             if first <= source < first + ref.shape[0]:
                 total = total + ref[source - first].astype(jnp.float32)
         total_ref[source - low] = total.astype(total_ref.dtype)
-        if rest:
+        if rest and source % 2:
+            pair = pl.ds(source - 1, 2)
             copies.append(
-                pltpu.make_async_copy(total_ref.at[source], out_ref.at[source], rest[1].at[source])
+                pltpu.make_async_copy(total_ref.at[pair], out_ref.at[pair], rest[1].at[source // 2])
             )
             copies[-1].start()
     for copy in copies:
@@ -435,7 +436,7 @@
 def sum_of(parts, low, high, dtype, after, final=False):
     firsts, values = zip(*parts)
     shape = (high - low,) + values[0].shape[1:]
-    scratch = [pltpu.VMEM(shape, dtype), pltpu.SemaphoreType.DMA((high - low,))]
+    scratch = [pltpu.VMEM(shape, dtype), pltpu.SemaphoreType.DMA(((high - low) // 2,))]
     return pl.pallas_call(
         functools.partial(sum_kernel, firsts, low),
         in_specs=[VMEM] * len(values) + [ANY],

time: 94.6 us -> 94.8 us (level)
  no operation moved by 1% of the time
where the time goes in v7:
time: 94.8 us; the launch traced here: 94.5 us
  waiting for transfers between devices  36.4 us (38%)
  Pallas kernels  29.9 us (32%)
  starting transfers between devices  27.6 us (29%)
    ppermute x11, waiting for transfers between devices, body(): over_hour = lambda value, pairs: lax.ppermute(value, 'hour', pairs)  29.5 us
    ppermute x11, starting transfers between devices, body(): over_hour = lambda value, pairs: lax.ppermute(value, 'hour', pairs)  18.8 us
    pallas_call x6, Pallas kernels, lags_of(): pl.pallas_call(functools.partial(lags_kernel, base, sources, done, hours)...  16 us
    ppermute x12, starting transfers between devices, body(): over_chan = lambda value, pairs: lax.ppermute(value, 'chan', pairs)  8.84 us
    ppermute x12, waiting for transfers between devices, body(): over_chan = lambda value, pairs: lax.ppermute(value, 'chan', pairs)  6.87 us
    pallas_call x1, Pallas kernels, front(): pl.pallas_call(front_kernel, in_specs=[HBM, HBM, HBM], out_specs=[VMEM] *...  3.84 us
    pallas_call x1, Pallas kernels, pick_rest(): pl.pallas_call(rest_kernel, in_specs=[VMEM] * 4 + [ANY], out_specs=[VMEM]...  2.34 us
    pallas_call x9, Pallas kernels, sum_of(): pl.pallas_call(functools.partial(sum_kernel, firsts, low), in_specs=[VMEM...  2.16 us
  transfers between devices with their start and end apart: 23, of which 14 were waited for; matrix products, arithmetic and copies ran while one was open for 0% of the time, Pallas kernels for 26%

profile of v7, /device:TPU:16, one launch (start us, length us, event | category | flops | bytes accessed | tf_op | source)
XLA Modules:
  0.0 94.5 jit_solution(5630793552748976743)
XLA Ops:
  0.0 3.8 %pick_first.1 = (bf16[400,256]{1,0:T(8,128)(2,1)S(1)}, bf16[400,256]{1,0:T(8,128)(2,1)S(1)}, bf16[2,16,800,128]{3,2,1,0:T(8,128)(2,1)S(1)}, f32[32,128]{1,0:T(8,...) custom-call(s32[32]{0:T(128)} %sources_hbm.1, bf16[2,16,800,128]{3,2,1,0:T(8,128)(2,1)} %spectra_hbm.1, ...), custom_call_target="tpu_custom_call" | custom-call | flops 1 | bytes 1 | tf_op jit(solution)/shard_map/pick_first/pallas_call | solution.py:145
  3.9 1.4 %collective-permute-done.refs_1_ = bf16[400,256]{1,0:T(8,128)(2,1)S(1)} collective-permute-done((bf16[400,256]{1,0:T(8,128)(2,1)S(1)}, bf16[400,256]{1,0:T(8,128)(2,1)S(1)}, u32[]{:S(2)}, u32[]{:S(2)}) %collective-permute-start) | collective-permute-done | bytes 204832 | tf_op jit(solution)/shard_map/ppermute | solution.py:465
  5.4 1.6 %collective-permute-start.3 = (bf16[400,256]{1,0:T(8,128)(2,1)S(1)}, bf16[400,256]{1,0:T(8,128)(2,1)S(1)}, u32[]{:S(2)}, u32[]{:S(2)}) collective-permute-start(bf16[400,256]{1,0:T(8,128)(2,1)S(1)} %add.9.after_ref.refs_0_), channel_id=1, source_target_pairs={{0,8},{4,20},{8,0},{12,28},{16,24},{20,4},{24,16},{28,12},{1,9},{5... | collective-permute-start | bytes 614408 | tf_op jit(solution)/shard_map/ppermute | solution.py:465
  7.0 2.3 %pick_rest.1 = (bf16[400,256]{1,0:T(8,128)(2,1)S(1)}, bf16[800,256]{1,0:T(8,128)(2,1)S(1)}, bf16[400,256]{1,0:T(8,128)(2,1)S(1)}, bf16[800,256]{1,0:T(8,128)(2,1)S(1)}, f32[16,128]{1,0:T(8,128)S(1)}) custom-call(bf16[2,16,800,128]{3,2,1,0:T(8,128)(2,1)S(1)} %get-tuple-element.18.data_ref, f32[32,128]{1,0:T(8,128)S(1)} %get-tuple-element.19.refs_2_.onehot_ref, ...), custom_call_target="tpu_custom_call" | custom-call | flops 1 | bytes 1 | tf_op jit(solution)/shard_map/pick_rest/pallas_call | solution.py:190
  9.4 1.8 %collective-permute-done.3.refs_1_ = bf16[400,256]{1,0:T(8,128)(2,1)S(1)} collective-permute-done((bf16[400,256]{1,0:T(8,128)(2,1)S(1)}, bf16[400,256]{1,0:T(8,128)(2,1)S(1)}, u32[]{:S(2)}, u32[]{:S(2)}) %collective-permute-start.3) | collective-permute-done | bytes 204832 | tf_op jit(solution)/shard_map/ppermute | solution.py:465
  11.3 1.6 %collective-permute-start.4 = (bf16[400,256]{1,0:T(8,128)(2,1)S(1)}, bf16[400,256]{1,0:T(8,128)(2,1)S(1)}, u32[]{:S(2)}, u32[]{:S(2)}) collective-permute-start(bf16[400,256]{1,0:T(8,128)(2,1)S(1)} %add.10.after_ref.refs_0_), channel_id=1, source_target_pairs={{0,16},{4,12},{8,24},{12,4},{16,0},{20,28},{24,8},{28,20},{1,17},{... | collective-permute-start | bytes 614408 | tf_op jit(solution)/shard_map/ppermute | solution.py:465
  12.9 1.5 %whiten_receivers.1.after_ref.refs_2_ = bf16[2,16,800,128]{3,2,1,0:T(8,128)(2,1)S(1)} custom-call(bf16[2,16,800,128]{3,2,1,0:T(8,128)(2,1)S(1)} %get-tuple-element.18.data_ref, f32[16,128]{1,0:T(8,128)S(1)} %get-tuple-element.28.refs_2_.scale_ref, bf16[400,256]{1,0:T(8,128)(2,1)S(1)} %add.10.after_ref.refs_0_), custom_call_target="tpu_custom_call" | custom-call | flops 1 | bytes 1 | tf_op jit(solution)/shard_map/whiten_receivers/pallas_call | solution.py:218
  14.4 1.9 %lag_table.1.refs_2_.refs_3_.table_ref = bf16[512,1600]{1,0:T(8,128)(2,1)S(1)} custom-call(bf16[2,16,800,128]{3,2,1,0:T(8,128)(2,1)S(1)} %whiten_receivers.1.after_ref.refs_2_), custom_call_target="tpu_custom_call" | custom-call | flops 1 | bytes 1 | tf_op jit(solution)/shard_map/lag_table/pallas_call | solution.py:271
  16.3 0.9 collective-permute-done.4.refs_1_
  17.3 1.6 %collective-permute-start.6 = (bf16[400,256]{1,0:T(8,128)(2,1)S(1)}, bf16[400,256]{1,0:T(8,128)(2,1)S(1)}, u32[]{:S(2)}, u32[]{:S(2)}) collective-permute-start(bf16[400,256]{1,0:T(8,128)(2,1)S(1)} %add.12.refs_2_.refs_0_), channel_id=1, source_target_pairs={{0,8},{4,20},{8,0},{12,28},{16,24},{20,4},{24,16},{28,12},{1,9},{5... | collective-permute-start | bytes 614408 | tf_op jit(solution)/shard_map/ppermute | solution.py:465
  19.0 0.6 collective-permute-start.5
  19.6 1.3 %collective-permute-start.10 = (bf16[4,512,128]{2,1,0:T(8,128)(2,1)S(1)}, bf16[4,512,128]{2,1,0:T(8,128)(2,1)S(1)}, u32[]{:S(2)}, u32[]{:S(2)}) collective-permute-start(bf16[4,512,128]{2,1,0:T(8,128)(2,1)S(1)} %lags.6.refs_2_), channel_id=1, source_target_pairs={{0,1},{3,2},{4,5},{7,6},{8,9},{11,10},{12,13},{15,14},{16,17},{19,... | collective-permute-start | bytes 1572872 | tf_op jit(solution)/shard_map/ppermute | solution.py:466
  20.9 2.3 %collective-permute-done.6.refs_1_ = bf16[400,256]{1,0:T(8,128)(2,1)S(1)} collective-permute-done((bf16[400,256]{1,0:T(8,128)(2,1)S(1)}, bf16[400,256]{1,0:T(8,128)(2,1)S(1)}, u32[]{:S(2)}, u32[]{:S(2)}) %collective-permute-start.6) | collective-permute-done | bytes 204832 | tf_op jit(solution)/shard_map/ppermute | solution.py:465
  23.2 1.6 %collective-permute-start.8 = (bf16[400,256]{1,0:T(8,128)(2,1)S(1)}, bf16[400,256]{1,0:T(8,128)(2,1)S(1)}, u32[]{:S(2)}, u32[]{:S(2)}) collective-permute-start(bf16[400,256]{1,0:T(8,128)(2,1)S(1)} %add.14.refs_4_.refs_0_), channel_id=1, source_target_pairs={{0,16},{4,12},{8,24},{12,4},{16,0},{20,28},{24,8},{28,20},{1,17},{... | collective-permute-start | bytes 614408 | tf_op jit(solution)/shard_map/ppermute | solution.py:465
  24.8 4.3 %lags.8.refs_2_.refs_0_ = bf16[8,512,128]{2,1,0:T(8,128)(2,1)S(1)} custom-call(bf16[400,256]{1,0:T(8,128)(2,1)S(1)} %add.11.refs_2_.refs_0_, bf16[400,256]{1,0:T(8,128)(2,1)S(1)} %collective-permute-done.7.refs_1_, bf16[2,16,800,128]{3,2,1,0:T(8,128)(2,1)S(1)} %whiten_receivers.1.after_ref.refs_2_, bf16[512,1600]{1,0:T(8,128)(2,1)S(1)} %lag_table.1.refs_2_.refs_3_.table_ref, ...), custom_call_target="tpu_custom_call" | custom-call | flops 1 | bytes 1 | tf_op jit(solution)/shard_map/lags/pallas_call | solution.py:388
  29.1 0.2 collective-permute-done.8.refs_1_
  29.3 0.2 collective-permute-done.5.refs_1_
  29.6 1.6 %collective-permute-start.9 = (bf16[800,256]{1,0:T(8,128)(2,1)S(1)}, bf16[800,256]{1,0:T(8,128)(2,1)S(1)}, u32[]{:S(2)}, u32[]{:S(2)}) collective-permute-start(bf16[800,256]{1,0:T(8,128)(2,1)S(1)} %add.16.refs_4_.refs_0_), channel_id=1, source_target_pairs={{0,16},{4,12},{8,24},{12,4},{16,0},{20,28},{24,8},{28,20},{1,17},{... | collective-permute-start | bytes 1228808 | tf_op jit(solution)/shard_map/ppermute | solution.py:465
  31.3 1.3 %collective-permute-start.13 = (bf16[4,512,128]{2,1,0:T(8,128)(2,1)S(1)}, bf16[4,512,128]{2,1,0:T(8,128)(2,1)S(1)}, u32[]{:S(2)}, u32[]{:S(2)}) collective-permute-start(bf16[4,512,128]{2,1,0:T(8,128)(2,1)S(1)} %lags.7.refs_4_), channel_id=1, source_target_pairs={{0,1},{3,2},{4,5},{7,6},{8,9},{11,10},{12,13},{15,14},{16,17},{19,... | collective-permute-start | bytes 1572872 | tf_op jit(solution)/shard_map/ppermute | solution.py:466
  32.7 2.9 %lags.9 = (bf16[2,512,128]{2,1,0:T(8,128)(2,1)S(1)}, bf16[3,1600,256]{2,1,0:T(8,128)(2,1)S(1)}) custom-call(bf16[400,256]{1,0:T(8,128)(2,1)S(1)} %add.15.refs_2_.refs_0_, bf16[400,256]{1,0:T(8,128)(2,1)S(1)} %collective-permute-done.11.refs_1_, bf16[2,16,800,128]{3,2,1,0:T(8,128)(2,1)S(1)} %whiten_receivers.1.after_ref.refs_2_, ...), custom_call_target="tpu_custom_call" | custom-call | flops 1 | bytes 1 | tf_op jit(solution)/shard_map/lags/pallas_call | solution.py:388
  35.5 2.3 %collective-permute-done.10.refs_1_ = bf16[4,512,128]{2,1,0:T(8,128)(2,1)S(1)} collective-permute-done((bf16[4,512,128]{2,1,0:T(8,128)(2,1)S(1)}, bf16[4,512,128]{2,1,0:T(8,128)(2,1)S(1)}, u32[]{:S(2)}, u32[]{:S(2)}) %collective-permute-start.10) | collective-permute-done | bytes 524320 | tf_op jit(solution)/shard_map/ppermute | solution.py:466
  37.8 0.1 sum.9.refs_2_
  37.9 1.9 %collective-permute-start.14 = (bf16[4,512,128]{2,1,0:T(8,128)(2,1)S(1)}, bf16[4,512,128]{2,1,0:T(8,128)(2,1)S(1)}, u32[]{:S(2)}, u32[]{:S(2)}) collective-permute-start(bf16[4,512,128]{2,1,0:T(8,128)(2,1)S(1)} %sum.9.refs_2_), channel_id=1, source_target_pairs={{1,2},{2,1},{5,6},{6,5},{9,10},{10,9},{13,14},{14,13},{17,18},{18,... | collective-permute-start | bytes 1572872 | tf_op jit(solution)/shard_map/ppermute | solution.py:466
  39.9 0.1 add.17.after_ref.refs_0_
  40.0 1.3 %collective-permute-start.15 = (bf16[2,512,128]{2,1,0:T(8,128)(2,1)S(1)}, bf16[2,512,128]{2,1,0:T(8,128)(2,1)S(1)}, u32[]{:S(2)}, u32[]{:S(2)}) collective-permute-start(bf16[2,512,128]{2,1,0:T(8,128)(2,1)S(1)} %get-tuple-element.29.refs_2_.refs_0_), channel_id=1, source_target_pairs={{0,1},{3,2},{4,5},{7,6},{8,9},{11,10},{12,13},{15,14},{16,17},{19,... | collective-permute-start | bytes 786440 | tf_op jit(solution)/shard_map/ppermute | solution.py:466
  41.3 1.6 %lags_rest.1.refs_2_.refs_0_ = bf16[6,512,128]{2,1,0:T(8,128)(2,1)S(1)} custom-call(bf16[3,1600,256]{2,1,0:T(8,128)(2,1)S(1)} %get-tuple-element.30.cross_ref, bf16[512,1600]{1,0:T(8,128)(2,1)S(1)} %lag_table.1.refs_2_.refs_3_.table_ref, bf16[800,256]{1,0:T(8,128)(2,1)S(1)} %add.17.after_ref.refs_0_), custom_call_target="tpu_custom_call" | custom-call | flops 1 | bytes 1 | tf_op jit(solution)/shard_map/lags_rest/pallas_call | solution.py:405
  43.0 1.3 %collective-permute-start.20 = (bf16[6,512,128]{2,1,0:T(8,128)(2,1)S(1)}, bf16[6,512,128]{2,1,0:T(8,128)(2,1)S(1)}, u32[]{:S(2)}, u32[]{:S(2)}) collective-permute-start(bf16[6,512,128]{2,1,0:T(8,128)(2,1)S(1)} %lags_rest.1.refs_2_.refs_0_), channel_id=1, source_target_pairs={{0,1},{3,2},{4,5},{7,6},{8,9},{11,10},{12,13},{15,14},{16,17},{19,... | collective-permute-start | bytes 2359304 | tf_op jit(solution)/shard_map/ppermute | solution.py:466
  44.3 4.8 %collective-permute-done.13.refs_1_ = bf16[4,512,128]{2,1,0:T(8,128)(2,1)S(1)} collective-permute-done((bf16[4,512,128]{2,1,0:T(8,128)(2,1)S(1)}, bf16[4,512,128]{2,1,0:T(8,128)(2,1)S(1)}, u32[]{:S(2)}, u32[]{:S(2)}) %collective-permute-start.13) | collective-permute-done | bytes 524320 | tf_op jit(solution)/shard_map/ppermute | solution.py:466
  49.0 0.1 sum.10.refs_4_
  49.2 1.9 %collective-permute-start.18 = (bf16[4,512,128]{2,1,0:T(8,128)(2,1)S(1)}, bf16[4,512,128]{2,1,0:T(8,128)(2,1)S(1)}, u32[]{:S(2)}, u32[]{:S(2)}) collective-permute-start(bf16[4,512,128]{2,1,0:T(8,128)(2,1)S(1)} %sum.10.refs_4_), channel_id=1, source_target_pairs={{1,2},{2,1},{5,6},{6,5},{9,10},{10,9},{13,14},{14,13},{17,18},{18,... | collective-permute-start | bytes 1572872 | tf_op jit(solution)/shard_map/ppermute | solution.py:466
  51.1 4.5 %lags.10.refs_2_.refs_0_ = bf16[8,512,128]{2,1,0:T(8,128)(2,1)S(1)} custom-call(bf16[800,256]{1,0:T(8,128)(2,1)S(1)} %add.17.after_ref.refs_0_, bf16[800,256]{1,0:T(8,128)(2,1)S(1)} %collective-permute-done.12.refs_1_, bf16[2,16,800,128]{3,2,1,0:T(8,128)(2,1)S(1)} %whiten_receivers.1.after_ref.refs_2_, ...), custom_call_target="tpu_custom_call" | custom-call | flops 1 | bytes 1 | tf_op jit(solution)/shard_map/lags/pallas_call | solution.py:388
  55.7 0.1 sum.12.refs_4_
  55.9 1.3 %collective-permute-start.16 = (bf16[4,512,128]{2,1,0:T(8,128)(2,1)S(1)}, bf16[4,512,128]{2,1,0:T(8,128)(2,1)S(1)}, u32[]{:S(2)}, u32[]{:S(2)}) collective-permute-start(bf16[4,512,128]{2,1,0:T(8,128)(2,1)S(1)} %sum.12.refs_4_), channel_id=1, source_target_pairs={{1,0},{2,3},{5,4},{6,7},{9,8},{10,11},{13,12},{14,15},{17,16},{18,... | collective-permute-start | bytes 1572872 | tf_op jit(solution)/shard_map/ppermute | solution.py:466
  57.2 3.9 %collective-permute-start.17 = (bf16[2,512,128]{2,1,0:T(8,128)(2,1)S(1)}, bf16[2,512,128]{2,1,0:T(8,128)(2,1)S(1)}, u32[]{:S(2)}, u32[]{:S(2)}) collective-permute-start(bf16[2,512,128]{2,1,0:T(8,128)(2,1)S(1)} %sum.11.refs_2_), channel_id=1, source_target_pairs={{1,2},{2,1},{5,6},{6,5},{9,10},{10,9},{13,14},{14,13},{17,18},{18,... | collective-permute-start | bytes 786440 | tf_op jit(solution)/shard_map/ppermute | solution.py:466
  61.1 1.3 %collective-permute-start.22 = (bf16[8,512,128]{2,1,0:T(8,128)(2,1)S(1)}, bf16[8,512,128]{2,1,0:T(8,128)(2,1)S(1)}, u32[]{:S(2)}, u32[]{:S(2)}) collective-permute-start(bf16[8,512,128]{2,1,0:T(8,128)(2,1)S(1)} %lags.10.refs_2_.refs_0_), channel_id=1, source_target_pairs={{0,1},{3,2},{4,5},{7,6},{8,9},{11,10},{12,13},{15,14},{16,17},{19,... | collective-permute-start | bytes 3145736 | tf_op jit(solution)/shard_map/ppermute | solution.py:466
  62.4 4.3 %lags.11.refs_2_.refs_0_ = bf16[8,512,128]{2,1,0:T(8,128)(2,1)S(1)} custom-call(bf16[800,256]{1,0:T(8,128)(2,1)S(1)} %add.17.after_ref.refs_0_, bf16[800,256]{1,0:T(8,128)(2,1)S(1)} %collective-permute-done.12.refs_1_, bf16[2,16,800,128]{3,2,1,0:T(8,128)(2,1)S(1)} %whiten_receivers.1.after_ref.refs_2_, ...), custom_call_target="tpu_custom_call" | custom-call | flops 1 | bytes 1 | tf_op jit(solution)/shard_map/lags/pallas_call | solution.py:388
  66.7 0.1 sum.13.refs_3_
  66.9 2.3 %collective-permute-done.17.refs_2_ = bf16[2,512,128]{2,1,0:T(8,128)(2,1)S(1)} collective-permute-done((bf16[2,512,128]{2,1,0:T(8,128)(2,1)S(1)}, bf16[2,512,128]{2,1,0:T(8,128)(2,1)S(1)}, u32[]{:S(2)}, u32[]{:S(2)}) %collective-permute-start.17) | collective-permute-done | bytes 262176 | tf_op jit(solution)/shard_map/ppermute | solution.py:466
  69.1 0.1 sum.14.refs_2_.refs_0_
  69.3 2.2 %collective-permute-done.20.refs_1_ = bf16[6,512,128]{2,1,0:T(8,128)(2,1)S(1)} collective-permute-done((bf16[6,512,128]{2,1,0:T(8,128)(2,1)S(1)}, bf16[6,512,128]{2,1,0:T(8,128)(2,1)S(1)}, u32[]{:S(2)}, u32[]{:S(2)}) %collective-permute-start.20) | collective-permute-done | bytes 786464 | tf_op jit(solution)/shard_map/ppermute | solution.py:466
  71.5 0.2 sum.15.refs_4_
  71.7 1.9 %collective-permute-start.21 = (bf16[6,512,128]{2,1,0:T(8,128)(2,1)S(1)}, bf16[6,512,128]{2,1,0:T(8,128)(2,1)S(1)}, u32[]{:S(2)}, u32[]{:S(2)}) collective-permute-start(bf16[6,512,128]{2,1,0:T(8,128)(2,1)S(1)} %sum.15.refs_4_), channel_id=1, source_target_pairs={{1,2},{2,1},{5,6},{6,5},{9,10},{10,9},{13,14},{14,13},{17,18},{18,... | collective-permute-start | bytes 2359304 | tf_op jit(solution)/shard_map/ppermute | solution.py:466
  73.6 1.3 %collective-permute-start.19 = (bf16[4,512,128]{2,1,0:T(8,128)(2,1)S(1)}, bf16[4,512,128]{2,1,0:T(8,128)(2,1)S(1)}, u32[]{:S(2)}, u32[]{:S(2)}) collective-permute-start(bf16[4,512,128]{2,1,0:T(8,128)(2,1)S(1)} %sum.13.refs_3_), channel_id=1, source_target_pairs={{1,0},{2,3},{5,4},{6,7},{9,8},{10,11},{13,12},{14,15},{17,16},{18,... | collective-permute-start | bytes 1572872 | tf_op jit(solution)/shard_map/ppermute | solution.py:466
  75.0 10.2 %collective-permute-done.19.refs_2_ = bf16[4,512,128]{2,1,0:T(8,128)(2,1)S(1)} collective-permute-done((bf16[4,512,128]{2,1,0:T(8,128)(2,1)S(1)}, bf16[4,512,128]{2,1,0:T(8,128)(2,1)S(1)}, u32[]{:S(2)}, u32[]{:S(2)}) %collective-permute-start.19) | collective-permute-done | bytes 524320 | tf_op jit(solution)/shard_map/ppermute | solution.py:466
  85.2 6.5 %collective-permute-done.21.refs_3_ = bf16[6,512,128]{2,1,0:T(8,128)(2,1)S(1)} collective-permute-done((bf16[6,512,128]{2,1,0:T(8,128)(2,1)S(1)}, bf16[6,512,128]{2,1,0:T(8,128)(2,1)S(1)}, u32[]{:S(2)}, u32[]{:S(2)}) %collective-permute-start.21) | collective-permute-done | bytes 786464 | tf_op jit(solution)/shard_map/ppermute | solution.py:466
  91.7 0.2 sum.16.refs_0_.refs_2_
  91.9 1.3 %collective-permute-done.22.refs_1_ = bf16[8,512,128]{2,1,0:T(8,128)(2,1)S(1)} collective-permute-done((bf16[8,512,128]{2,1,0:T(8,128)(2,1)S(1)}, bf16[8,512,128]{2,1,0:T(8,128)(2,1)S(1)}, u32[]{:S(2)}, u32[]{:S(2)}) %collective-permute-start.22) | collective-permute-done | bytes 1048608 | tf_op jit(solution)/shard_map/ppermute | solution.py:466
  93.2 1.0 %sum.17 = bf16[8,512,128]{2,1,0:T(8,128)(2,1)} custom-call(f32[8,512,128]{2,1,0:T(8,128)S(1)} %sum.16.refs_0_.refs_2_, bf16[8,512,128]{2,1,0:T(8,128)(2,1)S(1)} %collective-permute-done.22.refs_1_, f32[8,512,128]{2,1,0:T(8,128)S(1)} %sum.16.refs_0_.refs_2_), custom_call_target="tpu_custom_call" | custom-call | flops 1 | bytes 1 | tf_op jit(solution)/shard_map/sum/pallas_call | solution.py:440
  (28 shorter events, 1.1 us)
Async XLA Ops:
  3.8 1.5 %collective-permute-start = (bf16[400,256]{1,0:T(8,128)(2,1)S(1)}, bf16[400,256]{1,0:T(8,128)(2,1)S(1)}, u32[]{:S(2)}, u32[]{:S(2)}) collective-permute-start(bf16[400,256]{1,0:T(8,128)(2,1)S(1)} %get-tuple-element.23), channel_id=1, source_target_pairs={{0,4},{4,0},{8,12},{12,8},{16,20},{20,16},{24,28},{28,24},{1,5},{5... | collective-permute-start | bytes 614408 | tf_op jit(solution)/shard_map/ppermute | solution.py:465
  5.4 5.8 %collective-permute-start.3 = (bf16[400,256]{1,0:T(8,128)(2,1)S(1)}, bf16[400,256]{1,0:T(8,128)(2,1)S(1)}, u32[]{:S(2)}, u32[]{:S(2)}) collective-permute-start(bf16[400,256]{1,0:T(8,128)(2,1)S(1)} %add.9.after_ref.refs_0_), channel_id=1, source_target_pairs={{0,8},{4,20},{8,0},{12,28},{16,24},{20,4},{24,16},{28,12},{1,9},{5... | collective-permute-start | bytes 614408 | tf_op jit(solution)/shard_map/ppermute | solution.py:465
  9.3 9.6 %collective-permute-start.1 = (bf16[800,256]{1,0:T(8,128)(2,1)S(1)}, bf16[800,256]{1,0:T(8,128)(2,1)S(1)}, u32[]{:S(2)}, u32[]{:S(2)}) collective-permute-start(bf16[800,256]{1,0:T(8,128)(2,1)S(1)} %get-tuple-element.25), channel_id=1, source_target_pairs={{0,4},{4,0},{8,12},{12,8},{16,20},{20,16},{24,28},{28,24},{1,5},{5... | collective-permute-start | bytes 1228808 | tf_op jit(solution)/shard_map/ppermute | solution.py:465
  11.3 5.8 %collective-permute-start.4 = (bf16[400,256]{1,0:T(8,128)(2,1)S(1)}, bf16[400,256]{1,0:T(8,128)(2,1)S(1)}, u32[]{:S(2)}, u32[]{:S(2)}) collective-permute-start(bf16[400,256]{1,0:T(8,128)(2,1)S(1)} %add.10.after_ref.refs_0_), channel_id=1, source_target_pairs={{0,16},{4,12},{8,24},{12,4},{16,0},{20,28},{24,8},{28,20},{1,17},{... | collective-permute-start | bytes 614408 | tf_op jit(solution)/shard_map/ppermute | solution.py:465
  12.9 4.4 %collective-permute-start.2 = (bf16[400,256]{1,0:T(8,128)(2,1)S(1)}, bf16[400,256]{1,0:T(8,128)(2,1)S(1)}, u32[]{:S(2)}, u32[]{:S(2)}) collective-permute-start(bf16[400,256]{1,0:T(8,128)(2,1)S(1)} %get-tuple-element.27), channel_id=1, source_target_pairs={{0,4},{4,0},{8,12},{12,8},{16,20},{20,16},{24,28},{28,24},{1,5},{5... | collective-permute-start | bytes 614408 | tf_op jit(solution)/shard_map/ppermute | solution.py:465
  17.2 2.4 %collective-permute-start.7 = (bf16[400,256]{1,0:T(8,128)(2,1)S(1)}, bf16[400,256]{1,0:T(8,128)(2,1)S(1)}, u32[]{:S(2)}, u32[]{:S(2)}) collective-permute-start(bf16[400,256]{1,0:T(8,128)(2,1)S(1)} %add.11.refs_2_.refs_0_), channel_id=1, source_target_pairs={{0,4},{4,0},{8,12},{12,8},{16,20},{20,16},{24,28},{28,24},{1,5},{5... | collective-permute-start | bytes 614408 | tf_op jit(solution)/shard_map/ppermute | solution.py:465
  17.3 5.8 %collective-permute-start.6 = (bf16[400,256]{1,0:T(8,128)(2,1)S(1)}, bf16[400,256]{1,0:T(8,128)(2,1)S(1)}, u32[]{:S(2)}, u32[]{:S(2)}) collective-permute-start(bf16[400,256]{1,0:T(8,128)(2,1)S(1)} %add.12.refs_2_.refs_0_), channel_id=1, source_target_pairs={{0,8},{4,20},{8,0},{12,28},{16,24},{20,4},{24,16},{28,12},{1,9},{5... | collective-permute-start | bytes 614408 | tf_op jit(solution)/shard_map/ppermute | solution.py:465
  19.0 10.5 %collective-permute-start.5 = (bf16[800,256]{1,0:T(8,128)(2,1)S(1)}, bf16[800,256]{1,0:T(8,128)(2,1)S(1)}, u32[]{:S(2)}, u32[]{:S(2)}) collective-permute-start(bf16[800,256]{1,0:T(8,128)(2,1)S(1)} %add.13.refs_4_.refs_0_), channel_id=1, source_target_pairs={{0,8},{4,20},{8,0},{12,28},{16,24},{20,4},{24,16},{28,12},{1,9},{5... | collective-permute-start | bytes 1228808 | tf_op jit(solution)/shard_map/ppermute | solution.py:465
  19.6 18.2 %collective-permute-start.10 = (bf16[4,512,128]{2,1,0:T(8,128)(2,1)S(1)}, bf16[4,512,128]{2,1,0:T(8,128)(2,1)S(1)}, u32[]{:S(2)}, u32[]{:S(2)}) collective-permute-start(bf16[4,512,128]{2,1,0:T(8,128)(2,1)S(1)} %lags.6.refs_2_), channel_id=1, source_target_pairs={{0,1},{3,2},{4,5},{7,6},{8,9},{11,10},{12,13},{15,14},{16,17},{19,... | collective-permute-start | bytes 1572872 | tf_op jit(solution)/shard_map/ppermute | solution.py:466
  23.2 6.0 %collective-permute-start.8 = (bf16[400,256]{1,0:T(8,128)(2,1)S(1)}, bf16[400,256]{1,0:T(8,128)(2,1)S(1)}, u32[]{:S(2)}, u32[]{:S(2)}) collective-permute-start(bf16[400,256]{1,0:T(8,128)(2,1)S(1)} %add.14.refs_4_.refs_0_), channel_id=1, source_target_pairs={{0,16},{4,12},{8,24},{12,4},{16,0},{20,28},{24,8},{28,20},{1,17},{... | collective-permute-start | bytes 614408 | tf_op jit(solution)/shard_map/ppermute | solution.py:465
  29.6 10.2 %collective-permute-start.9 = (bf16[800,256]{1,0:T(8,128)(2,1)S(1)}, bf16[800,256]{1,0:T(8,128)(2,1)S(1)}, u32[]{:S(2)}, u32[]{:S(2)}) collective-permute-start(bf16[800,256]{1,0:T(8,128)(2,1)S(1)} %add.16.refs_4_.refs_0_), channel_id=1, source_target_pairs={{0,16},{4,12},{8,24},{12,4},{16,0},{20,28},{24,8},{28,20},{1,17},{... | collective-permute-start | bytes 1228808 | tf_op jit(solution)/shard_map/ppermute | solution.py:465
  31.2 1.5 %collective-permute-start.11 = (bf16[400,256]{1,0:T(8,128)(2,1)S(1)}, bf16[400,256]{1,0:T(8,128)(2,1)S(1)}, u32[]{:S(2)}, u32[]{:S(2)}) collective-permute-start(bf16[400,256]{1,0:T(8,128)(2,1)S(1)} %add.15.refs_2_.refs_0_), channel_id=1, source_target_pairs={{0,4},{4,0},{8,12},{12,8},{16,20},{20,16},{24,28},{28,24},{1,5},{5... | collective-permute-start | bytes 614408 | tf_op jit(solution)/shard_map/ppermute | solution.py:465
  31.3 17.7 %collective-permute-start.13 = (bf16[4,512,128]{2,1,0:T(8,128)(2,1)S(1)}, bf16[4,512,128]{2,1,0:T(8,128)(2,1)S(1)}, u32[]{:S(2)}, u32[]{:S(2)}) collective-permute-start(bf16[4,512,128]{2,1,0:T(8,128)(2,1)S(1)} %lags.7.refs_4_), channel_id=1, source_target_pairs={{0,1},{3,2},{4,5},{7,6},{8,9},{11,10},{12,13},{15,14},{16,17},{19,... | collective-permute-start | bytes 1572872 | tf_op jit(solution)/shard_map/ppermute | solution.py:466
  37.9 17.8 %collective-permute-start.14 = (bf16[4,512,128]{2,1,0:T(8,128)(2,1)S(1)}, bf16[4,512,128]{2,1,0:T(8,128)(2,1)S(1)}, u32[]{:S(2)}, u32[]{:S(2)}) collective-permute-start(bf16[4,512,128]{2,1,0:T(8,128)(2,1)S(1)} %sum.9.refs_2_), channel_id=1, source_target_pairs={{1,2},{2,1},{5,6},{6,5},{9,10},{10,9},{13,14},{14,13},{17,18},{18,... | collective-permute-start | bytes 1572872 | tf_op jit(solution)/shard_map/ppermute | solution.py:466
  40.0 11.1 %collective-permute-start.12 = (bf16[800,256]{1,0:T(8,128)(2,1)S(1)}, bf16[800,256]{1,0:T(8,128)(2,1)S(1)}, u32[]{:S(2)}, u32[]{:S(2)}) collective-permute-start(bf16[800,256]{1,0:T(8,128)(2,1)S(1)} %add.17.after_ref.refs_0_), channel_id=1, source_target_pairs={{0,4},{4,0},{8,12},{12,8},{16,20},{20,16},{24,28},{28,24},{1,5},{5... | collective-permute-start | bytes 1228808 | tf_op jit(solution)/shard_map/ppermute | solution.py:465
  40.0 15.6 %collective-permute-start.15 = (bf16[2,512,128]{2,1,0:T(8,128)(2,1)S(1)}, bf16[2,512,128]{2,1,0:T(8,128)(2,1)S(1)}, u32[]{:S(2)}, u32[]{:S(2)}) collective-permute-start(bf16[2,512,128]{2,1,0:T(8,128)(2,1)S(1)} %get-tuple-element.29.refs_2_.refs_0_), channel_id=1, source_target_pairs={{0,1},{3,2},{4,5},{7,6},{8,9},{11,10},{12,13},{15,14},{16,17},{19,... | collective-permute-start | bytes 786440 | tf_op jit(solution)/shard_map/ppermute | solution.py:466
  43.0 28.6 %collective-permute-start.20 = (bf16[6,512,128]{2,1,0:T(8,128)(2,1)S(1)}, bf16[6,512,128]{2,1,0:T(8,128)(2,1)S(1)}, u32[]{:S(2)}, u32[]{:S(2)}) collective-permute-start(bf16[6,512,128]{2,1,0:T(8,128)(2,1)S(1)} %lags_rest.1.refs_2_.refs_0_), channel_id=1, source_target_pairs={{0,1},{3,2},{4,5},{7,6},{8,9},{11,10},{12,13},{15,14},{16,17},{19,... | collective-permute-start | bytes 2359304 | tf_op jit(solution)/shard_map/ppermute | solution.py:466
  49.2 17.6 %collective-permute-start.18 = (bf16[4,512,128]{2,1,0:T(8,128)(2,1)S(1)}, bf16[4,512,128]{2,1,0:T(8,128)(2,1)S(1)}, u32[]{:S(2)}, u32[]{:S(2)}) collective-permute-start(bf16[4,512,128]{2,1,0:T(8,128)(2,1)S(1)} %sum.10.refs_4_), channel_id=1, source_target_pairs={{1,2},{2,1},{5,6},{6,5},{9,10},{10,9},{13,14},{14,13},{17,18},{18,... | collective-permute-start | bytes 1572872 | tf_op jit(solution)/shard_map/ppermute | solution.py:466
  55.9 13.3 %collective-permute-start.16 = (bf16[4,512,128]{2,1,0:T(8,128)(2,1)S(1)}, bf16[4,512,128]{2,1,0:T(8,128)(2,1)S(1)}, u32[]{:S(2)}, u32[]{:S(2)}) collective-permute-start(bf16[4,512,128]{2,1,0:T(8,128)(2,1)S(1)} %sum.12.refs_4_), channel_id=1, source_target_pairs={{1,0},{2,3},{5,4},{6,7},{9,8},{10,11},{13,12},{14,15},{17,16},{18,... | collective-permute-start | bytes 1572872 | tf_op jit(solution)/shard_map/ppermute | solution.py:466
  57.2 12.0 %collective-permute-start.17 = (bf16[2,512,128]{2,1,0:T(8,128)(2,1)S(1)}, bf16[2,512,128]{2,1,0:T(8,128)(2,1)S(1)}, u32[]{:S(2)}, u32[]{:S(2)}) collective-permute-start(bf16[2,512,128]{2,1,0:T(8,128)(2,1)S(1)} %sum.11.refs_2_), channel_id=1, source_target_pairs={{1,2},{2,1},{5,6},{6,5},{9,10},{10,9},{13,14},{14,13},{17,18},{18,... | collective-permute-start | bytes 786440 | tf_op jit(solution)/shard_map/ppermute | solution.py:466
  61.1 32.1 %collective-permute-start.22 = (bf16[8,512,128]{2,1,0:T(8,128)(2,1)S(1)}, bf16[8,512,128]{2,1,0:T(8,128)(2,1)S(1)}, u32[]{:S(2)}, u32[]{:S(2)}) collective-permute-start(bf16[8,512,128]{2,1,0:T(8,128)(2,1)S(1)} %lags.10.refs_2_.refs_0_), channel_id=1, source_target_pairs={{0,1},{3,2},{4,5},{7,6},{8,9},{11,10},{12,13},{15,14},{16,17},{19,... | collective-permute-start | bytes 3145736 | tf_op jit(solution)/shard_map/ppermute | solution.py:466
  71.7 20.0 %collective-permute-start.21 = (bf16[6,512,128]{2,1,0:T(8,128)(2,1)S(1)}, bf16[6,512,128]{2,1,0:T(8,128)(2,1)S(1)}, u32[]{:S(2)}, u32[]{:S(2)}) collective-permute-start(bf16[6,512,128]{2,1,0:T(8,128)(2,1)S(1)} %sum.15.refs_4_), channel_id=1, source_target_pairs={{1,2},{2,1},{5,6},{6,5},{9,10},{10,9},{13,14},{14,13},{17,18},{18,... | collective-permute-start | bytes 2359304 | tf_op jit(solution)/shard_map/ppermute | solution.py:466
  73.6 11.5 %collective-permute-start.19 = (bf16[4,512,128]{2,1,0:T(8,128)(2,1)S(1)}, bf16[4,512,128]{2,1,0:T(8,128)(2,1)S(1)}, u32[]{:S(2)}, u32[]{:S(2)}) collective-permute-start(bf16[4,512,128]{2,1,0:T(8,128)(2,1)S(1)} %sum.13.refs_3_), channel_id=1, source_target_pairs={{1,0},{2,3},{5,4},{6,7},{9,8},{10,11},{13,12},{14,15},{17,16},{18,... | collective-permute-start | bytes 1572872 | tf_op jit(solution)/shard_map/ppermute | solution.py:466

commit v8 on v7

--- a/solution.py
+++ b/solution.py
@@ -312,7 +312,16 @@
         lax.broadcasted_iota(jnp.int32, (wide, wide), 0) // GROUP
         == lax.broadcasted_iota(jnp.int32, (wide, wide), 1) // GROUP
     ).astype(jnp.float32)
-    power = jnp.dot(total, same, preferred_element_type=jnp.float32, precision=lax.Precision.HIGHEST)
+    terms, left_over = [], total
+    for _ in range(3):
+        terms.append(left_over.astype(jnp.bfloat16).astype(jnp.float32))
+        left_over = left_over - terms[-1]
+    power = jnp.dot(
+        jnp.concatenate(terms, 0).astype(jnp.bfloat16),
+        same.astype(jnp.bfloat16),
+        preferred_element_type=jnp.float32,
+    )
+    power = power[:8] + power[8:16] + power[16:]
     scale = lax.rsqrt(power / freq_count + 1e-06)
     scale = jnp.concatenate([scale, scale], 0)
 

time: 94.8 us -> 94.5 us (level)
  no operation moved by 1% of the time
where the time goes in v8:
time: 94.5 us; the launch traced here: 94.2 us
  waiting for transfers between devices  36.9 us (39%)
  Pallas kernels  29.1 us (31%)
  starting transfers between devices  27.6 us (29%)
    ppermute x11, waiting for transfers between devices, body(): over_hour = lambda value, pairs: lax.ppermute(value, 'hour', pairs)  29.9 us
    ppermute x11, starting transfers between devices, body(): over_hour = lambda value, pairs: lax.ppermute(value, 'hour', pairs)  18.8 us
    pallas_call x6, Pallas kernels, lags_of(): pl.pallas_call(functools.partial(lags_kernel, base, sources, done, hours)...  15.2 us
    ppermute x12, starting transfers between devices, body(): over_chan = lambda value, pairs: lax.ppermute(value, 'chan', pairs)  8.84 us
    ppermute x12, waiting for transfers between devices, body(): over_chan = lambda value, pairs: lax.ppermute(value, 'chan', pairs)  7.07 us
    pallas_call x1, Pallas kernels, front(): pl.pallas_call(front_kernel, in_specs=[HBM, HBM, HBM], out_specs=[VMEM] *...  3.84 us
    pallas_call x1, Pallas kernels, pick_rest(): pl.pallas_call(rest_kernel, in_specs=[VMEM] * 4 + [ANY], out_specs=[VMEM]...  2.34 us
    pallas_call x9, Pallas kernels, sum_of(): pl.pallas_call(functools.partial(sum_kernel, firsts, low), in_specs=[VMEM...  2.16 us
  transfers between devices with their start and end apart: 23, of which 14 were waited for; matrix products, arithmetic and copies ran while one was open for 0% of the time, Pallas kernels for 26%

profile of v8, /device:TPU:16, one launch (start us, length us, event | category | flops | bytes accessed | tf_op | source)
XLA Modules:
  0.0 94.2 jit_solution(11921608561977118669)
XLA Ops:
  0.0 3.8 %pick_first.1 = (bf16[400,256]{1,0:T(8,128)(2,1)S(1)}, bf16[400,256]{1,0:T(8,128)(2,1)S(1)}, bf16[2,16,800,128]{3,2,1,0:T(8,128)(2,1)S(1)}, f32[32,128]{1,0:T(8,...) custom-call(s32[32]{0:T(128)} %sources_hbm.1, bf16[2,16,800,128]{3,2,1,0:T(8,128)(2,1)} %spectra_hbm.1, ...), custom_call_target="tpu_custom_call" | custom-call | flops 1 | bytes 1 | tf_op jit(solution)/shard_map/pick_first/pallas_call | solution.py:145
  3.9 1.4 %collective-permute-done.refs_1_ = bf16[400,256]{1,0:T(8,128)(2,1)S(1)} collective-permute-done((bf16[400,256]{1,0:T(8,128)(2,1)S(1)}, bf16[400,256]{1,0:T(8,128)(2,1)S(1)}, u32[]{:S(2)}, u32[]{:S(2)}) %collective-permute-start) | collective-permute-done | bytes 204832 | tf_op jit(solution)/shard_map/ppermute | solution.py:474
  5.4 1.6 %collective-permute-start.3 = (bf16[400,256]{1,0:T(8,128)(2,1)S(1)}, bf16[400,256]{1,0:T(8,128)(2,1)S(1)}, u32[]{:S(2)}, u32[]{:S(2)}) collective-permute-start(bf16[400,256]{1,0:T(8,128)(2,1)S(1)} %add.9.after_ref.refs_0_), channel_id=1, source_target_pairs={{0,8},{4,20},{8,0},{12,28},{16,24},{20,4},{24,16},{28,12},{1,9},{5... | collective-permute-start | bytes 614408 | tf_op jit(solution)/shard_map/ppermute | solution.py:474
  7.0 2.3 %pick_rest.1 = (bf16[400,256]{1,0:T(8,128)(2,1)S(1)}, bf16[800,256]{1,0:T(8,128)(2,1)S(1)}, bf16[400,256]{1,0:T(8,128)(2,1)S(1)}, bf16[800,256]{1,0:T(8,128)(2,1)S(1)}, f32[16,128]{1,0:T(8,128)S(1)}) custom-call(bf16[2,16,800,128]{3,2,1,0:T(8,128)(2,1)S(1)} %get-tuple-element.18.data_ref, f32[32,128]{1,0:T(8,128)S(1)} %get-tuple-element.19.refs_2_.onehot_ref, ...), custom_call_target="tpu_custom_call" | custom-call | flops 1 | bytes 1 | tf_op jit(solution)/shard_map/pick_rest/pallas_call | solution.py:190
  9.4 1.8 %collective-permute-done.3.refs_1_ = bf16[400,256]{1,0:T(8,128)(2,1)S(1)} collective-permute-done((bf16[400,256]{1,0:T(8,128)(2,1)S(1)}, bf16[400,256]{1,0:T(8,128)(2,1)S(1)}, u32[]{:S(2)}, u32[]{:S(2)}) %collective-permute-start.3) | collective-permute-done | bytes 204832 | tf_op jit(solution)/shard_map/ppermute | solution.py:474
  11.3 1.6 %collective-permute-start.4 = (bf16[400,256]{1,0:T(8,128)(2,1)S(1)}, bf16[400,256]{1,0:T(8,128)(2,1)S(1)}, u32[]{:S(2)}, u32[]{:S(2)}) collective-permute-start(bf16[400,256]{1,0:T(8,128)(2,1)S(1)} %add.10.after_ref.refs_0_), channel_id=1, source_target_pairs={{0,16},{4,12},{8,24},{12,4},{16,0},{20,28},{24,8},{28,20},{1,17},{... | collective-permute-start | bytes 614408 | tf_op jit(solution)/shard_map/ppermute | solution.py:474
  12.9 1.5 %whiten_receivers.1.after_ref.refs_2_ = bf16[2,16,800,128]{3,2,1,0:T(8,128)(2,1)S(1)} custom-call(bf16[2,16,800,128]{3,2,1,0:T(8,128)(2,1)S(1)} %get-tuple-element.18.data_ref, f32[16,128]{1,0:T(8,128)S(1)} %get-tuple-element.28.refs_2_.scale_ref, bf16[400,256]{1,0:T(8,128)(2,1)S(1)} %add.10.after_ref.refs_0_), custom_call_target="tpu_custom_call" | custom-call | flops 1 | bytes 1 | tf_op jit(solution)/shard_map/whiten_receivers/pallas_call | solution.py:218
  14.4 1.9 %lag_table.1.refs_2_.refs_3_.table_ref = bf16[512,1600]{1,0:T(8,128)(2,1)S(1)} custom-call(bf16[2,16,800,128]{3,2,1,0:T(8,128)(2,1)S(1)} %whiten_receivers.1.after_ref.refs_2_), custom_call_target="tpu_custom_call" | custom-call | flops 1 | bytes 1 | tf_op jit(solution)/shard_map/lag_table/pallas_call | solution.py:271
  16.3 0.9 collective-permute-done.4.refs_1_
  17.3 1.6 %collective-permute-start.6 = (bf16[400,256]{1,0:T(8,128)(2,1)S(1)}, bf16[400,256]{1,0:T(8,128)(2,1)S(1)}, u32[]{:S(2)}, u32[]{:S(2)}) collective-permute-start(bf16[400,256]{1,0:T(8,128)(2,1)S(1)} %add.12.refs_2_.refs_0_), channel_id=1, source_target_pairs={{0,8},{4,20},{8,0},{12,28},{16,24},{20,4},{24,16},{28,12},{1,9},{5... | collective-permute-start | bytes 614408 | tf_op jit(solution)/shard_map/ppermute | solution.py:474
  19.0 0.6 collective-permute-start.5
  19.6 1.3 %collective-permute-start.10 = (bf16[4,512,128]{2,1,0:T(8,128)(2,1)S(1)}, bf16[4,512,128]{2,1,0:T(8,128)(2,1)S(1)}, u32[]{:S(2)}, u32[]{:S(2)}) collective-permute-start(bf16[4,512,128]{2,1,0:T(8,128)(2,1)S(1)} %lags.6.refs_2_), channel_id=1, source_target_pairs={{0,1},{3,2},{4,5},{7,6},{8,9},{11,10},{12,13},{15,14},{16,17},{19,... | collective-permute-start | bytes 1572872 | tf_op jit(solution)/shard_map/ppermute | solution.py:475
  20.9 2.3 %collective-permute-done.6.refs_1_ = bf16[400,256]{1,0:T(8,128)(2,1)S(1)} collective-permute-done((bf16[400,256]{1,0:T(8,128)(2,1)S(1)}, bf16[400,256]{1,0:T(8,128)(2,1)S(1)}, u32[]{:S(2)}, u32[]{:S(2)}) %collective-permute-start.6) | collective-permute-done | bytes 204832 | tf_op jit(solution)/shard_map/ppermute | solution.py:474
  23.2 1.6 %collective-permute-start.8 = (bf16[400,256]{1,0:T(8,128)(2,1)S(1)}, bf16[400,256]{1,0:T(8,128)(2,1)S(1)}, u32[]{:S(2)}, u32[]{:S(2)}) collective-permute-start(bf16[400,256]{1,0:T(8,128)(2,1)S(1)} %add.14.refs_4_.refs_0_), channel_id=1, source_target_pairs={{0,16},{4,12},{8,24},{12,4},{16,0},{20,28},{24,8},{28,20},{1,17},{... | collective-permute-start | bytes 614408 | tf_op jit(solution)/shard_map/ppermute | solution.py:474
  24.8 4.1 %lags.8.refs_2_.refs_0_ = bf16[8,512,128]{2,1,0:T(8,128)(2,1)S(1)} custom-call(bf16[400,256]{1,0:T(8,128)(2,1)S(1)} %add.11.refs_2_.refs_0_, bf16[400,256]{1,0:T(8,128)(2,1)S(1)} %collective-permute-done.7.refs_1_, bf16[2,16,800,128]{3,2,1,0:T(8,128)(2,1)S(1)} %whiten_receivers.1.after_ref.refs_2_, bf16[512,1600]{1,0:T(8,128)(2,1)S(1)} %lag_table.1.refs_2_.refs_3_.table_ref, ...), custom_call_target="tpu_custom_call" | custom-call | flops 1 | bytes 1 | tf_op jit(solution)/shard_map/lags/pallas_call | solution.py:397
  28.9 0.3 collective-permute-done.8.refs_1_
  29.3 0.2 collective-permute-done.5.refs_1_
  29.6 1.6 %collective-permute-start.9 = (bf16[800,256]{1,0:T(8,128)(2,1)S(1)}, bf16[800,256]{1,0:T(8,128)(2,1)S(1)}, u32[]{:S(2)}, u32[]{:S(2)}) collective-permute-start(bf16[800,256]{1,0:T(8,128)(2,1)S(1)} %add.16.refs_4_.refs_0_), channel_id=1, source_target_pairs={{0,16},{4,12},{8,24},{12,4},{16,0},{20,28},{24,8},{28,20},{1,17},{... | collective-permute-start | bytes 1228808 | tf_op jit(solution)/shard_map/ppermute | solution.py:474
  31.3 1.3 %collective-permute-start.13 = (bf16[4,512,128]{2,1,0:T(8,128)(2,1)S(1)}, bf16[4,512,128]{2,1,0:T(8,128)(2,1)S(1)}, u32[]{:S(2)}, u32[]{:S(2)}) collective-permute-start(bf16[4,512,128]{2,1,0:T(8,128)(2,1)S(1)} %lags.7.refs_4_), channel_id=1, source_target_pairs={{0,1},{3,2},{4,5},{7,6},{8,9},{11,10},{12,13},{15,14},{16,17},{19,... | collective-permute-start | bytes 1572872 | tf_op jit(solution)/shard_map/ppermute | solution.py:475
  32.7 2.7 %lags.9 = (bf16[2,512,128]{2,1,0:T(8,128)(2,1)S(1)}, bf16[3,1600,256]{2,1,0:T(8,128)(2,1)S(1)}) custom-call(bf16[400,256]{1,0:T(8,128)(2,1)S(1)} %add.15.refs_2_.refs_0_, bf16[400,256]{1,0:T(8,128)(2,1)S(1)} %collective-permute-done.11.refs_1_, bf16[2,16,800,128]{3,2,1,0:T(8,128)(2,1)S(1)} %whiten_receivers.1.after_ref.refs_2_, ...), custom_call_target="tpu_custom_call" | custom-call | flops 1 | bytes 1 | tf_op jit(solution)/shard_map/lags/pallas_call | solution.py:397
  35.3 2.0 %collective-permute-done.10.refs_1_ = bf16[4,512,128]{2,1,0:T(8,128)(2,1)S(1)} collective-permute-done((bf16[4,512,128]{2,1,0:T(8,128)(2,1)S(1)}, bf16[4,512,128]{2,1,0:T(8,128)(2,1)S(1)}, u32[]{:S(2)}, u32[]{:S(2)}) %collective-permute-start.10) | collective-permute-done | bytes 524320 | tf_op jit(solution)/shard_map/ppermute | solution.py:475
  37.3 0.1 sum.9.refs_2_
  37.5 1.9 %collective-permute-start.14 = (bf16[4,512,128]{2,1,0:T(8,128)(2,1)S(1)}, bf16[4,512,128]{2,1,0:T(8,128)(2,1)S(1)}, u32[]{:S(2)}, u32[]{:S(2)}) collective-permute-start(bf16[4,512,128]{2,1,0:T(8,128)(2,1)S(1)} %sum.9.refs_2_), channel_id=1, source_target_pairs={{1,2},{2,1},{5,6},{6,5},{9,10},{10,9},{13,14},{14,13},{17,18},{18,... | collective-permute-start | bytes 1572872 | tf_op jit(solution)/shard_map/ppermute | solution.py:475
  39.4 0.1 add.17.after_ref.refs_0_
  39.6 1.3 %collective-permute-start.15 = (bf16[2,512,128]{2,1,0:T(8,128)(2,1)S(1)}, bf16[2,512,128]{2,1,0:T(8,128)(2,1)S(1)}, u32[]{:S(2)}, u32[]{:S(2)}) collective-permute-start(bf16[2,512,128]{2,1,0:T(8,128)(2,1)S(1)} %get-tuple-element.29.refs_2_.refs_0_), channel_id=1, source_target_pairs={{0,1},{3,2},{4,5},{7,6},{8,9},{11,10},{12,13},{15,14},{16,17},{19,... | collective-permute-start | bytes 786440 | tf_op jit(solution)/shard_map/ppermute | solution.py:475
  40.9 1.6 %lags_rest.1.refs_2_.refs_0_ = bf16[6,512,128]{2,1,0:T(8,128)(2,1)S(1)} custom-call(bf16[3,1600,256]{2,1,0:T(8,128)(2,1)S(1)} %get-tuple-element.30.cross_ref, bf16[512,1600]{1,0:T(8,128)(2,1)S(1)} %lag_table.1.refs_2_.refs_3_.table_ref, bf16[800,256]{1,0:T(8,128)(2,1)S(1)} %add.17.after_ref.refs_0_), custom_call_target="tpu_custom_call" | custom-call | flops 1 | bytes 1 | tf_op jit(solution)/shard_map/lags_rest/pallas_call | solution.py:414
  42.5 1.3 %collective-permute-start.20 = (bf16[6,512,128]{2,1,0:T(8,128)(2,1)S(1)}, bf16[6,512,128]{2,1,0:T(8,128)(2,1)S(1)}, u32[]{:S(2)}, u32[]{:S(2)}) collective-permute-start(bf16[6,512,128]{2,1,0:T(8,128)(2,1)S(1)} %lags_rest.1.refs_2_.refs_0_), channel_id=1, source_target_pairs={{0,1},{3,2},{4,5},{7,6},{8,9},{11,10},{12,13},{15,14},{16,17},{19,... | collective-permute-start | bytes 2359304 | tf_op jit(solution)/shard_map/ppermute | solution.py:475
  43.8 4.8 %collective-permute-done.13.refs_1_ = bf16[4,512,128]{2,1,0:T(8,128)(2,1)S(1)} collective-permute-done((bf16[4,512,128]{2,1,0:T(8,128)(2,1)S(1)}, bf16[4,512,128]{2,1,0:T(8,128)(2,1)S(1)}, u32[]{:S(2)}, u32[]{:S(2)}) %collective-permute-start.13) | collective-permute-done | bytes 524320 | tf_op jit(solution)/shard_map/ppermute | solution.py:475
  48.6 0.1 sum.10.refs_4_
  48.7 1.9 %collective-permute-start.18 = (bf16[4,512,128]{2,1,0:T(8,128)(2,1)S(1)}, bf16[4,512,128]{2,1,0:T(8,128)(2,1)S(1)}, u32[]{:S(2)}, u32[]{:S(2)}) collective-permute-start(bf16[4,512,128]{2,1,0:T(8,128)(2,1)S(1)} %sum.10.refs_4_), channel_id=1, source_target_pairs={{1,2},{2,1},{5,6},{6,5},{9,10},{10,9},{13,14},{14,13},{17,18},{18,... | collective-permute-start | bytes 1572872 | tf_op jit(solution)/shard_map/ppermute | solution.py:475
  50.6 4.3 %lags.10.refs_2_.refs_0_ = bf16[8,512,128]{2,1,0:T(8,128)(2,1)S(1)} custom-call(bf16[800,256]{1,0:T(8,128)(2,1)S(1)} %add.17.after_ref.refs_0_, bf16[800,256]{1,0:T(8,128)(2,1)S(1)} %collective-permute-done.12.refs_1_, bf16[2,16,800,128]{3,2,1,0:T(8,128)(2,1)S(1)} %whiten_receivers.1.after_ref.refs_2_, ...), custom_call_target="tpu_custom_call" | custom-call | flops 1 | bytes 1 | tf_op jit(solution)/shard_map/lags/pallas_call | solution.py:397
  55.1 0.1 sum.12.refs_4_
  55.2 1.3 %collective-permute-start.16 = (bf16[4,512,128]{2,1,0:T(8,128)(2,1)S(1)}, bf16[4,512,128]{2,1,0:T(8,128)(2,1)S(1)}, u32[]{:S(2)}, u32[]{:S(2)}) collective-permute-start(bf16[4,512,128]{2,1,0:T(8,128)(2,1)S(1)} %sum.12.refs_4_), channel_id=1, source_target_pairs={{1,0},{2,3},{5,4},{6,7},{9,8},{10,11},{13,12},{14,15},{17,16},{18,... | collective-permute-start | bytes 1572872 | tf_op jit(solution)/shard_map/ppermute | solution.py:475
  56.5 3.9 %collective-permute-start.17 = (bf16[2,512,128]{2,1,0:T(8,128)(2,1)S(1)}, bf16[2,512,128]{2,1,0:T(8,128)(2,1)S(1)}, u32[]{:S(2)}, u32[]{:S(2)}) collective-permute-start(bf16[2,512,128]{2,1,0:T(8,128)(2,1)S(1)} %sum.11.refs_2_), channel_id=1, source_target_pairs={{1,2},{2,1},{5,6},{6,5},{9,10},{10,9},{13,14},{14,13},{17,18},{18,... | collective-permute-start | bytes 786440 | tf_op jit(solution)/shard_map/ppermute | solution.py:475
  60.5 1.3 %collective-permute-start.22 = (bf16[8,512,128]{2,1,0:T(8,128)(2,1)S(1)}, bf16[8,512,128]{2,1,0:T(8,128)(2,1)S(1)}, u32[]{:S(2)}, u32[]{:S(2)}) collective-permute-start(bf16[8,512,128]{2,1,0:T(8,128)(2,1)S(1)} %lags.10.refs_2_.refs_0_), channel_id=1, source_target_pairs={{0,1},{3,2},{4,5},{7,6},{8,9},{11,10},{12,13},{15,14},{16,17},{19,... | collective-permute-start | bytes 3145736 | tf_op jit(solution)/shard_map/ppermute | solution.py:475
  61.8 4.1 %lags.11.refs_2_.refs_0_ = bf16[8,512,128]{2,1,0:T(8,128)(2,1)S(1)} custom-call(bf16[800,256]{1,0:T(8,128)(2,1)S(1)} %add.17.after_ref.refs_0_, bf16[800,256]{1,0:T(8,128)(2,1)S(1)} %collective-permute-done.12.refs_1_, bf16[2,16,800,128]{3,2,1,0:T(8,128)(2,1)S(1)} %whiten_receivers.1.after_ref.refs_2_, ...), custom_call_target="tpu_custom_call" | custom-call | flops 1 | bytes 1 | tf_op jit(solution)/shard_map/lags/pallas_call | solution.py:397
  65.9 0.1 sum.13.refs_3_
  66.0 3.0 %collective-permute-done.17.refs_2_ = bf16[2,512,128]{2,1,0:T(8,128)(2,1)S(1)} collective-permute-done((bf16[2,512,128]{2,1,0:T(8,128)(2,1)S(1)}, bf16[2,512,128]{2,1,0:T(8,128)(2,1)S(1)}, u32[]{:S(2)}, u32[]{:S(2)}) %collective-permute-start.17) | collective-permute-done | bytes 262176 | tf_op jit(solution)/shard_map/ppermute | solution.py:475
  69.1 0.1 sum.14.refs_2_.refs_0_
  69.2 1.8 %collective-permute-done.20.refs_1_ = bf16[6,512,128]{2,1,0:T(8,128)(2,1)S(1)} collective-permute-done((bf16[6,512,128]{2,1,0:T(8,128)(2,1)S(1)}, bf16[6,512,128]{2,1,0:T(8,128)(2,1)S(1)}, u32[]{:S(2)}, u32[]{:S(2)}) %collective-permute-start.20) | collective-permute-done | bytes 786464 | tf_op jit(solution)/shard_map/ppermute | solution.py:475
  71.0 0.2 sum.15.refs_4_
  71.2 1.9 %collective-permute-start.21 = (bf16[6,512,128]{2,1,0:T(8,128)(2,1)S(1)}, bf16[6,512,128]{2,1,0:T(8,128)(2,1)S(1)}, u32[]{:S(2)}, u32[]{:S(2)}) collective-permute-start(bf16[6,512,128]{2,1,0:T(8,128)(2,1)S(1)} %sum.15.refs_4_), channel_id=1, source_target_pairs={{1,2},{2,1},{5,6},{6,5},{9,10},{10,9},{13,14},{14,13},{17,18},{18,... | collective-permute-start | bytes 2359304 | tf_op jit(solution)/shard_map/ppermute | solution.py:475
  73.2 1.3 %collective-permute-start.19 = (bf16[4,512,128]{2,1,0:T(8,128)(2,1)S(1)}, bf16[4,512,128]{2,1,0:T(8,128)(2,1)S(1)}, u32[]{:S(2)}, u32[]{:S(2)}) collective-permute-start(bf16[4,512,128]{2,1,0:T(8,128)(2,1)S(1)} %sum.13.refs_3_), channel_id=1, source_target_pairs={{1,0},{2,3},{5,4},{6,7},{9,8},{10,11},{13,12},{14,15},{17,16},{18,... | collective-permute-start | bytes 1572872 | tf_op jit(solution)/shard_map/ppermute | solution.py:475
  74.5 10.6 %collective-permute-done.19.refs_2_ = bf16[4,512,128]{2,1,0:T(8,128)(2,1)S(1)} collective-permute-done((bf16[4,512,128]{2,1,0:T(8,128)(2,1)S(1)}, bf16[4,512,128]{2,1,0:T(8,128)(2,1)S(1)}, u32[]{:S(2)}, u32[]{:S(2)}) %collective-permute-start.19) | collective-permute-done | bytes 524320 | tf_op jit(solution)/shard_map/ppermute | solution.py:475
  85.1 6.5 %collective-permute-done.21.refs_3_ = bf16[6,512,128]{2,1,0:T(8,128)(2,1)S(1)} collective-permute-done((bf16[6,512,128]{2,1,0:T(8,128)(2,1)S(1)}, bf16[6,512,128]{2,1,0:T(8,128)(2,1)S(1)}, u32[]{:S(2)}, u32[]{:S(2)}) %collective-permute-start.21) | collective-permute-done | bytes 786464 | tf_op jit(solution)/shard_map/ppermute | solution.py:475
  91.6 0.2 sum.16.refs_0_.refs_2_
  91.9 1.1 %collective-permute-done.22.refs_1_ = bf16[8,512,128]{2,1,0:T(8,128)(2,1)S(1)} collective-permute-done((bf16[8,512,128]{2,1,0:T(8,128)(2,1)S(1)}, bf16[8,512,128]{2,1,0:T(8,128)(2,1)S(1)}, u32[]{:S(2)}, u32[]{:S(2)}) %collective-permute-start.22) | collective-permute-done | bytes 1048608 | tf_op jit(solution)/shard_map/ppermute | solution.py:475
  93.0 1.0 %sum.17 = bf16[8,512,128]{2,1,0:T(8,128)(2,1)} custom-call(f32[8,512,128]{2,1,0:T(8,128)S(1)} %sum.16.refs_0_.refs_2_, bf16[8,512,128]{2,1,0:T(8,128)(2,1)S(1)} %collective-permute-done.22.refs_1_, f32[8,512,128]{2,1,0:T(8,128)S(1)} %sum.16.refs_0_.refs_2_), custom_call_target="tpu_custom_call" | custom-call | flops 1 | bytes 1 | tf_op jit(solution)/shard_map/sum/pallas_call | solution.py:449
  (28 shorter events, 1.1 us)
Async XLA Ops:
  3.8 1.5 %collective-permute-start = (bf16[400,256]{1,0:T(8,128)(2,1)S(1)}, bf16[400,256]{1,0:T(8,128)(2,1)S(1)}, u32[]{:S(2)}, u32[]{:S(2)}) collective-permute-start(bf16[400,256]{1,0:T(8,128)(2,1)S(1)} %get-tuple-element.23), channel_id=1, source_target_pairs={{0,4},{4,0},{8,12},{12,8},{16,20},{20,16},{24,28},{28,24},{1,5},{5... | collective-permute-start | bytes 614408 | tf_op jit(solution)/shard_map/ppermute | solution.py:474
  5.4 5.8 %collective-permute-start.3 = (bf16[400,256]{1,0:T(8,128)(2,1)S(1)}, bf16[400,256]{1,0:T(8,128)(2,1)S(1)}, u32[]{:S(2)}, u32[]{:S(2)}) collective-permute-start(bf16[400,256]{1,0:T(8,128)(2,1)S(1)} %add.9.after_ref.refs_0_), channel_id=1, source_target_pairs={{0,8},{4,20},{8,0},{12,28},{16,24},{20,4},{24,16},{28,12},{1,9},{5... | collective-permute-start | bytes 614408 | tf_op jit(solution)/shard_map/ppermute | solution.py:474
  9.3 9.6 %collective-permute-start.1 = (bf16[800,256]{1,0:T(8,128)(2,1)S(1)}, bf16[800,256]{1,0:T(8,128)(2,1)S(1)}, u32[]{:S(2)}, u32[]{:S(2)}) collective-permute-start(bf16[800,256]{1,0:T(8,128)(2,1)S(1)} %get-tuple-element.25), channel_id=1, source_target_pairs={{0,4},{4,0},{8,12},{12,8},{16,20},{20,16},{24,28},{28,24},{1,5},{5... | collective-permute-start | bytes 1228808 | tf_op jit(solution)/shard_map/ppermute | solution.py:474
  11.3 5.8 %collective-permute-start.4 = (bf16[400,256]{1,0:T(8,128)(2,1)S(1)}, bf16[400,256]{1,0:T(8,128)(2,1)S(1)}, u32[]{:S(2)}, u32[]{:S(2)}) collective-permute-start(bf16[400,256]{1,0:T(8,128)(2,1)S(1)} %add.10.after_ref.refs_0_), channel_id=1, source_target_pairs={{0,16},{4,12},{8,24},{12,4},{16,0},{20,28},{24,8},{28,20},{1,17},{... | collective-permute-start | bytes 614408 | tf_op jit(solution)/shard_map/ppermute | solution.py:474
  12.9 4.4 %collective-permute-start.2 = (bf16[400,256]{1,0:T(8,128)(2,1)S(1)}, bf16[400,256]{1,0:T(8,128)(2,1)S(1)}, u32[]{:S(2)}, u32[]{:S(2)}) collective-permute-start(bf16[400,256]{1,0:T(8,128)(2,1)S(1)} %get-tuple-element.27), channel_id=1, source_target_pairs={{0,4},{4,0},{8,12},{12,8},{16,20},{20,16},{24,28},{28,24},{1,5},{5... | collective-permute-start | bytes 614408 | tf_op jit(solution)/shard_map/ppermute | solution.py:474
  17.2 2.4 %collective-permute-start.7 = (bf16[400,256]{1,0:T(8,128)(2,1)S(1)}, bf16[400,256]{1,0:T(8,128)(2,1)S(1)}, u32[]{:S(2)}, u32[]{:S(2)}) collective-permute-start(bf16[400,256]{1,0:T(8,128)(2,1)S(1)} %add.11.refs_2_.refs_0_), channel_id=1, source_target_pairs={{0,4},{4,0},{8,12},{12,8},{16,20},{20,16},{24,28},{28,24},{1,5},{5... | collective-permute-start | bytes 614408 | tf_op jit(solution)/shard_map/ppermute | solution.py:474
  17.3 5.8 %collective-permute-start.6 = (bf16[400,256]{1,0:T(8,128)(2,1)S(1)}, bf16[400,256]{1,0:T(8,128)(2,1)S(1)}, u32[]{:S(2)}, u32[]{:S(2)}) collective-permute-start(bf16[400,256]{1,0:T(8,128)(2,1)S(1)} %add.12.refs_2_.refs_0_), channel_id=1, source_target_pairs={{0,8},{4,20},{8,0},{12,28},{16,24},{20,4},{24,16},{28,12},{1,9},{5... | collective-permute-start | bytes 614408 | tf_op jit(solution)/shard_map/ppermute | solution.py:474
  19.0 10.5 %collective-permute-start.5 = (bf16[800,256]{1,0:T(8,128)(2,1)S(1)}, bf16[800,256]{1,0:T(8,128)(2,1)S(1)}, u32[]{:S(2)}, u32[]{:S(2)}) collective-permute-start(bf16[800,256]{1,0:T(8,128)(2,1)S(1)} %add.13.refs_4_.refs_0_), channel_id=1, source_target_pairs={{0,8},{4,20},{8,0},{12,28},{16,24},{20,4},{24,16},{28,12},{1,9},{5... | collective-permute-start | bytes 1228808 | tf_op jit(solution)/shard_map/ppermute | solution.py:474
  19.6 17.8 %collective-permute-start.10 = (bf16[4,512,128]{2,1,0:T(8,128)(2,1)S(1)}, bf16[4,512,128]{2,1,0:T(8,128)(2,1)S(1)}, u32[]{:S(2)}, u32[]{:S(2)}) collective-permute-start(bf16[4,512,128]{2,1,0:T(8,128)(2,1)S(1)} %lags.6.refs_2_), channel_id=1, source_target_pairs={{0,1},{3,2},{4,5},{7,6},{8,9},{11,10},{12,13},{15,14},{16,17},{19,... | collective-permute-start | bytes 1572872 | tf_op jit(solution)/shard_map/ppermute | solution.py:475
  23.2 6.0 %collective-permute-start.8 = (bf16[400,256]{1,0:T(8,128)(2,1)S(1)}, bf16[400,256]{1,0:T(8,128)(2,1)S(1)}, u32[]{:S(2)}, u32[]{:S(2)}) collective-permute-start(bf16[400,256]{1,0:T(8,128)(2,1)S(1)} %add.14.refs_4_.refs_0_), channel_id=1, source_target_pairs={{0,16},{4,12},{8,24},{12,4},{16,0},{20,28},{24,8},{28,20},{1,17},{... | collective-permute-start | bytes 614408 | tf_op jit(solution)/shard_map/ppermute | solution.py:474
  29.6 9.8 %collective-permute-start.9 = (bf16[800,256]{1,0:T(8,128)(2,1)S(1)}, bf16[800,256]{1,0:T(8,128)(2,1)S(1)}, u32[]{:S(2)}, u32[]{:S(2)}) collective-permute-start(bf16[800,256]{1,0:T(8,128)(2,1)S(1)} %add.16.refs_4_.refs_0_), channel_id=1, source_target_pairs={{0,16},{4,12},{8,24},{12,4},{16,0},{20,28},{24,8},{28,20},{1,17},{... | collective-permute-start | bytes 1228808 | tf_op jit(solution)/shard_map/ppermute | solution.py:474
  31.2 1.5 %collective-permute-start.11 = (bf16[400,256]{1,0:T(8,128)(2,1)S(1)}, bf16[400,256]{1,0:T(8,128)(2,1)S(1)}, u32[]{:S(2)}, u32[]{:S(2)}) collective-permute-start(bf16[400,256]{1,0:T(8,128)(2,1)S(1)} %add.15.refs_2_.refs_0_), channel_id=1, source_target_pairs={{0,4},{4,0},{8,12},{12,8},{16,20},{20,16},{24,28},{28,24},{1,5},{5... | collective-permute-start | bytes 614408 | tf_op jit(solution)/shard_map/ppermute | solution.py:474
  31.3 17.3 %collective-permute-start.13 = (bf16[4,512,128]{2,1,0:T(8,128)(2,1)S(1)}, bf16[4,512,128]{2,1,0:T(8,128)(2,1)S(1)}, u32[]{:S(2)}, u32[]{:S(2)}) collective-permute-start(bf16[4,512,128]{2,1,0:T(8,128)(2,1)S(1)} %lags.7.refs_4_), channel_id=1, source_target_pairs={{0,1},{3,2},{4,5},{7,6},{8,9},{11,10},{12,13},{15,14},{16,17},{19,... | collective-permute-start | bytes 1572872 | tf_op jit(solution)/shard_map/ppermute | solution.py:475
  37.5 17.6 %collective-permute-start.14 = (bf16[4,512,128]{2,1,0:T(8,128)(2,1)S(1)}, bf16[4,512,128]{2,1,0:T(8,128)(2,1)S(1)}, u32[]{:S(2)}, u32[]{:S(2)}) collective-permute-start(bf16[4,512,128]{2,1,0:T(8,128)(2,1)S(1)} %sum.9.refs_2_), channel_id=1, source_target_pairs={{1,2},{2,1},{5,6},{6,5},{9,10},{10,9},{13,14},{14,13},{17,18},{18,... | collective-permute-start | bytes 1572872 | tf_op jit(solution)/shard_map/ppermute | solution.py:475
  39.5 11.1 %collective-permute-start.12 = (bf16[800,256]{1,0:T(8,128)(2,1)S(1)}, bf16[800,256]{1,0:T(8,128)(2,1)S(1)}, u32[]{:S(2)}, u32[]{:S(2)}) collective-permute-start(bf16[800,256]{1,0:T(8,128)(2,1)S(1)} %add.17.after_ref.refs_0_), channel_id=1, source_target_pairs={{0,4},{4,0},{8,12},{12,8},{16,20},{20,16},{24,28},{28,24},{1,5},{5... | collective-permute-start | bytes 1228808 | tf_op jit(solution)/shard_map/ppermute | solution.py:474
  39.6 15.4 %collective-permute-start.15 = (bf16[2,512,128]{2,1,0:T(8,128)(2,1)S(1)}, bf16[2,512,128]{2,1,0:T(8,128)(2,1)S(1)}, u32[]{:S(2)}, u32[]{:S(2)}) collective-permute-start(bf16[2,512,128]{2,1,0:T(8,128)(2,1)S(1)} %get-tuple-element.29.refs_2_.refs_0_), channel_id=1, source_target_pairs={{0,1},{3,2},{4,5},{7,6},{8,9},{11,10},{12,13},{15,14},{16,17},{19,... | collective-permute-start | bytes 786440 | tf_op jit(solution)/shard_map/ppermute | solution.py:475
  42.5 28.6 %collective-permute-start.20 = (bf16[6,512,128]{2,1,0:T(8,128)(2,1)S(1)}, bf16[6,512,128]{2,1,0:T(8,128)(2,1)S(1)}, u32[]{:S(2)}, u32[]{:S(2)}) collective-permute-start(bf16[6,512,128]{2,1,0:T(8,128)(2,1)S(1)} %lags_rest.1.refs_2_.refs_0_), channel_id=1, source_target_pairs={{0,1},{3,2},{4,5},{7,6},{8,9},{11,10},{12,13},{15,14},{16,17},{19,... | collective-permute-start | bytes 2359304 | tf_op jit(solution)/shard_map/ppermute | solution.py:475
  48.7 17.2 %collective-permute-start.18 = (bf16[4,512,128]{2,1,0:T(8,128)(2,1)S(1)}, bf16[4,512,128]{2,1,0:T(8,128)(2,1)S(1)}, u32[]{:S(2)}, u32[]{:S(2)}) collective-permute-start(bf16[4,512,128]{2,1,0:T(8,128)(2,1)S(1)} %sum.10.refs_4_), channel_id=1, source_target_pairs={{1,2},{2,1},{5,6},{6,5},{9,10},{10,9},{13,14},{14,13},{17,18},{18,... | collective-permute-start | bytes 1572872 | tf_op jit(solution)/shard_map/ppermute | solution.py:475
  55.2 13.9 %collective-permute-start.16 = (bf16[4,512,128]{2,1,0:T(8,128)(2,1)S(1)}, bf16[4,512,128]{2,1,0:T(8,128)(2,1)S(1)}, u32[]{:S(2)}, u32[]{:S(2)}) collective-permute-start(bf16[4,512,128]{2,1,0:T(8,128)(2,1)S(1)} %sum.12.refs_4_), channel_id=1, source_target_pairs={{1,0},{2,3},{5,4},{6,7},{9,8},{10,11},{13,12},{14,15},{17,16},{18,... | collective-permute-start | bytes 1572872 | tf_op jit(solution)/shard_map/ppermute | solution.py:475
  56.5 12.5 %collective-permute-start.17 = (bf16[2,512,128]{2,1,0:T(8,128)(2,1)S(1)}, bf16[2,512,128]{2,1,0:T(8,128)(2,1)S(1)}, u32[]{:S(2)}, u32[]{:S(2)}) collective-permute-start(bf16[2,512,128]{2,1,0:T(8,128)(2,1)S(1)} %sum.11.refs_2_), channel_id=1, source_target_pairs={{1,2},{2,1},{5,6},{6,5},{9,10},{10,9},{13,14},{14,13},{17,18},{18,... | collective-permute-start | bytes 786440 | tf_op jit(solution)/shard_map/ppermute | solution.py:475
  60.5 32.5 %collective-permute-start.22 = (bf16[8,512,128]{2,1,0:T(8,128)(2,1)S(1)}, bf16[8,512,128]{2,1,0:T(8,128)(2,1)S(1)}, u32[]{:S(2)}, u32[]{:S(2)}) collective-permute-start(bf16[8,512,128]{2,1,0:T(8,128)(2,1)S(1)} %lags.10.refs_2_.refs_0_), channel_id=1, source_target_pairs={{0,1},{3,2},{4,5},{7,6},{8,9},{11,10},{12,13},{15,14},{16,17},{19,... | collective-permute-start | bytes 3145736 | tf_op jit(solution)/shard_map/ppermute | solution.py:475
  71.2 20.4 %collective-permute-start.21 = (bf16[6,512,128]{2,1,0:T(8,128)(2,1)S(1)}, bf16[6,512,128]{2,1,0:T(8,128)(2,1)S(1)}, u32[]{:S(2)}, u32[]{:S(2)}) collective-permute-start(bf16[6,512,128]{2,1,0:T(8,128)(2,1)S(1)} %sum.15.refs_4_), channel_id=1, source_target_pairs={{1,2},{2,1},{5,6},{6,5},{9,10},{10,9},{13,14},{14,13},{17,18},{18,... | collective-permute-start | bytes 2359304 | tf_op jit(solution)/shard_map/ppermute | solution.py:475
  73.2 11.9 %collective-permute-start.19 = (bf16[4,512,128]{2,1,0:T(8,128)(2,1)S(1)}, bf16[4,512,128]{2,1,0:T(8,128)(2,1)S(1)}, u32[]{:S(2)}, u32[]{:S(2)}) collective-permute-start(bf16[4,512,128]{2,1,0:T(8,128)(2,1)S(1)} %sum.13.refs_3_), channel_id=1, source_target_pairs={{1,0},{2,3},{5,4},{6,7},{9,8},{10,11},{13,12},{14,15},{17,16},{18,... | collective-permute-start | bytes 1572872 | tf_op jit(solution)/shard_map/ppermute | solution.py:475
